TPU v7x, 32 devices: a whole 2x2x4 slice. The times are simulated.
32 devices in a mesh: groups: 2 (over y), rep: 4 (over x, core), tp: 4 (over z).
Axes of the slice: x: 2, y: 2, z: 4, core: 2. Of those that a mesh axis runs over, the one named last changes fastest.
Arguments:
- activations: bfloat16 [4096, 8192], P(('groups', 'rep'), 'tp'), parts along dimension 0, may hold values from -6 to 6
- row_adapter: int32 [4096, 1], P(('groups', 'rep')), parts along dimension 0, may hold values from 0 to 31; in each aligned block of 512 rows (0 to 511, 512 to 1023, ...) at most 16 rows name the same one
- base_weight: bfloat16 [8192, 4096], P(None, 'tp'), may hold values from -0.0625 to 0.0625
- basis_down: bfloat16 [8192, 256], P('tp'), may hold values from -0.0625 to 0.0625
- adapter_cores: bfloat16 [32, 256, 256], P('rep'), may hold values from -0.375 to 0.375
- basis_up: bfloat16 [256, 4096], P(None, 'tp'), may hold values from -0.375 to 0.375
Outputs:
- queries: bfloat16 [4096, 4096], P(('groups', 'rep'), 'tp'), parts along dimension 0
There are 2 independent parts, one for each index of `groups`. A program takes and returns all parts, laid end to end along the dimension named above; an argument that names none is the same for every part. Nothing has to cross between parts.
Inputs may be any that keep to these rules, and one draw needn't show every extreme that they name: `row_adapter`: in each aligned block of 512 rows (the rows of one replica) no adapter is named by more than 16 rows.
All inputs are finite; a program needn't handle non-finite values.
Results may differ from a plain program's by a relative error of at most 0.0047.
Values may be sent and summed in bfloat16 or wider, within the bound.
No kernel may reach another device: no remote copies, remote signals or barrier semaphores. Data moves between devices by JAX's collectives and lax.ppermute only.
A program may use at most 128 MiB of HBM per device.

v0:
```python
import jax
import jax.numpy as jnp
from jax import lax
from jax.sharding import PartitionSpec as P

BLK = 16


def on_device(activations, row_adapter, base_weight, basis_down, adapter_cores, basis_up):
    width = basis_down.shape[1]
    local_count = adapter_cores.shape[0]
    owners = lax.axis_size("rep")
    all_adapters = local_count * owners
    slot_count = all_adapters * BLK
    base = jnp.dot(
        lax.all_gather(activations, "tp", axis=1, tiled=True),
        base_weight,
        preferred_element_type=jnp.float32,
    )
    partial_value = jnp.dot(activations, basis_down, preferred_element_type=jnp.float32)
    adapter_ids = row_adapter[:, 0]
    onehot = (adapter_ids[:, None] == jnp.arange(all_adapters, dtype=jnp.int32)[None, :]).astype(
        jnp.int32
    )
    earlier = jnp.cumsum(onehot, axis=0) - onehot
    within = jnp.sum(earlier * onehot, axis=1)
    slot_index = adapter_ids * BLK + within
    coded = lax.psum(partial_value, "tp").astype(jnp.bfloat16)
    packed = jnp.zeros((slot_count, width), jnp.bfloat16).at[slot_index].set(coded)
    packed = packed.reshape(owners, local_count, BLK, width)
    mixed_slots = jnp.einsum(
        "nasr,arq->nasq",
        lax.all_to_all(packed, "rep", split_axis=0, concat_axis=0, tiled=True),
        adapter_cores,
        preferred_element_type=jnp.float32,
    ).astype(jnp.bfloat16)
    returned = lax.all_to_all(mixed_slots, "rep", split_axis=0, concat_axis=0, tiled=True).reshape(
        slot_count, width
    )
    mixed = returned[slot_index]
    result = base + jnp.dot(mixed, basis_up, preferred_element_type=jnp.float32)
    return result.astype(jnp.bfloat16)


def solution(mesh):
    placed = (
        P(("groups", "rep"), "tp"),
        P(("groups", "rep"), None),
        P(None, "tp"),
        P("tp", None),
        P("rep", None, None),
        P(None, "tp"),
    )
    return jax.shard_map(
        on_device, mesh=mesh, in_specs=placed, out_specs=P(("groups", "rep"), "tp"), check_vma=False
    )
```

profile of v0, /device:TPU:0, one launch (start us, length us, event | category | flops | bytes accessed | tf_op | source)
XLA Modules:
  0.0 225.8 jit_solution(17492328951910657458)
XLA Ops:
  6.5 0.0 copy-start
  6.5 0.0 all-reduce.2.cloned.1.call-start
  6.5 1.2 copy-done
  7.8 3.1 %fusion.10 = f32[512,256]{1,0:T(8,128)} fusion(bf16[512,2048]{1,0:T(8,128)(2,1)} %param.6, bf16[2048,256]{1,0:T(8,128)(2,1)S(1)} %copy-done), kind=kOutput, calls=%fused_computation.21 | convolution fusion | flops 536870912 | bytes 3670016 | tf_op jit(solution)/shard_map/dot_general | solution.py:20
  10.9 0.0 copy-start.2
  10.9 0.0 copy-start.1
  10.9 0.0 all-reduce.2.cloned.1.call-update
  10.9 0.0 all-gather.2.cloned.1.call-start
  10.9 0.7 all-gather.2.cloned.1.call-update
  11.6 0.0 copy-done.2
  11.7 1.2 reduce-window.6
  12.8 0.2 slice_reduce_fusion
  13.1 0.1 fusion.8
  13.2 38.8 %all-reduce.2.cloned.1.call-done = f32[512,256]{1,0:T(8,128)} async-done(((f32[512,256]{1,0:T(8,128)}), f32[512,256]{1,0:T(8,128)}) %all-reduce.2.cloned.1.call-update) | async-done | bytes 524304 | tf_op jit(solution)/shard_map/psum | solution.py:28
  52.0 2.9 %scatter_custom_fusion = bf16[512,256]{1,0:T(8,128)(2,1)S(1)} fusion(s32[512]{0:T(512)S(1)} %bitcast.43, f32[512,256]{1,0:T(8,128)} %all-reduce.2.cloned.1.call-done, bf16[]{:T(256)} %constant.4.clone.1), kind=kCustom, calls=%fused_computation.7 | custom fusion | flops 131072 | bytes 786434 | tf_op jit(solution)/shard_map/scatter | solution.py:29
  54.9 8.6 %all_to_all.10 = bf16[4,8,16,256]{3,2,1,0:T(8,128)(2,1)S(1)} all-to-all(bf16[4,8,16,256]{3,2,1,0:T(8,128)(2,1)S(1)} %bitcast.40), channel_id=1, replica_groups=mesh['groups'=2,'rep'=4,'tp'=4] {'rep'}, dimensions={0} | all-to-all | bytes 524288 | tf_op jit(solution)/shard_map/all_to_all | solution.py:33
  63.5 0.0 copy-done.1
  63.5 0.3 fusion
  63.8 0.7 copy.12
  64.5 3.4 %all-to-all-start.1 = ((bf16[4,8,16,256]{3,2,1,0:T(8,128)(2,1)}), bf16[4,8,16,256]{3,2,1,0:T(8,128)(2,1)S(1)}, u32[]{:S(2)}, u32[]{:S(2)}) async-start(bf16[4,8,16,256]{3,2,1,0:T(8,128)(2,1)} %copy.12), calls=%async_computation.1 | async-start | bytes 524288 | tf_op jit(solution)/shard_map/all_to_all | solution.py:37
  67.9 6.0 %all-to-all-done.1 = bf16[4,8,16,256]{3,2,1,0:T(8,128)(2,1)S(1)} async-done(((bf16[4,8,16,256]{3,2,1,0:T(8,128)(2,1)}), bf16[4,8,16,256]{3,2,1,0:T(8,128)(2,1)S(1)}, u32[]{:S(2)}, u32[]{:S(2)}) %all-to-all-start.1) | async-done | bytes 262176 | tf_op jit(solution)/shard_map/all_to_all | solution.py:37
  73.9 1.9 gather_fusion
  75.9 1.5 fusion.11
  77.4 125.9 %all-gather.2.cloned.1.call-done = bf16[512,8192]{1,0:T(8,128)(2,1)} async-done(((bf16[512,2048]{1,0:T(8,128)(2,1)}), bf16[512,8192]{1,0:T(8,128)(2,1)}) %all-gather.2.cloned.1.call-update) | async-done | bytes 8388624 | tf_op jit(solution)/shard_map/all_gather | solution.py:16
  203.2 15.7 %add_convert_fusion = bf16[512,1024]{1,0:T(8,128)(2,1)} fusion(f32[512,1024]{1,0:T(8,128)S(1)} %fusion.11, bf16[512,8192]{1,0:T(8,128)(2,1)} %all-gather.2.cloned.1.call-done, bf16[8192,1024]{1,0:T(8,128)(2,1)} %param.8), kind=kOutput, calls=%fused_computation.2 | convolution fusion | flops 8590983168 | bytes 28311552 | tf_op jit(solution)/shard_map/dot_general | solution.py:15
  (5 shorter events, 0.1 us)
Async XLA Ops:
  6.5 1.2 copy-start
  6.5 45.5 %all-reduce.2.cloned.1.call-start = ((), (), s32[]{:S(2)}) async-start(), calls=%async_computation.3 | async-start | bytes 1048576 | tf_op jit(solution)/shard_map/psum | solution.py:28
  10.9 0.8 copy-start.2
  10.9 52.6 %copy-start.1 = (bf16[8,256,256]{2,1,0:T(8,128)(2,1)S(1)}, bf16[8,256,256]{2,1,0:T(8,128)(2,1)}, u32[]{:S(2)}) copy-start(bf16[8,256,256]{2,1,0:T(8,128)(2,1)} %param.10) | copy-start | bytes 3145732
  10.9 192.4 %all-gather.2.cloned.1.call-start = ((), (), s32[]{:S(2)}) async-start(), calls=%async_computation.2 | async-start | bytes 10485760 | tf_op jit(solution)/shard_map/all_gather | solution.py:16
  64.5 9.4 %all-to-all-start.1 = ((bf16[4,8,16,256]{3,2,1,0:T(8,128)(2,1)}), bf16[4,8,16,256]{3,2,1,0:T(8,128)(2,1)S(1)}, u32[]{:S(2)}, u32[]{:S(2)}) async-start(bf16[4,8,16,256]{3,2,1,0:T(8,128)(2,1)} %copy.12), calls=%async_computation.1 | async-start | bytes 524288 | tf_op jit(solution)/shard_map/all_to_all | solution.py:37
Sparse Core Ops, SparseCore 0:
  11.0 40.9 all-reduce.1
  53.6 149.6 all-gather.1
where the time goes:
time: 226 us
  waiting for transfers between devices  171 us (76%)
  matrix products  20.6 us (9%)
  between operations  13.5 us (6%)
  blocking collectives  8.58 us (4%)
  other arithmetic  4.2 us (2%)
  local copies, waits for them, and re-layouts  4.13 us (2%)
  starting transfers between devices  3.46 us (2%)
    all_gather x1, waiting for transfers between devices, on_device(): lax.all_gather(activations, 'tp', axis=1, tiled=True)  126 us
    psum x1, waiting for transfers between devices, on_device(): coded = lax.psum(partial_value, 'tp').astype(jnp.bfloat16)  38.8 us
    dot_general x1, matrix products, on_device(): jnp.dot(lax.all_gather(activations, 'tp', axis=1, tiled=True), base_weigh...  15.7 us
    all_to_all x1, blocking collectives, on_device(): lax.all_to_all(packed, 'rep', split_axis=0, concat_axis=0, tiled=True)  8.58 us
    all_to_all x1, waiting for transfers between devices, on_device(): lax.all_to_all(mixed_slots, 'rep', split_axis=0, concat_axis=0, tiled=True)  5.99 us
  transfers between devices with their start and end apart: 3, of which 3 were waited for; matrix products, arithmetic and copies ran while one was open for 4% of the time, Pallas kernels for 0%

commit v1 on v0

--- a/solution.py
+++ b/solution.py
@@ -1,23 +1,117 @@
+import functools
+
 import jax
 import jax.numpy as jnp
 from jax import lax
+from jax.experimental import pallas as pl
+from jax.experimental.pallas import tpu as pltpu
 from jax.sharding import PartitionSpec as P
 
 BLK = 16
 
 
-def on_device(activations, row_adapter, base_weight, basis_down, adapter_cores, basis_up):
+def dot(a, b):
+    return jnp.dot(a, b, preferred_element_type=jnp.float32)
+
+
+def shift(x, axis, by):
+    n = lax.axis_size(axis)
+    return lax.ppermute(x, axis, [(i, (i + by) % n) for i in range(n)])
+
+
+def mix_kernel(ids_ref, coded_ref, cores_ref, mixed_ref, slots_ref):
+    rows = coded_ref.shape[0]
+    adapters = cores_ref.shape[0]
+    ids = ids_ref[...]
+    named = ids == lax.broadcasted_iota(jnp.int32, (rows, adapters), 1)
+    below = lax.broadcasted_iota(jnp.int32, (rows, rows), 0) > lax.broadcasted_iota(
+        jnp.int32, (rows, rows), 1
+    )
+    earlier = dot(below.astype(jnp.bfloat16), named.astype(jnp.bfloat16))
+    within = jnp.sum(jnp.where(named, earlier, 0.0), axis=1, keepdims=True).astype(jnp.int32)
+    slot = ids * BLK + within
+    place = (slot == lax.broadcasted_iota(jnp.int32, (rows, adapters * BLK), 1)).astype(
+        jnp.bfloat16
+    )
+    packed = lax.dot_general(
+        place, coded_ref[...], (((0,), (0,)), ((), ())), preferred_element_type=jnp.float32
+    ).astype(jnp.bfloat16)
+    for a in range(adapters):
+        slots_ref[a * BLK : (a + 1) * BLK, :] = dot(
+            packed[a * BLK : (a + 1) * BLK, :], cores_ref[a]
+        ).astype(jnp.bfloat16)
+    mixed_ref[...] = dot(place, slots_ref[...]).astype(jnp.bfloat16)
+
+
+def mix(ids, coded, cores):
+    rows, width = coded.shape
+    adapters = cores.shape[0]
+    return pl.pallas_call(
+        mix_kernel,
+        out_shape=jax.ShapeDtypeStruct((rows, width), jnp.bfloat16),
+        scratch_shapes=[pltpu.VMEM((adapters * BLK, width), jnp.bfloat16)],
+        compiler_params=pltpu.CompilerParams(vmem_limit_bytes=32 * 2**20),
+        cost_estimate=pl.CostEstimate(
+            flops=2 * rows * width * (3 * adapters * BLK),
+            bytes_accessed=cores.size * 2 + rows * width * 4,
+            transcendentals=0,
+        ),
+        name="mix",
+    )(ids, coded, cores)
+
+
+def all_cores(cores):
+    rep = lax.axis_index("rep")
+    core, x = rep % 2, rep // 2
+    mate = lax.ppermute(cores, "rep", [(i, i ^ 1) for i in range(4)])
+    across = lax.ppermute(cores, "rep", [(i, i ^ 2) for i in range(4)])
+    corner = lax.ppermute(across, "rep", [(i, i ^ 1) for i in range(4)])
+    held = [cores, mate, across, corner]
+
+    def from_rep(r):
+        other = rep ^ r
+        return lax.select_n(other, *held)
+
+    return jnp.concatenate([from_rep(r) for r in range(4)], axis=0)
+
+
+def on_line(activations, row_adapter, base_weight, basis_down, adapter_cores, basis_up):
+    me = lax.axis_index("tp")
+    depth = activations.shape[1]
+    half = activations.shape[0] // 2
+
+    def weight_of(owner):
+        return lax.dynamic_slice_in_dim(base_weight, (owner % 4) * depth, depth, 0)
+
+    partial_value = dot(activations, basis_down)
+    top, bottom = activations[:half], activations[half:]
+    right_top = shift(top, "tp", 1)
+    left_bottom = shift(bottom, "tp", -1)
+    right_bottom = shift(bottom, "tp", 1)
+    left_top = shift(top, "tp", -1)
+    far_top = shift(right_top, "tp", 1)
+    far_bottom = shift(left_bottom, "tp", -1)
+
+    pair = partial_value + lax.ppermute(partial_value, "tp", [(0, 1), (1, 0), (2, 3), (3, 2)])
+    total = pair + lax.ppermute(pair, "tp", [(0, 3), (3, 0), (1, 2), (2, 1)])
+    coded = total.astype(jnp.bfloat16)
+    mixed = mix(row_adapter, coded, all_cores(adapter_cores))
+
+    base = dot(activations, weight_of(me)) + dot(mixed, basis_up)
+    base = base + dot(jnp.concatenate([right_top, right_bottom], 0), weight_of(me + 3))
+    base = base + dot(jnp.concatenate([left_top, left_bottom], 0), weight_of(me + 1))
+    base = base + dot(jnp.concatenate([far_top, far_bottom], 0), weight_of(me + 2))
+    return base.astype(jnp.bfloat16)
+
+
+def on_any(activations, row_adapter, base_weight, basis_down, adapter_cores, basis_up):
     width = basis_down.shape[1]
     local_count = adapter_cores.shape[0]
     owners = lax.axis_size("rep")
     all_adapters = local_count * owners
     slot_count = all_adapters * BLK
-    base = jnp.dot(
-        lax.all_gather(activations, "tp", axis=1, tiled=True),
-        base_weight,
-        preferred_element_type=jnp.float32,
-    )
-    partial_value = jnp.dot(activations, basis_down, preferred_element_type=jnp.float32)
+    base = dot(lax.all_gather(activations, "tp", axis=1, tiled=True), base_weight)
+    partial_value = dot(activations, basis_down)
     adapter_ids = row_adapter[:, 0]
     onehot = (adapter_ids[:, None] == jnp.arange(all_adapters, dtype=jnp.int32)[None, :]).astype(
         jnp.int32
@@ -38,8 +132,7 @@
         slot_count, width
     )
     mixed = returned[slot_index]
-    result = base + jnp.dot(mixed, basis_up, preferred_element_type=jnp.float32)
-    return result.astype(jnp.bfloat16)
+    return (base + dot(mixed, basis_up)).astype(jnp.bfloat16)
 
 
 def solution(mesh):
@@ -51,6 +144,11 @@
         P("rep", None, None),
         P(None, "tp"),
     )
+    short = mesh.shape["tp"] == 4 and mesh.shape["rep"] == 4
     return jax.shard_map(
-        on_device, mesh=mesh, in_specs=placed, out_specs=P(("groups", "rep"), "tp"), check_vma=False
+        on_line if short else on_any,
+        mesh=mesh,
+        in_specs=placed,
+        out_specs=P(("groups", "rep"), "tp"),
+        check_vma=False,
     )

time: 226 us -> 182 us (0.81)
  the two profiles are of different devices: /device:TPU:0 before, /device:TPU:14 now
where the time goes in v1:
time: 182 us; the launch traced here: 181 us
  waiting for transfers between devices  138 us (76%)
  matrix products  24.4 us (13%)
  starting transfers between devices  10.4 us (6%)
  local copies, waits for them, and re-layouts  3.67 us (2%)
  other arithmetic  2.8 us (2%)
  Pallas kernels  2.07 us (1%)
    ppermute x6, waiting for transfers between devices, shift(): return lax.ppermute(x, axis, [(i, (i + by) % n) for i in range(n)])  73.3 us
    ppermute x1, waiting for transfers between devices, on_line(): total = pair + lax.ppermute(pair, 'tp', [(0, 3), (3, 0), (1, 2), (2, 1)])  51.8 us
    dot_general x6, matrix products, dot(): return jnp.dot(a, b, preferred_element_type=jnp.float32)  24.4 us
    ppermute x1, waiting for transfers between devices, on_line(): lax.ppermute(partial_value, 'tp', [(0, 1), (1, 0), (2, 3), (3, 2)])  10.2 us
    ppermute x6, starting transfers between devices, shift(): return lax.ppermute(x, axis, [(i, (i + by) % n) for i in range(n)])  7.67 us
  transfers between devices with their start and end apart: 11, of which 6 were waited for; matrix products, arithmetic and copies ran while one was open for 13% of the time, Pallas kernels for 1%

profile of v1, /device:TPU:14, one launch (start us, length us, event | category | flops | bytes accessed | tf_op | source)
XLA Modules:
  0.0 181.4 jit_solution(17003613624928059040)
XLA Ops:
  0.0 0.0 copy-start
  0.0 0.0 copy-start.1
  0.0 0.5 collective-permute-start.3
  0.5 0.7 copy-done
  1.2 2.3 %fusion.33 = f32[512,256]{1,0:T(8,128)S(1)} fusion(bf16[512,2048]{1,0:T(8,128)(2,1)} %param.6, bf16[2048,256]{1,0:T(8,128)(2,1)S(1)} %copy-done), kind=kOutput, calls=%fused_computation.36 | convolution fusion | flops 536870912 | bytes 3670016 | tf_op jit(solution)/shard_map/dot_general | solution.py:14
  3.5 0.0 copy-start.2
  3.5 0.5 collective-permute-start
  4.1 0.0 copy-done.1
  4.1 1.5 fusion.32
  5.6 2.7 %collective-permute-start.5 = (bf16[256,2048]{1,0:T(8,128)(2,1)}, bf16[256,2048]{1,0:T(8,128)(2,1)}, u32[]{:S(2)}, u32[]{:S(2)}) collective-permute-start(bf16[256,2048]{1,0:T(8,128)(2,1)} %get-tuple-element.9), channel_id=1, source_target_pairs={{0,1},{1,2},{2,3},{3,0},{4,5},{5,6},{6,7},{7,4},{8,9},{9,10},{10,1... | collective-permute-start | bytes 3145736 | tf_op jit(solution)/shard_map/ppermute | solution.py:19
  8.3 10.2 %collective-permute-done = f32[512,256]{1,0:T(8,128)S(1)} collective-permute-done((f32[512,256]{1,0:T(8,128)S(1)}, f32[512,256]{1,0:T(8,128)S(1)}, u32[]{:S(2)}, u32[]{:S(2)}) %collective-permute-start) | collective-permute-done | bytes 524320 | tf_op jit(solution)/shard_map/ppermute | solution.py:95
  18.4 0.1 add.54
  18.5 1.6 collective-permute-start.1
  20.1 2.5 %collective-permute-start.8 = (bf16[256,2048]{1,0:T(8,128)(2,1)}, bf16[256,2048]{1,0:T(8,128)(2,1)}, u32[]{:S(2)}, u32[]{:S(2)}) collective-permute-start(bf16[256,2048]{1,0:T(8,128)(2,1)} %get-tuple-element.10), channel_id=1, source_target_pairs={{0,3},{1,0},{2,1},{3,2},{4,7},{5,4},{6,5},{7,6},{8,11},{9,8},{10,9... | collective-permute-start | bytes 3145736 | tf_op jit(solution)/shard_map/ppermute | solution.py:19
  22.6 0.0 collective-permute-start.6
  22.6 0.0 copy-start.4
  22.6 2.6 %collective-permute-done.3 = bf16[8,256,256]{2,1,0:T(8,128)(2,1)} collective-permute-done((bf16[8,256,256]{2,1,0:T(8,128)(2,1)}, bf16[8,256,256]{2,1,0:T(8,128)(2,1)}, u32[]{:S(2)}, u32[]{:S(2)}) %collective-permute-start.3) | collective-permute-done | bytes 1048608 | tf_op jit(solution)/shard_map/ppermute | solution.py:67
  25.2 0.0 copy-done.2
  25.2 0.0 collective-permute-start.2
  25.2 51.8 %collective-permute-done.1 = f32[512,256]{1,0:T(8,128)S(1)} collective-permute-done((f32[512,256]{1,0:T(8,128)S(1)}, f32[512,256]{1,0:T(8,128)S(1)}, u32[]{:S(2)}, u32[]{:S(2)}) %collective-permute-start.1) | collective-permute-done | bytes 524320 | tf_op jit(solution)/shard_map/ppermute | solution.py:96
  77.0 0.0 collective-permute-start.7
  77.0 0.0 collective-permute-done.5
  77.0 0.0 collective-permute-start.4
  77.0 6.6 %fusion.6 = f32[1024,512]{1,0:T(8,128)} fusion(bf16[512,2048]{1,0:T(8,128)(2,1)} %param.6, bf16[8192,1024]{1,0:T(8,128)(2,1)} %param.8, s32[]{:T(128)S(6)} %select_n.140), kind=kOutput, calls=%fused_computation.7 | convolution fusion | flops 2147483648 | bytes 8388612 | tf_op jit(solution)/shard_map/dot_general | solution.py:14
  83.6 0.0 copy-done.4
  83.6 0.1 copy.7.ids_ref
  83.8 0.1 add_convert_fusion.coded_ref
  83.9 24.5 %collective-permute-done.8 = bf16[256,2048]{1,0:T(8,128)(2,1)} collective-permute-done((bf16[256,2048]{1,0:T(8,128)(2,1)}, bf16[256,2048]{1,0:T(8,128)(2,1)}, u32[]{:S(2)}, u32[]{:S(2)}) %collective-permute-start.8) | collective-permute-done | bytes 1048608 | tf_op jit(solution)/shard_map/ppermute | solution.py:19
  108.4 0.0 collective-permute-start.10
  108.4 34.7 %collective-permute-done.6 = bf16[256,2048]{1,0:T(8,128)(2,1)} collective-permute-done((bf16[256,2048]{1,0:T(8,128)(2,1)}, bf16[256,2048]{1,0:T(8,128)(2,1)}, u32[]{:S(2)}, u32[]{:S(2)}) %collective-permute-start.6) | collective-permute-done | bytes 1048608 | tf_op jit(solution)/shard_map/ppermute | solution.py:19
  143.1 2.5 %collective-permute-start.9 = (bf16[256,2048]{1,0:T(8,128)(2,1)}, bf16[256,2048]{1,0:T(8,128)(2,1)S(1)}, u32[]{:S(2)}, u32[]{:S(2)}) collective-permute-start(bf16[256,2048]{1,0:T(8,128)(2,1)} %collective-permute-done.5), channel_id=1, source_target_pairs={{0,1},{1,2},{2,3},{3,0},{4,5},{5,6},{6,7},{7,4},{8,9},{9,10},{10,1... | collective-permute-start | bytes 3145736 | tf_op jit(solution)/shard_map/ppermute | solution.py:19
  145.6 5.2 %fusion.4 = f32[512,1024]{0,1:T(8,128)S(1)} fusion(bf16[8192,1024]{1,0:T(8,128)(2,1)} %param.8, s32[]{:T(128)S(6)} %select_n.178, bf16[256,2048]{1,0:T(8,128)(2,1)} %collective-permute-done.6, bf16[256,2048]{1,0:T(8,128)(2,1)} %collective-permute-done.5), kind=kOutput, calls=%fused_computation.5 | convolution fusion | flops 2151677952 | bytes 8388612 | tf_op jit(solution)/shard_map/dot_general | solution.py:14
  150.8 0.0 collective-permute-done.7
  150.8 5.2 %fusion.2 = f32[512,1024]{0,1:T(8,128)S(1)} fusion(bf16[8192,1024]{1,0:T(8,128)(2,1)} %param.8, s32[]{:T(128)S(6)} %select_n.180, bf16[256,2048]{1,0:T(8,128)(2,1)} %collective-permute-done.8, bf16[256,2048]{1,0:T(8,128)(2,1)} %collective-permute-done.7), kind=kOutput, calls=%fused_computation.3 | convolution fusion | flops 2151677952 | bytes 8388612 | tf_op jit(solution)/shard_map/dot_general | solution.py:14
  156.0 0.0 collective-permute-done.2
  156.0 0.0 collective-permute-done.4
  156.0 2.1 %select_select_fusion.3 = (bf16[8,256,256]{2,1,0:T(8,128)(2,1)S(1)}, bf16[8,256,256]{2,1,0:T(8,128)(2,1)S(1)}, bf16[8,256,256]{2,1,0:T(8,128)(2,1)S(1)}, bf16[8,256,256]{2,1,0:T(8,128)(2,1)S(1)}) fusion(bf16[8,256,256]{2,1,0:T(8,128)(2,1)} %collective-permute-done.3, bf16[8,256,256]{2,1,0:T(8,128)(2,1)} %collective-permute-done.4, ...), kind=kLoop, calls=%fused_computation.26 | loop fusion | flops 6291456 | bytes 8388620 | tf_op jit(solution)/shard_map/select_n | solution.py:73
  158.1 0.6 pad_maximum_fusion.cores_ref
  158.7 0.0 copy-start.3
  158.7 2.1 %mix.1 = bf16[512,256]{1,0:T(8,128)(2,1)S(1)} custom-call(s32[512,1]{1,0:T(8,128)S(1)} %copy.7.ids_ref, bf16[512,256]{1,0:T(8,128)(2,1)S(1)} %add_convert_fusion.coded_ref, bf16[32,256,256]{2,1,0:T(8,128)(2,1)S(1)} %pad_maximum_fusion.cores_ref), custom_call_target="tpu_custom_call" | custom-call | flops 402653184 | bytes 4718592 | tf_op jit(solution)/shard_map/mix/pallas_call | solution.py:49
  160.8 0.0 copy-done.3
  160.8 0.0 copy-start.5
  160.8 0.5 fusion.34
  161.3 14.1 %collective-permute-done.10 = bf16[256,2048]{1,0:T(8,128)(2,1)S(1)} collective-permute-done((bf16[256,2048]{1,0:T(8,128)(2,1)}, bf16[256,2048]{1,0:T(8,128)(2,1)S(1)}, u32[]{:S(2)}, u32[]{:S(2)}) %collective-permute-start.10) | collective-permute-done | bytes 1048608 | tf_op jit(solution)/shard_map/ppermute | solution.py:19
  175.4 0.0 collective-permute-done.9
  175.4 0.0 copy-done.5
  175.4 4.7 %fusion.20 = bf16[512,1024]{0,1:T(8,128)(2,1)S(1)} fusion(f32[512,1024]{0,1:T(8,128)S(1)} %fusion.2, f32[512,1024]{0,1:T(8,128)S(1)} %fusion.4, f32[512,1024]{0,1:T(8,128)S(1)} %fusion.34, f32[1024,512]{1,0:T(8,128)S(1)} %copy-done.5, bf16[8192,1024]{1,0:T(8,128)(2,1)} %param.8, s32[]{:T(128)S(6)} %select_n.182, ...), kind=kOutput, calls=%fused_computation.22 | convolution fusion | flops 2154299392 | bytes 15728644 | tf_op jit(solution)/shard_map/dot_general | solution.py:14
  180.1 1.3 copy.12
Async XLA Ops:
  0.0 1.2 copy-start
  0.0 4.1 %copy-start.1 = (bf16[512,2048]{1,0:T(8,128)(2,1)S(1)}, bf16[512,2048]{1,0:T(8,128)(2,1)}, u32[]{:S(2)}) copy-start(bf16[512,2048]{1,0:T(8,128)(2,1)} %param.6) | copy-start | bytes 6291460
  0.0 25.2 %collective-permute-start.3 = (bf16[8,256,256]{2,1,0:T(8,128)(2,1)}, bf16[8,256,256]{2,1,0:T(8,128)(2,1)}, u32[]{:S(2)}, u32[]{:S(2)}) collective-permute-start(bf16[8,256,256]{2,1,0:T(8,128)(2,1)} %param.10), channel_id=1, source_target_pairs={{0,8},{4,12},{8,0},{12,4},{1,9},{5,13},{9,1},{13,5},{2,10},{6,14},... | collective-permute-start | bytes 3145736 | tf_op jit(solution)/shard_map/ppermute | solution.py:67
  3.5 21.7 %copy-start.2 = (bf16[8,256,256]{2,1,0:T(8,128)(2,1)S(1)}, bf16[8,256,256]{2,1,0:T(8,128)(2,1)}, u32[]{:S(2)}) copy-start(bf16[8,256,256]{2,1,0:T(8,128)(2,1)} %param.10) | copy-start | bytes 3145732
  3.5 14.9 %collective-permute-start = (f32[512,256]{1,0:T(8,128)S(1)}, f32[512,256]{1,0:T(8,128)S(1)}, u32[]{:S(2)}, u32[]{:S(2)}) collective-permute-start(f32[512,256]{1,0:T(8,128)S(1)} %fusion.33), channel_id=1, source_target_pairs={{0,1},{1,0},{2,3},{3,2},{4,5},{5,4},{6,7},{7,6},{8,9},{9,8},{10,11... | collective-permute-start | bytes 1572872 | tf_op jit(solution)/shard_map/ppermute | solution.py:95
  5.6 71.5 %collective-permute-start.5 = (bf16[256,2048]{1,0:T(8,128)(2,1)}, bf16[256,2048]{1,0:T(8,128)(2,1)}, u32[]{:S(2)}, u32[]{:S(2)}) collective-permute-start(bf16[256,2048]{1,0:T(8,128)(2,1)} %get-tuple-element.9), channel_id=1, source_target_pairs={{0,1},{1,2},{2,3},{3,0},{4,5},{5,6},{6,7},{7,4},{8,9},{9,10},{10,1... | collective-permute-start | bytes 3145736 | tf_op jit(solution)/shard_map/ppermute | solution.py:19
  18.5 58.5 %collective-permute-start.1 = (f32[512,256]{1,0:T(8,128)S(1)}, f32[512,256]{1,0:T(8,128)S(1)}, u32[]{:S(2)}, u32[]{:S(2)}) collective-permute-start(f32[512,256]{1,0:T(8,128)S(1)} %add.54), channel_id=1, source_target_pairs={{0,3},{3,0},{1,2},{2,1},{4,7},{7,4},{5,6},{6,5},{8,11},{11,8},{9,1... | collective-permute-start | bytes 1572872 | tf_op jit(solution)/shard_map/ppermute | solution.py:96
  20.1 88.2 %collective-permute-start.8 = (bf16[256,2048]{1,0:T(8,128)(2,1)}, bf16[256,2048]{1,0:T(8,128)(2,1)}, u32[]{:S(2)}, u32[]{:S(2)}) collective-permute-start(bf16[256,2048]{1,0:T(8,128)(2,1)} %get-tuple-element.10), channel_id=1, source_target_pairs={{0,3},{1,0},{2,1},{3,2},{4,7},{5,4},{6,5},{7,6},{8,11},{9,8},{10,9... | collective-permute-start | bytes 3145736 | tf_op jit(solution)/shard_map/ppermute | solution.py:19
  22.6 120.5 %collective-permute-start.6 = (bf16[256,2048]{1,0:T(8,128)(2,1)}, bf16[256,2048]{1,0:T(8,128)(2,1)}, u32[]{:S(2)}, u32[]{:S(2)}) collective-permute-start(bf16[256,2048]{1,0:T(8,128)(2,1)} %get-tuple-element.10), channel_id=1, source_target_pairs={{0,1},{1,2},{2,3},{3,0},{4,5},{5,6},{6,7},{7,4},{8,9},{9,10},{10,1... | collective-permute-start | bytes 3145736 | tf_op jit(solution)/shard_map/ppermute | solution.py:19
  22.6 61.0 %copy-start.4 = (s32[512,1]{0,1:T(1,128)S(1)}, s32[512,1]{0,1:T(1,128)}, u32[]{:S(2)}) copy-start(s32[512,1]{0,1:T(1,128)} %param.7) | copy-start | bytes 6148
  25.2 130.8 %collective-permute-start.2 = (bf16[8,256,256]{2,1,0:T(8,128)(2,1)S(1)}, bf16[8,256,256]{2,1,0:T(8,128)(2,1)}, u32[]{:S(2)}, u32[]{:S(2)}) collective-permute-start(bf16[8,256,256]{2,1,0:T(8,128)(2,1)S(1)} %copy-done.2), channel_id=1, source_target_pairs={{0,4},{4,0},{8,12},{12,8},{1,5},{5,1},{9,13},{13,9},{2,6},{6,2},{1... | collective-permute-start | bytes 3145736 | tf_op jit(solution)/shard_map/ppermute | solution.py:66
  77.0 73.7 %collective-permute-start.7 = (bf16[256,2048]{1,0:T(8,128)(2,1)}, bf16[256,2048]{1,0:T(8,128)(2,1)}, u32[]{:S(2)}, u32[]{:S(2)}) collective-permute-start(bf16[256,2048]{1,0:T(8,128)(2,1)} %get-tuple-element.9), channel_id=1, source_target_pairs={{0,3},{1,0},{2,1},{3,2},{4,7},{5,4},{6,5},{7,6},{8,11},{9,8},{10,9... | collective-permute-start | bytes 3145736 | tf_op jit(solution)/shard_map/ppermute | solution.py:19
  77.0 79.0 %collective-permute-start.4 = (bf16[8,256,256]{2,1,0:T(8,128)(2,1)}, bf16[8,256,256]{2,1,0:T(8,128)(2,1)}, u32[]{:S(2)}, u32[]{:S(2)}) collective-permute-start(bf16[8,256,256]{2,1,0:T(8,128)(2,1)} %collective-permute-done.3), channel_id=1, source_target_pairs={{0,4},{4,0},{8,12},{12,8},{1,5},{5,1},{9,13},{13,9},{2,6},{6,2},{1... | collective-permute-start | bytes 3145736 | tf_op jit(solution)/shard_map/ppermute | solution.py:68
  108.4 67.0 %collective-permute-start.10 = (bf16[256,2048]{1,0:T(8,128)(2,1)}, bf16[256,2048]{1,0:T(8,128)(2,1)S(1)}, u32[]{:S(2)}, u32[]{:S(2)}) collective-permute-start(bf16[256,2048]{1,0:T(8,128)(2,1)} %collective-permute-done.8), channel_id=1, source_target_pairs={{0,3},{1,0},{2,1},{3,2},{4,7},{5,4},{6,5},{7,6},{8,11},{9,8},{10,9... | collective-permute-start | bytes 3145736 | tf_op jit(solution)/shard_map/ppermute | solution.py:19
  143.1 32.3 %collective-permute-start.9 = (bf16[256,2048]{1,0:T(8,128)(2,1)}, bf16[256,2048]{1,0:T(8,128)(2,1)S(1)}, u32[]{:S(2)}, u32[]{:S(2)}) collective-permute-start(bf16[256,2048]{1,0:T(8,128)(2,1)} %collective-permute-done.5), channel_id=1, source_target_pairs={{0,1},{1,2},{2,3},{3,0},{4,5},{5,6},{6,7},{7,4},{8,9},{9,10},{10,1... | collective-permute-start | bytes 3145736 | tf_op jit(solution)/shard_map/ppermute | solution.py:19
  158.7 2.1 %copy-start.3 = (bf16[256,1024]{1,0:T(8,128)(2,1)S(1)}, bf16[256,1024]{1,0:T(8,128)(2,1)}, u32[]{:S(2)}) copy-start(bf16[256,1024]{1,0:T(8,128)(2,1)} %param.11) | copy-start | bytes 1572868
  160.8 14.6 %copy-start.5 = (f32[1024,512]{1,0:T(8,128)S(1)}, f32[1024,512]{1,0:T(8,128)}, u32[]{:S(2)}) copy-start(f32[1024,512]{1,0:T(8,128)} %fusion.6) | copy-start | bytes 6291460

commit v2 on v1

--- a/solution.py
+++ b/solution.py
@@ -12,11 +12,6 @@
 
 def dot(a, b):
     return jnp.dot(a, b, preferred_element_type=jnp.float32)
-
-
-def shift(x, axis, by):
-    n = lax.axis_size(axis)
-    return lax.ppermute(x, axis, [(i, (i + by) % n) for i in range(n)])
 
 
 def mix_kernel(ids_ref, coded_ref, cores_ref, mixed_ref, slots_ref):
@@ -60,11 +55,54 @@
     )(ids, coded, cores)
 
 
-def all_cores(cores):
+def lend_kernel(spot_ref, x_ref, *rest, blocks, width):
+    count = 1 + max(b[0] for b in blocks)
+    weights, out_ref = rest[:count], rest[-1]
+    add_ref = rest[count] if len(rest) > count + 1 else None
+    spot = spot_ref[0]
+    pieces = sum(len(b[2]) for b in blocks)
+    piece = x_ref.shape[1] // pieces
+    columns = [
+        jnp.concatenate(
+            [x_ref[:, pl.ds(pl.multiple_of((spot ^ m) * piece, piece), piece)] for m in masks],
+            axis=1,
+        )
+        for _, _, masks in blocks
+    ]
+    for n in range(0, out_ref.shape[1], width):
+        part = slice(n, n + width)
+        value = 0.0 if add_ref is None else add_ref[:, part]
+        for x, (operand, row, masks) in zip(columns, blocks):
+            value = value + dot(x, weights[operand][row : row + piece * len(masks), part])
+        out_ref[:, part] = value.astype(out_ref.dtype)
+
+
+def lend(spot, x, weights, blocks, add, dtype, name):
+    rows, depth = x.shape
+    columns = weights[0].shape[1]
+    whole = pl.BlockSpec(memory_space=pltpu.VMEM)
+    operands = (spot.reshape(1), x, *weights) + (() if add is None else (add,))
+    return pl.pallas_call(
+        functools.partial(lend_kernel, blocks=blocks, width=256),
+        out_shape=jax.ShapeDtypeStruct((rows, columns), dtype),
+        in_specs=[pl.BlockSpec(memory_space=pltpu.SMEM)] + [whole] * (len(operands) - 1),
+        out_specs=whole,
+        compiler_params=pltpu.CompilerParams(vmem_limit_bytes=24 * 2**20),
+        cost_estimate=pl.CostEstimate(
+            flops=2 * rows * depth * columns,
+            bytes_accessed=depth * columns * 2 + rows * (depth + columns) * 2,
+            transcendentals=0,
+        ),
+        name=name,
+    )(*operands)
+
+
+def all_cores(cores, ahead):
     rep = lax.axis_index("rep")
     core, x = rep % 2, rep // 2
     mate = lax.ppermute(cores, "rep", [(i, i ^ 1) for i in range(4)])
     across = lax.ppermute(cores, "rep", [(i, i ^ 2) for i in range(4)])
+    across, mate, ahead = lax.optimization_barrier((across, mate, ahead))
     corner = lax.ppermute(across, "rep", [(i, i ^ 1) for i in range(4)])
     held = [cores, mate, across, corner]
 
@@ -72,36 +110,95 @@
         other = rep ^ r
         return lax.select_n(other, *held)
 
-    return jnp.concatenate([from_rep(r) for r in range(4)], axis=0)
+    return jnp.concatenate([from_rep(r) for r in range(4)], axis=0), ahead
+
+
+IN = [(0, 1), (3, 2)]
+OUT = [(1, 0), (2, 3)]
+SWAP = [(1, 2), (2, 1)]
+
+
+def send(x, pairs):
+    return lax.ppermute(x, "tp", pairs)
+
+
+def swap_rep(x, bit):
+    return lax.ppermute(x, "rep", [(i, i ^ bit) for i in range(4)])
+
+
+def swap_groups(x):
+    return lax.ppermute(x, "groups", [(0, 1), (1, 0)])
 
 
 def on_line(activations, row_adapter, base_weight, basis_down, adapter_cores, basis_up):
     me = lax.axis_index("tp")
-    depth = activations.shape[1]
-    half = activations.shape[0] // 2
+    inner = (me == 1) | (me == 2)
+    left = me < 2
+    near_in, far_in = jnp.where(left, 1, 2), jnp.where(left, 2, 1)
+    near_out, far_out = jnp.where(left, 0, 3), jnp.where(left, 3, 0)
+    spot = lax.axis_index("groups") * 4 + lax.axis_index("rep")
+    rows, depth = activations.shape
+    piece = depth // 8
+    cuts = (0, rows // 2, rows * 3 // 4, rows)
+    parts = [slice(a, b) for a, b in zip(cuts, cuts[1:])]
 
     def weight_of(owner):
-        return lax.dynamic_slice_in_dim(base_weight, (owner % 4) * depth, depth, 0)
-
+        return lax.dynamic_slice_in_dim(base_weight, owner * depth, depth, 0)
+
+    def piece_of(owner):
+        return lax.dynamic_slice_in_dim(base_weight, owner * depth + spot * piece, piece, 0)
+
+    pieces = send(jnp.concatenate([piece_of(near_in), piece_of(far_out)], axis=0), IN)
+    first = send(activations[: rows // 2], SWAP)
     partial_value = dot(activations, basis_down)
-    top, bottom = activations[:half], activations[half:]
-    right_top = shift(top, "tp", 1)
-    left_bottom = shift(bottom, "tp", -1)
-    right_bottom = shift(bottom, "tp", 1)
-    left_top = shift(top, "tp", -1)
-    far_top = shift(right_top, "tp", 1)
-    far_bottom = shift(left_bottom, "tp", -1)
-
-    pair = partial_value + lax.ppermute(partial_value, "tp", [(0, 1), (1, 0), (2, 3), (3, 2)])
-    total = pair + lax.ppermute(pair, "tp", [(0, 3), (3, 0), (1, 2), (2, 1)])
-    coded = total.astype(jnp.bfloat16)
-    mixed = mix(row_adapter, coded, all_cores(adapter_cores))
+    side = partial_value + send(partial_value, IN)
+    cores, _ = all_cores(adapter_cores, first)
+    second, first = lax.optimization_barrier((activations[rows // 2 :], first))
+    second = send(second, SWAP)
+
+    near, far = pieces[:piece], pieces[piece:]
+    near = jnp.concatenate([near, swap_groups(near)], axis=0)
+    far = jnp.concatenate([far, swap_rep(far, 2)], axis=0)
+    near, far, cores = lax.optimization_barrier((near, far, cores))
+    near_more, far_more = swap_rep(near, 2), swap_groups(far)
+    mate = swap_rep(jnp.concatenate([near, far], axis=0), 1)
+    mate_more = swap_rep(jnp.concatenate([near_more, far_more], axis=0), 1)
+    two = 2 * piece
+    near_blocks = ((0, 0, (0, 4)), (1, 0, (2, 6)), (2, 0, (1, 5)), (3, 0, (3, 7)))
+    far_blocks = ((0, 0, (0, 2)), (1, 0, (4, 6)), (2, two, (1, 3)), (3, two, (5, 7)))
+
+    received = jnp.concatenate([first, second], axis=0)
+    turned = [send(jnp.where(inner, received[p], activations[p]), IN + OUT) for p in parts]
+    half, turned[0] = lax.optimization_barrier((side.astype(jnp.bfloat16), turned[0]))
+    coded = (side + send(half, SWAP).astype(jnp.float32)).astype(jnp.bfloat16)
+    coded, turned[1] = lax.optimization_barrier((coded, turned[1]))
+    coded = jnp.where(inner, coded, send(coded, OUT))
+    mixed = mix(row_adapter, coded, cores)
 
     base = dot(activations, weight_of(me)) + dot(mixed, basis_up)
-    base = base + dot(jnp.concatenate([right_top, right_bottom], 0), weight_of(me + 3))
-    base = base + dot(jnp.concatenate([left_top, left_bottom], 0), weight_of(me + 1))
-    base = base + dot(jnp.concatenate([far_top, far_bottom], 0), weight_of(me + 2))
-    return base.astype(jnp.bfloat16)
+    base = base + dot(received, weight_of(far_in))
+    base = base + dot(jnp.concatenate(turned, 0), weight_of(jnp.where(inner, near_out, far_in)))
+    lent = lend(
+        spot, activations, (near, near_more, mate, mate_more), near_blocks, None, jnp.float32,
+        "lend_near",
+    )
+    last_weight = weight_of(far_out)
+    crossed, sent = [], []
+    for i, p in enumerate(parts):
+        x = turned[i]
+        if i > 1:
+            x, sent[i - 2] = lax.optimization_barrier((x, sent[i - 2]))
+        crossed.append(send(x, SWAP))
+        x = crossed[i]
+        if i:
+            x, sent[i - 1] = lax.optimization_barrier((x, sent[i - 1]))
+        weights = (far, far_more, mate, mate_more)
+        sent.append(lend(spot, x, weights, far_blocks, lent[p], jnp.bfloat16, "lend_far"))
+    out = []
+    for p, x, y in zip(parts, crossed, sent):
+        whole = base[p] + dot(x, last_weight) + send(y, OUT).astype(jnp.float32)
+        out.append(whole.astype(jnp.bfloat16))
+    return jnp.concatenate(out, axis=0)
 
 
 def on_any(activations, row_adapter, base_weight, basis_down, adapter_cores, basis_up):
@@ -144,7 +241,7 @@
         P("rep", None, None),
         P(None, "tp"),
     )
-    short = mesh.shape["tp"] == 4 and mesh.shape["rep"] == 4
+    short = (mesh.shape["groups"], mesh.shape["rep"], mesh.shape["tp"]) == (2, 4, 4)
     return jax.shard_map(
         on_line if short else on_any,
         mesh=mesh,

time: 182 us -> 170 us (0.934)
  the two profiles are of different devices: /device:TPU:14 before, /device:TPU:0 now
where the time goes in v2:
time: 170 us
  waiting for transfers between devices  67.4 us (40%)
  starting transfers between devices  38.7 us (23%)
  matrix products  21.6 us (13%)
  other arithmetic  18.9 us (11%)
  Pallas kernels  15.5 us (9%)
  local copies, waits for them, and re-layouts  7.17 us (4%)
    ppermute x15, waiting for transfers between devices, send(): return lax.ppermute(x, 'tp', pairs)  50.8 us
    ppermute x15, starting transfers between devices, send(): return lax.ppermute(x, 'tp', pairs)  31.4 us
    dot_general x8, matrix products, dot(): return jnp.dot(a, b, preferred_element_type=jnp.float32)  21.6 us
    pallas_call x4, Pallas kernels, lend(): pl.pallas_call(functools.partial(lend_kernel, blocks=blocks, width=256),...  13.4 us
    ppermute x1, waiting for transfers between devices, all_cores(): across = lax.ppermute(cores, 'rep', [(i, i ^ 2) for i in range(4)])  10 us
    ppermute x2, waiting for transfers between devices, swap_groups(): return lax.ppermute(x, 'groups', [(0, 1), (1, 0)])  6.39 us
    select_n x2, other arithmetic, on_line(): jnp.where(inner, received[p], activations[p])  3.45 us
  transfers between devices with their start and end apart: 24, of which 10 were waited for; matrix products, arithmetic and copies ran while one was open for 26% of the time, Pallas kernels for 9%

profile of v2, /device:TPU:0, one launch (start us, length us, event | category | flops | bytes accessed | tf_op | source)
XLA Modules:
  0.0 169.7 jit_solution(13019028091012101660)
XLA Ops:
  0.0 2.9 %collective-permute-start.10 = (bf16[8,256,256]{2,1,0:T(8,128)(2,1)}, bf16[8,256,256]{2,1,0:T(8,128)(2,1)}, u32[]{:S(2)}, u32[]{:S(2)}) collective-permute-start(bf16[8,256,256]{2,1,0:T(8,128)(2,1)} %param.10), channel_id=1, source_target_pairs={{0,8},{4,12},{8,0},{12,4},{1,9},{5,13},{9,1},{13,5},{2,10},{6,14},... | collective-permute-start | bytes 3145736 | tf_op jit(solution)/shard_map/ppermute | solution.py:104
  2.9 3.1 %fusion.48 = (bf16[256,2048]{1,0:T(8,128)(2,1)}, bf16[256,2048]{1,0:T(8,128)(2,1)}) fusion(bf16[512,2048]{1,0:T(8,128)(2,1)} %x_ref.1), kind=kLoop, calls=%fused_computation.60 | loop fusion | bytes 4194304 | tf_op jit(solution)/shard_map/slice | solution.py:152
  6.1 1.7 collective-permute-start.1
  7.7 1.3 constant_dynamic-slice_fusion.1
  9.0 1.1 pad_maximum_fusion.3
  10.1 6.3 %collective-permute-start.7 = (bf16[512,1024]{1,0:T(8,128)(2,1)}, bf16[512,1024]{1,0:T(8,128)(2,1)}, u32[]{:S(2)}, u32[]{:S(2)}) collective-permute-start(bf16[512,1024]{1,0:T(8,128)(2,1)} %pad_maximum_fusion.3), channel_id=1, source_target_pairs={{0,1},{3,2},{4,5},{7,6},{8,9},{11,10},{12,13},{15,14},{16,17},{19,... | collective-permute-start | bytes 3145736 | tf_op jit(solution)/shard_map/ppermute | solution.py:122
  16.4 10.0 %collective-permute-done.10 = bf16[8,256,256]{2,1,0:T(8,128)(2,1)} collective-permute-done((bf16[8,256,256]{2,1,0:T(8,128)(2,1)}, bf16[8,256,256]{2,1,0:T(8,128)(2,1)}, u32[]{:S(2)}, u32[]{:S(2)}) %collective-permute-start.10) | collective-permute-done | bytes 1048608 | tf_op jit(solution)/shard_map/ppermute | solution.py:104
  26.4 12.1 %collective-permute-done.7 = bf16[512,1024]{1,0:T(8,128)(2,1)} collective-permute-done((bf16[512,1024]{1,0:T(8,128)(2,1)}, bf16[512,1024]{1,0:T(8,128)(2,1)}, u32[]{:S(2)}, u32[]{:S(2)}) %collective-permute-start.7) | collective-permute-done | bytes 1048608 | tf_op jit(solution)/shard_map/ppermute | solution.py:122
  38.5 1.3 fusion.49
  39.8 1.6 collective-permute-start.8
  41.4 0.5 collective-permute-start.9
  41.9 1.1 broadcast_select_fusion
  43.0 3.7 %collective-permute-start.2 = (bf16[256,2048]{1,0:T(8,128)(2,1)}, bf16[256,2048]{1,0:T(8,128)(2,1)}, u32[]{:S(2)}, u32[]{:S(2)}) collective-permute-start(bf16[256,2048]{1,0:T(8,128)(2,1)} %broadcast_select_fusion), channel_id=1, source_target_pairs={{0,1},{3,2},{1,0},{2,3},{4,5},{7,6},{5,4},{6,7},{8,9},{11,10},{9,8... | collective-permute-start | bytes 3145736 | tf_op jit(solution)/shard_map/ppermute | solution.py:122
  46.7 6.4 %collective-permute-done.8 = bf16[256,1024]{1,0:T(8,128)(2,1)S(1)} collective-permute-done((bf16[256,1024]{1,0:T(8,128)(2,1)S(1)}, bf16[256,1024]{1,0:T(8,128)(2,1)S(1)}, u32[]{:S(2)}, u32[]{:S(2)}) %collective-permute-start.8) | collective-permute-done | bytes 524320 | tf_op jit(solution)/shard_map/ppermute | solution.py:130
  53.1 1.1 pad_maximum_fusion.4.rest_0_
  54.2 0.2 collective-permute-done.9
  54.3 0.1 pad_maximum_fusion.5.rest_0_
  54.4 1.8 %select_select_fusion.3 = (bf16[8,256,256]{2,1,0:T(8,128)(2,1)S(1)}, bf16[8,256,256]{2,1,0:T(8,128)(2,1)S(1)}, bf16[8,256,256]{2,1,0:T(8,128)(2,1)S(1)}, bf16[8,256,256]{2,1,0:T(8,128)(2,1)S(1)}) fusion(bf16[8,256,256]{2,1,0:T(8,128)(2,1)} %collective-permute-done.10, bf16[8,256,256]{2,1,0:T(8,128)(2,1)S(1)} %collective-permute-done.12, ...), kind=kLoop, calls=%fused_computation.36 | loop fusion | flops 6291456 | bytes 8388620 | tf_op jit(solution)/shard_map/select_n | solution.py:111
  56.2 2.3 %pad_maximum_fusion.cores_ref = bf16[32,256,256]{2,1,0:T(8,128)(2,1)} fusion(bf16[8,256,256]{2,1,0:T(8,128)(2,1)S(1)} %get-tuple-element.44, bf16[8,256,256]{2,1,0:T(8,128)(2,1)S(1)} %get-tuple-element.45, bf16[8,256,256]{2,1,0:T(8,128)(2,1)S(1)} %get-tuple-element.46, bf16[8,256,256]{2,1,0:T(8,128)(2,1)S(1)} %get-tuple-element.43), kind=kLoop, calls=%fused_computation | loop fusion | flops 6291456 | bytes 8388608 | tf_op jit(solution)/shard_map/concatenate | solution.py:113
  58.5 1.4 collective-permute-start.16
  59.9 0.5 collective-permute-start.18
  60.4 0.7 fusion.50
  61.1 4.4 %collective-permute-start = (f32[512,256]{1,0:T(8,128)S(1)}, f32[512,256]{1,0:T(8,128)S(1)}, u32[]{:S(2)}, u32[]{:S(2)}) collective-permute-start(f32[512,256]{1,0:T(8,128)S(1)} %fusion.50), channel_id=1, source_target_pairs={{0,1},{3,2},{4,5},{7,6},{8,9},{11,10},{12,13},{15,14},{16,17},{19,... | collective-permute-start | bytes 1572872 | tf_op jit(solution)/shard_map/ppermute | solution.py:122
  65.5 1.6 collective-permute-start.4
  67.2 12.4 %collective-permute-done = f32[512,256]{1,0:T(8,128)S(1)} collective-permute-done((f32[512,256]{1,0:T(8,128)S(1)}, f32[512,256]{1,0:T(8,128)S(1)}, u32[]{:S(2)}, u32[]{:S(2)}) %collective-permute-start) | collective-permute-done | bytes 524320 | tf_op jit(solution)/shard_map/ppermute | solution.py:122
  79.6 1.0 fusion.46
  80.5 1.4 collective-permute-start.3
  81.9 2.7 %pad_maximum_fusion.1 = bf16[1024,1024]{1,0:T(8,128)(2,1)} fusion(bf16[512,1024]{1,0:T(8,128)(2,1)S(1)} %pad_maximum_fusion.5.rest_0_, bf16[512,1024]{1,0:T(8,128)(2,1)} %pad_maximum_fusion.4.rest_0_), kind=kLoop, calls=%fused_computation.21 | loop fusion | flops 4194304 | bytes 4194304 | tf_op jit(solution)/shard_map/concatenate | solution.py:164
  84.6 3.3 %pad_maximum_fusion.2 = bf16[1024,1024]{1,0:T(8,128)(2,1)} fusion(bf16[512,1024]{1,0:T(8,128)(2,1)} %collective-permute-done.16.rest_1_, bf16[512,1024]{1,0:T(8,128)(2,1)} %collective-permute-done.18.rest_1_), kind=kLoop, calls=%fused_computation.22 | loop fusion | flops 4194304 | bytes 4194304 | tf_op jit(solution)/shard_map/concatenate | solution.py:165
  87.9 0.4 collective-permute-start.19
  88.3 2.4 %slice_select_fusion = (bf16[128,2048]{1,0:T(8,128)(2,1)}, bf16[128,2048]{1,0:T(8,128)(2,1)}) fusion(bf16[256,2048]{1,0:T(8,128)(2,1)} %collective-permute-done.4, bf16[512,2048]{1,0:T(8,128)(2,1)S(1)} %copy-done.4, pred[]{:T(512)S(6)} %or.3), kind=kLoop, calls=%fused_computation.44 | loop fusion | flops 524288 | bytes 3145729 | tf_op jit(solution)/shard_map/jit(_where)/select_n | solution.py:171
  90.6 4.8 %collective-permute-start.5 = (bf16[128,2048]{1,0:T(8,128)(2,1)}, bf16[128,2048]{1,0:T(8,128)(2,1)}, u32[]{:S(2)}, u32[]{:S(2)}) collective-permute-start(bf16[128,2048]{1,0:T(8,128)(2,1)} %get-tuple-element.48), channel_id=1, source_target_pairs={{0,1},{3,2},{1,0},{2,3},{4,5},{7,6},{5,4},{6,7},{8,9},{11,10},{9,8... | collective-permute-start | bytes 1572872 | tf_op jit(solution)/shard_map/ppermute | solution.py:122
  95.4 6.0 %fusion.4 = f32[1024,512]{0,1:T(8,128)} fusion(bf16[512,2048]{1,0:T(8,128)(2,1)S(1)} %copy-done.4, bf16[8192,1024]{1,0:T(8,128)(2,1)} %param.8, s32[]{:T(128)S(6)} %select_n.171), kind=kOutput, calls=%fused_computation.5 | convolution fusion | flops 2147483648 | bytes 8388612 | tf_op jit(solution)/shard_map/dot_general | solution.py:14
  101.3 0.1 copy.7.ids_ref
  101.5 0.1 collective-permute-start.13
  101.6 0.7 collective-permute-start.14
  102.3 1.2 add_convert_fusion
  103.5 5.1 %collective-permute-done.5 = bf16[128,2048]{1,0:T(8,128)(2,1)} collective-permute-done((bf16[128,2048]{1,0:T(8,128)(2,1)}, bf16[128,2048]{1,0:T(8,128)(2,1)}, u32[]{:S(2)}, u32[]{:S(2)}) %collective-permute-start.5) | collective-permute-done | bytes 524320 | tf_op jit(solution)/shard_map/ppermute | solution.py:122
  108.5 1.3 collective-permute-start.6
  109.9 6.6 %fusion.2 = f32[512,1024]{1,0:T(8,128)} fusion(bf16[8192,1024]{1,0:T(8,128)(2,1)} %param.8, s32[]{:T(128)S(6)} %select_n.219, bf16[256,2048]{1,0:T(8,128)(2,1)} %collective-permute-done.4, bf16[256,2048]{1,0:T(8,128)(2,1)} %collective-permute-done.1), kind=kOutput, calls=%fused_computation.3 | convolution fusion | flops 2151677952 | bytes 8388612 | tf_op jit(solution)/shard_map/dot_general | solution.py:14
  116.5 6.9 %collective-permute-done.6 = bf16[512,256]{1,0:T(8,128)(2,1)S(1)} collective-permute-done((bf16[512,256]{1,0:T(8,128)(2,1)S(1)}, bf16[512,256]{1,0:T(8,128)(2,1)S(1)}, u32[]{:S(2)}, u32[]{:S(2)}) %collective-permute-start.6) | collective-permute-done | bytes 262176 | tf_op jit(solution)/shard_map/ppermute | solution.py:122
  123.4 0.9 collective-permute-start.15
  124.3 2.1 %mix.1 = bf16[512,256]{1,0:T(8,128)(2,1)S(1)} custom-call(s32[512,1]{1,0:T(8,128)S(1)} %copy.7.ids_ref, bf16[512,256]{1,0:T(8,128)(2,1)S(1)} %broadcast_select_fusion.1.coded_ref, bf16[32,256,256]{2,1,0:T(8,128)(2,1)S(1)} %copy-done.6), custom_call_target="tpu_custom_call" | custom-call | flops 402653184 | bytes 4718592 | tf_op jit(solution)/shard_map/mix/pallas_call | solution.py:44
  126.4 0.0 slice-start.2
  126.5 0.4 fusion.51
  126.9 1.1 copy-done.5
  128.0 4.9 %lend_near.1 = f32[512,1024]{1,0:T(8,128)S(1)} custom-call(s32[1]{0:T(128)} %bitcast.1.spot_ref, bf16[512,2048]{1,0:T(8,128)(2,1)S(1)} %copy-done.5, bf16[512,1024]{1,0:T(8,128)(2,1)} %pad_maximum_fusion.4.rest_0_, bf16[512,1024]{1,0:T(8,128)(2,1)} %collective-permute-done.18.rest_1_, bf16[1024,1024]{1,0:T(8,128)(2,1)S(1)} %collective-permute-done.17.rest_2_, ...), custom_call_target="tpu_custom_call" | custom-call | flops 2147483648 | bytes 7340032 | tf_op jit(solution)/shard_map/lend_near/pallas_call | solution.py:85
  132.9 0.1 slice.62.rest_4_
  133.0 3.2 %lend_far.3 = bf16[256,1024]{1,0:T(8,128)(2,1)S(1)} custom-call(s32[1]{0:T(128)} %bitcast.1.spot_ref, bf16[256,2048]{1,0:T(8,128)(2,1)S(1)} %collective-permute-done.14.x_ref, bf16[512,1024]{1,0:T(8,128)(2,1)S(1)} %pad_maximum_fusion.5.rest_0_, bf16[512,1024]{1,0:T(8,128)(2,1)} %collective-permute-done.16.rest_1_, ...), custom_call_target="tpu_custom_call" | custom-call | flops 1073741824 | bytes 5767168 | tf_op jit(solution)/shard_map/lend_far/pallas_call | solution.py:85
  136.3 0.7 collective-permute-start.21
  137.0 1.3 collective-permute-start.20
  138.3 5.1 %fusion.21 = f32[512,1024]{1,0:T(8,128)S(1)} fusion(f32[512,1024]{1,0:T(8,128)} %fusion.2, f32[512,1024]{1,0:T(8,128)S(1)} %fusion.51, f32[1024,512]{0,1:T(8,128)} %fusion.4, bf16[8192,1024]{1,0:T(8,128)(2,1)S(1)} %bitcast.16, s32[]{:T(128)S(6)} %select_n.223, bf16[128,2048]{1,0:T(8,128)(2,1)S(1)} %collective-permute-done.13, ...), kind=kOutput, calls=%fused_computation.25 | convolution fusion | flops 2155347968 | bytes 14680068 | tf_op jit(solution)/shard_map/dot_general | solution.py:14
  143.4 0.1 fusion.47
  143.5 2.7 %lend_far.4 = bf16[128,1024]{1,0:T(8,128)(2,1)S(1)} custom-call(s32[1]{0:T(128)} %bitcast.1.spot_ref, bf16[128,2048]{1,0:T(8,128)(2,1)S(1)} %collective-permute-done.15.x_ref, bf16[512,1024]{1,0:T(8,128)(2,1)S(1)} %pad_maximum_fusion.5.rest_0_, bf16[512,1024]{1,0:T(8,128)(2,1)} %collective-permute-done.16.rest_1_, ...), custom_call_target="tpu_custom_call" | custom-call | flops 536870912 | bytes 4980736 | tf_op jit(solution)/shard_map/lend_far/pallas_call | solution.py:85
  146.2 2.7 %lend_far.5 = bf16[128,1024]{1,0:T(8,128)(2,1)S(1)} custom-call(s32[1]{0:T(128)} %bitcast.1.spot_ref, bf16[128,2048]{1,0:T(8,128)(2,1)S(1)} %collective-permute-done.21.x_ref, bf16[512,1024]{1,0:T(8,128)(2,1)S(1)} %pad_maximum_fusion.5.rest_0_, bf16[512,1024]{1,0:T(8,128)(2,1)} %collective-permute-done.16.rest_1_, ...), custom_call_target="tpu_custom_call" | custom-call | flops 536870912 | bytes 4980736 | tf_op jit(solution)/shard_map/lend_far/pallas_call | solution.py:85
  148.9 1.3 collective-permute-start.23
  150.2 1.3 collective-permute-start.22
  151.5 3.9 %collective-permute-done.20 = bf16[256,1024]{1,0:T(8,128)(2,1)S(1)} collective-permute-done((bf16[256,1024]{1,0:T(8,128)(2,1)S(1)}, bf16[256,1024]{1,0:T(8,128)(2,1)S(1)}, u32[]{:S(2)}, u32[]{:S(2)}) %collective-permute-start.20) | collective-permute-done | bytes 524320 | tf_op jit(solution)/shard_map/ppermute | solution.py:122
  155.4 1.3 fusion.23
  156.7 8.4 %collective-permute-done.23 = bf16[128,1024]{1,0:T(8,128)(2,1)S(1)} collective-permute-done((bf16[128,1024]{1,0:T(8,128)(2,1)S(1)}, bf16[128,1024]{1,0:T(8,128)(2,1)S(1)}, u32[]{:S(2)}, u32[]{:S(2)}) %collective-permute-start.23) | collective-permute-done | bytes 262176 | tf_op jit(solution)/shard_map/ppermute | solution.py:122
  165.1 0.8 fusion.25
  165.8 2.0 %collective-permute-done.22 = bf16[128,1024]{1,0:T(8,128)(2,1)S(1)} collective-permute-done((bf16[128,1024]{1,0:T(8,128)(2,1)S(1)}, bf16[128,1024]{1,0:T(8,128)(2,1)S(1)}, u32[]{:S(2)}, u32[]{:S(2)}) %collective-permute-start.22) | collective-permute-done | bytes 262176 | tf_op jit(solution)/shard_map/ppermute | solution.py:122
  167.9 0.7 fusion.27
  168.6 1.0 pad_maximum_fusion.6
  (45 shorter events, 0.1 us)
Async XLA Ops:
  0.0 60.4 %copy-start = (bf16[2048,256]{1,0:T(8,128)(2,1)S(1)}, bf16[2048,256]{1,0:T(8,128)(2,1)}, u32[]{:S(2)}) copy-start(bf16[2048,256]{1,0:T(8,128)(2,1)} %param.9) | copy-start | bytes 3145732
  0.0 26.4 %collective-permute-start.10 = (bf16[8,256,256]{2,1,0:T(8,128)(2,1)}, bf16[8,256,256]{2,1,0:T(8,128)(2,1)}, u32[]{:S(2)}, u32[]{:S(2)}) collective-permute-start(bf16[8,256,256]{2,1,0:T(8,128)(2,1)} %param.10), channel_id=1, source_target_pairs={{0,8},{4,12},{8,0},{12,4},{1,9},{5,13},{9,1},{13,5},{2,10},{6,14},... | collective-permute-start | bytes 3145736 | tf_op jit(solution)/shard_map/ppermute | solution.py:104
  2.9 23.5 %collective-permute-start.11 = (bf16[8,256,256]{2,1,0:T(8,128)(2,1)}, bf16[8,256,256]{2,1,0:T(8,128)(2,1)}, u32[]{:S(2)}, u32[]{:S(2)}) collective-permute-start(bf16[8,256,256]{2,1,0:T(8,128)(2,1)} %param.10), channel_id=1, source_target_pairs={{0,4},{4,0},{8,12},{12,8},{1,5},{5,1},{9,13},{13,9},{2,6},{6,2},{1... | collective-permute-start | bytes 3145736 | tf_op jit(solution)/shard_map/ppermute | solution.py:103
  6.1 10.3 %collective-permute-start.1 = (bf16[256,2048]{1,0:T(8,128)(2,1)}, bf16[256,2048]{1,0:T(8,128)(2,1)}, u32[]{:S(2)}, u32[]{:S(2)}) collective-permute-start(bf16[256,2048]{1,0:T(8,128)(2,1)} %get-tuple-element.51), channel_id=1, source_target_pairs={{1,2},{2,1},{5,6},{6,5},{9,10},{10,9},{13,14},{14,13},{17,18},{18,... | collective-permute-start | bytes 3145736 | tf_op jit(solution)/shard_map/ppermute | solution.py:122
  9.0 32.9 %copy-start.2 = (bf16[512,2048]{1,0:T(8,128)(2,1)S(1)}, bf16[512,2048]{1,0:T(8,128)(2,1)}, u32[]{:S(2)}) copy-start(bf16[512,2048]{1,0:T(8,128)(2,1)} %x_ref.1) | copy-start | bytes 6291460
  10.1 28.4 %collective-permute-start.7 = (bf16[512,1024]{1,0:T(8,128)(2,1)}, bf16[512,1024]{1,0:T(8,128)(2,1)}, u32[]{:S(2)}, u32[]{:S(2)}) collective-permute-start(bf16[512,1024]{1,0:T(8,128)(2,1)} %pad_maximum_fusion.3), channel_id=1, source_target_pairs={{0,1},{3,2},{4,5},{7,6},{8,9},{11,10},{12,13},{15,14},{16,17},{19,... | collective-permute-start | bytes 3145736 | tf_op jit(solution)/shard_map/ppermute | solution.py:122
  26.4 28.0 %collective-permute-start.12 = (bf16[8,256,256]{2,1,0:T(8,128)(2,1)}, bf16[8,256,256]{2,1,0:T(8,128)(2,1)S(1)}, u32[]{:S(2)}, u32[]{:S(2)}) collective-permute-start(bf16[8,256,256]{2,1,0:T(8,128)(2,1)} %collective-permute-done.10), channel_id=1, source_target_pairs={{0,4},{4,0},{8,12},{12,8},{1,5},{5,1},{9,13},{13,9},{2,6},{6,2},{1... | collective-permute-start | bytes 3145736 | tf_op jit(solution)/shard_map/ppermute | solution.py:106
  39.8 13.3 %collective-permute-start.8 = (bf16[256,1024]{1,0:T(8,128)(2,1)S(1)}, bf16[256,1024]{1,0:T(8,128)(2,1)S(1)}, u32[]{:S(2)}, u32[]{:S(2)}) collective-permute-start(bf16[256,1024]{1,0:T(8,128)(2,1)S(1)} %get-tuple-element.54), channel_id=1, source_target_pairs={{0,16},{16,0},{1,17},{17,1},{2,18},{18,2},{3,19},{19,3},{4,20},{20... | collective-permute-start | bytes 1572872 | tf_op jit(solution)/shard_map/ppermute | solution.py:130
  41.4 13.0 %collective-permute-start.9 = (bf16[256,1024]{1,0:T(8,128)(2,1)S(1)}, bf16[256,1024]{1,0:T(8,128)(2,1)S(1)}, u32[]{:S(2)}, u32[]{:S(2)}) collective-permute-start(bf16[256,1024]{1,0:T(8,128)(2,1)S(1)} %get-tuple-element.53), channel_id=1, source_target_pairs={{0,8},{4,12},{8,0},{12,4},{1,9},{5,13},{9,1},{13,5},{2,10},{6,14},... | collective-permute-start | bytes 1572872 | tf_op jit(solution)/shard_map/ppermute | solution.py:126
  43.0 11.4 %copy-start.7 = (bf16[8,256,256]{2,1,0:T(8,128)(2,1)S(1)}, bf16[8,256,256]{2,1,0:T(8,128)(2,1)}, u32[]{:S(2)}) copy-start(bf16[8,256,256]{2,1,0:T(8,128)(2,1)} %param.10) | copy-start | bytes 3145732
  43.0 37.5 %collective-permute-start.2 = (bf16[256,2048]{1,0:T(8,128)(2,1)}, bf16[256,2048]{1,0:T(8,128)(2,1)}, u32[]{:S(2)}, u32[]{:S(2)}) collective-permute-start(bf16[256,2048]{1,0:T(8,128)(2,1)} %broadcast_select_fusion), channel_id=1, source_target_pairs={{0,1},{3,2},{1,0},{2,3},{4,5},{7,6},{5,4},{6,7},{8,9},{11,10},{9,8... | collective-permute-start | bytes 3145736 | tf_op jit(solution)/shard_map/ppermute | solution.py:122
  56.2 4.2 %copy-start.3 = (bf16[512,2048]{1,0:T(8,128)(2,1)S(1)}, bf16[512,2048]{1,0:T(8,128)(2,1)}, u32[]{:S(2)}) copy-start(bf16[512,2048]{1,0:T(8,128)(2,1)} %x_ref.1) | copy-start | bytes 6291460
  58.5 26.1 %collective-permute-start.16 = (bf16[512,1024]{1,0:T(8,128)(2,1)S(1)}, bf16[512,1024]{1,0:T(8,128)(2,1)}, u32[]{:S(2)}, u32[]{:S(2)}) collective-permute-start(bf16[512,1024]{1,0:T(8,128)(2,1)S(1)} %pad_maximum_fusion.5.rest_0_), channel_id=1, source_target_pairs={{0,16},{16,0},{1,17},{17,1},{2,18},{18,2},{3,19},{19,3},{4,20},{20... | collective-permute-start | bytes 3145736 | tf_op jit(solution)/shard_map/ppermute | solution.py:130
  59.9 24.8 %collective-permute-start.18 = (bf16[512,1024]{1,0:T(8,128)(2,1)}, bf16[512,1024]{1,0:T(8,128)(2,1)}, u32[]{:S(2)}, u32[]{:S(2)}) collective-permute-start(bf16[512,1024]{1,0:T(8,128)(2,1)} %pad_maximum_fusion.4.rest_0_), channel_id=1, source_target_pairs={{0,8},{4,12},{8,0},{12,4},{1,9},{5,13},{9,1},{13,5},{2,10},{6,14},... | collective-permute-start | bytes 3145736 | tf_op jit(solution)/shard_map/ppermute | solution.py:126
  61.1 18.5 %collective-permute-start = (f32[512,256]{1,0:T(8,128)S(1)}, f32[512,256]{1,0:T(8,128)S(1)}, u32[]{:S(2)}, u32[]{:S(2)}) collective-permute-start(f32[512,256]{1,0:T(8,128)S(1)} %fusion.50), channel_id=1, source_target_pairs={{0,1},{3,2},{4,5},{7,6},{8,9},{11,10},{12,13},{15,14},{16,17},{19,... | collective-permute-start | bytes 1572872 | tf_op jit(solution)/shard_map/ppermute | solution.py:122
  65.5 22.7 %collective-permute-start.4 = (bf16[256,2048]{1,0:T(8,128)(2,1)}, bf16[256,2048]{1,0:T(8,128)(2,1)}, u32[]{:S(2)}, u32[]{:S(2)}) collective-permute-start(bf16[256,2048]{1,0:T(8,128)(2,1)} %get-tuple-element.24), channel_id=1, source_target_pairs={{1,2},{2,1},{5,6},{6,5},{9,10},{10,9},{13,14},{14,13},{17,18},{18,... | collective-permute-start | bytes 3145736 | tf_op jit(solution)/shard_map/ppermute | solution.py:122
  80.5 21.0 %collective-permute-start.3 = (bf16[512,256]{1,0:T(8,128)(2,1)}, bf16[512,256]{1,0:T(8,128)(2,1)}, u32[]{:S(2)}, u32[]{:S(2)}) collective-permute-start(bf16[512,256]{1,0:T(8,128)(2,1)} %get-tuple-element.23), channel_id=1, source_target_pairs={{1,2},{2,1},{5,6},{6,5},{9,10},{10,9},{13,14},{14,13},{17,18},{18,... | collective-permute-start | bytes 786440 | tf_op jit(solution)/shard_map/ppermute | solution.py:122
  84.6 3.7 %copy-start.4 = (bf16[512,2048]{1,0:T(8,128)(2,1)S(1)}, bf16[512,2048]{1,0:T(8,128)(2,1)}, u32[]{:S(2)}) copy-start(bf16[512,2048]{1,0:T(8,128)(2,1)} %x_ref.1) | copy-start | bytes 6291460
  84.6 42.3 %collective-permute-start.17 = (bf16[1024,1024]{1,0:T(8,128)(2,1)}, bf16[1024,1024]{1,0:T(8,128)(2,1)S(1)}, u32[]{:S(2)}, u32[]{:S(2)}) collective-permute-start(bf16[1024,1024]{1,0:T(8,128)(2,1)} %pad_maximum_fusion.1), channel_id=1, source_target_pairs={{0,4},{4,0},{8,12},{12,8},{1,5},{5,1},{9,13},{13,9},{2,6},{6,2},{1... | collective-permute-start | bytes 6291464 | tf_op jit(solution)/shard_map/ppermute | solution.py:126
  87.9 39.0 %collective-permute-start.19 = (bf16[1024,1024]{1,0:T(8,128)(2,1)}, bf16[1024,1024]{1,0:T(8,128)(2,1)}, u32[]{:S(2)}, u32[]{:S(2)}) collective-permute-start(bf16[1024,1024]{1,0:T(8,128)(2,1)} %pad_maximum_fusion.2), channel_id=1, source_target_pairs={{0,4},{4,0},{8,12},{12,8},{1,5},{5,1},{9,13},{13,9},{2,6},{6,2},{1... | collective-permute-start | bytes 6291464 | tf_op jit(solution)/shard_map/ppermute | solution.py:126
  90.6 10.7 %copy-start.9 = (s32[512,1]{0,1:T(1,128)S(1)}, s32[512,1]{0,1:T(1,128)}, u32[]{:S(2)}) copy-start(s32[512,1]{0,1:T(1,128)} %param.7) | copy-start | bytes 6148
  90.6 17.9 %collective-permute-start.5 = (bf16[128,2048]{1,0:T(8,128)(2,1)}, bf16[128,2048]{1,0:T(8,128)(2,1)}, u32[]{:S(2)}, u32[]{:S(2)}) collective-permute-start(bf16[128,2048]{1,0:T(8,128)(2,1)} %get-tuple-element.48), channel_id=1, source_target_pairs={{0,1},{3,2},{1,0},{2,3},{4,5},{7,6},{5,4},{6,7},{8,9},{11,10},{9,8... | collective-permute-start | bytes 1572872 | tf_op jit(solution)/shard_map/ppermute | solution.py:122
  101.5 34.8 %collective-permute-start.13 = (bf16[128,2048]{1,0:T(8,128)(2,1)}, bf16[128,2048]{1,0:T(8,128)(2,1)S(1)}, u32[]{:S(2)}, u32[]{:S(2)}) collective-permute-start(bf16[128,2048]{1,0:T(8,128)(2,1)} %get-tuple-element.47), channel_id=1, source_target_pairs={{0,1},{3,2},{1,0},{2,3},{4,5},{7,6},{5,4},{6,7},{8,9},{11,10},{9,8... | collective-permute-start | bytes 1572872 | tf_op jit(solution)/shard_map/ppermute | solution.py:122
  101.6 31.5 %collective-permute-start.14 = (bf16[256,2048]{1,0:T(8,128)(2,1)}, bf16[256,2048]{1,0:T(8,128)(2,1)S(1)}, u32[]{:S(2)}, u32[]{:S(2)}) collective-permute-start(bf16[256,2048]{1,0:T(8,128)(2,1)} %collective-permute-done.2), channel_id=1, source_target_pairs={{1,2},{2,1},{5,6},{6,5},{9,10},{10,9},{13,14},{14,13},{17,18},{18,... | collective-permute-start | bytes 3145736 | tf_op jit(solution)/shard_map/ppermute | solution.py:122
  108.5 14.9 %collective-permute-start.6 = (bf16[512,256]{1,0:T(8,128)(2,1)S(1)}, bf16[512,256]{1,0:T(8,128)(2,1)S(1)}, u32[]{:S(2)}, u32[]{:S(2)}) collective-permute-start(bf16[512,256]{1,0:T(8,128)(2,1)S(1)} %add_convert_fusion), channel_id=1, source_target_pairs={{1,0},{2,3},{5,4},{6,7},{9,8},{10,11},{13,12},{14,15},{17,16},{18,... | collective-permute-start | bytes 786440 | tf_op jit(solution)/shard_map/ppermute | solution.py:122
  109.8 14.5 %copy-start.6 = (bf16[32,256,256]{2,1,0:T(8,128)(2,1)S(1)}, bf16[32,256,256]{2,1,0:T(8,128)(2,1)}, u32[]{:S(2)}) copy-start(bf16[32,256,256]{2,1,0:T(8,128)(2,1)} %pad_maximum_fusion.cores_ref) | copy-start | bytes 12582916
  109.8 28.4 %slice-start = ((s8[16777216]{0:T(1024)(128)(4,1)}), s8[4194304]{0:T(1024)(128)(4,1)S(1)}, s32[]{:S(2)}) async-start(s8[16777216]{0:T(1024)(128)(4,1)} %bitcast.15), calls=%async_computation | async-start | bytes 8388608
  109.8 28.4 %slice-start.1 = ((s8[16777216]{0:T(1024)(128)(4,1)}), s8[4194304]{0:T(1024)(128)(4,1)S(1)}, s32[]{:S(2)}) async-start(s8[16777216]{0:T(1024)(128)(4,1)} %bitcast.15), calls=%async_computation.1 | async-start | bytes 8388608
  123.4 12.8 %collective-permute-start.15 = (bf16[128,2048]{1,0:T(8,128)(2,1)}, bf16[128,2048]{1,0:T(8,128)(2,1)S(1)}, u32[]{:S(2)}, u32[]{:S(2)}) collective-permute-start(bf16[128,2048]{1,0:T(8,128)(2,1)} %collective-permute-done.5), channel_id=1, source_target_pairs={{1,2},{2,1},{5,6},{6,5},{9,10},{10,9},{13,14},{14,13},{17,18},{18,... | collective-permute-start | bytes 1572872 | tf_op jit(solution)/shard_map/ppermute | solution.py:122
  124.3 2.1 %copy-start.8 = (bf16[256,1024]{1,0:T(8,128)(2,1)S(1)}, bf16[256,1024]{1,0:T(8,128)(2,1)}, u32[]{:S(2)}) copy-start(bf16[256,1024]{1,0:T(8,128)(2,1)} %param.11) | copy-start | bytes 1572868
  126.4 1.6 copy-start.5
  126.4 11.8 %slice-start.2 = ((s8[16777216]{0:T(1024)(128)(4,1)}), s8[4194304]{0:T(1024)(128)(4,1)S(1)}, s32[]{:S(2)}) async-start(s8[16777216]{0:T(1024)(128)(4,1)} %bitcast.15), calls=%async_computation.2 | async-start | bytes 8388608
  128.0 10.3 %slice-start.3 = ((s8[16777216]{0:T(1024)(128)(4,1)}), s8[4194304]{0:T(1024)(128)(4,1)S(1)}, s32[]{:S(2)}) async-start(s8[16777216]{0:T(1024)(128)(4,1)} %bitcast.15), calls=%async_computation.3 | async-start | bytes 8388608
  136.3 9.9 %collective-permute-start.21 = (bf16[128,2048]{1,0:T(8,128)(2,1)S(1)}, bf16[128,2048]{1,0:T(8,128)(2,1)S(1)}, u32[]{:S(2)}, u32[]{:S(2)}) collective-permute-start(bf16[128,2048]{1,0:T(8,128)(2,1)S(1)} %collective-permute-done.13), channel_id=1, source_target_pairs={{1,2},{2,1},{5,6},{6,5},{9,10},{10,9},{13,14},{14,13},{17,18},{18,... | collective-permute-start | bytes 1572872 | tf_op jit(solution)/shard_map/ppermute | solution.py:122
  137.0 18.4 %collective-permute-start.20 = (bf16[256,1024]{1,0:T(8,128)(2,1)S(1)}, bf16[256,1024]{1,0:T(8,128)(2,1)S(1)}, u32[]{:S(2)}, u32[]{:S(2)}) collective-permute-start(bf16[256,1024]{1,0:T(8,128)(2,1)S(1)} %lend_far.3), channel_id=1, source_target_pairs={{1,0},{2,3},{5,4},{6,7},{9,8},{10,11},{13,12},{14,15},{17,16},{18,... | collective-permute-start | bytes 1572872 | tf_op jit(solution)/shard_map/ppermute | solution.py:122
  148.9 16.2 %collective-permute-start.23 = (bf16[128,1024]{1,0:T(8,128)(2,1)S(1)}, bf16[128,1024]{1,0:T(8,128)(2,1)S(1)}, u32[]{:S(2)}, u32[]{:S(2)}) collective-permute-start(bf16[128,1024]{1,0:T(8,128)(2,1)S(1)} %lend_far.5), channel_id=1, source_target_pairs={{1,0},{2,3},{5,4},{6,7},{9,8},{10,11},{13,12},{14,15},{17,16},{18,... | collective-permute-start | bytes 786440 | tf_op jit(solution)/shard_map/ppermute | solution.py:122
  150.2 17.7 %collective-permute-start.22 = (bf16[128,1024]{1,0:T(8,128)(2,1)S(1)}, bf16[128,1024]{1,0:T(8,128)(2,1)S(1)}, u32[]{:S(2)}, u32[]{:S(2)}) collective-permute-start(bf16[128,1024]{1,0:T(8,128)(2,1)S(1)} %lend_far.4), channel_id=1, source_target_pairs={{1,0},{2,3},{5,4},{6,7},{9,8},{10,11},{13,12},{14,15},{17,16},{18,... | collective-permute-start | bytes 786440 | tf_op jit(solution)/shard_map/ppermute | solution.py:122
  167.9 1.8 %copy-start.1 = (bf16[2048,256]{1,0:T(8,128)(2,1)S(1)}, bf16[2048,256]{1,0:T(8,128)(2,1)}, u32[]{:S(2)}) copy-start(bf16[2048,256]{1,0:T(8,128)(2,1)} %param.9) | copy-start | bytes 3145732

commit v3 on v2

--- a/solution.py
+++ b/solution.py
@@ -97,12 +97,12 @@
     )(*operands)
 
 
-def all_cores(cores, ahead):
+def all_cores(cores):
     rep = lax.axis_index("rep")
     core, x = rep % 2, rep // 2
     mate = lax.ppermute(cores, "rep", [(i, i ^ 1) for i in range(4)])
     across = lax.ppermute(cores, "rep", [(i, i ^ 2) for i in range(4)])
-    across, mate, ahead = lax.optimization_barrier((across, mate, ahead))
+    across, mate = lax.optimization_barrier((across, mate))
     corner = lax.ppermute(across, "rep", [(i, i ^ 1) for i in range(4)])
     held = [cores, mate, across, corner]
 
@@ -110,7 +110,7 @@
         other = rep ^ r
         return lax.select_n(other, *held)
 
-    return jnp.concatenate([from_rep(r) for r in range(4)], axis=0), ahead
+    return jnp.concatenate([from_rep(r) for r in range(4)], axis=0)
 
 
 IN = [(0, 1), (3, 2)]
@@ -148,56 +148,56 @@
     def piece_of(owner):
         return lax.dynamic_slice_in_dim(base_weight, owner * depth + spot * piece, piece, 0)
 
-    pieces = send(jnp.concatenate([piece_of(near_in), piece_of(far_out)], axis=0), IN)
-    first = send(activations[: rows // 2], SWAP)
+    swapped = send(activations, SWAP)
+    pieces = send(jnp.concatenate([piece_of(far_in), piece_of(far_out)], axis=0), IN)
     partial_value = dot(activations, basis_down)
-    side = partial_value + send(partial_value, IN)
-    cores, _ = all_cores(adapter_cores, first)
-    second, first = lax.optimization_barrier((activations[rows // 2 :], first))
-    second = send(second, SWAP)
+    side = send(partial_value.astype(jnp.bfloat16), IN).astype(jnp.float32) + partial_value
+    whole = side + send(side.astype(jnp.bfloat16), SWAP).astype(jnp.float32)
+    coded = whole.astype(jnp.bfloat16)
+    cores = all_cores(adapter_cores)
 
     near, far = pieces[:piece], pieces[piece:]
+    top, near = lax.optimization_barrier((activations[: rows // 2], near))
+    turned = [send(top, IN + OUT)]
     near = jnp.concatenate([near, swap_groups(near)], axis=0)
     far = jnp.concatenate([far, swap_rep(far, 2)], axis=0)
     near, far, cores = lax.optimization_barrier((near, far, cores))
     near_more, far_more = swap_rep(near, 2), swap_groups(far)
-    mate = swap_rep(jnp.concatenate([near, far], axis=0), 1)
-    mate_more = swap_rep(jnp.concatenate([near_more, far_more], axis=0), 1)
-    two = 2 * piece
+    near_weights = (near, near_more, swap_rep(near, 1), swap_rep(near_more, 1))
+    far_weights = (far, far_more, swap_rep(far, 1), swap_rep(far_more, 1))
     near_blocks = ((0, 0, (0, 4)), (1, 0, (2, 6)), (2, 0, (1, 5)), (3, 0, (3, 7)))
-    far_blocks = ((0, 0, (0, 2)), (1, 0, (4, 6)), (2, two, (1, 3)), (3, two, (5, 7)))
-
-    received = jnp.concatenate([first, second], axis=0)
-    turned = [send(jnp.where(inner, received[p], activations[p]), IN + OUT) for p in parts]
-    half, turned[0] = lax.optimization_barrier((side.astype(jnp.bfloat16), turned[0]))
-    coded = (side + send(half, SWAP).astype(jnp.float32)).astype(jnp.bfloat16)
-    coded, turned[1] = lax.optimization_barrier((coded, turned[1]))
+    far_blocks = ((0, 0, (0, 2)), (1, 0, (4, 6)), (2, 0, (1, 3)), (3, 0, (5, 7)))
+
+    bottom, turned[0], swapped, coded = lax.optimization_barrier(
+        (activations[rows // 2 :], turned[0], swapped, coded)
+    )
     coded = jnp.where(inner, coded, send(coded, OUT))
+    turned.append(send(bottom, IN + OUT))
     mixed = mix(row_adapter, coded, cores)
 
     base = dot(activations, weight_of(me)) + dot(mixed, basis_up)
-    base = base + dot(received, weight_of(far_in))
-    base = base + dot(jnp.concatenate(turned, 0), weight_of(jnp.where(inner, near_out, far_in)))
-    lent = lend(
-        spot, activations, (near, near_more, mate, mate_more), near_blocks, None, jnp.float32,
-        "lend_near",
-    )
+    base = base + dot(swapped, weight_of(far_in))
+    base = base + dot(
+        jnp.concatenate(turned, 0), weight_of(jnp.where(inner, near_out, near_in))
+    )
+    lent = lend(spot, swapped, near_weights, near_blocks, None, jnp.float32, "lend_near")
     last_weight = weight_of(far_out)
     crossed, sent = [], []
     for i, p in enumerate(parts):
-        x = turned[i]
+        x = turned[0] if i == 0 else turned[1][p.start - rows // 2 : p.stop - rows // 2]
         if i > 1:
             x, sent[i - 2] = lax.optimization_barrier((x, sent[i - 2]))
         crossed.append(send(x, SWAP))
         x = crossed[i]
         if i:
             x, sent[i - 1] = lax.optimization_barrier((x, sent[i - 1]))
-        weights = (far, far_more, mate, mate_more)
-        sent.append(lend(spot, x, weights, far_blocks, lent[p], jnp.bfloat16, "lend_far"))
-    out = []
+        sent.append(lend(spot, x, far_weights, far_blocks, lent[p], jnp.bfloat16, "lend_far"))
+    out, back = [], None
     for p, x, y in zip(parts, crossed, sent):
-        whole = base[p] + dot(x, last_weight) + send(y, OUT).astype(jnp.float32)
-        out.append(whole.astype(jnp.bfloat16))
+        if back is not None:
+            y, back = lax.optimization_barrier((y, back))
+        back = send(y, OUT)
+        out.append((base[p] + dot(x, last_weight) + back.astype(jnp.float32)).astype(jnp.bfloat16))
     return jnp.concatenate(out, axis=0)
 
 

time: 170 us -> 185 us (1.088)
  waiting for transfers between devices: 67.4 us -> 90.7 us
  other arithmetic: 18.9 us -> 7.34 us
  starting transfers between devices: 38.7 us -> 49.7 us
  Pallas kernels: 15.5 us -> 7.19 us
    ppermute x15 -> x13, waiting for transfers between devices: 50.8 us -> 83.2 us  [send(): return lax.ppermute(x, 'tp', pairs)]
    ppermute x15 -> x13, starting transfers between devices: 31.4 us -> 42.2 us  [send(): return lax.ppermute(x, 'tp', pairs)]
    ppermute x1, waiting for transfers between devices: 10 us -> 0.01 us  [all_cores(): across = lax.ppermute(cores, 'rep', [(i, i ^ 2) for i in range(4)])]
    concatenate x4 -> x2, other arithmetic: 9.34 us -> 0.64 us  [the longest x1 0.57 us: all_cores(): return jnp.concatenate([from_rep(r) for r in range(4)], axis=0)]
    pallas_call x4, Pallas kernels: 13.4 us -> 5.11 us  [lend(): pl.pallas_call(functools.partial(lend_kernel, blocks=blocks, width=256),...]
    select_n x2 -> x0, other arithmetic: 3.45 us -> none  [on_line(): jnp.where(inner, received[p], activations[p])]
    slice x1 -> x2, local copies, waits for them, and re-layouts: 3.11 us -> 4.45 us  [the longest x1 3.09 us: on_line(): top, near = lax.optimization_barrier((activations[:rows // 2], near))]
  transfers between devices with their start and end apart: 24 -> 24, of which waited for: 10 -> 9; matrix products, arithmetic and copies ran while one was open for 26% -> 15% of each run, Pallas kernels for 9% -> 4%
where the time goes in v3:
time: 185 us; the launch traced here: 184 us
  waiting for transfers between devices  90.7 us (49%)
  starting transfers between devices  49.7 us (27%)
  matrix products  20.6 us (11%)
  local copies, waits for them, and re-layouts  8.46 us (5%)
  other arithmetic  7.34 us (4%)
  Pallas kernels  7.19 us (4%)
    ppermute x13, waiting for transfers between devices, send(): return lax.ppermute(x, 'tp', pairs)  83.2 us
    ppermute x13, starting transfers between devices, send(): return lax.ppermute(x, 'tp', pairs)  42.2 us
    dot_general x8, matrix products, dot(): return jnp.dot(a, b, preferred_element_type=jnp.float32)  20.6 us
    ppermute x2, waiting for transfers between devices, swap_groups(): return lax.ppermute(x, 'groups', [(0, 1), (1, 0)])  6.56 us
    pallas_call x4, Pallas kernels, lend(): pl.pallas_call(functools.partial(lend_kernel, blocks=blocks, width=256),...  5.11 us
  transfers between devices with their start and end apart: 24, of which 9 were waited for; matrix products, arithmetic and copies ran while one was open for 15% of the time, Pallas kernels for 4%

profile of v3, /device:TPU:0, one launch (start us, length us, event | category | flops | bytes accessed | tf_op | source)
XLA Modules:
  0.0 184.5 jit_solution(11130618864374825132)
XLA Ops:
  0.0 1.4 constant_dynamic-slice_fusion.1
  1.4 0.1 pad_maximum_fusion.1
  1.5 5.0 %collective-permute-start = (bf16[512,1024]{1,0:T(8,128)(2,1)S(1)}, bf16[512,1024]{1,0:T(8,128)(2,1)S(1)}, u32[]{:S(2)}, u32[]{:S(2)}) collective-permute-start(bf16[512,1024]{1,0:T(8,128)(2,1)S(1)} %pad_maximum_fusion.1), channel_id=1, source_target_pairs={{0,1},{3,2},{4,5},{7,6},{8,9},{11,10},{12,13},{15,14},{16,17},{19,... | collective-permute-start | bytes 3145736 | tf_op jit(solution)/shard_map/ppermute | solution.py:122
  6.5 1.6 collective-permute-start.8
  8.1 0.8 collective-permute-start.2
  8.9 2.3 %fusion.45 = (bf16[512,256]{1,0:T(8,128)(2,1)S(1)}, f32[512,256]{1,0:T(8,128)S(1)}) fusion(bf16[512,2048]{1,0:T(8,128)(2,1)} %param.6, bf16[2048,256]{1,0:T(8,128)(2,1)S(1)} %copy-done), kind=kOutput, calls=%fused_computation.53 | convolution fusion | flops 537001984 | bytes 3932160 | tf_op jit(solution)/shard_map/dot_general | solution.py:14
  11.2 4.0 %collective-permute-start.3 = (bf16[512,256]{1,0:T(8,128)(2,1)S(1)}, bf16[512,256]{1,0:T(8,128)(2,1)S(1)}, u32[]{:S(2)}, u32[]{:S(2)}) collective-permute-start(bf16[512,256]{1,0:T(8,128)(2,1)S(1)} %get-tuple-element.57), channel_id=1, source_target_pairs={{0,1},{3,2},{4,5},{7,6},{8,9},{11,10},{12,13},{15,14},{16,17},{19,... | collective-permute-start | bytes 786440 | tf_op jit(solution)/shard_map/ppermute | solution.py:122
  15.2 3.1 %fusion.42 = (bf16[256,2048]{1,0:T(8,128)(2,1)}, bf16[256,2048]{1,0:T(8,128)(2,1)}) fusion(bf16[512,2048]{1,0:T(8,128)(2,1)} %param.6), kind=kLoop, calls=%fused_computation.50 | loop fusion | bytes 4194304 | tf_op jit(solution)/shard_map/slice | solution.py:160
  18.3 11.7 %collective-permute-done = bf16[512,1024]{1,0:T(8,128)(2,1)S(1)} collective-permute-done((bf16[512,1024]{1,0:T(8,128)(2,1)S(1)}, bf16[512,1024]{1,0:T(8,128)(2,1)S(1)}, u32[]{:S(2)}, u32[]{:S(2)}) %collective-permute-start) | collective-permute-done | bytes 1048608 | tf_op jit(solution)/shard_map/ppermute | solution.py:122
  30.0 0.1 fusion.44
  30.1 2.5 %collective-permute-start.1 = (bf16[256,2048]{1,0:T(8,128)(2,1)}, bf16[256,2048]{1,0:T(8,128)(2,1)}, u32[]{:S(2)}, u32[]{:S(2)}) collective-permute-start(bf16[256,2048]{1,0:T(8,128)(2,1)} %get-tuple-element.24), channel_id=1, source_target_pairs={{0,1},{3,2},{1,0},{2,3},{4,5},{7,6},{5,4},{6,7},{8,9},{11,10},{9,8... | collective-permute-start | bytes 3145736 | tf_op jit(solution)/shard_map/ppermute | solution.py:122
  32.6 0.1 collective-permute-start.10
  32.7 2.9 %collective-permute-done.3 = bf16[512,256]{1,0:T(8,128)(2,1)S(1)} collective-permute-done((bf16[512,256]{1,0:T(8,128)(2,1)S(1)}, bf16[512,256]{1,0:T(8,128)(2,1)S(1)}, u32[]{:S(2)}, u32[]{:S(2)}) %collective-permute-start.3) | collective-permute-done | bytes 262176 | tf_op jit(solution)/shard_map/ppermute | solution.py:122
  35.6 0.1 fusion.23
  35.7 0.7 collective-permute-start.4
  36.4 1.6 collective-permute-start.6
  38.0 0.7 copy-done.13
  38.7 1.5 collective-permute-start.7
  40.2 0.1 copy.7.ids_ref
  40.3 1.3 add_convert_fusion
  41.6 0.0 copy-start.5
  41.6 0.0 copy-start.7
  41.6 6.6 %collective-permute-done.6 = bf16[256,1024]{1,0:T(8,128)(2,1)} collective-permute-done((bf16[256,1024]{1,0:T(8,128)(2,1)S(1)}, bf16[256,1024]{1,0:T(8,128)(2,1)}, u32[]{:S(2)}, u32[]{:S(2)}) %collective-permute-start.6) | collective-permute-done | bytes 524320 | tf_op jit(solution)/shard_map/ppermute | solution.py:130
  48.2 1.1 pad_maximum_fusion.2.rest_0_
  49.3 0.8 collective-permute-done.7
  50.1 1.3 pad_maximum_fusion.3.rest_0_
  51.4 5.6 %collective-permute-done.1 = bf16[256,2048]{1,0:T(8,128)(2,1)} collective-permute-done((bf16[256,2048]{1,0:T(8,128)(2,1)}, bf16[256,2048]{1,0:T(8,128)(2,1)}, u32[]{:S(2)}, u32[]{:S(2)}) %collective-permute-start.1) | collective-permute-done | bytes 1048608 | tf_op jit(solution)/shard_map/ppermute | solution.py:122
  57.1 0.0 slice-start
  57.1 1.9 %select_select_fusion.3 = (bf16[8,256,256]{2,1,0:T(8,128)(2,1)S(1)}, bf16[8,256,256]{2,1,0:T(8,128)(2,1)S(1)}, bf16[8,256,256]{2,1,0:T(8,128)(2,1)S(1)}, bf16[8,256,256]{2,1,0:T(8,128)(2,1)S(1)}) fusion(bf16[8,256,256]{2,1,0:T(8,128)(2,1)} %collective-permute-done.8, bf16[8,256,256]{2,1,0:T(8,128)(2,1)} %collective-permute-done.10, ...), kind=kLoop, calls=%fused_computation.29 | loop fusion | flops 6291456 | bytes 8388620 | tf_op jit(solution)/shard_map/select_n | solution.py:111
  59.0 0.0 slice-start.2
  59.0 0.6 pad_maximum_fusion.cores_ref
  59.6 1.4 copy-done.11
  61.0 21.8 %collective-permute-start.11 = (bf16[256,2048]{1,0:T(8,128)(2,1)S(1)}, bf16[256,2048]{1,0:T(8,128)(2,1)S(1)}, u32[]{:S(2)}, u32[]{:S(2)}) collective-permute-start(bf16[256,2048]{1,0:T(8,128)(2,1)S(1)} %copy-done.11), channel_id=1, source_target_pairs={{0,1},{3,2},{1,0},{2,3},{4,5},{7,6},{5,4},{6,7},{8,9},{11,10},{9,8... | collective-permute-start | bytes 3145736 | tf_op jit(solution)/shard_map/ppermute | solution.py:122
  82.8 1.5 collective-permute-start.14
  84.3 0.5 collective-permute-start.17
  84.9 6.5 %fusion.4 = f32[1024,512]{0,1:T(8,128)} fusion(bf16[512,2048]{1,0:T(8,128)(2,1)} %param.6, bf16[8192,1024]{1,0:T(8,128)(2,1)} %param.8, s32[]{:T(128)S(6)} %select_n.151), kind=kOutput, calls=%fused_computation.5 | convolution fusion | flops 2147483648 | bytes 8388612 | tf_op jit(solution)/shard_map/dot_general | solution.py:14
  91.4 1.3 collective-permute-start.5
  92.7 3.7 %fusion.2 = f32[512,1024]{1,0:T(8,128)} fusion(bf16[512,2048]{1,0:T(8,128)(2,1)S(1)} %collective-permute-done.2.x_ref, bf16[8192,1024]{1,0:T(8,128)(2,1)S(1)} %bitcast.17, s32[]{:T(128)S(6)} %select_n.194), kind=kOutput, calls=%fused_computation.3 | convolution fusion | flops 2147483648 | bytes 8388612 | tf_op jit(solution)/shard_map/dot_general | solution.py:14
  96.4 14.2 %collective-permute-done.5 = bf16[512,256]{1,0:T(8,128)(2,1)S(1)} collective-permute-done((bf16[512,256]{1,0:T(8,128)(2,1)S(1)}, bf16[512,256]{1,0:T(8,128)(2,1)S(1)}, u32[]{:S(2)}, u32[]{:S(2)}) %collective-permute-start.5) | collective-permute-done | bytes 262176 | tf_op jit(solution)/shard_map/ppermute | solution.py:122
  110.6 0.7 collective-permute-start.12
  111.3 0.6 collective-permute-start.16
  111.9 0.2 collective-permute-start.19
  112.1 2.1 %mix.1 = bf16[512,256]{1,0:T(8,128)(2,1)S(1)} custom-call(s32[512,1]{1,0:T(8,128)S(1)} %copy.7.ids_ref, bf16[512,256]{1,0:T(8,128)(2,1)S(1)} %broadcast_select_fusion.coded_ref, bf16[32,256,256]{2,1,0:T(8,128)(2,1)S(1)} %pad_maximum_fusion.cores_ref), custom_call_target="tpu_custom_call" | custom-call | flops 402653184 | bytes 4718592 | tf_op jit(solution)/shard_map/mix/pallas_call | solution.py:44
  114.2 1.4 fusion.43
  115.6 0.7 collective-permute-start.13
  116.3 0.4 fusion.46
  116.7 2.3 %lend_near.1 = f32[512,1024]{1,0:T(8,128)S(1)} custom-call(s32[1]{0:T(128)} %bitcast.1.spot_ref, bf16[512,2048]{1,0:T(8,128)(2,1)S(1)} %collective-permute-done.2.x_ref, bf16[512,1024]{1,0:T(8,128)(2,1)S(1)} %pad_maximum_fusion.2.rest_0_, bf16[512,1024]{1,0:T(8,128)(2,1)S(1)} %collective-permute-done.17.rest_1_, ...), custom_call_target="tpu_custom_call" | custom-call | flops 2147483648 | bytes 7340032 | tf_op jit(solution)/shard_map/lend_near/pallas_call | solution.py:85
  119.1 0.1 slice.53.rest_4_
  119.2 1.3 lend_far.3
  120.5 0.9 collective-permute-start.21
  121.4 1.3 collective-permute-start.20
  122.7 4.9 %fusion.16 = f32[512,1024]{1,0:T(8,128)S(1)} fusion(f32[512,1024]{1,0:T(8,128)} %fusion.2, f32[512,1024]{1,0:T(8,128)S(1)} %fusion.46, f32[1024,512]{0,1:T(8,128)} %fusion.4, bf16[8192,1024]{1,0:T(8,128)(2,1)S(1)} %bitcast.17, s32[]{:T(128)S(6)} %select_n.198, bf16[256,2048]{1,0:T(8,128)(2,1)S(1)} %copy-done.9, bf16[256,2048]{1,0:T(8,128)(2,1)} %collective-permute-done.1), kind=kOutput, calls=%fused_computation.18 | convolution fusion | flops 2153250816 | bytes 14680068 | tf_op jit(solution)/shard_map/dot_general | solution.py:14
  127.6 0.1 fusion.41
  127.7 0.7 lend_far.4
  128.5 37.0 %collective-permute-done.20 = bf16[256,1024]{1,0:T(8,128)(2,1)S(1)} collective-permute-done((bf16[256,1024]{1,0:T(8,128)(2,1)S(1)}, bf16[256,1024]{1,0:T(8,128)(2,1)S(1)}, u32[]{:S(2)}, u32[]{:S(2)}) %collective-permute-start.20) | collective-permute-done | bytes 524320 | tf_op jit(solution)/shard_map/ppermute | solution.py:122
  165.5 1.3 collective-permute-start.22
  166.8 0.8 lend_far.5
  167.5 1.3 fusion.18
  168.8 5.6 %collective-permute-done.22 = bf16[128,1024]{1,0:T(8,128)(2,1)S(1)} collective-permute-done((bf16[128,1024]{1,0:T(8,128)(2,1)S(1)}, bf16[128,1024]{1,0:T(8,128)(2,1)S(1)}, u32[]{:S(2)}, u32[]{:S(2)}) %collective-permute-start.22) | collective-permute-done | bytes 262176 | tf_op jit(solution)/shard_map/ppermute | solution.py:122
  174.4 1.3 collective-permute-start.23
  175.7 0.8 fusion.22
  176.5 6.2 %collective-permute-done.23 = bf16[128,1024]{1,0:T(8,128)(2,1)S(1)} collective-permute-done((bf16[128,1024]{1,0:T(8,128)(2,1)S(1)}, bf16[128,1024]{1,0:T(8,128)(2,1)S(1)}, u32[]{:S(2)}, u32[]{:S(2)}) %collective-permute-start.23) | collective-permute-done | bytes 262176 | tf_op jit(solution)/shard_map/ppermute | solution.py:122
  182.7 0.7 fusion.20
  183.4 1.0 pad_maximum_fusion.4
  (52 shorter events, 0.1 us)
Async XLA Ops:
  0.0 8.9 %copy-start = (bf16[2048,256]{1,0:T(8,128)(2,1)S(1)}, bf16[2048,256]{1,0:T(8,128)(2,1)}, u32[]{:S(2)}) copy-start(bf16[2048,256]{1,0:T(8,128)(2,1)} %param.9) | copy-start | bytes 3145732
  0.0 6.5 %copy-start.4 = (bf16[8,256,256]{2,1,0:T(8,128)(2,1)S(1)}, bf16[8,256,256]{2,1,0:T(8,128)(2,1)}, u32[]{:S(2)}) copy-start(bf16[8,256,256]{2,1,0:T(8,128)(2,1)} %param.10) | copy-start | bytes 3145732
  1.5 28.5 %collective-permute-start = (bf16[512,1024]{1,0:T(8,128)(2,1)S(1)}, bf16[512,1024]{1,0:T(8,128)(2,1)S(1)}, u32[]{:S(2)}, u32[]{:S(2)}) collective-permute-start(bf16[512,1024]{1,0:T(8,128)(2,1)S(1)} %pad_maximum_fusion.1), channel_id=1, source_target_pairs={{0,1},{3,2},{4,5},{7,6},{8,9},{11,10},{12,13},{15,14},{16,17},{19,... | collective-permute-start | bytes 3145736 | tf_op jit(solution)/shard_map/ppermute | solution.py:122
  6.5 26.1 %collective-permute-start.8 = (bf16[8,256,256]{2,1,0:T(8,128)(2,1)S(1)}, bf16[8,256,256]{2,1,0:T(8,128)(2,1)}, u32[]{:S(2)}, u32[]{:S(2)}) collective-permute-start(bf16[8,256,256]{2,1,0:T(8,128)(2,1)S(1)} %copy-done.4), channel_id=1, source_target_pairs={{0,8},{4,12},{8,0},{12,4},{1,9},{5,13},{9,1},{13,5},{2,10},{6,14},... | collective-permute-start | bytes 3145736 | tf_op jit(solution)/shard_map/ppermute | solution.py:104
  8.1 24.5 %collective-permute-start.9 = (bf16[8,256,256]{2,1,0:T(8,128)(2,1)S(1)}, bf16[8,256,256]{2,1,0:T(8,128)(2,1)S(1)}, u32[]{:S(2)}, u32[]{:S(2)}) collective-permute-start(bf16[8,256,256]{2,1,0:T(8,128)(2,1)S(1)} %copy-done.4), channel_id=1, source_target_pairs={{0,4},{4,0},{8,12},{12,8},{1,5},{5,1},{9,13},{13,9},{2,6},{6,2},{1... | collective-permute-start | bytes 3145736 | tf_op jit(solution)/shard_map/ppermute | solution.py:103
  8.1 49.0 %collective-permute-start.2 = (bf16[512,2048]{1,0:T(8,128)(2,1)}, bf16[512,2048]{1,0:T(8,128)(2,1)S(1)}, u32[]{:S(2)}, u32[]{:S(2)}) collective-permute-start(bf16[512,2048]{1,0:T(8,128)(2,1)} %param.6), channel_id=1, source_target_pairs={{1,2},{2,1},{5,6},{6,5},{9,10},{10,9},{13,14},{14,13},{17,18},{18,... | collective-permute-start | bytes 6291464 | tf_op jit(solution)/shard_map/ppermute | solution.py:122
  11.2 24.4 %copy-start.2 = (f32[512,256]{1,0:T(8,128)}, f32[512,256]{1,0:T(8,128)S(1)}, u32[]{:S(2)}) copy-start(f32[512,256]{1,0:T(8,128)S(1)} %get-tuple-element.58) | copy-start | bytes 1572868
  11.2 24.4 %collective-permute-start.3 = (bf16[512,256]{1,0:T(8,128)(2,1)S(1)}, bf16[512,256]{1,0:T(8,128)(2,1)S(1)}, u32[]{:S(2)}, u32[]{:S(2)}) collective-permute-start(bf16[512,256]{1,0:T(8,128)(2,1)S(1)} %get-tuple-element.57), channel_id=1, source_target_pairs={{0,1},{3,2},{4,5},{7,6},{8,9},{11,10},{12,13},{15,14},{16,17},{19,... | collective-permute-start | bytes 786440 | tf_op jit(solution)/shard_map/ppermute | solution.py:122
  18.3 21.9 %copy-start.14 = (s32[512,1]{0,1:T(1,128)S(1)}, s32[512,1]{0,1:T(1,128)}, u32[]{:S(2)}) copy-start(s32[512,1]{0,1:T(1,128)} %param.7) | copy-start | bytes 6148
  30.1 19.2 %copy-start.3 = (bf16[256,1024]{1,0:T(8,128)(2,1)}, bf16[256,1024]{1,0:T(8,128)(2,1)S(1)}, u32[]{:S(2)}) copy-start(bf16[256,1024]{1,0:T(8,128)(2,1)S(1)} %get-tuple-element.55) | copy-start | bytes 1572868
  30.1 27.0 %collective-permute-start.1 = (bf16[256,2048]{1,0:T(8,128)(2,1)}, bf16[256,2048]{1,0:T(8,128)(2,1)}, u32[]{:S(2)}, u32[]{:S(2)}) collective-permute-start(bf16[256,2048]{1,0:T(8,128)(2,1)} %get-tuple-element.24), channel_id=1, source_target_pairs={{0,1},{3,2},{1,0},{2,3},{4,5},{7,6},{5,4},{6,7},{8,9},{11,10},{9,8... | collective-permute-start | bytes 3145736 | tf_op jit(solution)/shard_map/ppermute | solution.py:122
  32.6 5.3 %copy-start.6 = (bf16[8,256,256]{2,1,0:T(8,128)(2,1)}, bf16[8,256,256]{2,1,0:T(8,128)(2,1)S(1)}, u32[]{:S(2)}) copy-start(bf16[8,256,256]{2,1,0:T(8,128)(2,1)S(1)} %collective-permute-done.9) | copy-start | bytes 3145732
  32.6 24.4 %collective-permute-start.10 = (bf16[8,256,256]{2,1,0:T(8,128)(2,1)}, bf16[8,256,256]{2,1,0:T(8,128)(2,1)}, u32[]{:S(2)}, u32[]{:S(2)}) collective-permute-start(bf16[8,256,256]{2,1,0:T(8,128)(2,1)} %collective-permute-done.8), channel_id=1, source_target_pairs={{0,4},{4,0},{8,12},{12,8},{1,5},{5,1},{9,13},{13,9},{2,6},{6,2},{1... | collective-permute-start | bytes 3145736 | tf_op jit(solution)/shard_map/ppermute | solution.py:106
  35.6 2.3 %copy-start.10 = (bf16[512,256]{1,0:T(8,128)(2,1)}, bf16[512,256]{1,0:T(8,128)(2,1)S(1)}, u32[]{:S(2)}) copy-start(bf16[512,256]{1,0:T(8,128)(2,1)S(1)} %collective-permute-done.3) | copy-start | bytes 786436
  35.7 2.3 %collective-permute-start.4 = (bf16[512,256]{1,0:T(8,128)(2,1)S(1)}, bf16[512,256]{1,0:T(8,128)(2,1)S(1)}, u32[]{:S(2)}, u32[]{:S(2)}) collective-permute-start(bf16[512,256]{1,0:T(8,128)(2,1)S(1)} %fusion.23), channel_id=1, source_target_pairs={{1,2},{2,1},{5,6},{6,5},{9,10},{10,9},{13,14},{14,13},{17,18},{18,... | collective-permute-start | bytes 786440 | tf_op jit(solution)/shard_map/ppermute | solution.py:122
  36.4 11.8 %collective-permute-start.6 = (bf16[256,1024]{1,0:T(8,128)(2,1)S(1)}, bf16[256,1024]{1,0:T(8,128)(2,1)}, u32[]{:S(2)}, u32[]{:S(2)}) collective-permute-start(bf16[256,1024]{1,0:T(8,128)(2,1)S(1)} %get-tuple-element.26), channel_id=1, source_target_pairs={{0,16},{16,0},{1,17},{17,1},{2,18},{18,2},{3,19},{19,3},{4,20},{20... | collective-permute-start | bytes 1572872 | tf_op jit(solution)/shard_map/ppermute | solution.py:130
  37.9 0.7 copy-start.13
  38.7 11.5 %collective-permute-start.7 = (bf16[256,1024]{1,0:T(8,128)(2,1)S(1)}, bf16[256,1024]{1,0:T(8,128)(2,1)}, u32[]{:S(2)}, u32[]{:S(2)}) collective-permute-start(bf16[256,1024]{1,0:T(8,128)(2,1)S(1)} %get-tuple-element.55), channel_id=1, source_target_pairs={{0,8},{4,12},{8,0},{12,4},{1,9},{5,13},{9,1},{13,5},{2,10},{6,14},... | collective-permute-start | bytes 1572872 | tf_op jit(solution)/shard_map/ppermute | solution.py:126
  41.6 15.4 %copy-start.5 = (bf16[8,256,256]{2,1,0:T(8,128)(2,1)S(1)}, bf16[8,256,256]{2,1,0:T(8,128)(2,1)}, u32[]{:S(2)}) copy-start(bf16[8,256,256]{2,1,0:T(8,128)(2,1)} %param.10) | copy-start | bytes 3145732
  41.6 15.4 %copy-start.7 = (bf16[8,256,256]{2,1,0:T(8,128)(2,1)S(1)}, bf16[8,256,256]{2,1,0:T(8,128)(2,1)}, u32[]{:S(2)}) copy-start(bf16[8,256,256]{2,1,0:T(8,128)(2,1)} %copy-done.6) | copy-start | bytes 3145732
  57.1 35.6 %slice-start = ((s8[16777216]{0:T(1024)(128)(4,1)}), s8[4194304]{0:T(1024)(128)(4,1)S(1)}, s32[]{:S(2)}) async-start(s8[16777216]{0:T(1024)(128)(4,1)} %bitcast.16), calls=%async_computation | async-start | bytes 8388608
  57.1 35.6 %slice-start.1 = ((s8[16777216]{0:T(1024)(128)(4,1)}), s8[4194304]{0:T(1024)(128)(4,1)S(1)}, s32[]{:S(2)}) async-start(s8[16777216]{0:T(1024)(128)(4,1)} %bitcast.16), calls=%async_computation.1 | async-start | bytes 8388608
  59.0 2.0 %copy-start.11 = (bf16[256,2048]{1,0:T(8,128)(2,1)S(1)}, bf16[256,2048]{1,0:T(8,128)(2,1)}, u32[]{:S(2)}) copy-start(bf16[256,2048]{1,0:T(8,128)(2,1)} %get-tuple-element.32) | copy-start | bytes 3145732
  59.0 33.7 %slice-start.2 = ((s8[16777216]{0:T(1024)(128)(4,1)}), s8[4194304]{0:T(1024)(128)(4,1)S(1)}, s32[]{:S(2)}) async-start(s8[16777216]{0:T(1024)(128)(4,1)} %bitcast.16), calls=%async_computation.2 | async-start | bytes 8388608
  61.0 31.7 %slice-start.3 = ((s8[16777216]{0:T(1024)(128)(4,1)}), s8[4194304]{0:T(1024)(128)(4,1)S(1)}, s32[]{:S(2)}) async-start(s8[16777216]{0:T(1024)(128)(4,1)} %bitcast.16), calls=%async_computation.3 | async-start | bytes 8388608
  61.0 49.6 %collective-permute-start.11 = (bf16[256,2048]{1,0:T(8,128)(2,1)S(1)}, bf16[256,2048]{1,0:T(8,128)(2,1)S(1)}, u32[]{:S(2)}, u32[]{:S(2)}) collective-permute-start(bf16[256,2048]{1,0:T(8,128)(2,1)S(1)} %copy-done.11), channel_id=1, source_target_pairs={{0,1},{3,2},{1,0},{2,3},{4,5},{7,6},{5,4},{6,7},{8,9},{11,10},{9,8... | collective-permute-start | bytes 3145736 | tf_op jit(solution)/shard_map/ppermute | solution.py:122
  82.8 28.5 %collective-permute-start.14 = (bf16[512,1024]{1,0:T(8,128)(2,1)S(1)}, bf16[512,1024]{1,0:T(8,128)(2,1)S(1)}, u32[]{:S(2)}, u32[]{:S(2)}) collective-permute-start(bf16[512,1024]{1,0:T(8,128)(2,1)S(1)} %pad_maximum_fusion.3.rest_0_), channel_id=1, source_target_pairs={{0,16},{16,0},{1,17},{17,1},{2,18},{18,2},{3,19},{19,3},{4,20},{20... | collective-permute-start | bytes 3145736 | tf_op jit(solution)/shard_map/ppermute | solution.py:130
  84.3 27.6 %collective-permute-start.17 = (bf16[512,1024]{1,0:T(8,128)(2,1)S(1)}, bf16[512,1024]{1,0:T(8,128)(2,1)S(1)}, u32[]{:S(2)}, u32[]{:S(2)}) collective-permute-start(bf16[512,1024]{1,0:T(8,128)(2,1)S(1)} %pad_maximum_fusion.2.rest_0_), channel_id=1, source_target_pairs={{0,8},{4,12},{8,0},{12,4},{1,9},{5,13},{9,1},{13,5},{2,10},{6,14},... | collective-permute-start | bytes 3145736 | tf_op jit(solution)/shard_map/ppermute | solution.py:126
  91.4 24.2 %collective-permute-start.18 = (bf16[512,1024]{1,0:T(8,128)(2,1)S(1)}, bf16[512,1024]{1,0:T(8,128)(2,1)S(1)}, u32[]{:S(2)}, u32[]{:S(2)}) collective-permute-start(bf16[512,1024]{1,0:T(8,128)(2,1)S(1)} %pad_maximum_fusion.2.rest_0_), channel_id=1, source_target_pairs={{0,4},{4,0},{8,12},{12,8},{1,5},{5,1},{9,13},{13,9},{2,6},{6,2},{1... | collective-permute-start | bytes 3145736 | tf_op jit(solution)/shard_map/ppermute | solution.py:126
  91.4 19.2 %collective-permute-start.5 = (bf16[512,256]{1,0:T(8,128)(2,1)S(1)}, bf16[512,256]{1,0:T(8,128)(2,1)S(1)}, u32[]{:S(2)}, u32[]{:S(2)}) collective-permute-start(bf16[512,256]{1,0:T(8,128)(2,1)S(1)} %add_convert_fusion), channel_id=1, source_target_pairs={{1,0},{2,3},{5,4},{6,7},{9,8},{10,11},{13,12},{14,15},{17,16},{18,... | collective-permute-start | bytes 786440 | tf_op jit(solution)/shard_map/ppermute | solution.py:122
  110.6 8.6 %collective-permute-start.15 = (bf16[512,1024]{1,0:T(8,128)(2,1)S(1)}, bf16[512,1024]{1,0:T(8,128)(2,1)S(1)}, u32[]{:S(2)}, u32[]{:S(2)}) collective-permute-start(bf16[512,1024]{1,0:T(8,128)(2,1)S(1)} %pad_maximum_fusion.3.rest_0_), channel_id=1, source_target_pairs={{0,4},{4,0},{8,12},{12,8},{1,5},{5,1},{9,13},{13,9},{2,6},{6,2},{1... | collective-permute-start | bytes 3145736 | tf_op jit(solution)/shard_map/ppermute | solution.py:126
  110.6 1.3 copy-start.8
  110.6 8.6 %collective-permute-start.12 = (bf16[256,2048]{1,0:T(8,128)(2,1)}, bf16[256,2048]{1,0:T(8,128)(2,1)S(1)}, u32[]{:S(2)}, u32[]{:S(2)}) collective-permute-start(bf16[256,2048]{1,0:T(8,128)(2,1)} %collective-permute-done.1), channel_id=1, source_target_pairs={{1,2},{2,1},{5,6},{6,5},{9,10},{10,9},{13,14},{14,13},{17,18},{18,... | collective-permute-start | bytes 3145736 | tf_op jit(solution)/shard_map/ppermute | solution.py:122
  111.3 7.9 %collective-permute-start.16 = (bf16[512,1024]{1,0:T(8,128)(2,1)S(1)}, bf16[512,1024]{1,0:T(8,128)(2,1)S(1)}, u32[]{:S(2)}, u32[]{:S(2)}) collective-permute-start(bf16[512,1024]{1,0:T(8,128)(2,1)S(1)} %collective-permute-done.14.rest_1_), channel_id=1, source_target_pairs={{0,4},{4,0},{8,12},{12,8},{1,5},{5,1},{9,13},{13,9},{2,6},{6,2},{1... | collective-permute-start | bytes 3145736 | tf_op jit(solution)/shard_map/ppermute | solution.py:126
  111.9 4.8 %collective-permute-start.19 = (bf16[512,1024]{1,0:T(8,128)(2,1)S(1)}, bf16[512,1024]{1,0:T(8,128)(2,1)S(1)}, u32[]{:S(2)}, u32[]{:S(2)}) collective-permute-start(bf16[512,1024]{1,0:T(8,128)(2,1)S(1)} %collective-permute-done.17.rest_1_), channel_id=1, source_target_pairs={{0,4},{4,0},{8,12},{12,8},{1,5},{5,1},{9,13},{13,9},{2,6},{6,2},{1... | collective-permute-start | bytes 3145736 | tf_op jit(solution)/shard_map/ppermute | solution.py:126
  114.2 2.1 %copy-start.12 = (bf16[256,1024]{1,0:T(8,128)(2,1)S(1)}, bf16[256,1024]{1,0:T(8,128)(2,1)}, u32[]{:S(2)}) copy-start(bf16[256,1024]{1,0:T(8,128)(2,1)} %param.11) | copy-start | bytes 1572868
  115.6 4.9 %collective-permute-start.13 = (bf16[128,2048]{1,0:T(8,128)(2,1)S(1)}, bf16[128,2048]{1,0:T(8,128)(2,1)S(1)}, u32[]{:S(2)}, u32[]{:S(2)}) collective-permute-start(bf16[128,2048]{1,0:T(8,128)(2,1)S(1)} %get-tuple-element.53), channel_id=1, source_target_pairs={{1,2},{2,1},{5,6},{6,5},{9,10},{10,9},{13,14},{14,13},{17,18},{18,... | collective-permute-start | bytes 1572872 | tf_op jit(solution)/shard_map/ppermute | solution.py:122
  119.2 3.5 %copy-start.9 = (bf16[256,2048]{1,0:T(8,128)(2,1)S(1)}, bf16[256,2048]{1,0:T(8,128)(2,1)}, u32[]{:S(2)}) copy-start(bf16[256,2048]{1,0:T(8,128)(2,1)} %copy-done.8) | copy-start | bytes 3145732
  120.5 8.0 %collective-permute-start.21 = (bf16[128,2048]{1,0:T(8,128)(2,1)S(1)}, bf16[128,2048]{1,0:T(8,128)(2,1)S(1)}, u32[]{:S(2)}, u32[]{:S(2)}) collective-permute-start(bf16[128,2048]{1,0:T(8,128)(2,1)S(1)} %get-tuple-element.37), channel_id=1, source_target_pairs={{1,2},{2,1},{5,6},{6,5},{9,10},{10,9},{13,14},{14,13},{17,18},{18,... | collective-permute-start | bytes 1572872 | tf_op jit(solution)/shard_map/ppermute | solution.py:122
  121.4 44.1 %collective-permute-start.20 = (bf16[256,1024]{1,0:T(8,128)(2,1)S(1)}, bf16[256,1024]{1,0:T(8,128)(2,1)S(1)}, u32[]{:S(2)}, u32[]{:S(2)}) collective-permute-start(bf16[256,1024]{1,0:T(8,128)(2,1)S(1)} %lend_far.3), channel_id=1, source_target_pairs={{1,0},{2,3},{5,4},{6,7},{9,8},{10,11},{13,12},{14,15},{17,16},{18,... | collective-permute-start | bytes 1572872 | tf_op jit(solution)/shard_map/ppermute | solution.py:122
  165.5 8.9 %collective-permute-start.22 = (bf16[128,1024]{1,0:T(8,128)(2,1)S(1)}, bf16[128,1024]{1,0:T(8,128)(2,1)S(1)}, u32[]{:S(2)}, u32[]{:S(2)}) collective-permute-start(bf16[128,1024]{1,0:T(8,128)(2,1)S(1)} %lend_far.4), channel_id=1, source_target_pairs={{1,0},{2,3},{5,4},{6,7},{9,8},{10,11},{13,12},{14,15},{17,16},{18,... | collective-permute-start | bytes 786440 | tf_op jit(solution)/shard_map/ppermute | solution.py:122
  174.4 8.3 %collective-permute-start.23 = (bf16[128,1024]{1,0:T(8,128)(2,1)S(1)}, bf16[128,1024]{1,0:T(8,128)(2,1)S(1)}, u32[]{:S(2)}, u32[]{:S(2)}) collective-permute-start(bf16[128,1024]{1,0:T(8,128)(2,1)S(1)} %lend_far.5), channel_id=1, source_target_pairs={{1,0},{2,3},{5,4},{6,7},{9,8},{10,11},{13,12},{14,15},{17,16},{18,... | collective-permute-start | bytes 786440 | tf_op jit(solution)/shard_map/ppermute | solution.py:122
  182.7 1.8 copy-start.1

commit v4 on v3

--- a/solution.py
+++ b/solution.py
@@ -150,54 +150,53 @@
 
     swapped = send(activations, SWAP)
     pieces = send(jnp.concatenate([piece_of(far_in), piece_of(far_out)], axis=0), IN)
+    cores = all_cores(adapter_cores)
+    near, far = pieces[:piece], pieces[piece:]
     partial_value = dot(activations, basis_down)
-    side = send(partial_value.astype(jnp.bfloat16), IN).astype(jnp.float32) + partial_value
-    whole = side + send(side.astype(jnp.bfloat16), SWAP).astype(jnp.float32)
-    coded = whole.astype(jnp.bfloat16)
-    cores = all_cores(adapter_cores)
-
-    near, far = pieces[:piece], pieces[piece:]
-    top, near = lax.optimization_barrier((activations[: rows // 2], near))
+    top, near, side = lax.optimization_barrier(
+        (activations[: rows // 2], near, partial_value.astype(jnp.bfloat16))
+    )
     turned = [send(top, IN + OUT)]
+    side = send(side, IN).astype(jnp.float32) + partial_value
+
+    near, far, cores, own = lax.optimization_barrier((near, far, cores, activations))
+    base = dot(own, weight_of(me))
     near = jnp.concatenate([near, swap_groups(near)], axis=0)
     far = jnp.concatenate([far, swap_rep(far, 2)], axis=0)
-    near, far, cores = lax.optimization_barrier((near, far, cores))
     near_more, far_more = swap_rep(near, 2), swap_groups(far)
     near_weights = (near, near_more, swap_rep(near, 1), swap_rep(near_more, 1))
     far_weights = (far, far_more, swap_rep(far, 1), swap_rep(far_more, 1))
     near_blocks = ((0, 0, (0, 4)), (1, 0, (2, 6)), (2, 0, (1, 5)), (3, 0, (3, 7)))
     far_blocks = ((0, 0, (0, 2)), (1, 0, (4, 6)), (2, 0, (1, 3)), (3, 0, (5, 7)))
 
-    bottom, turned[0], swapped, coded = lax.optimization_barrier(
-        (activations[rows // 2 :], turned[0], swapped, coded)
-    )
+    bottom, turned[0], swapped, base, half = lax.optimization_barrier(
+        (activations[rows // 2 :], turned[0], swapped, base, side.astype(jnp.bfloat16))
+    )
+    turned.append(send(bottom, IN + OUT))
+    coded = (side + send(half, SWAP).astype(jnp.float32)).astype(jnp.bfloat16)
     coded = jnp.where(inner, coded, send(coded, OUT))
-    turned.append(send(bottom, IN + OUT))
-    mixed = mix(row_adapter, coded, cores)
-
-    base = dot(activations, weight_of(me)) + dot(mixed, basis_up)
+    base = base + dot(mix(row_adapter, coded, cores), basis_up)
     base = base + dot(swapped, weight_of(far_in))
     base = base + dot(
         jnp.concatenate(turned, 0), weight_of(jnp.where(inner, near_out, near_in))
     )
     lent = lend(spot, swapped, near_weights, near_blocks, None, jnp.float32, "lend_near")
     last_weight = weight_of(far_out)
-    crossed, sent = [], []
+    crossed, sent, back, out = [], [], [], []
     for i, p in enumerate(parts):
         x = turned[0] if i == 0 else turned[1][p.start - rows // 2 : p.stop - rows // 2]
+        if i == 1:
+            x, crossed[0] = lax.optimization_barrier((x, crossed[0]))
         if i > 1:
             x, sent[i - 2] = lax.optimization_barrier((x, sent[i - 2]))
         crossed.append(send(x, SWAP))
         x = crossed[i]
         if i:
-            x, sent[i - 1] = lax.optimization_barrier((x, sent[i - 1]))
+            x, back[i - 1] = lax.optimization_barrier((x, back[i - 1]))
         sent.append(lend(spot, x, far_weights, far_blocks, lent[p], jnp.bfloat16, "lend_far"))
-    out, back = [], None
-    for p, x, y in zip(parts, crossed, sent):
-        if back is not None:
-            y, back = lax.optimization_barrier((y, back))
-        back = send(y, OUT)
-        out.append((base[p] + dot(x, last_weight) + back.astype(jnp.float32)).astype(jnp.bfloat16))
+        back.append(send(sent[i], OUT))
+    for p, x, y in zip(parts, crossed, back):
+        out.append((base[p] + dot(x, last_weight) + y.astype(jnp.float32)).astype(jnp.bfloat16))
     return jnp.concatenate(out, axis=0)
 
 

time: 185 us -> 142 us (0.77)
  waiting for transfers between devices: 90.7 us -> 64.4 us
  starting transfers between devices: 49.7 us -> 28.4 us
  matrix products: 20.6 us -> 24.6 us
    ppermute x13, waiting for transfers between devices: 83.2 us -> 49.8 us  [send(): return lax.ppermute(x, 'tp', pairs)]
    ppermute x13, starting transfers between devices: 42.2 us -> 20.2 us  [send(): return lax.ppermute(x, 'tp', pairs)]
    ppermute x1, waiting for transfers between devices: 0.01 us -> 14.7 us  [all_cores(): across = lax.ppermute(cores, 'rep', [(i, i ^ 2) for i in range(4)])]
    ppermute x2, waiting for transfers between devices: 6.56 us -> 0.01 us  [swap_groups(): return lax.ppermute(x, 'groups', [(0, 1), (1, 0)])]
    dot_general x8, matrix products: 20.6 us -> 24.6 us  [dot(): return jnp.dot(a, b, preferred_element_type=jnp.float32)]
    concatenate x2 -> x0, other arithmetic: 2.38 us -> none  [the longest x1 1.27 us: on_line(): far = jnp.concatenate([far, swap_rep(far, 2)], axis=0)]
    unnamed x39 -> x37, local copies, waits for them, and re-layouts: 2.33 us -> 0.3 us
  transfers between devices with their start and end apart: 24 -> 24, of which waited for: 9 -> 8; matrix products, arithmetic and copies ran while one was open for 15% -> 27% of each run, Pallas kernels for 4% -> 6%
where the time goes in v4:
time: 142 us
  waiting for transfers between devices  64.4 us (45%)
  starting transfers between devices  28.4 us (20%)
  matrix products  24.6 us (17%)
  Pallas kernels  8.59 us (6%)
  other arithmetic  7.96 us (6%)
  local copies, waits for them, and re-layouts  7.45 us (5%)
    ppermute x13, waiting for transfers between devices, send(): return lax.ppermute(x, 'tp', pairs)  49.8 us
    dot_general x8, matrix products, dot(): return jnp.dot(a, b, preferred_element_type=jnp.float32)  24.6 us
    ppermute x13, starting transfers between devices, send(): return lax.ppermute(x, 'tp', pairs)  20.2 us
    ppermute x1, waiting for transfers between devices, all_cores(): across = lax.ppermute(cores, 'rep', [(i, i ^ 2) for i in range(4)])  14.7 us
    pallas_call x4, Pallas kernels, lend(): pl.pallas_call(functools.partial(lend_kernel, blocks=blocks, width=256),...  6.52 us
    ppermute x2, starting transfers between devices, swap_groups(): return lax.ppermute(x, 'groups', [(0, 1), (1, 0)])  3.1 us
    slice x1, local copies, waits for them, and re-layouts, on_line(): activations[:rows // 2]  3.09 us
    ppermute x1, starting transfers between devices, all_cores(): across = lax.ppermute(cores, 'rep', [(i, i ^ 2) for i in range(4)])  2.94 us
  transfers between devices with their start and end apart: 24, of which 8 were waited for; matrix products, arithmetic and copies ran while one was open for 27% of the time, Pallas kernels for 6%

profile of v4, /device:TPU:0, one launch (start us, length us, event | category | flops | bytes accessed | tf_op | source)
XLA Modules:
  0.0 142.0 jit_solution(10105826867898638386)
XLA Ops:
  0.0 2.9 %collective-permute-start.3 = (bf16[8,256,256]{2,1,0:T(8,128)(2,1)}, bf16[8,256,256]{2,1,0:T(8,128)(2,1)}, u32[]{:S(2)}, u32[]{:S(2)}) collective-permute-start(bf16[8,256,256]{2,1,0:T(8,128)(2,1)} %param.10), channel_id=1, source_target_pairs={{0,8},{4,12},{8,0},{12,4},{1,9},{5,13},{9,1},{13,5},{2,10},{6,14},... | collective-permute-start | bytes 3145736 | tf_op jit(solution)/shard_map/ppermute | solution.py:104
  2.9 1.3 constant_dynamic-slice_fusion.1
  4.2 0.1 pad_maximum_fusion.1
  4.3 3.5 %collective-permute-start = (bf16[512,1024]{1,0:T(8,128)(2,1)S(1)}, bf16[512,1024]{1,0:T(8,128)(2,1)S(1)}, u32[]{:S(2)}, u32[]{:S(2)}) collective-permute-start(bf16[512,1024]{1,0:T(8,128)(2,1)S(1)} %pad_maximum_fusion.1), channel_id=1, source_target_pairs={{0,1},{3,2},{4,5},{7,6},{8,9},{11,10},{12,13},{15,14},{16,17},{19,... | collective-permute-start | bytes 3145736 | tf_op jit(solution)/shard_map/ppermute | solution.py:122
  7.8 0.8 collective-permute-start.2
  8.7 3.1 %fusion.38 = (bf16[256,2048]{1,0:T(8,128)(2,1)}, bf16[256,2048]{1,0:T(8,128)(2,1)}) fusion(bf16[512,2048]{1,0:T(8,128)(2,1)} %param.6), kind=kLoop, calls=%fused_computation.50 | loop fusion | bytes 4194304 | tf_op jit(solution)/shard_map/slice | solution.py:157
  11.7 14.7 %collective-permute-done.3 = bf16[8,256,256]{2,1,0:T(8,128)(2,1)} collective-permute-done((bf16[8,256,256]{2,1,0:T(8,128)(2,1)}, bf16[8,256,256]{2,1,0:T(8,128)(2,1)}, u32[]{:S(2)}, u32[]{:S(2)}) %collective-permute-start.3) | collective-permute-done | bytes 1048608 | tf_op jit(solution)/shard_map/ppermute | solution.py:104
  26.4 0.0 collective-permute-start.5
  26.4 3.1 %fusion.41 = (bf16[512,256]{1,0:T(8,128)(2,1)S(1)}, f32[512,256]{1,0:T(8,128)}) fusion(bf16[512,2048]{1,0:T(8,128)(2,1)} %param.6, bf16[2048,256]{1,0:T(8,128)(2,1)S(1)} %copy-done), kind=kOutput, calls=%fused_computation.53 | convolution fusion | flops 537001984 | bytes 3932160 | tf_op jit(solution)/shard_map/dot_general | solution.py:14
  29.6 1.3 collective-permute-done
  30.9 1.1 fusion.40
  31.9 4.4 %collective-permute-start.6 = (bf16[512,256]{1,0:T(8,128)(2,1)S(1)}, bf16[512,256]{1,0:T(8,128)(2,1)S(1)}, u32[]{:S(2)}, u32[]{:S(2)}) collective-permute-start(bf16[512,256]{1,0:T(8,128)(2,1)S(1)} %get-tuple-element.31), channel_id=1, source_target_pairs={{0,1},{3,2},{4,5},{7,6},{8,9},{11,10},{12,13},{15,14},{16,17},{19,... | collective-permute-start | bytes 786440 | tf_op jit(solution)/shard_map/ppermute | solution.py:122
  36.3 0.1 collective-permute-start.1
  36.4 6.6 %collective-permute-done.6 = bf16[512,256]{1,0:T(8,128)(2,1)S(1)} collective-permute-done((bf16[512,256]{1,0:T(8,128)(2,1)S(1)}, bf16[512,256]{1,0:T(8,128)(2,1)S(1)}, u32[]{:S(2)}, u32[]{:S(2)}) %collective-permute-start.6) | collective-permute-done | bytes 262176 | tf_op jit(solution)/shard_map/ppermute | solution.py:122
  43.0 0.8 fusion.21
  43.8 2.4 %select_select_fusion.3 = (bf16[8,256,256]{2,1,0:T(8,128)(2,1)S(1)}, bf16[8,256,256]{2,1,0:T(8,128)(2,1)S(1)}, bf16[8,256,256]{2,1,0:T(8,128)(2,1)S(1)}, bf16[8,256,256]{2,1,0:T(8,128)(2,1)S(1)}) fusion(bf16[8,256,256]{2,1,0:T(8,128)(2,1)} %collective-permute-done.3, bf16[8,256,256]{2,1,0:T(8,128)(2,1)} %collective-permute-done.5, ...), kind=kLoop, calls=%fused_computation.25 | loop fusion | flops 6291456 | bytes 8388620 | tf_op jit(solution)/shard_map/select_n | solution.py:111
  46.2 2.3 %pad_maximum_fusion.cores_ref = bf16[32,256,256]{2,1,0:T(8,128)(2,1)} fusion(bf16[8,256,256]{2,1,0:T(8,128)(2,1)S(1)} %get-tuple-element.50, bf16[8,256,256]{2,1,0:T(8,128)(2,1)S(1)} %get-tuple-element.51, bf16[8,256,256]{2,1,0:T(8,128)(2,1)S(1)} %get-tuple-element.52, bf16[8,256,256]{2,1,0:T(8,128)(2,1)S(1)} %get-tuple-element.49), kind=kLoop, calls=%fused_computation | loop fusion | flops 6291456 | bytes 8388608 | tf_op jit(solution)/shard_map/concatenate | solution.py:113
  48.5 1.5 %collective-permute-start.16 = (bf16[256,1024]{1,0:T(8,128)(2,1)S(1)}, bf16[256,1024]{1,0:T(8,128)(2,1)S(1)}, u32[]{:S(2)}, u32[]{:S(2)}) collective-permute-start(bf16[256,1024]{1,0:T(8,128)(2,1)S(1)} %copy-done.7), channel_id=1, source_target_pairs={{0,16},{16,0},{1,17},{17,1},{2,18},{18,2},{3,19},{19,3},{4,20},{20... | collective-permute-start | bytes 1572872 | tf_op jit(solution)/shard_map/ppermute | solution.py:130
  50.0 0.5 collective-permute-start.12
  50.6 6.5 %fusion.4 = f32[512,1024]{1,0:T(8,128)} fusion(bf16[512,2048]{1,0:T(8,128)(2,1)} %param.6, bf16[8192,1024]{1,0:T(8,128)(2,1)} %param.8, s32[]{:T(128)S(6)} %select_n.191), kind=kOutput, calls=%fused_computation.5 | convolution fusion | flops 2147483648 | bytes 8388612 | tf_op jit(solution)/shard_map/dot_general | solution.py:14
  57.1 7.2 %collective-permute-done.1 = bf16[256,2048]{1,0:T(8,128)(2,1)S(1)} collective-permute-done((bf16[256,2048]{1,0:T(8,128)(2,1)}, bf16[256,2048]{1,0:T(8,128)(2,1)S(1)}, u32[]{:S(2)}, u32[]{:S(2)}) %collective-permute-start.1) | collective-permute-done | bytes 1048608 | tf_op jit(solution)/shard_map/ppermute | solution.py:122
  64.3 0.0 collective-permute-done.2.x_ref
  64.3 2.4 %collective-permute-start.9 = (bf16[256,2048]{1,0:T(8,128)(2,1)}, bf16[256,2048]{1,0:T(8,128)(2,1)}, u32[]{:S(2)}, u32[]{:S(2)}) collective-permute-start(bf16[256,2048]{1,0:T(8,128)(2,1)} %get-tuple-element.37), channel_id=1, source_target_pairs={{0,1},{3,2},{1,0},{2,3},{4,5},{7,6},{5,4},{6,7},{8,9},{11,10},{9,8... | collective-permute-start | bytes 3145736 | tf_op jit(solution)/shard_map/ppermute | solution.py:122
  66.8 1.4 collective-permute-start.7
  68.3 0.6 collective-permute-start.17
  68.9 1.6 %collective-permute-start.13 = (bf16[512,1024]{1,0:T(8,128)(2,1)S(1)}, bf16[512,1024]{1,0:T(8,128)(2,1)S(1)}, u32[]{:S(2)}, u32[]{:S(2)}) collective-permute-start(bf16[512,1024]{1,0:T(8,128)(2,1)S(1)} %constant_dynamic-update-slice_fusion.rest_0_), channel_id=1, source_target_pairs={{0,16},{16,0},{1,17},{17,1},{2,18},{18,2},{3,19},{19,3},{4,20},{20... | collective-permute-start | bytes 3145736 | tf_op jit(solution)/shard_map/ppermute | solution.py:130
  70.5 0.1 copy.7.ids_ref
  70.6 0.7 collective-permute-start.10
  71.4 1.3 add_convert_fusion
  72.7 1.3 collective-permute-start.8
  74.0 0.0 slice-start
  74.0 6.6 %fusion.2 = f32[512,1024]{1,0:T(8,128)} fusion(bf16[512,2048]{1,0:T(8,128)(2,1)} %copy-done.3, bf16[8192,1024]{1,0:T(8,128)(2,1)} %param.8, s32[]{:T(128)S(6)} %select_n.194), kind=kOutput, calls=%fused_computation.3 | convolution fusion | flops 2147483648 | bytes 8388612 | tf_op jit(solution)/shard_map/dot_general | solution.py:14
  80.6 14.1 %collective-permute-done.8 = bf16[512,256]{1,0:T(8,128)(2,1)S(1)} collective-permute-done((bf16[512,256]{1,0:T(8,128)(2,1)S(1)}, bf16[512,256]{1,0:T(8,128)(2,1)S(1)}, u32[]{:S(2)}, u32[]{:S(2)}) %collective-permute-start.8) | collective-permute-done | bytes 262176 | tf_op jit(solution)/shard_map/ppermute | solution.py:122
  94.8 0.5 collective-permute-start.14
  95.3 0.1 collective-permute-start.19
  95.3 0.4 collective-permute-start.15
  95.8 0.0 copy-start.9
  95.8 2.1 %mix.1 = bf16[512,256]{1,0:T(8,128)(2,1)S(1)} custom-call(s32[512,1]{1,0:T(8,128)S(1)} %copy.7.ids_ref, bf16[512,256]{1,0:T(8,128)(2,1)S(1)} %broadcast_select_fusion.coded_ref, bf16[32,256,256]{2,1,0:T(8,128)(2,1)S(1)} %copy-done.2), custom_call_target="tpu_custom_call" | custom-call | flops 402653184 | bytes 4718592 | tf_op jit(solution)/shard_map/mix/pallas_call | solution.py:44
  97.9 0.0 slice-start.2
  97.9 0.4 fusion.42
  98.4 1.5 %fusion.39 = (bf16[128,2048]{1,0:T(8,128)(2,1)S(1)}, bf16[128,2048]{1,0:T(8,128)(2,1)S(1)}) fusion(bf16[256,2048]{1,0:T(8,128)(2,1)} %collective-permute-done.9), kind=kLoop, calls=%fused_computation.51 | loop fusion | bytes 2097152 | tf_op jit(solution)/shard_map/slice | solution.py:187
  99.9 0.8 collective-permute-start.11
  100.7 0.0 slice-start.3
  100.7 3.7 %lend_near.1 = f32[512,1024]{1,0:T(8,128)S(1)} custom-call(s32[1]{0:T(128)} %bitcast.spot_ref, bf16[512,2048]{1,0:T(8,128)(2,1)S(1)} %copy-done.4, bf16[512,1024]{1,0:T(8,128)(2,1)S(1)} %constant_dynamic-update-slice_fusion.2.rest_0_, bf16[512,1024]{1,0:T(8,128)(2,1)} %collective-permute-done.17.rest_1_, ...), custom_call_target="tpu_custom_call" | custom-call | flops 2147483648 | bytes 7340032 | tf_op jit(solution)/shard_map/lend_near/pallas_call | solution.py:85
  104.5 0.1 slice.52.rest_4_
  104.6 0.0 copy-start.12
  104.6 1.3 lend_far.3
  105.9 1.5 %collective-permute-start.20 = (bf16[256,1024]{1,0:T(8,128)(2,1)S(1)}, bf16[256,1024]{1,0:T(8,128)(2,1)S(1)}, u32[]{:S(2)}, u32[]{:S(2)}) collective-permute-start(bf16[256,1024]{1,0:T(8,128)(2,1)S(1)} %lend_far.3), channel_id=1, source_target_pairs={{1,0},{2,3},{5,4},{6,7},{9,8},{10,11},{13,12},{14,15},{17,16},{18,... | collective-permute-start | bytes 1572872 | tf_op jit(solution)/shard_map/ppermute | solution.py:122
  107.5 5.1 %add_add_fusion = f32[512,1024]{1,0:T(8,128)S(1)} fusion(f32[512,1024]{1,0:T(8,128)} %fusion.2, f32[512,1024]{1,0:T(8,128)} %fusion.4, f32[512,1024]{1,0:T(8,128)S(1)} %fusion.42, bf16[8192,1024]{1,0:T(8,128)(2,1)S(1)} %bitcast.11, s32[]{:T(128)S(6)} %select_n.198, bf16[256,2048]{1,0:T(8,128)(2,1)} %collective-permute-done.9, ...), kind=kOutput, calls=%fused_computation.16 | convolution fusion | flops 2153250816 | bytes 14680068 | tf_op jit(solution)/shard_map/dot_general | solution.py:14
  112.5 0.7 collective-permute-start.21
  113.2 0.1 fusion.37
  113.4 8.3 %collective-permute-done.20 = bf16[256,1024]{1,0:T(8,128)(2,1)S(1)} collective-permute-done((bf16[256,1024]{1,0:T(8,128)(2,1)S(1)}, bf16[256,1024]{1,0:T(8,128)(2,1)S(1)}, u32[]{:S(2)}, u32[]{:S(2)}) %collective-permute-start.20) | collective-permute-done | bytes 524320 | tf_op jit(solution)/shard_map/ppermute | solution.py:122
  121.7 0.8 lend_far.4
  122.5 1.3 collective-permute-start.22
  123.8 1.3 fusion.16
  125.1 0.8 fusion.6
  125.9 5.9 %collective-permute-done.22 = bf16[128,1024]{1,0:T(8,128)(2,1)S(1)} collective-permute-done((bf16[128,1024]{1,0:T(8,128)(2,1)S(1)}, bf16[128,1024]{1,0:T(8,128)(2,1)S(1)}, u32[]{:S(2)}, u32[]{:S(2)}) %collective-permute-start.22) | collective-permute-done | bytes 262176 | tf_op jit(solution)/shard_map/ppermute | solution.py:122
  131.7 0.7 lend_far.5
  132.5 1.3 collective-permute-start.23
  133.8 0.0 copy-start.1
  133.8 0.8 fusion.20
  134.5 6.3 %collective-permute-done.23 = bf16[128,1024]{1,0:T(8,128)(2,1)S(1)} collective-permute-done((bf16[128,1024]{1,0:T(8,128)(2,1)S(1)}, bf16[128,1024]{1,0:T(8,128)(2,1)S(1)}, u32[]{:S(2)}, u32[]{:S(2)}) %collective-permute-start.23) | collective-permute-done | bytes 262176 | tf_op jit(solution)/shard_map/ppermute | solution.py:122
  140.8 0.1 fusion.18
  140.9 1.0 pad_maximum_fusion.2
  (51 shorter events, 0.3 us)
Async XLA Ops:
  0.0 26.4 %copy-start = (bf16[2048,256]{1,0:T(8,128)(2,1)S(1)}, bf16[2048,256]{1,0:T(8,128)(2,1)}, u32[]{:S(2)}) copy-start(bf16[2048,256]{1,0:T(8,128)(2,1)} %param.9) | copy-start | bytes 3145732
  0.0 26.4 %collective-permute-start.3 = (bf16[8,256,256]{2,1,0:T(8,128)(2,1)}, bf16[8,256,256]{2,1,0:T(8,128)(2,1)}, u32[]{:S(2)}, u32[]{:S(2)}) collective-permute-start(bf16[8,256,256]{2,1,0:T(8,128)(2,1)} %param.10), channel_id=1, source_target_pairs={{0,8},{4,12},{8,0},{12,4},{1,9},{5,13},{9,1},{13,5},{2,10},{6,14},... | collective-permute-start | bytes 3145736 | tf_op jit(solution)/shard_map/ppermute | solution.py:104
  2.9 23.5 %collective-permute-start.4 = (bf16[8,256,256]{2,1,0:T(8,128)(2,1)}, bf16[8,256,256]{2,1,0:T(8,128)(2,1)}, u32[]{:S(2)}, u32[]{:S(2)}) collective-permute-start(bf16[8,256,256]{2,1,0:T(8,128)(2,1)} %param.10), channel_id=1, source_target_pairs={{0,4},{4,0},{8,12},{12,8},{1,5},{5,1},{9,13},{13,9},{2,6},{6,2},{1... | collective-permute-start | bytes 3145736 | tf_op jit(solution)/shard_map/ppermute | solution.py:103
  4.3 26.6 %collective-permute-start = (bf16[512,1024]{1,0:T(8,128)(2,1)S(1)}, bf16[512,1024]{1,0:T(8,128)(2,1)S(1)}, u32[]{:S(2)}, u32[]{:S(2)}) collective-permute-start(bf16[512,1024]{1,0:T(8,128)(2,1)S(1)} %pad_maximum_fusion.1), channel_id=1, source_target_pairs={{0,1},{3,2},{4,5},{7,6},{8,9},{11,10},{12,13},{15,14},{16,17},{19,... | collective-permute-start | bytes 3145736 | tf_op jit(solution)/shard_map/ppermute | solution.py:122
  7.8 56.5 %collective-permute-start.2 = (bf16[512,2048]{1,0:T(8,128)(2,1)}, bf16[512,2048]{1,0:T(8,128)(2,1)S(1)}, u32[]{:S(2)}, u32[]{:S(2)}) collective-permute-start(bf16[512,2048]{1,0:T(8,128)(2,1)} %param.6), channel_id=1, source_target_pairs={{1,2},{2,1},{5,6},{6,5},{9,10},{10,9},{13,14},{14,13},{17,18},{18,... | collective-permute-start | bytes 6291464 | tf_op jit(solution)/shard_map/ppermute | solution.py:122
  26.4 17.4 %collective-permute-start.5 = (bf16[8,256,256]{2,1,0:T(8,128)(2,1)}, bf16[8,256,256]{2,1,0:T(8,128)(2,1)}, u32[]{:S(2)}, u32[]{:S(2)}) collective-permute-start(bf16[8,256,256]{2,1,0:T(8,128)(2,1)} %collective-permute-done.3), channel_id=1, source_target_pairs={{0,4},{4,0},{8,12},{12,8},{1,5},{5,1},{9,13},{13,9},{2,6},{6,2},{1... | collective-permute-start | bytes 3145736 | tf_op jit(solution)/shard_map/ppermute | solution.py:106
  29.5 13.5 %copy-start.5 = (f32[512,256]{1,0:T(8,128)S(1)}, f32[512,256]{1,0:T(8,128)}, u32[]{:S(2)}) copy-start(f32[512,256]{1,0:T(8,128)} %get-tuple-element.62) | copy-start | bytes 1572868
  31.9 11.1 %collective-permute-start.6 = (bf16[512,256]{1,0:T(8,128)(2,1)S(1)}, bf16[512,256]{1,0:T(8,128)(2,1)S(1)}, u32[]{:S(2)}, u32[]{:S(2)}) collective-permute-start(bf16[512,256]{1,0:T(8,128)(2,1)S(1)} %get-tuple-element.31), channel_id=1, source_target_pairs={{0,1},{3,2},{4,5},{7,6},{8,9},{11,10},{12,13},{15,14},{16,17},{19,... | collective-permute-start | bytes 786440 | tf_op jit(solution)/shard_map/ppermute | solution.py:122
  36.3 28.0 %collective-permute-start.1 = (bf16[256,2048]{1,0:T(8,128)(2,1)}, bf16[256,2048]{1,0:T(8,128)(2,1)S(1)}, u32[]{:S(2)}, u32[]{:S(2)}) collective-permute-start(bf16[256,2048]{1,0:T(8,128)(2,1)} %get-tuple-element.26), channel_id=1, source_target_pairs={{0,1},{3,2},{1,0},{2,3},{4,5},{7,6},{5,4},{6,7},{8,9},{11,10},{9,8... | collective-permute-start | bytes 3145736 | tf_op jit(solution)/shard_map/ppermute | solution.py:122
  43.0 0.8 copy-start.8
  46.2 2.3 %copy-start.7 = (bf16[256,1024]{1,0:T(8,128)(2,1)S(1)}, bf16[256,1024]{1,0:T(8,128)(2,1)}, u32[]{:S(2)}) copy-start(bf16[256,1024]{1,0:T(8,128)(2,1)} %get-tuple-element.41) | copy-start | bytes 1572868
  46.2 3.8 %copy-start.6 = (bf16[256,1024]{1,0:T(8,128)(2,1)S(1)}, bf16[256,1024]{1,0:T(8,128)(2,1)}, u32[]{:S(2)}) copy-start(bf16[256,1024]{1,0:T(8,128)(2,1)} %get-tuple-element.40) | copy-start | bytes 1572868
  48.5 19.7 %collective-permute-start.16 = (bf16[256,1024]{1,0:T(8,128)(2,1)S(1)}, bf16[256,1024]{1,0:T(8,128)(2,1)S(1)}, u32[]{:S(2)}, u32[]{:S(2)}) collective-permute-start(bf16[256,1024]{1,0:T(8,128)(2,1)S(1)} %copy-done.7), channel_id=1, source_target_pairs={{0,16},{16,0},{1,17},{17,1},{2,18},{18,2},{3,19},{19,3},{4,20},{20... | collective-permute-start | bytes 1572872 | tf_op jit(solution)/shard_map/ppermute | solution.py:130
  50.0 18.8 %collective-permute-start.12 = (bf16[256,1024]{1,0:T(8,128)(2,1)S(1)}, bf16[256,1024]{1,0:T(8,128)(2,1)S(1)}, u32[]{:S(2)}, u32[]{:S(2)}) collective-permute-start(bf16[256,1024]{1,0:T(8,128)(2,1)S(1)} %copy-done.6), channel_id=1, source_target_pairs={{0,8},{4,12},{8,0},{12,4},{1,9},{5,13},{9,1},{13,5},{2,10},{6,14},... | collective-permute-start | bytes 1572872 | tf_op jit(solution)/shard_map/ppermute | solution.py:126
  64.3 4.6 %copy-start.11 = (bf16[256,2048]{1,0:T(8,128)(2,1)}, bf16[256,2048]{1,0:T(8,128)(2,1)S(1)}, u32[]{:S(2)}) copy-start(bf16[256,2048]{1,0:T(8,128)(2,1)S(1)} %collective-permute-done.1) | copy-start | bytes 3145732
  64.3 2.5 %copy-start.3 = (bf16[512,2048]{1,0:T(8,128)(2,1)}, bf16[512,2048]{1,0:T(8,128)(2,1)S(1)}, u32[]{:S(2)}) copy-start(bf16[512,2048]{1,0:T(8,128)(2,1)S(1)} %collective-permute-done.2.x_ref) | copy-start | bytes 6291460
  64.3 6.2 %copy-start.10 = (s32[512,1]{0,1:T(1,128)S(1)}, s32[512,1]{0,1:T(1,128)}, u32[]{:S(2)}) copy-start(s32[512,1]{0,1:T(1,128)} %param.7) | copy-start | bytes 6148
  64.3 30.4 %collective-permute-start.9 = (bf16[256,2048]{1,0:T(8,128)(2,1)}, bf16[256,2048]{1,0:T(8,128)(2,1)}, u32[]{:S(2)}, u32[]{:S(2)}) collective-permute-start(bf16[256,2048]{1,0:T(8,128)(2,1)} %get-tuple-element.37), channel_id=1, source_target_pairs={{0,1},{3,2},{1,0},{2,3},{4,5},{7,6},{5,4},{6,7},{8,9},{11,10},{9,8... | collective-permute-start | bytes 3145736 | tf_op jit(solution)/shard_map/ppermute | solution.py:122
  66.8 4.6 %collective-permute-start.7 = (bf16[512,256]{1,0:T(8,128)(2,1)}, bf16[512,256]{1,0:T(8,128)(2,1)}, u32[]{:S(2)}, u32[]{:S(2)}) collective-permute-start(bf16[512,256]{1,0:T(8,128)(2,1)} %fusion.21), channel_id=1, source_target_pairs={{1,2},{2,1},{5,6},{6,5},{9,10},{10,9},{13,14},{14,13},{17,18},{18,... | collective-permute-start | bytes 786440 | tf_op jit(solution)/shard_map/ppermute | solution.py:122
  68.3 27.0 %collective-permute-start.17 = (bf16[512,1024]{1,0:T(8,128)(2,1)S(1)}, bf16[512,1024]{1,0:T(8,128)(2,1)}, u32[]{:S(2)}, u32[]{:S(2)}) collective-permute-start(bf16[512,1024]{1,0:T(8,128)(2,1)S(1)} %constant_dynamic-update-slice_fusion.2.rest_0_), channel_id=1, source_target_pairs={{0,8},{4,12},{8,0},{12,4},{1,9},{5,13},{9,1},{13,5},{2,10},{6,14},... | collective-permute-start | bytes 3145736 | tf_op jit(solution)/shard_map/ppermute | solution.py:126
  68.9 26.4 %collective-permute-start.13 = (bf16[512,1024]{1,0:T(8,128)(2,1)S(1)}, bf16[512,1024]{1,0:T(8,128)(2,1)S(1)}, u32[]{:S(2)}, u32[]{:S(2)}) collective-permute-start(bf16[512,1024]{1,0:T(8,128)(2,1)S(1)} %constant_dynamic-update-slice_fusion.rest_0_), channel_id=1, source_target_pairs={{0,16},{16,0},{1,17},{17,1},{2,18},{18,2},{3,19},{19,3},{4,20},{20... | collective-permute-start | bytes 3145736 | tf_op jit(solution)/shard_map/ppermute | solution.py:130
  70.6 29.2 %collective-permute-start.10 = (bf16[256,2048]{1,0:T(8,128)(2,1)}, bf16[256,2048]{1,0:T(8,128)(2,1)S(1)}, u32[]{:S(2)}, u32[]{:S(2)}) collective-permute-start(bf16[256,2048]{1,0:T(8,128)(2,1)} %copy-done.11), channel_id=1, source_target_pairs={{1,2},{2,1},{5,6},{6,5},{9,10},{10,9},{13,14},{14,13},{17,18},{18,... | collective-permute-start | bytes 3145736 | tf_op jit(solution)/shard_map/ppermute | solution.py:122
  72.7 22.1 %collective-permute-start.8 = (bf16[512,256]{1,0:T(8,128)(2,1)S(1)}, bf16[512,256]{1,0:T(8,128)(2,1)S(1)}, u32[]{:S(2)}, u32[]{:S(2)}) collective-permute-start(bf16[512,256]{1,0:T(8,128)(2,1)S(1)} %add_convert_fusion), channel_id=1, source_target_pairs={{1,0},{2,3},{5,4},{6,7},{9,8},{10,11},{13,12},{14,15},{17,16},{18,... | collective-permute-start | bytes 786440 | tf_op jit(solution)/shard_map/ppermute | solution.py:122
  74.0 21.9 %copy-start.2 = (bf16[32,256,256]{2,1,0:T(8,128)(2,1)S(1)}, bf16[32,256,256]{2,1,0:T(8,128)(2,1)}, u32[]{:S(2)}) copy-start(bf16[32,256,256]{2,1,0:T(8,128)(2,1)} %pad_maximum_fusion.cores_ref) | copy-start | bytes 12582916
  74.0 33.4 %slice-start = ((s8[16777216]{0:T(1024)(128)(4,1)}), s8[4194304]{0:T(1024)(128)(4,1)S(1)}, s32[]{:S(2)}) async-start(s8[16777216]{0:T(1024)(128)(4,1)} %bitcast.10), calls=%async_computation | async-start | bytes 8388608
  74.0 33.4 %slice-start.1 = ((s8[16777216]{0:T(1024)(128)(4,1)}), s8[4194304]{0:T(1024)(128)(4,1)S(1)}, s32[]{:S(2)}) async-start(s8[16777216]{0:T(1024)(128)(4,1)} %bitcast.10), calls=%async_computation.1 | async-start | bytes 8388608
  94.8 6.0 %collective-permute-start.18 = (bf16[512,1024]{1,0:T(8,128)(2,1)S(1)}, bf16[512,1024]{1,0:T(8,128)(2,1)S(1)}, u32[]{:S(2)}, u32[]{:S(2)}) collective-permute-start(bf16[512,1024]{1,0:T(8,128)(2,1)S(1)} %constant_dynamic-update-slice_fusion.2.rest_0_), channel_id=1, source_target_pairs={{0,4},{4,0},{8,12},{12,8},{1,5},{5,1},{9,13},{13,9},{2,6},{6,2},{1... | collective-permute-start | bytes 3145736 | tf_op jit(solution)/shard_map/ppermute | solution.py:126
  94.8 9.9 %collective-permute-start.14 = (bf16[512,1024]{1,0:T(8,128)(2,1)S(1)}, bf16[512,1024]{1,0:T(8,128)(2,1)S(1)}, u32[]{:S(2)}, u32[]{:S(2)}) collective-permute-start(bf16[512,1024]{1,0:T(8,128)(2,1)S(1)} %constant_dynamic-update-slice_fusion.rest_0_), channel_id=1, source_target_pairs={{0,4},{4,0},{8,12},{12,8},{1,5},{5,1},{9,13},{13,9},{2,6},{6,2},{1... | collective-permute-start | bytes 3145736 | tf_op jit(solution)/shard_map/ppermute | solution.py:126
  95.3 5.5 %collective-permute-start.19 = (bf16[512,1024]{1,0:T(8,128)(2,1)}, bf16[512,1024]{1,0:T(8,128)(2,1)S(1)}, u32[]{:S(2)}, u32[]{:S(2)}) collective-permute-start(bf16[512,1024]{1,0:T(8,128)(2,1)} %collective-permute-done.17.rest_1_), channel_id=1, source_target_pairs={{0,4},{4,0},{8,12},{12,8},{1,5},{5,1},{9,13},{13,9},{2,6},{6,2},{1... | collective-permute-start | bytes 3145736 | tf_op jit(solution)/shard_map/ppermute | solution.py:126
  95.3 9.3 %collective-permute-start.15 = (bf16[512,1024]{1,0:T(8,128)(2,1)S(1)}, bf16[512,1024]{1,0:T(8,128)(2,1)S(1)}, u32[]{:S(2)}, u32[]{:S(2)}) collective-permute-start(bf16[512,1024]{1,0:T(8,128)(2,1)S(1)} %collective-permute-done.13.rest_1_), channel_id=1, source_target_pairs={{0,4},{4,0},{8,12},{12,8},{1,5},{5,1},{9,13},{13,9},{2,6},{6,2},{1... | collective-permute-start | bytes 3145736 | tf_op jit(solution)/shard_map/ppermute | solution.py:126
  95.8 2.1 %copy-start.9 = (bf16[256,1024]{1,0:T(8,128)(2,1)S(1)}, bf16[256,1024]{1,0:T(8,128)(2,1)}, u32[]{:S(2)}) copy-start(bf16[256,1024]{1,0:T(8,128)(2,1)} %param.11) | copy-start | bytes 1572868
  97.9 2.8 %copy-start.4 = (bf16[512,2048]{1,0:T(8,128)(2,1)S(1)}, bf16[512,2048]{1,0:T(8,128)(2,1)}, u32[]{:S(2)}) copy-start(bf16[512,2048]{1,0:T(8,128)(2,1)} %copy-done.3) | copy-start | bytes 6291460
  97.9 9.5 %slice-start.2 = ((s8[16777216]{0:T(1024)(128)(4,1)}), s8[4194304]{0:T(1024)(128)(4,1)S(1)}, s32[]{:S(2)}) async-start(s8[16777216]{0:T(1024)(128)(4,1)} %bitcast.10), calls=%async_computation.2 | async-start | bytes 8388608
  99.9 13.5 %collective-permute-start.11 = (bf16[128,2048]{1,0:T(8,128)(2,1)S(1)}, bf16[128,2048]{1,0:T(8,128)(2,1)S(1)}, u32[]{:S(2)}, u32[]{:S(2)}) collective-permute-start(bf16[128,2048]{1,0:T(8,128)(2,1)S(1)} %get-tuple-element.39), channel_id=1, source_target_pairs={{1,2},{2,1},{5,6},{6,5},{9,10},{10,9},{13,14},{14,13},{17,18},{18,... | collective-permute-start | bytes 1572872 | tf_op jit(solution)/shard_map/ppermute | solution.py:122
  100.7 6.7 %slice-start.3 = ((s8[16777216]{0:T(1024)(128)(4,1)}), s8[4194304]{0:T(1024)(128)(4,1)S(1)}, s32[]{:S(2)}) async-start(s8[16777216]{0:T(1024)(128)(4,1)} %bitcast.10), calls=%async_computation.3 | async-start | bytes 8388608
  104.6 2.8 %copy-start.12 = (bf16[256,2048]{1,0:T(8,128)(2,1)S(1)}, bf16[256,2048]{1,0:T(8,128)(2,1)}, u32[]{:S(2)}) copy-start(bf16[256,2048]{1,0:T(8,128)(2,1)} %copy-done.11) | copy-start | bytes 3145732
  105.9 15.8 %collective-permute-start.20 = (bf16[256,1024]{1,0:T(8,128)(2,1)S(1)}, bf16[256,1024]{1,0:T(8,128)(2,1)S(1)}, u32[]{:S(2)}, u32[]{:S(2)}) collective-permute-start(bf16[256,1024]{1,0:T(8,128)(2,1)S(1)} %lend_far.3), channel_id=1, source_target_pairs={{1,0},{2,3},{5,4},{6,7},{9,8},{10,11},{13,12},{14,15},{17,16},{18,... | collective-permute-start | bytes 1572872 | tf_op jit(solution)/shard_map/ppermute | solution.py:122
  112.5 12.5 %collective-permute-start.21 = (bf16[128,2048]{1,0:T(8,128)(2,1)S(1)}, bf16[128,2048]{1,0:T(8,128)(2,1)S(1)}, u32[]{:S(2)}, u32[]{:S(2)}) collective-permute-start(bf16[128,2048]{1,0:T(8,128)(2,1)S(1)} %get-tuple-element.43), channel_id=1, source_target_pairs={{1,2},{2,1},{5,6},{6,5},{9,10},{10,9},{13,14},{14,13},{17,18},{18,... | collective-permute-start | bytes 1572872 | tf_op jit(solution)/shard_map/ppermute | solution.py:122
  122.5 9.3 %collective-permute-start.22 = (bf16[128,1024]{1,0:T(8,128)(2,1)S(1)}, bf16[128,1024]{1,0:T(8,128)(2,1)S(1)}, u32[]{:S(2)}, u32[]{:S(2)}) collective-permute-start(bf16[128,1024]{1,0:T(8,128)(2,1)S(1)} %lend_far.4), channel_id=1, source_target_pairs={{1,0},{2,3},{5,4},{6,7},{9,8},{10,11},{13,12},{14,15},{17,16},{18,... | collective-permute-start | bytes 786440 | tf_op jit(solution)/shard_map/ppermute | solution.py:122
  132.5 8.4 %collective-permute-start.23 = (bf16[128,1024]{1,0:T(8,128)(2,1)S(1)}, bf16[128,1024]{1,0:T(8,128)(2,1)S(1)}, u32[]{:S(2)}, u32[]{:S(2)}) collective-permute-start(bf16[128,1024]{1,0:T(8,128)(2,1)S(1)} %lend_far.5), channel_id=1, source_target_pairs={{1,0},{2,3},{5,4},{6,7},{9,8},{10,11},{13,12},{14,15},{17,16},{18,... | collective-permute-start | bytes 786440 | tf_op jit(solution)/shard_map/ppermute | solution.py:122
  133.8 8.2 %copy-start.1 = (bf16[2048,256]{1,0:T(8,128)(2,1)S(1)}, bf16[2048,256]{1,0:T(8,128)(2,1)}, u32[]{:S(2)}) copy-start(bf16[2048,256]{1,0:T(8,128)(2,1)} %param.9) | copy-start | bytes 3145732

commit v5 on v4

v5 whole, which is shorter than its diff:
```python
import functools

import jax
import jax.numpy as jnp
from jax import lax
from jax.experimental import pallas as pl
from jax.experimental.pallas import tpu as pltpu
from jax.sharding import PartitionSpec as P

BLK = 16


def dot(a, b):
    return jnp.dot(a, b, preferred_element_type=jnp.float32)


def mix_kernel(ids_ref, coded_ref, *rest):
    cores, (mixed_ref, slots_ref) = rest[:-2], rest[-2:]
    rows = coded_ref.shape[0]
    each = cores[0].shape[0]
    adapters = each * len(cores)
    ids = ids_ref[...]
    named = ids == lax.broadcasted_iota(jnp.int32, (rows, adapters), 1)
    below = lax.broadcasted_iota(jnp.int32, (rows, rows), 0) > lax.broadcasted_iota(
        jnp.int32, (rows, rows), 1
    )
    earlier = dot(below.astype(jnp.bfloat16), named.astype(jnp.bfloat16))
    within = jnp.sum(jnp.where(named, earlier, 0.0), axis=1, keepdims=True).astype(jnp.int32)
    slot = ids * BLK + within
    place = (slot == lax.broadcasted_iota(jnp.int32, (rows, adapters * BLK), 1)).astype(
        jnp.bfloat16
    )
    packed = lax.dot_general(
        place, coded_ref[...], (((0,), (0,)), ((), ())), preferred_element_type=jnp.float32
    ).astype(jnp.bfloat16)
    for a in range(adapters):
        slots_ref[a * BLK : (a + 1) * BLK, :] = dot(
            packed[a * BLK : (a + 1) * BLK, :], cores[a // each][a % each]
        ).astype(jnp.bfloat16)
    mixed_ref[...] = dot(place, slots_ref[...]).astype(jnp.bfloat16)


def mix(ids, coded, cores):
    rows, width = coded.shape
    adapters = sum(c.shape[0] for c in cores)
    return pl.pallas_call(
        mix_kernel,
        out_shape=jax.ShapeDtypeStruct((rows, width), jnp.bfloat16),
        scratch_shapes=[pltpu.VMEM((adapters * BLK, width), jnp.bfloat16)],
        compiler_params=pltpu.CompilerParams(vmem_limit_bytes=32 * 2**20),
        cost_estimate=pl.CostEstimate(
            flops=2 * rows * width * (3 * adapters * BLK),
            bytes_accessed=adapters * width * width * 2 + rows * width * 4,
            transcendentals=0,
        ),
        name="mix",
    )(ids, coded, *cores)


def put_beside(out_ref, column, value):
    rows, width = out_ref.shape[0], value.shape[1]
    for b in range(value.shape[0] // rows):
        out_ref[:, column + b * width : column + (b + 1) * width] = value[
            b * rows : (b + 1) * rows
        ]


def pack_kernel(x_ref, value_ref, more_ref, out_ref):
    out_ref[:, : x_ref.shape[1]] = x_ref[...]
    total = value_ref[...] + more_ref[...].astype(jnp.float32)
    put_beside(out_ref, x_ref.shape[1], total.astype(out_ref.dtype))


def pack(x, value, more):
    rows, columns = x.shape
    extra = value.size // rows
    return pl.pallas_call(
        pack_kernel,
        out_shape=jax.ShapeDtypeStruct((rows, columns + extra), x.dtype),
        compiler_params=pltpu.CompilerParams(vmem_limit_bytes=16 * 2**20),
        cost_estimate=pl.CostEstimate(
            flops=value.size, bytes_accessed=4 * rows * (columns + extra), transcendentals=0
        ),
        name="pack",
    )(x, value, more)


def lend_kernel(spot_ref, x_ref, *rest, blocks, width, columns):
    count = 1 + max(b[0] for b in blocks)
    weights, out_ref = rest[:count], rest[-1]
    add_ref = rest[count] if len(rest) > count + 1 else None
    if len(rest) > count + 2:
        put_beside(out_ref, columns, rest[count + 1][...])
    spot = spot_ref[0]
    pieces = sum(len(b[2]) for b in blocks)
    piece = x_ref.shape[1] // pieces
    xs = [
        jnp.concatenate(
            [x_ref[:, pl.ds(pl.multiple_of((spot ^ m) * piece, piece), piece)] for m in masks],
            axis=1,
        )
        for _, _, masks in blocks
    ]
    for n in range(0, columns, width):
        part = slice(n, n + width)
        value = 0.0 if add_ref is None else add_ref[:, part]
        for x, (operand, row, masks) in zip(xs, blocks):
            value = value + dot(x, weights[operand][row : row + piece * len(masks), part])
        out_ref[:, part] = value.astype(out_ref.dtype)


def lend(spot, x, weights, blocks, name, add=None, beside=None, dtype=jnp.bfloat16):
    rows, depth = x.shape
    columns = weights[0].shape[1]
    extra = 0 if beside is None else beside.size // rows
    whole = pl.BlockSpec(memory_space=pltpu.VMEM)
    operands = (spot.reshape(1), x, *weights) + tuple(v for v in (add, beside) if v is not None)
    return pl.pallas_call(
        functools.partial(lend_kernel, blocks=blocks, width=256, columns=columns),
        out_shape=jax.ShapeDtypeStruct((rows, columns + extra), dtype),
        in_specs=[pl.BlockSpec(memory_space=pltpu.SMEM)] + [whole] * (len(operands) - 1),
        out_specs=whole,
        compiler_params=pltpu.CompilerParams(vmem_limit_bytes=24 * 2**20),
        cost_estimate=pl.CostEstimate(
            flops=2 * rows * depth * columns,
            bytes_accessed=depth * columns * 2 + rows * (depth + columns) * 2,
            transcendentals=0,
        ),
        name=name,
    )(*operands)


IN = [(0, 1), (3, 2)]
OUT = [(1, 0), (2, 3)]
SWAP = [(1, 2), (2, 1)]

TURNS = [4, 4]
CROSSINGS = [4, 3, 1]
AFTER = {
    "corner": ("mate", "across"),
    "turn1": ("pieces",),
    "near1": ("across",),
    "far1": ("mate",),
    "own": ("pieces",),
    "near2": ("own",),
    "far2": ("corner",),
    "near4": ("near3",),
    "cross0": ("swap",),
    "cross1": ("own",),
    "cross2": ("lend0",),
    "lend2": ("back0",),
}


def send(x, pairs):
    return lax.ppermute(x, "tp", pairs)


def swap_rep(x, bit):
    return lax.ppermute(x, "rep", [(i, i ^ bit) for i in range(4)])


def swap_groups(x):
    return lax.ppermute(x, "groups", [(0, 1), (1, 0)])


def row_cuts(rows, eighths):
    ends = [0]
    for e in eighths:
        ends.append(ends[-1] + e * rows // 8)
    return list(zip(ends, ends[1:]))


def on_line(activations, row_adapter, base_weight, basis_down, adapter_cores, basis_up):
    me, rep = lax.axis_index("tp"), lax.axis_index("rep")
    inner = (me == 1) | (me == 2)
    left = me < 2
    near_in, far_in = jnp.where(left, 1, 2), jnp.where(left, 2, 1)
    near_out, far_out = jnp.where(left, 0, 3), jnp.where(left, 3, 0)
    spot = lax.axis_index("groups") * 4 + rep
    rows, depth = activations.shape
    width, columns = basis_up.shape
    piece = depth // 8
    turns, crossings = row_cuts(rows, TURNS), row_cuts(rows, CROSSINGS)
    done = {}

    def after(name, value):
        waits = AFTER.get(name, ())
        if not waits:
            return value
        value, held = lax.optimization_barrier((value, [done[w] for w in waits]))
        done.update(zip(waits, held))
        return value

    def move(name, value, how, *args):
        done[name] = how(after(name, value), *args)
        return done[name]

    def weight_of(owner):
        return lax.dynamic_slice_in_dim(base_weight, owner * depth, depth, 0)

    def piece_of(owner):
        return lax.dynamic_slice_in_dim(base_weight, owner * depth + spot * piece, piece, 0)

    def apart(x, start):
        blocks = jnp.split(x[:, start:], (x.shape[1] - start) // width, axis=1)
        return x[:, :start], jnp.concatenate(blocks, axis=0)

    move("swap", activations, send, SWAP)
    partial_value = dot(activations, basis_down)
    pieces = jnp.concatenate([piece_of(far_in), piece_of(far_out)], axis=0)
    pieces = jnp.concatenate([pieces, partial_value.astype(jnp.bfloat16)], axis=1)
    move("pieces", pieces, send, IN)

    move("across", adapter_cores, swap_rep, 2)
    move("mate", adapter_cores, swap_rep, 1)
    move("corner", done["across"], swap_rep, 1)
    each = adapter_cores.shape[0]
    ids = (row_adapter // each ^ rep) * each + row_adapter % each

    def turn(i):
        move(f"turn{i}", activations[slice(*turns[i])], send, IN + OUT)

    def own_dot():
        done["own"] = dot(after("own", activations), weight_of(me))

    turn(0)
    move("near1", done["pieces"][:piece, :columns], swap_groups)
    move("far1", done["pieces"][piece:, :columns], swap_rep, 2)
    turn(1)
    own_dot()
    near = jnp.concatenate([done["pieces"][:piece, :columns], done["near1"]], axis=0)
    far = jnp.concatenate([done["pieces"][piece:, :columns], done["far1"]], axis=0)
    move("near2", near, swap_rep, 2)
    move("far2", far, swap_groups)
    move("near3", near, swap_rep, 1)
    move("far3", far, swap_rep, 1)
    for i in range(2, len(turns)):
        turn(i)
    move("near4", done["near2"], swap_rep, 1)
    move("far4", done["far2"], swap_rep, 1)
    near_blocks = ((0, 0, (0, 4)), (1, 0, (2, 6)), (2, 0, (1, 5)), (3, 0, (3, 7)))
    far_blocks = ((0, 0, (0, 2)), (1, 0, (4, 6)), (2, 0, (1, 3)), (3, 0, (5, 7)))

    def cross(i):
        a, b = crossings[i]
        j = [a >= start and b <= stop for start, stop in turns].index(True)
        x = done[f"turn{j}"][a - turns[j][0] : b - turns[j][0]]
        if i == 0:
            x = pack(x, partial_value, done["pieces"][:, columns:])
        move(f"cross{i}", x, send, SWAP)
        if i == 0:
            done["cross0"], done["side"] = apart(done["cross0"], depth)

    cross(0)
    side = done["pieces"][:, columns:].astype(jnp.float32) + partial_value
    coded = (side + done["side"].astype(jnp.float32)).astype(jnp.bfloat16)
    cross(1)

    done["swap dot"] = dot(after("swap dot", done["swap"]), weight_of(far_in))
    last_weight = weight_of(far_out)
    for i, (a, b) in enumerate(crossings):
        if i == 0:
            weights = (near, done["near2"], done["near3"], done["near4"])
            lent = lend(spot, done["swap"], weights, near_blocks, "lend_near", dtype=jnp.float32)
        x = after(f"lend{i}", done[f"cross{i}"])
        weights = (far, done["far2"], done["far3"], done["far4"])
        done[f"lend{i}"] = lend(
            spot, x, weights, far_blocks, "lend_far", lent[a:b], coded if i == 0 else None
        )
        move(f"back{i}", done[f"lend{i}"], send, OUT)
        if i == 0:
            done["back0"], done["coded"] = apart(done["back0"], columns)
        if i + 2 < len(crossings):
            cross(i + 2)
        if i == 0:
            turned = jnp.concatenate([done[f"turn{j}"] for j in range(len(turns))], 0)
            turned = dot(turned, weight_of(jnp.where(inner, near_out, near_in)))
            base = done["own"] + done["swap dot"] + turned

    cores = (adapter_cores, done["mate"], done["across"], done["corner"])
    mixed = mix(ids, jnp.where(inner, coded, done["coded"]), cores)
    base = base + dot(mixed, basis_up)
    out = []
    for i, (a, b) in enumerate(crossings):
        value = base[a:b] + dot(done[f"cross{i}"], last_weight)
        out.append((value + done[f"back{i}"].astype(jnp.float32)).astype(jnp.bfloat16))
    return jnp.concatenate(out, axis=0)


def on_any(activations, row_adapter, base_weight, basis_down, adapter_cores, basis_up):
    width = basis_down.shape[1]
    local_count = adapter_cores.shape[0]
    owners = lax.axis_size("rep")
    all_adapters = local_count * owners
    slot_count = all_adapters * BLK
    base = dot(lax.all_gather(activations, "tp", axis=1, tiled=True), base_weight)
    partial_value = dot(activations, basis_down)
    adapter_ids = row_adapter[:, 0]
    onehot = (adapter_ids[:, None] == jnp.arange(all_adapters, dtype=jnp.int32)[None, :]).astype(
        jnp.int32
    )
    earlier = jnp.cumsum(onehot, axis=0) - onehot
    within = jnp.sum(earlier * onehot, axis=1)
    slot_index = adapter_ids * BLK + within
    coded = lax.psum(partial_value, "tp").astype(jnp.bfloat16)
    packed = jnp.zeros((slot_count, width), jnp.bfloat16).at[slot_index].set(coded)
    packed = packed.reshape(owners, local_count, BLK, width)
    mixed_slots = jnp.einsum(
        "nasr,arq->nasq",
        lax.all_to_all(packed, "rep", split_axis=0, concat_axis=0, tiled=True),
        adapter_cores,
        preferred_element_type=jnp.float32,
    ).astype(jnp.bfloat16)
    returned = lax.all_to_all(mixed_slots, "rep", split_axis=0, concat_axis=0, tiled=True).reshape(
        slot_count, width
    )
    mixed = returned[slot_index]
    return (base + dot(mixed, basis_up)).astype(jnp.bfloat16)


def solution(mesh):
    placed = (
        P(("groups", "rep"), "tp"),
        P(("groups", "rep"), None),
        P(None, "tp"),
        P("tp", None),
        P("rep", None, None),
        P(None, "tp"),
    )
    short = (mesh.shape["groups"], mesh.shape["rep"], mesh.shape["tp"]) == (2, 4, 4)
    return jax.shard_map(
        on_line if short else on_any,
        mesh=mesh,
        in_specs=placed,
        out_specs=P(("groups", "rep"), "tp"),
        check_vma=False,
    )
```

time: 142 us -> 142 us (level)
  waiting for transfers between devices: 64.4 us -> 52.7 us
  Pallas kernels: 8.59 us -> 17.9 us
  local copies, waits for them, and re-layouts: 7.45 us -> 16 us
  other arithmetic: 7.96 us -> 3.76 us
  matrix products: 24.6 us -> 22.6 us
    ppermute x6 -> x9, waiting for transfers between devices: 0.02 us -> 28.1 us  [swap_rep(): return lax.ppermute(x, 'rep', [(i, i ^ bit) for i in range(4)])]
    ppermute x13 -> x10, waiting for transfers between devices: 49.8 us -> 23.8 us  [send(): return lax.ppermute(x, 'tp', pairs)]
    ppermute x3 -> x0, waiting for transfers between devices: 14.7 us -> none  [the longest x1 14.7 us: all_cores(): across = lax.ppermute(cores, 'rep', [(i, i ^ 2) for i in range(4)])]
    pallas_call x4 -> x5, Pallas kernels: 6.52 us -> 14.5 us  [the longest x4 12 us: lend(): pl.pallas_call(functools.partial(lend_kernel, blocks=blocks, width=256, c...]
    slice x5 -> x12, local copies, waits for them, and re-layouts: 5.81 us -> 10.9 us  [the longest x1 3.09 us: turn(): move(f'turn{i}', activations[slice(*turns[i])], send, IN + OUT)]
    ppermute x6 -> x9, starting transfers between devices: 2.16 us -> 5.21 us  [swap_rep(): return lax.ppermute(x, 'rep', [(i, i ^ bit) for i in range(4)])]
    ppermute x3 -> x0, starting transfers between devices: 2.94 us -> none  [the longest x1 2.94 us: all_cores(): across = lax.ppermute(cores, 'rep', [(i, i ^ 2) for i in range(4)])]
    select_n x2 -> x1, other arithmetic: 2.42 us -> 0.07 us  [on_line(): mixed = mix(ids, jnp.where(inner, coded, done['coded']), cores)]
  transfers between devices with their start and end apart: 24 -> 21, of which waited for: 8 -> 8; matrix products, arithmetic and copies ran while one was open for 27% -> 23% of each run, Pallas kernels for 6% -> 13%
where the time goes in v5:
time: 142 us; the launch traced here: 141 us
  waiting for transfers between devices  52.7 us (37%)
  starting transfers between devices  27.3 us (19%)
  matrix products  22.6 us (16%)
  Pallas kernels  17.9 us (13%)
  local copies, waits for them, and re-layouts  16 us (11%)
  other arithmetic  3.76 us (3%)
    ppermute x9, waiting for transfers between devices, swap_rep(): return lax.ppermute(x, 'rep', [(i, i ^ bit) for i in range(4)])  28.1 us
    ppermute x10, waiting for transfers between devices, send(): return lax.ppermute(x, 'tp', pairs)  23.8 us
    dot_general x8, matrix products, dot(): return jnp.dot(a, b, preferred_element_type=jnp.float32)  22.6 us
    ppermute x10, starting transfers between devices, send(): return lax.ppermute(x, 'tp', pairs)  19.9 us
    pallas_call x4, Pallas kernels, lend(): pl.pallas_call(functools.partial(lend_kernel, blocks=blocks, width=256, c...  12 us
    ppermute x9, starting transfers between devices, swap_rep(): return lax.ppermute(x, 'rep', [(i, i ^ bit) for i in range(4)])  5.21 us
    pallas_call x1, Pallas kernels, mix(): pl.pallas_call(mix_kernel, out_shape=jax.ShapeDtypeStruct((rows, width),...  3.45 us
    slice x1, local copies, waits for them, and re-layouts, turn(): move(f'turn{i}', activations[slice(*turns[i])], send, IN + OUT)  3.09 us
  transfers between devices with their start and end apart: 21, of which 8 were waited for; matrix products, arithmetic and copies ran while one was open for 23% of the time, Pallas kernels for 13%

profile of v5, /device:TPU:0, one launch (start us, length us, event | category | flops | bytes accessed | tf_op | source)
XLA Modules:
  0.0 140.8 jit_solution(10461928166478996087)
XLA Ops:
  0.0 1.2 copy-done
  1.2 2.3 %fusion.62 = (bf16[512,256]{1,0:T(8,128)(2,1)S(1)}, f32[512,256]{1,0:T(8,128)S(1)}) fusion(bf16[512,2048]{1,0:T(8,128)(2,1)} %param.6, bf16[2048,256]{1,0:T(8,128)(2,1)S(1)} %copy-done), kind=kOutput, calls=%fused_computation.60 | convolution fusion | flops 537001984 | bytes 3932160 | tf_op jit(solution)/shard_map/dot_general | solution.py:14
  3.6 1.5 %constant_dynamic-slice_fusion.1 = (bf16[256,1024]{1,0:T(8,128)(2,1)S(1)}, bf16[256,1024]{1,0:T(8,128)(2,1)S(1)}) fusion(bf16[8192,1024]{1,0:T(8,128)(2,1)} %param.8, s32[]{:T(128)S(6)} %select_n.56, s32[]{:T(128)S(6)} %select_n.58), kind=kLoop, calls=%fused_computation.51 | loop fusion | bytes 2097160 | tf_op jit(solution)/shard_map/dynamic_slice | solution.py:203
  5.0 1.2 pad_maximum_fusion
  6.2 6.0 %collective-permute-start = (bf16[512,1280]{1,0:T(8,128)(2,1)}, bf16[512,1280]{1,0:T(8,128)(2,1)}, u32[]{:S(2)}, u32[]{:S(2)}) collective-permute-start(bf16[512,1280]{1,0:T(8,128)(2,1)} %pad_maximum_fusion), channel_id=1, source_target_pairs={{0,1},{3,2},{4,5},{7,6},{8,9},{11,10},{12,13},{15,14},{16,17},{19,... | collective-permute-start | bytes 3932168 | tf_op jit(solution)/shard_map/ppermute | solution.py:156
  12.2 1.5 %collective-permute-start.2 = (bf16[8,256,256]{2,1,0:T(8,128)(2,1)S(1)}, bf16[8,256,256]{2,1,0:T(8,128)(2,1)S(1)}, u32[]{:S(2)}, u32[]{:S(2)}) collective-permute-start(bf16[8,256,256]{2,1,0:T(8,128)(2,1)S(1)} %copy-done.6), channel_id=1, source_target_pairs={{0,8},{4,12},{8,0},{12,4},{1,9},{5,13},{9,1},{13,5},{2,10},{6,14},... | collective-permute-start | bytes 3145736 | tf_op jit(solution)/shard_map/ppermute | solution.py:160
  13.7 2.0 %collective-permute-start.6 = (bf16[512,2048]{1,0:T(8,128)(2,1)}, bf16[512,2048]{1,0:T(8,128)(2,1)}, u32[]{:S(2)}, u32[]{:S(2)}) collective-permute-start(bf16[512,2048]{1,0:T(8,128)(2,1)} %param.6), channel_id=1, source_target_pairs={{1,2},{2,1},{5,6},{6,5},{9,10},{10,9},{13,14},{14,13},{17,18},{18,... | collective-permute-start | bytes 6291464 | tf_op jit(solution)/shard_map/ppermute | solution.py:156
  15.7 3.1 %fusion.57 = (bf16[256,2048]{1,0:T(8,128)(2,1)}, bf16[256,2048]{1,0:T(8,128)(2,1)}) fusion(bf16[512,2048]{1,0:T(8,128)(2,1)} %param.6), kind=kLoop, calls=%fused_computation.55 | loop fusion | bytes 4194304 | tf_op jit(solution)/shard_map/slice | solution.py:222
  18.8 18.0 %collective-permute-done.2.rest_2_ = bf16[8,256,256]{2,1,0:T(8,128)(2,1)S(1)} collective-permute-done((bf16[8,256,256]{2,1,0:T(8,128)(2,1)S(1)}, bf16[8,256,256]{2,1,0:T(8,128)(2,1)S(1)}, u32[]{:S(2)}, u32[]{:S(2)}) %collective-permute-start.2) | collective-permute-done | bytes 1048608 | tf_op jit(solution)/shard_map/ppermute | solution.py:160
  36.8 3.8 %collective-permute-done = bf16[512,1280]{1,0:T(8,128)(2,1)} collective-permute-done((bf16[512,1280]{1,0:T(8,128)(2,1)}, bf16[512,1280]{1,0:T(8,128)(2,1)}, u32[]{:S(2)}, u32[]{:S(2)}) %collective-permute-start) | collective-permute-done | bytes 1310752 | tf_op jit(solution)/shard_map/ppermute | solution.py:156
  40.6 1.3 fusion.60
  41.9 1.6 %collective-permute-start.4 = (bf16[256,1024]{1,0:T(8,128)(2,1)S(1)}, bf16[256,1024]{1,0:T(8,128)(2,1)S(1)}, u32[]{:S(2)}, u32[]{:S(2)}) collective-permute-start(bf16[256,1024]{1,0:T(8,128)(2,1)S(1)} %get-tuple-element.33), channel_id=1, source_target_pairs={{0,16},{16,0},{1,17},{17,1},{2,18},{18,2},{3,19},{19,3},{4,20},{20... | collective-permute-start | bytes 1572872 | tf_op jit(solution)/shard_map/ppermute | solution.py:164
  43.5 1.5 %collective-permute-start.8 = (bf16[256,1024]{1,0:T(8,128)(2,1)S(1)}, bf16[256,1024]{1,0:T(8,128)(2,1)S(1)}, u32[]{:S(2)}, u32[]{:S(2)}) collective-permute-start(bf16[256,1024]{1,0:T(8,128)(2,1)S(1)} %get-tuple-element.40), channel_id=1, source_target_pairs={{0,8},{4,12},{8,0},{12,4},{1,9},{5,13},{9,1},{13,5},{2,10},{6,14},... | collective-permute-start | bytes 1572872 | tf_op jit(solution)/shard_map/ppermute | solution.py:160
  45.0 6.5 %fusion.4 = f32[512,1024]{1,0:T(8,128)} fusion(bf16[512,2048]{1,0:T(8,128)(2,1)} %param.6, bf16[8192,1024]{1,0:T(8,128)(2,1)} %param.8, s32[]{:T(128)S(6)} %select_n.59), kind=kOutput, calls=%fused_computation.4 | convolution fusion | flops 2147483648 | bytes 8388612 | tf_op jit(solution)/shard_map/dot_general | solution.py:14
  51.5 1.3 fusion.59
  52.7 0.9 collective-permute-done.4
  53.6 0.1 pad_maximum_fusion.1.rest_0_
  53.7 0.1 collective-permute-start.14
  53.8 1.1 collective-permute-done.8
  54.8 1.5 %collective-permute-start.13 = (bf16[512,1024]{1,0:T(8,128)(2,1)S(1)}, bf16[512,1024]{1,0:T(8,128)(2,1)}, u32[]{:S(2)}, u32[]{:S(2)}) collective-permute-start(bf16[512,1024]{1,0:T(8,128)(2,1)S(1)} %pad_maximum_fusion.1.rest_0_), channel_id=1, source_target_pairs={{0,8},{4,12},{8,0},{12,4},{1,9},{5,13},{9,1},{13,5},{2,10},{6,14},... | collective-permute-start | bytes 3145736 | tf_op jit(solution)/shard_map/ppermute | solution.py:160
  56.3 0.1 pad_maximum_fusion.2.rest_0_
  56.4 0.6 collective-permute-start.10
  57.0 1.0 slice.63.more_ref
  58.0 4.0 %collective-permute-done.5.x_ref = bf16[256,2048]{1,0:T(8,128)(2,1)} collective-permute-done((bf16[256,2048]{1,0:T(8,128)(2,1)}, bf16[256,2048]{1,0:T(8,128)(2,1)}, u32[]{:S(2)}, u32[]{:S(2)}) %collective-permute-start.5) | collective-permute-done | bytes 1048608 | tf_op jit(solution)/shard_map/ppermute | solution.py:156
  62.0 2.5 %pack.1 = bf16[256,2560]{1,0:T(8,128)(2,1)} custom-call(bf16[256,2048]{1,0:T(8,128)(2,1)} %collective-permute-done.5.x_ref, f32[512,256]{1,0:T(8,128)S(1)} %get-tuple-element.66.value_ref, bf16[512,256]{1,0:T(8,128)(2,1)S(1)} %slice.63.more_ref), custom_call_target="tpu_custom_call" | custom-call | flops 131072 | bytes 2621440 | tf_op jit(solution)/shard_map/pack/pallas_call | solution.py:77
  64.5 1.8 %collective-permute-start.7 = (bf16[256,2560]{1,0:T(8,128)(2,1)}, bf16[256,2560]{1,0:T(8,128)(2,1)}, u32[]{:S(2)}, u32[]{:S(2)}) collective-permute-start(bf16[256,2560]{1,0:T(8,128)(2,1)} %pack.1), channel_id=1, source_target_pairs={{1,2},{2,1},{5,6},{6,5},{9,10},{10,9},{13,14},{14,13},{17,18},{18,... | collective-permute-start | bytes 3932168 | tf_op jit(solution)/shard_map/ppermute | solution.py:156
  66.2 4.3 %collective-permute-start.1 = (bf16[256,2048]{1,0:T(8,128)(2,1)}, bf16[256,2048]{1,0:T(8,128)(2,1)}, u32[]{:S(2)}, u32[]{:S(2)}) collective-permute-start(bf16[256,2048]{1,0:T(8,128)(2,1)} %get-tuple-element.29), channel_id=1, source_target_pairs={{0,1},{3,2},{1,0},{2,3},{4,5},{7,6},{5,4},{6,7},{8,9},{11,10},{9,8... | collective-permute-start | bytes 3145736 | tf_op jit(solution)/shard_map/ppermute | solution.py:156
  70.5 8.9 %collective-permute-done.13.rest_1_ = bf16[512,1024]{1,0:T(8,128)(2,1)} collective-permute-done((bf16[512,1024]{1,0:T(8,128)(2,1)S(1)}, bf16[512,1024]{1,0:T(8,128)(2,1)}, u32[]{:S(2)}, u32[]{:S(2)}) %collective-permute-start.13) | collective-permute-done | bytes 1048608 | tf_op jit(solution)/shard_map/ppermute | solution.py:160
  79.5 1.0 copy-done.12
  80.4 0.1 copy.9
  80.6 0.6 collective-permute-start.11
  81.2 0.1 collective-permute-start.12
  81.2 0.2 copy.14
  81.4 0.3 fusion.44.ids_ref
  81.7 11.1 %collective-permute-done.1 = bf16[256,2048]{1,0:T(8,128)(2,1)} collective-permute-done((bf16[256,2048]{1,0:T(8,128)(2,1)}, bf16[256,2048]{1,0:T(8,128)(2,1)}, u32[]{:S(2)}, u32[]{:S(2)}) %collective-permute-start.1) | collective-permute-done | bytes 1048608 | tf_op jit(solution)/shard_map/ppermute | solution.py:156
  92.8 1.2 slice.75
  94.0 0.8 collective-permute-start.18
  94.9 1.3 slice.77.x_ref
  96.2 1.0 fusion.58
  97.2 1.0 add_convert_fusion.rest_5_
  98.3 4.7 %lend_near.1 = f32[512,1024]{1,0:T(8,128)S(1)} custom-call(s32[1]{0:T(128)} %bitcast.spot_ref, bf16[512,2048]{1,0:T(8,128)(2,1)} %collective-permute-done.6.x_ref, bf16[512,1024]{1,0:T(8,128)(2,1)S(1)} %copy-done.5, bf16[512,1024]{1,0:T(8,128)(2,1)} %collective-permute-done.13.rest_1_, bf16[512,1024]{1,0:T(8,128)(2,1)S(1)} %copy-done.13, ...), custom_call_target="tpu_custom_call" | custom-call | flops 2147483648 | bytes 7340032 | tf_op jit(solution)/shard_map/lend_near/pallas_call | solution.py:118
  103.0 0.1 slice.79.rest_4_
  103.1 0.0 slice-start.2
  103.2 2.7 %lend_far.3 = bf16[256,1536]{1,0:T(8,128)(2,1)S(1)} custom-call(s32[1]{0:T(128)} %bitcast.spot_ref, bf16[256,2048]{1,0:T(8,128)(2,1)S(1)} %slice.77.x_ref, bf16[512,1024]{1,0:T(8,128)(2,1)S(1)} %pad_maximum_fusion.2.rest_0_, bf16[512,1024]{1,0:T(8,128)(2,1)S(1)} %collective-permute-done.10.rest_1_, bf16[512,1024]{1,0:T(8,128)(2,1)S(1)} %collective-permute-done.11.rest_2_, ...), custom_call_target="tpu_custom_call" | custom-call | flops 1073741824 | bytes 5767168 | tf_op jit(solution)/shard_map/lend_far/pallas_call | solution.py:118
  105.8 0.0 slice-start.3
  105.8 1.6 %collective-permute-start.16 = (bf16[256,1536]{1,0:T(8,128)(2,1)S(1)}, bf16[256,1536]{1,0:T(8,128)(2,1)S(1)}, u32[]{:S(2)}, u32[]{:S(2)}) collective-permute-start(bf16[256,1536]{1,0:T(8,128)(2,1)S(1)} %lend_far.3), channel_id=1, source_target_pairs={{1,0},{2,3},{5,4},{6,7},{9,8},{10,11},{13,12},{14,15},{17,16},{18,... | collective-permute-start | bytes 2359304 | tf_op jit(solution)/shard_map/ppermute | solution.py:156
  107.4 5.2 %fusion.2 = f32[512,1024]{1,0:T(8,128)S(1)} fusion(bf16[512,2048]{1,0:T(8,128)(2,1)} %collective-permute-done.6.x_ref, bf16[8192,1024]{1,0:T(8,128)(2,1)} %param.8, s32[]{:T(128)S(6)} %select_n.60), kind=kOutput, calls=%fused_computation.2 | convolution fusion | flops 2147483648 | bytes 8388612 | tf_op jit(solution)/shard_map/dot_general | solution.py:14
  112.6 1.0 slice.81
  113.5 0.9 collective-permute-start.17
  114.4 3.9 %fusion = f32[512,1024]{1,0:T(8,128)S(1)} fusion(bf16[8192,1024]{1,0:T(8,128)(2,1)S(1)} %bitcast.10, s32[]{:T(128)S(6)} %select_n.64, bf16[256,2048]{1,0:T(8,128)(2,1)} %collective-permute-done.1, bf16[256,2048]{1,0:T(8,128)(2,1)} %collective-permute-done.5.x_ref), kind=kOutput, calls=%fused_computation | convolution fusion | flops 2151677952 | bytes 8388612 | tf_op jit(solution)/shard_map/dot_general | solution.py:14
  118.3 0.1 slice.84.rest_4_
  118.4 2.2 %lend_far.4 = bf16[192,1024]{1,0:T(8,128)(2,1)S(1)} custom-call(s32[1]{0:T(128)} %bitcast.spot_ref, bf16[192,2048]{1,0:T(8,128)(2,1)S(1)} %collective-permute-done.18.x_ref, bf16[512,1024]{1,0:T(8,128)(2,1)S(1)} %pad_maximum_fusion.2.rest_0_, bf16[512,1024]{1,0:T(8,128)(2,1)S(1)} %collective-permute-done.10.rest_1_, ...), custom_call_target="tpu_custom_call" | custom-call | flops 805306368 | bytes 5373952 | tf_op jit(solution)/shard_map/lend_far/pallas_call | solution.py:118
  120.7 1.3 collective-permute-start.19
  122.0 5.0 %collective-permute-done.16 = bf16[256,1536]{1,0:T(8,128)(2,1)S(1)} collective-permute-done((bf16[256,1536]{1,0:T(8,128)(2,1)S(1)}, bf16[256,1536]{1,0:T(8,128)(2,1)S(1)}, u32[]{:S(2)}, u32[]{:S(2)}) %collective-permute-start.16) | collective-permute-done | bytes 786464 | tf_op jit(solution)/shard_map/ppermute | solution.py:156
  127.0 2.4 %lend_far.5 = bf16[64,1024]{1,0:T(8,128)(2,1)S(1)} custom-call(s32[1]{0:T(128)} %bitcast.spot_ref, bf16[64,2048]{1,0:T(8,128)(2,1)S(1)} %collective-permute-done.17.x_ref, bf16[512,1024]{1,0:T(8,128)(2,1)S(1)} %pad_maximum_fusion.2.rest_0_, bf16[512,1024]{1,0:T(8,128)(2,1)S(1)} %collective-permute-done.10.rest_1_, ...), custom_call_target="tpu_custom_call" | custom-call | flops 268435456 | bytes 4587520 | tf_op jit(solution)/shard_map/lend_far/pallas_call | solution.py:118
  129.4 1.3 collective-permute-start.20
  130.8 0.1 maximum_select_fusion.coded_ref
  130.9 3.4 %mix.1 = bf16[512,256]{1,0:T(8,128)(2,1)S(1)} custom-call(s32[512,1]{1,0:T(8,128)S(1)} %fusion.44.ids_ref, bf16[512,256]{1,0:T(8,128)(2,1)S(1)} %maximum_select_fusion.coded_ref, bf16[8,256,256]{2,1,0:T(8,128)(2,1)S(1)} %copy-done.7, bf16[8,256,256]{2,1,0:T(8,128)(2,1)} %collective-permute-done.3.rest_1_, bf16[8,256,256]{2,1,0:T(8,128)(2,1)S(1)} %copy-done.9, ...), custom_call_target="tpu_custom_call" | custom-call | flops 402653184 | bytes 4718592 | tf_op jit(solution)/shard_map/mix/pallas_call | solution.py:46
  134.4 0.5 add_add_fusion
  134.8 0.6 slice-done.4
  135.4 2.5 %fusion.21 = bf16[256,1024]{1,0:T(8,128)(2,1)S(1)} fusion(bf16[8192,1024]{1,0:T(8,128)(2,1)S(1)} %bitcast.10, s32[]{:T(128)S(6)} %select_n.69, f32[512,1024]{1,0:T(8,128)S(1)} %add_add_fusion, bf16[256,1024]{1,0:T(8,128)(2,1)S(1)} %slice-done.4, bf16[256,2560]{1,0:T(8,128)(2,1)} %collective-permute-done.7), kind=kOutput, calls=%fused_computation.19 | convolution fusion | flops 1074790400 | bytes 7340036 | tf_op jit(solution)/shard_map/dot_general | solution.py:14
  137.9 1.0 fusion.30
  138.9 0.9 fusion.39
  139.8 1.0 pad_maximum_fusion.3
  (62 shorter events, 0.2 us)
Async XLA Ops:
  0.0 1.2 copy-start
  3.5 58.4 %copy-start.2 = (f32[512,256]{1,0:T(8,128)}, f32[512,256]{1,0:T(8,128)S(1)}, u32[]{:S(2)}) copy-start(f32[512,256]{1,0:T(8,128)S(1)} %get-tuple-element.66.value_ref) | copy-start | bytes 1572868
  3.5 8.7 %copy-start.6 = (bf16[8,256,256]{2,1,0:T(8,128)(2,1)S(1)}, bf16[8,256,256]{2,1,0:T(8,128)(2,1)}, u32[]{:S(2)}) copy-start(bf16[8,256,256]{2,1,0:T(8,128)(2,1)} %rest_0_.1) | copy-start | bytes 3145732
  6.2 34.4 %collective-permute-start = (bf16[512,1280]{1,0:T(8,128)(2,1)}, bf16[512,1280]{1,0:T(8,128)(2,1)}, u32[]{:S(2)}, u32[]{:S(2)}) collective-permute-start(bf16[512,1280]{1,0:T(8,128)(2,1)} %pad_maximum_fusion), channel_id=1, source_target_pairs={{0,1},{3,2},{4,5},{7,6},{8,9},{11,10},{12,13},{15,14},{16,17},{19,... | collective-permute-start | bytes 3932168 | tf_op jit(solution)/shard_map/ppermute | solution.py:156
  12.2 24.6 %collective-permute-start.2 = (bf16[8,256,256]{2,1,0:T(8,128)(2,1)S(1)}, bf16[8,256,256]{2,1,0:T(8,128)(2,1)S(1)}, u32[]{:S(2)}, u32[]{:S(2)}) collective-permute-start(bf16[8,256,256]{2,1,0:T(8,128)(2,1)S(1)} %copy-done.6), channel_id=1, source_target_pairs={{0,8},{4,12},{8,0},{12,4},{1,9},{5,13},{9,1},{13,5},{2,10},{6,14},... | collective-permute-start | bytes 3145736 | tf_op jit(solution)/shard_map/ppermute | solution.py:160
  13.7 23.1 %collective-permute-start.3 = (bf16[8,256,256]{2,1,0:T(8,128)(2,1)S(1)}, bf16[8,256,256]{2,1,0:T(8,128)(2,1)}, u32[]{:S(2)}, u32[]{:S(2)}) collective-permute-start(bf16[8,256,256]{2,1,0:T(8,128)(2,1)S(1)} %copy-done.6), channel_id=1, source_target_pairs={{0,4},{4,0},{8,12},{12,8},{1,5},{5,1},{9,13},{13,9},{2,6},{6,2},{1... | collective-permute-start | bytes 3145736 | tf_op jit(solution)/shard_map/ppermute | solution.py:160
  13.7 50.8 %collective-permute-start.6 = (bf16[512,2048]{1,0:T(8,128)(2,1)}, bf16[512,2048]{1,0:T(8,128)(2,1)}, u32[]{:S(2)}, u32[]{:S(2)}) collective-permute-start(bf16[512,2048]{1,0:T(8,128)(2,1)} %param.6), channel_id=1, source_target_pairs={{1,2},{2,1},{5,6},{6,5},{9,10},{10,9},{13,14},{14,13},{17,18},{18,... | collective-permute-start | bytes 6291464 | tf_op jit(solution)/shard_map/ppermute | solution.py:156
  18.8 43.1 %collective-permute-start.5 = (bf16[256,2048]{1,0:T(8,128)(2,1)}, bf16[256,2048]{1,0:T(8,128)(2,1)}, u32[]{:S(2)}, u32[]{:S(2)}) collective-permute-start(bf16[256,2048]{1,0:T(8,128)(2,1)} %get-tuple-element.55), channel_id=1, source_target_pairs={{0,1},{3,2},{1,0},{2,3},{4,5},{7,6},{5,4},{6,7},{8,9},{11,10},{9,8... | collective-permute-start | bytes 3145736 | tf_op jit(solution)/shard_map/ppermute | solution.py:156
  36.8 14.6 %copy-start.8 = (bf16[8,256,256]{2,1,0:T(8,128)(2,1)}, bf16[8,256,256]{2,1,0:T(8,128)(2,1)S(1)}, u32[]{:S(2)}) copy-start(bf16[8,256,256]{2,1,0:T(8,128)(2,1)S(1)} %collective-permute-done.2.rest_2_) | copy-start | bytes 3145732
  36.8 19.6 %collective-permute-start.9 = (bf16[8,256,256]{2,1,0:T(8,128)(2,1)S(1)}, bf16[8,256,256]{2,1,0:T(8,128)(2,1)S(1)}, u32[]{:S(2)}, u32[]{:S(2)}) collective-permute-start(bf16[8,256,256]{2,1,0:T(8,128)(2,1)S(1)} %collective-permute-done.2.rest_2_), channel_id=1, source_target_pairs={{0,4},{4,0},{8,12},{12,8},{1,5},{5,1},{9,13},{13,9},{2,6},{6,2},{1... | collective-permute-start | bytes 3145736 | tf_op jit(solution)/shard_map/ppermute | solution.py:160
  41.9 11.7 %collective-permute-start.4 = (bf16[256,1024]{1,0:T(8,128)(2,1)S(1)}, bf16[256,1024]{1,0:T(8,128)(2,1)S(1)}, u32[]{:S(2)}, u32[]{:S(2)}) collective-permute-start(bf16[256,1024]{1,0:T(8,128)(2,1)S(1)} %get-tuple-element.33), channel_id=1, source_target_pairs={{0,16},{16,0},{1,17},{17,1},{2,18},{18,2},{3,19},{19,3},{4,20},{20... | collective-permute-start | bytes 1572872 | tf_op jit(solution)/shard_map/ppermute | solution.py:164
  43.5 11.4 %collective-permute-start.8 = (bf16[256,1024]{1,0:T(8,128)(2,1)S(1)}, bf16[256,1024]{1,0:T(8,128)(2,1)S(1)}, u32[]{:S(2)}, u32[]{:S(2)}) collective-permute-start(bf16[256,1024]{1,0:T(8,128)(2,1)S(1)} %get-tuple-element.40), channel_id=1, source_target_pairs={{0,8},{4,12},{8,0},{12,4},{1,9},{5,13},{9,1},{13,5},{2,10},{6,14},... | collective-permute-start | bytes 1572872 | tf_op jit(solution)/shard_map/ppermute | solution.py:160
  53.7 10.8 %copy-start.4 = (bf16[512,1024]{1,0:T(8,128)(2,1)}, bf16[512,1024]{1,0:T(8,128)(2,1)S(1)}, u32[]{:S(2)}) copy-start(bf16[512,1024]{1,0:T(8,128)(2,1)S(1)} %pad_maximum_fusion.1.rest_0_) | copy-start | bytes 3145732
  53.7 25.8 %collective-permute-start.14 = (bf16[512,1024]{1,0:T(8,128)(2,1)S(1)}, bf16[512,1024]{1,0:T(8,128)(2,1)S(1)}, u32[]{:S(2)}, u32[]{:S(2)}) collective-permute-start(bf16[512,1024]{1,0:T(8,128)(2,1)S(1)} %pad_maximum_fusion.1.rest_0_), channel_id=1, source_target_pairs={{0,4},{4,0},{8,12},{12,8},{1,5},{5,1},{9,13},{13,9},{2,6},{6,2},{1... | collective-permute-start | bytes 3145736 | tf_op jit(solution)/shard_map/ppermute | solution.py:160
  54.8 24.6 %collective-permute-start.13 = (bf16[512,1024]{1,0:T(8,128)(2,1)S(1)}, bf16[512,1024]{1,0:T(8,128)(2,1)}, u32[]{:S(2)}, u32[]{:S(2)}) collective-permute-start(bf16[512,1024]{1,0:T(8,128)(2,1)S(1)} %pad_maximum_fusion.1.rest_0_), channel_id=1, source_target_pairs={{0,8},{4,12},{8,0},{12,4},{1,9},{5,13},{9,1},{13,5},{2,10},{6,14},... | collective-permute-start | bytes 3145736 | tf_op jit(solution)/shard_map/ppermute | solution.py:160
  56.4 24.0 %copy-start.17 = (s32[512,1]{0,1:T(1,128)S(1)}, s32[512,1]{0,1:T(1,128)}, u32[]{:S(2)}) copy-start(s32[512,1]{0,1:T(1,128)} %param.7) | copy-start | bytes 6148
  56.4 23.0 %copy-start.10 = (bf16[8,256,256]{2,1,0:T(8,128)(2,1)}, bf16[8,256,256]{2,1,0:T(8,128)(2,1)S(1)}, u32[]{:S(2)}) copy-start(bf16[8,256,256]{2,1,0:T(8,128)(2,1)S(1)} %collective-permute-done.9.rest_3_) | copy-start | bytes 3145732
  56.4 24.7 %collective-permute-start.10 = (bf16[512,1024]{1,0:T(8,128)(2,1)S(1)}, bf16[512,1024]{1,0:T(8,128)(2,1)S(1)}, u32[]{:S(2)}, u32[]{:S(2)}) collective-permute-start(bf16[512,1024]{1,0:T(8,128)(2,1)S(1)} %pad_maximum_fusion.2.rest_0_), channel_id=1, source_target_pairs={{0,16},{16,0},{1,17},{17,1},{2,18},{18,2},{3,19},{19,3},{4,20},{20... | collective-permute-start | bytes 3145736 | tf_op jit(solution)/shard_map/ppermute | solution.py:164
  64.5 30.4 %collective-permute-start.7 = (bf16[256,2560]{1,0:T(8,128)(2,1)}, bf16[256,2560]{1,0:T(8,128)(2,1)}, u32[]{:S(2)}, u32[]{:S(2)}) collective-permute-start(bf16[256,2560]{1,0:T(8,128)(2,1)} %pack.1), channel_id=1, source_target_pairs={{1,2},{2,1},{5,6},{6,5},{9,10},{10,9},{13,14},{14,13},{17,18},{18,... | collective-permute-start | bytes 3932168 | tf_op jit(solution)/shard_map/ppermute | solution.py:156
  66.2 26.6 %collective-permute-start.1 = (bf16[256,2048]{1,0:T(8,128)(2,1)}, bf16[256,2048]{1,0:T(8,128)(2,1)}, u32[]{:S(2)}, u32[]{:S(2)}) collective-permute-start(bf16[256,2048]{1,0:T(8,128)(2,1)} %get-tuple-element.29), channel_id=1, source_target_pairs={{0,1},{3,2},{1,0},{2,3},{4,5},{7,6},{5,4},{6,7},{8,9},{11,10},{9,8... | collective-permute-start | bytes 3145736 | tf_op jit(solution)/shard_map/ppermute | solution.py:156
  79.4 1.0 copy-start.12
  80.4 17.9 %collective-permute-start.15 = (bf16[512,1024]{1,0:T(8,128)(2,1)}, bf16[512,1024]{1,0:T(8,128)(2,1)}, u32[]{:S(2)}, u32[]{:S(2)}) collective-permute-start(bf16[512,1024]{1,0:T(8,128)(2,1)} %collective-permute-done.13.rest_1_), channel_id=1, source_target_pairs={{0,4},{4,0},{8,12},{12,8},{1,5},{5,1},{9,13},{13,9},{2,6},{6,2},{1... | collective-permute-start | bytes 3145736 | tf_op jit(solution)/shard_map/ppermute | solution.py:160
  80.6 22.6 %collective-permute-start.11 = (bf16[512,1024]{1,0:T(8,128)(2,1)S(1)}, bf16[512,1024]{1,0:T(8,128)(2,1)S(1)}, u32[]{:S(2)}, u32[]{:S(2)}) collective-permute-start(bf16[512,1024]{1,0:T(8,128)(2,1)S(1)} %pad_maximum_fusion.2.rest_0_), channel_id=1, source_target_pairs={{0,4},{4,0},{8,12},{12,8},{1,5},{5,1},{9,13},{13,9},{2,6},{6,2},{1... | collective-permute-start | bytes 3145736 | tf_op jit(solution)/shard_map/ppermute | solution.py:160
  81.2 22.0 %collective-permute-start.12 = (bf16[512,1024]{1,0:T(8,128)(2,1)S(1)}, bf16[512,1024]{1,0:T(8,128)(2,1)}, u32[]{:S(2)}, u32[]{:S(2)}) collective-permute-start(bf16[512,1024]{1,0:T(8,128)(2,1)S(1)} %collective-permute-done.10.rest_1_), channel_id=1, source_target_pairs={{0,4},{4,0},{8,12},{12,8},{1,5},{5,1},{9,13},{13,9},{2,6},{6,2},{1... | collective-permute-start | bytes 3145736 | tf_op jit(solution)/shard_map/ppermute | solution.py:160
  81.7 15.5 %copy-start.3 = (f32[512,256]{1,0:T(8,128)S(1)}, f32[512,256]{1,0:T(8,128)}, u32[]{:S(2)}) copy-start(f32[512,256]{1,0:T(8,128)} %copy-done.2) | copy-start | bytes 1572868
  94.0 4.3 %copy-start.5 = (bf16[512,1024]{1,0:T(8,128)(2,1)S(1)}, bf16[512,1024]{1,0:T(8,128)(2,1)}, u32[]{:S(2)}) copy-start(bf16[512,1024]{1,0:T(8,128)(2,1)} %copy-done.4) | copy-start | bytes 3145732
  94.0 4.3 %copy-start.13 = (bf16[512,1024]{1,0:T(8,128)(2,1)S(1)}, bf16[512,1024]{1,0:T(8,128)(2,1)}, u32[]{:S(2)}) copy-start(bf16[512,1024]{1,0:T(8,128)(2,1)} %copy-done.12) | copy-start | bytes 3145732
  94.0 24.4 %collective-permute-start.18 = (bf16[192,2048]{1,0:T(8,128)(2,1)S(1)}, bf16[192,2048]{1,0:T(8,128)(2,1)S(1)}, u32[]{:S(2)}, u32[]{:S(2)}) collective-permute-start(bf16[192,2048]{1,0:T(8,128)(2,1)S(1)} %slice.75), channel_id=1, source_target_pairs={{1,2},{2,1},{5,6},{6,5},{9,10},{10,9},{13,14},{14,13},{17,18},{18,... | collective-permute-start | bytes 2359304 | tf_op jit(solution)/shard_map/ppermute | solution.py:156
  98.3 16.1 %slice-start = ((s8[16777216]{0:T(1024)(128)(4,1)}), s8[4194304]{0:T(1024)(128)(4,1)S(1)}, s32[]{:S(2)}) async-start(s8[16777216]{0:T(1024)(128)(4,1)} %bitcast.9), calls=%async_computation | async-start | bytes 8388608
  98.3 16.1 %slice-start.1 = ((s8[16777216]{0:T(1024)(128)(4,1)}), s8[4194304]{0:T(1024)(128)(4,1)S(1)}, s32[]{:S(2)}) async-start(s8[16777216]{0:T(1024)(128)(4,1)} %bitcast.9), calls=%async_computation.1 | async-start | bytes 8388608
  103.1 11.3 %slice-start.2 = ((s8[16777216]{0:T(1024)(128)(4,1)}), s8[4194304]{0:T(1024)(128)(4,1)S(1)}, s32[]{:S(2)}) async-start(s8[16777216]{0:T(1024)(128)(4,1)} %bitcast.9), calls=%async_computation.2 | async-start | bytes 8388608
  105.8 8.6 %slice-start.3 = ((s8[16777216]{0:T(1024)(128)(4,1)}), s8[4194304]{0:T(1024)(128)(4,1)S(1)}, s32[]{:S(2)}) async-start(s8[16777216]{0:T(1024)(128)(4,1)} %bitcast.9), calls=%async_computation.3 | async-start | bytes 8388608
  105.8 21.2 %collective-permute-start.16 = (bf16[256,1536]{1,0:T(8,128)(2,1)S(1)}, bf16[256,1536]{1,0:T(8,128)(2,1)S(1)}, u32[]{:S(2)}, u32[]{:S(2)}) collective-permute-start(bf16[256,1536]{1,0:T(8,128)(2,1)S(1)} %lend_far.3), channel_id=1, source_target_pairs={{1,0},{2,3},{5,4},{6,7},{9,8},{10,11},{13,12},{14,15},{17,16},{18,... | collective-permute-start | bytes 2359304 | tf_op jit(solution)/shard_map/ppermute | solution.py:156
  113.5 13.5 %collective-permute-start.17 = (bf16[64,2048]{1,0:T(8,128)(2,1)S(1)}, bf16[64,2048]{1,0:T(8,128)(2,1)S(1)}, u32[]{:S(2)}, u32[]{:S(2)}) collective-permute-start(bf16[64,2048]{1,0:T(8,128)(2,1)S(1)} %slice.81), channel_id=1, source_target_pairs={{1,2},{2,1},{5,6},{6,5},{9,10},{10,9},{13,14},{14,13},{17,18},{18,... | collective-permute-start | bytes 786440 | tf_op jit(solution)/shard_map/ppermute | solution.py:156
  120.7 17.2 %collective-permute-start.19 = (bf16[192,1024]{1,0:T(8,128)(2,1)S(1)}, bf16[192,1024]{1,0:T(8,128)(2,1)S(1)}, u32[]{:S(2)}, u32[]{:S(2)}) collective-permute-start(bf16[192,1024]{1,0:T(8,128)(2,1)S(1)} %lend_far.4), channel_id=1, source_target_pairs={{1,0},{2,3},{5,4},{6,7},{9,8},{10,11},{13,12},{14,15},{17,16},{18,... | collective-permute-start | bytes 1179656 | tf_op jit(solution)/shard_map/ppermute | solution.py:156
  127.0 3.7 %copy-start.15 = (bf16[256,1536]{1,0:T(8,128)(2,1)}, bf16[256,1536]{1,0:T(8,128)(2,1)S(1)}, u32[]{:S(2)}) copy-start(bf16[256,1536]{1,0:T(8,128)(2,1)S(1)} %collective-permute-done.16) | copy-start | bytes 2359300
  127.0 3.8 %copy-start.7 = (bf16[8,256,256]{2,1,0:T(8,128)(2,1)S(1)}, bf16[8,256,256]{2,1,0:T(8,128)(2,1)}, u32[]{:S(2)}) copy-start(bf16[8,256,256]{2,1,0:T(8,128)(2,1)} %rest_0_.1) | copy-start | bytes 3145732
  127.0 3.8 %copy-start.9 = (bf16[8,256,256]{2,1,0:T(8,128)(2,1)S(1)}, bf16[8,256,256]{2,1,0:T(8,128)(2,1)}, u32[]{:S(2)}) copy-start(bf16[8,256,256]{2,1,0:T(8,128)(2,1)} %copy-done.8) | copy-start | bytes 3145732
  127.0 3.9 %copy-start.11 = (bf16[8,256,256]{2,1,0:T(8,128)(2,1)S(1)}, bf16[8,256,256]{2,1,0:T(8,128)(2,1)}, u32[]{:S(2)}) copy-start(bf16[8,256,256]{2,1,0:T(8,128)(2,1)} %copy-done.10) | copy-start | bytes 3145732
  129.4 9.5 %collective-permute-start.20 = (bf16[64,1024]{1,0:T(8,128)(2,1)S(1)}, bf16[64,1024]{1,0:T(8,128)(2,1)S(1)}, u32[]{:S(2)}, u32[]{:S(2)}) collective-permute-start(bf16[64,1024]{1,0:T(8,128)(2,1)S(1)} %lend_far.5), channel_id=1, source_target_pairs={{1,0},{2,3},{5,4},{6,7},{9,8},{10,11},{13,12},{14,15},{17,16},{18,... | collective-permute-start | bytes 393224 | tf_op jit(solution)/shard_map/ppermute | solution.py:156
  130.9 3.5 %copy-start.14 = (f32[512,1024]{1,0:T(8,128)S(1)}, f32[512,1024]{1,0:T(8,128)}, u32[]{:S(2)}) copy-start(f32[512,1024]{1,0:T(8,128)} %fusion.4) | copy-start | bytes 6291460
  130.9 3.5 %copy-start.16 = (bf16[256,1024]{1,0:T(8,128)(2,1)S(1)}, bf16[256,1024]{1,0:T(8,128)(2,1)}, u32[]{:S(2)}) copy-start(bf16[256,1024]{1,0:T(8,128)(2,1)} %param.11) | copy-start | bytes 1572868
  134.4 1.0 slice-start.4
  138.9 1.9 %copy-start.1 = (bf16[2048,256]{1,0:T(8,128)(2,1)S(1)}, bf16[2048,256]{1,0:T(8,128)(2,1)}, u32[]{:S(2)}) copy-start(bf16[2048,256]{1,0:T(8,128)(2,1)} %param.9) | copy-start | bytes 3145732

commit v6 on v1

v6 whole, which is shorter than its diff:
```python
import functools

import jax
import jax.numpy as jnp
from jax import lax
from jax.experimental import pallas as pl
from jax.experimental.pallas import tpu as pltpu
from jax.sharding import PartitionSpec as P

BLK = 16


def dot(a, b):
    return jnp.dot(a, b, preferred_element_type=jnp.float32)


def mix_kernel(ids_ref, coded_ref, *rest):
    cores, (mixed_ref, slots_ref) = rest[:4], rest[-2:]
    rows = coded_ref.shape[0]
    each = cores[0].shape[0]
    adapters = each * len(cores)
    ids = ids_ref[...]
    named = ids == lax.broadcasted_iota(jnp.int32, (rows, adapters), 1)
    below = lax.broadcasted_iota(jnp.int32, (rows, rows), 0) > lax.broadcasted_iota(
        jnp.int32, (rows, rows), 1
    )
    earlier = dot(below.astype(jnp.bfloat16), named.astype(jnp.bfloat16))
    within = jnp.sum(jnp.where(named, earlier, 0.0), axis=1, keepdims=True).astype(jnp.int32)
    slot = ids * BLK + within
    place = (slot == lax.broadcasted_iota(jnp.int32, (rows, adapters * BLK), 1)).astype(
        jnp.bfloat16
    )
    packed = lax.dot_general(
        place, coded_ref[...], (((0,), (0,)), ((), ())), preferred_element_type=jnp.float32
    ).astype(jnp.bfloat16)
    for a in range(adapters):
        slots_ref[a * BLK : (a + 1) * BLK, :] = dot(
            packed[a * BLK : (a + 1) * BLK, :], cores[a // each][a % each]
        ).astype(jnp.bfloat16)
    mixed_ref[...] = dot(place, slots_ref[...]).astype(jnp.bfloat16)


def mix(ids, coded, cores, waits):
    rows, width = coded.shape
    adapters = sum(c.shape[0] for c in cores)
    return pl.pallas_call(
        mix_kernel,
        out_shape=jax.ShapeDtypeStruct((rows, width), jnp.bfloat16),
        in_specs=[pl.BlockSpec(memory_space=pltpu.VMEM)] * (2 + len(cores))
        + [pl.BlockSpec(memory_space=pl.ANY)] * len(waits),
        scratch_shapes=[pltpu.VMEM((adapters * BLK, width), jnp.bfloat16)],
        compiler_params=pltpu.CompilerParams(vmem_limit_bytes=10 * 2**20),
        cost_estimate=pl.CostEstimate(
            flops=2 * rows * width * (3 * adapters * BLK),
            bytes_accessed=adapters * width * width * 2 + rows * width * 4,
            transcendentals=0,
        ),
        name="mix",
    )(ids, coded, *cores, *waits)


def pick_kernel(which_ref, x_ref, beside_ref, out_ref):
    columns = x_ref.shape[1]
    out_ref[:, :columns] = x_ref[...]
    out_ref[:, columns:] = beside_ref[...]


def pick(x, blocks, rows, beside):
    columns, more = x.shape[1], beside.shape[1]
    return pl.pallas_call(
        pick_kernel,
        out_shape=jax.ShapeDtypeStruct((blocks.size * rows, columns + more), x.dtype),
        grid_spec=pltpu.PrefetchScalarGridSpec(
            num_scalar_prefetch=1,
            grid=(blocks.size,),
            in_specs=[
                pl.BlockSpec((rows, columns), lambda i, which: (which[i], 0)),
                pl.BlockSpec((rows, more), lambda i, which: (i, 0)),
            ],
            out_specs=pl.BlockSpec((rows, columns + more), lambda i, which: (i, 0)),
        ),
        cost_estimate=pl.CostEstimate(
            flops=0, bytes_accessed=4 * blocks.size * rows * columns, transcendentals=0
        ),
        name="pick",
    )(blocks, x, beside)


def lend_kernel(spot_ref, *refs, count, blocks, width, added):
    xs, rest = refs[:count], refs[count:]
    out_ref = rest[-1]
    piece = xs[0].shape[1] // sum(len(masks) for _, masks in blocks)
    spot = spot_ref[0]
    start = 0
    for x_ref in xs:
        rows = slice(start, start + x_ref.shape[0])
        start = rows.stop
        columns = [
            jnp.concatenate(
                [x_ref[:, pl.ds(pl.multiple_of((spot ^ m) * piece, piece), piece)] for m in masks],
                axis=1,
            )
            for _, masks in blocks
        ]
        for n in range(0, out_ref.shape[1], width):
            part = slice(n, n + width)
            value = rest[len(blocks)][rows, part] if added else 0.0
            for x, (operand, _) in zip(columns, blocks):
                value = value + dot(x, rest[operand][:, part])
            out_ref[rows, part] = value.astype(out_ref.dtype)


def lend(spot, xs, weights, masks, name, add=None, waits=(), dtype=jnp.bfloat16):
    rows, depth = sum(x.shape[0] for x in xs), xs[0].shape[1]
    columns = weights[0].shape[1]
    whole = pl.BlockSpec(memory_space=pltpu.VMEM)
    operands = (*xs, *weights, *(() if add is None else (add,)))
    return pl.pallas_call(
        functools.partial(
            lend_kernel,
            count=len(xs),
            blocks=tuple(enumerate(masks)),
            width=256,
            added=add is not None,
        ),
        out_shape=jax.ShapeDtypeStruct((rows, columns), dtype),
        in_specs=[pl.BlockSpec(memory_space=pltpu.SMEM)]
        + [whole] * len(operands)
        + [pl.BlockSpec(memory_space=pl.ANY)] * len(waits),
        out_specs=whole,
        compiler_params=pltpu.CompilerParams(vmem_limit_bytes=12 * 2**20),
        cost_estimate=pl.CostEstimate(
            flops=2 * rows * depth * columns,
            bytes_accessed=depth * columns * 2 + rows * (depth + columns) * 2,
            transcendentals=0,
        ),
        name=name,
    )(spot.reshape(1), *operands, *waits)


IN = [(0, 1), (3, 2)]
OUT = [(1, 0), (2, 3)]
SWAP = [(1, 2), (2, 1)]

TURNS = (3, 3, 2)
CROSSINGS = (3, 3, 1, 1)
LENDS = (2, 2)
AFTER = {
    "corner": ("mate", "own"),
    "near1": ("corner",),
    "far1": ("corner",),
    "near2": ("far3",),
    "far2": ("far3",),
    "turn1": ("turn0", "swap", "half", "near1", "far1"),
    "turn2": ("turn1", "cross0", "far3"),
    "near4": ("coded", "cross0", "turn1", "turn2"),
    "far4": ("coded", "cross0", "turn2"),
    "lend0": ("turn2",),
    "lend1": ("base", "cross2"),
    "mix": ("lent",),
    "lent": ("far4",),
    "near3": ("coded",),
}


def send(x, pairs):
    return lax.ppermute(x, "tp", pairs)


def swap_rep(x, bit):
    return lax.ppermute(x, "rep", [(i, i ^ bit) for i in range(4)])


def swap_groups(x):
    return lax.ppermute(x, "groups", [(0, 1), (1, 0)])


def row_cuts(rows, eighths):
    ends = [0]
    for e in eighths:
        ends.append(ends[-1] + e * rows // 8)
    return list(zip(ends, ends[1:]))


def on_line(activations, row_adapter, base_weight, basis_down, adapter_cores, basis_up):
    me, rep = lax.axis_index("tp"), lax.axis_index("rep")
    inner = (me == 1) | (me == 2)
    left = me < 2
    near_in, far_in = jnp.where(left, 1, 2), jnp.where(left, 2, 1)
    near_out, far_out = jnp.where(left, 0, 3), jnp.where(left, 3, 0)
    spot = lax.axis_index("groups") * 4 + rep
    rows, depth = activations.shape
    piece = depth // 8
    turns, crossings = row_cuts(rows, TURNS), row_cuts(rows, CROSSINGS)
    done = {}

    def after(name, value):
        waits = AFTER.get(name, ())
        if not waits:
            return value
        value, held = lax.optimization_barrier((value, [done[w] for w in waits]))
        done.update(zip(waits, held))
        return value

    def held(name):
        return [done[w] for w in AFTER.get(name, ())]

    def move(name, value, how, *args):
        done[name] = how(after(name, value), *args)
        return done[name]

    def weight_of(owner):
        return lax.dynamic_slice_in_dim(base_weight, owner * depth, depth, 0)

    move("swap", activations, send, SWAP)
    eighths = jnp.stack([far_in * 8 + spot, far_out * 8 + spot]).astype(jnp.int32)
    partial_value = dot(activations, basis_down)
    pieces = pick(base_weight, eighths, piece, partial_value.astype(jnp.bfloat16))
    move("pieces", pieces, send, IN)
    columns = base_weight.shape[1]

    move("across", adapter_cores, swap_rep, 2)
    move("mate", adapter_cores, swap_rep, 1)
    done["own"] = dot(after("own", activations), weight_of(me))
    move("corner", done["across"], swap_rep, 1)
    each = adapter_cores.shape[0]
    ids = (row_adapter // each ^ rep) * each + row_adapter % each

    def turn(i):
        move(f"turn{i}", activations[slice(*turns[i])], send, IN + OUT)

    def turned(a, b):
        j = [a >= start and b <= stop for start, stop in turns].index(True)
        return done[f"turn{j}"][a - turns[j][0] : b - turns[j][0]]

    def cross(i):
        move(f"cross{i}", turned(*crossings[i]), send, SWAP)

    turn(0)
    side = done["pieces"][:, columns:].astype(jnp.float32) + partial_value
    move("half", side.astype(jnp.bfloat16), send, SWAP)
    move("near1", done["pieces"][:piece, :columns], swap_groups)
    move("far1", done["pieces"][piece:, :columns], swap_rep, 2)
    turn(1)
    done["swap dot"] = done["own"] + dot(after("swap dot", done["swap"]), weight_of(far_in))
    coded = (side + done["half"].astype(jnp.float32)).astype(jnp.bfloat16)
    move("coded", coded, send, OUT)
    near = jnp.concatenate([done["pieces"][:piece, :columns], done["near1"]], axis=0)
    far = jnp.concatenate([done["pieces"][piece:, :columns], done["far1"]], axis=0)
    move("near3", near, swap_rep, 1)
    move("far3", far, swap_rep, 1)
    move("near2", near, swap_rep, 2)
    move("far2", far, swap_groups)
    cross(0)
    for i in range(2, len(turns)):
        turn(i)
    near_masks, far_masks = ((0, 4), (2, 6), (1, 5), (3, 7)), ((0, 2), (4, 6), (1, 3), (5, 7))

    for i in range(1, len(crossings)):
        cross(i)
    move("near4", done["near2"], swap_rep, 1)
    move("far4", done["far2"], swap_rep, 1)

    weights = (near, done["near2"], done["near3"], done["near4"])
    done["lent"] = lend(
        spot, [done["swap"]], weights, near_masks, "lend_near", None, held("lent"), jnp.float32
    )
    weights = (far, done["far2"], done["far3"], done["far4"])
    first = 0
    for i, count in enumerate(LENDS):
        chunks = range(first, first + count)
        first += count
        xs, add = [done[f"cross{j}"] for j in chunks], done["lent"]
        add = add[crossings[chunks[0]][0] : crossings[chunks[-1]][1]]
        done[f"lend{i}"] = lend(spot, xs, weights, far_masks, "lend_far", add, held(f"lend{i}"))
        move(f"back{i}", done[f"lend{i}"], send, OUT)
        if i == 0:
            cores = (adapter_cores, done["mate"], done["across"], done["corner"])
            mixed = mix(ids, jnp.where(inner, coded, done["coded"]), cores, held("mix"))
            done["base"] = done["swap dot"] + dot(mixed, basis_up)

    last_weight = weight_of(far_out)
    turned_weight = weight_of(jnp.where(inner, near_out, near_in))
    back = [done[f"back{i}"] for i in range(len(LENDS))]
    out = []
    first = 0
    for i, count in enumerate(LENDS):
        start = crossings[first][0]
        for a, b in crossings[first : first + count]:
            value = done["base"][a:b] + dot(turned(a, b), turned_weight)
            value = value + dot(done[f"cross{len(out)}"], last_weight)
            value = value + back[i][a - start : b - start].astype(jnp.float32)
            out.append(value.astype(jnp.bfloat16))
        first += count
    return jnp.concatenate(out, axis=0)


def on_any(activations, row_adapter, base_weight, basis_down, adapter_cores, basis_up):
    width = basis_down.shape[1]
    local_count = adapter_cores.shape[0]
    owners = lax.axis_size("rep")
    all_adapters = local_count * owners
    slot_count = all_adapters * BLK
    base = dot(lax.all_gather(activations, "tp", axis=1, tiled=True), base_weight)
    partial_value = dot(activations, basis_down)
    adapter_ids = row_adapter[:, 0]
    onehot = (adapter_ids[:, None] == jnp.arange(all_adapters, dtype=jnp.int32)[None, :]).astype(
        jnp.int32
    )
    earlier = jnp.cumsum(onehot, axis=0) - onehot
    within = jnp.sum(earlier * onehot, axis=1)
    slot_index = adapter_ids * BLK + within
    coded = lax.psum(partial_value, "tp").astype(jnp.bfloat16)
    packed = jnp.zeros((slot_count, width), jnp.bfloat16).at[slot_index].set(coded)
    packed = packed.reshape(owners, local_count, BLK, width)
    mixed_slots = jnp.einsum(
        "nasr,arq->nasq",
        lax.all_to_all(packed, "rep", split_axis=0, concat_axis=0, tiled=True),
        adapter_cores,
        preferred_element_type=jnp.float32,
    ).astype(jnp.bfloat16)
    returned = lax.all_to_all(mixed_slots, "rep", split_axis=0, concat_axis=0, tiled=True).reshape(
        slot_count, width
    )
    mixed = returned[slot_index]
    return (base + dot(mixed, basis_up)).astype(jnp.bfloat16)


def solution(mesh):
    placed = (
        P(("groups", "rep"), "tp"),
        P(("groups", "rep"), None),
        P(None, "tp"),
        P("tp", None),
        P("rep", None, None),
        P(None, "tp"),
    )
    short = (mesh.shape["groups"], mesh.shape["rep"], mesh.shape["tp"]) == (2, 4, 4)
    return jax.shard_map(
        on_line if short else on_any,
        mesh=mesh,
        in_specs=placed,
        out_specs=P(("groups", "rep"), "tp"),
        check_vma=False,
    )
```

time: 182 us -> 156 us (0.86)
  the two profiles are of different devices: /device:TPU:14 before, /device:TPU:0 now
where the time goes in v6:
time: 156 us; the launch traced here: 155 us
  waiting for transfers between devices  64.6 us (41%)
  starting transfers between devices  32.4 us (21%)
  matrix products  31.5 us (20%)
  Pallas kernels  13.9 us (9%)
  local copies, waits for them, and re-layouts  6.26 us (4%)
  other arithmetic  5.66 us (4%)
    ppermute x13, waiting for transfers between devices, send(): return lax.ppermute(x, 'tp', pairs)  62.5 us
    dot_general x12, matrix products, dot(): return jnp.dot(a, b, preferred_element_type=jnp.float32)  31.5 us
    ppermute x13, starting transfers between devices, send(): return lax.ppermute(x, 'tp', pairs)  24.6 us
    pallas_call x3, Pallas kernels, lend(): pl.pallas_call(functools.partial(lend_kernel, count=len(xs), blocks=tuple...  7.06 us
    ppermute x9, starting transfers between devices, swap_rep(): return lax.ppermute(x, 'rep', [(i, i ^ bit) for i in range(4)])  4.79 us
    pallas_call x1, Pallas kernels, mix(): pl.pallas_call(mix_kernel, out_shape=jax.ShapeDtypeStruct((rows, width),...  3.95 us
  transfers between devices with their start and end apart: 24, of which 6 were waited for; matrix products, arithmetic and copies ran while one was open for 23% of the time, Pallas kernels for 9%

profile of v6, /device:TPU:0, one launch (start us, length us, event | category | flops | bytes accessed | tf_op | source)
XLA Modules:
  0.0 154.9 jit_solution(657005210481257149)
XLA Ops:
  0.0 2.9 %collective-permute-start = (bf16[8,256,256]{2,1,0:T(8,128)(2,1)}, bf16[8,256,256]{2,1,0:T(8,128)(2,1)}, u32[]{:S(2)}, u32[]{:S(2)}) collective-permute-start(bf16[8,256,256]{2,1,0:T(8,128)(2,1)} %rest_0_.1), channel_id=1, source_target_pairs={{0,8},{4,12},{8,0},{12,4},{1,9},{5,13},{9,1},{13,5},{2,10},{6,14},... | collective-permute-start | bytes 3145736 | tf_op jit(solution)/shard_map/ppermute | solution.py:171
  2.9 0.8 collective-permute-start.3
  3.8 0.7 pad_add_fusion.which_ref
  4.4 3.2 %fusion.74 = (bf16[512,256]{1,0:T(8,128)(2,1)}, f32[512,256]{1,0:T(8,128)}) fusion(bf16[512,2048]{1,0:T(8,128)(2,1)} %param.6, bf16[2048,256]{1,0:T(8,128)(2,1)S(1)} %copy-done), kind=kOutput, calls=%fused_computation.75 | convolution fusion | flops 537001984 | bytes 3932160 | tf_op jit(solution)/shard_map/dot_general | solution.py:14
  7.6 2.8 %pick.1 = bf16[512,1280]{1,0:T(8,128)(2,1)} custom-call(s32[2]{0:T(128)} %pad_add_fusion.which_ref, bf16[8192,1024]{1,0:T(8,128)(2,1)} %x_ref.1, bf16[512,256]{1,0:T(8,128)(2,1)} %get-tuple-element.75.beside_ref), custom_call_target="tpu_custom_call" | custom-call | bytes 2097152 | tf_op jit(solution)/shard_map/pick/pallas_call | solution.py:70
  10.5 7.3 %collective-permute-start.4 = (bf16[512,1280]{1,0:T(8,128)(2,1)}, bf16[512,1280]{1,0:T(8,128)(2,1)}, u32[]{:S(2)}, u32[]{:S(2)}) collective-permute-start(bf16[512,1280]{1,0:T(8,128)(2,1)} %pick.1), channel_id=1, source_target_pairs={{0,1},{3,2},{4,5},{7,6},{8,9},{11,10},{12,13},{15,14},{16,17},{19,... | collective-permute-start | bytes 3932168 | tf_op jit(solution)/shard_map/ppermute | solution.py:167
  17.7 6.6 %fusion.20 = f32[512,1024]{1,0:T(8,128)} fusion(bf16[512,2048]{1,0:T(8,128)(2,1)} %param.6, bf16[8192,1024]{1,0:T(8,128)(2,1)} %x_ref.1, s32[]{:T(128)S(6)} %select_n.49), kind=kOutput, calls=%fused_computation.21 | convolution fusion | flops 2147483648 | bytes 8388612 | tf_op jit(solution)/shard_map/dot_general | solution.py:14
  24.3 2.1 %collective-permute-done.rest_2_ = bf16[8,256,256]{2,1,0:T(8,128)(2,1)} collective-permute-done((bf16[8,256,256]{2,1,0:T(8,128)(2,1)}, bf16[8,256,256]{2,1,0:T(8,128)(2,1)}, u32[]{:S(2)}, u32[]{:S(2)}) %collective-permute-start) | collective-permute-done | bytes 1048608 | tf_op jit(solution)/shard_map/ppermute | solution.py:171
  26.4 1.0 fusion.71
  27.5 1.8 %collective-permute-start.2 = (bf16[192,2048]{1,0:T(8,128)(2,1)S(1)}, bf16[192,2048]{1,0:T(8,128)(2,1)S(1)}, u32[]{:S(2)}, u32[]{:S(2)}) collective-permute-start(bf16[192,2048]{1,0:T(8,128)(2,1)S(1)} %get-tuple-element.69), channel_id=1, source_target_pairs={{0,1},{3,2},{1,0},{2,3},{4,5},{7,6},{5,4},{6,7},{8,9},{11,10},{9,8... | collective-permute-start | bytes 2359304 | tf_op jit(solution)/shard_map/ppermute | solution.py:167
  29.3 16.8 %collective-permute-done.4 = bf16[512,1280]{1,0:T(8,128)(2,1)} collective-permute-done((bf16[512,1280]{1,0:T(8,128)(2,1)}, bf16[512,1280]{1,0:T(8,128)(2,1)}, u32[]{:S(2)}, u32[]{:S(2)}) %collective-permute-start.4) | collective-permute-done | bytes 1310752 | tf_op jit(solution)/shard_map/ppermute | solution.py:167
  46.0 1.3 fusion.72
  47.4 0.6 collective-permute-start.8
  48.0 1.5 collective-permute-start.7
  49.5 1.0 fusion.47
  50.5 0.7 collective-permute-start.5
  51.2 10.9 %collective-permute-done.2 = bf16[192,2048]{1,0:T(8,128)(2,1)S(1)} collective-permute-done((bf16[192,2048]{1,0:T(8,128)(2,1)S(1)}, bf16[192,2048]{1,0:T(8,128)(2,1)S(1)}, u32[]{:S(2)}, u32[]{:S(2)}) %collective-permute-start.2) | collective-permute-done | bytes 786464 | tf_op jit(solution)/shard_map/ppermute | solution.py:167
  62.1 0.8 copy-done.11
  63.0 0.1 copy-done.16
  63.1 0.7 copy-done.1
  63.8 0.8 copy-done.15
  64.6 0.1 pad_maximum_fusion.refs_2_
  64.7 0.1 collective-permute-start.9
  64.7 0.8 slice.67
  65.6 0.1 copy.8
  65.7 2.5 %collective-permute-start.13 = (bf16[192,2048]{1,0:T(8,128)(2,1)}, bf16[192,2048]{1,0:T(8,128)(2,1)}, u32[]{:S(2)}, u32[]{:S(2)}) collective-permute-start(bf16[192,2048]{1,0:T(8,128)(2,1)} %get-tuple-element.50), channel_id=1, source_target_pairs={{0,1},{3,2},{1,0},{2,3},{4,5},{7,6},{5,4},{6,7},{8,9},{11,10},{9,8... | collective-permute-start | bytes 2359304 | tf_op jit(solution)/shard_map/ppermute | solution.py:167
  68.3 1.5 collective-permute-start.14
  69.8 0.2 copy.13
  70.1 0.3 fusion.50.ids_ref
  70.3 1.4 pad_maximum_fusion.1.refs_1_
  71.8 0.6 collective-permute-start.11
  72.4 1.5 collective-permute-start.10
  73.9 1.1 add_convert_fusion
  75.0 1.4 collective-permute-start.12
  76.5 10.5 %collective-permute-done.13 = bf16[192,2048]{1,0:T(8,128)(2,1)} collective-permute-done((bf16[192,2048]{1,0:T(8,128)(2,1)}, bf16[192,2048]{1,0:T(8,128)(2,1)}, u32[]{:S(2)}, u32[]{:S(2)}) %collective-permute-start.13) | collective-permute-done | bytes 786464 | tf_op jit(solution)/shard_map/ppermute | solution.py:167
  87.0 3.5 %collective-permute-start.15 = (bf16[128,2048]{1,0:T(8,128)(2,1)S(1)}, bf16[128,2048]{1,0:T(8,128)(2,1)S(1)}, u32[]{:S(2)}, u32[]{:S(2)}) collective-permute-start(bf16[128,2048]{1,0:T(8,128)(2,1)S(1)} %copy-done.14), channel_id=1, source_target_pairs={{0,1},{3,2},{1,0},{2,3},{4,5},{7,6},{5,4},{6,7},{8,9},{11,10},{9,8... | collective-permute-start | bytes 1572872 | tf_op jit(solution)/shard_map/ppermute | solution.py:167
  90.5 4.5 %fusion = f32[512,1024]{1,0:T(8,128)S(1)} fusion(bf16[512,2048]{1,0:T(8,128)(2,1)S(1)} %copy-done.2, bf16[8192,1024]{1,0:T(8,128)(2,1)} %x_ref.1, s32[]{:T(128)S(6)} %select_n.52), kind=kOutput, calls=%fused_computation | convolution fusion | flops 2147483648 | bytes 8388612 | tf_op jit(solution)/shard_map/dot_general | solution.py:14
  95.0 3.2 %fusion.18 = f32[192,1024]{1,0:T(8,128)S(1)} fusion(bf16[192,2048]{1,0:T(8,128)(2,1)S(1)} %copy-done.12, bf16[8192,1024]{1,0:T(8,128)(2,1)} %x_ref.1, s32[]{:T(128)S(6)} %select_n.60), kind=kOutput, calls=%fused_computation.18 | convolution fusion | flops 805306368 | bytes 5767172 | tf_op jit(solution)/shard_map/dot_general | solution.py:14
  98.2 0.1 collective-permute-start.16
  98.3 0.7 collective-permute-start.19
  99.0 4.5 %collective-permute-done.15.refs_7_ = bf16[128,2048]{1,0:T(8,128)(2,1)S(1)} collective-permute-done((bf16[128,2048]{1,0:T(8,128)(2,1)S(1)}, bf16[128,2048]{1,0:T(8,128)(2,1)S(1)}, u32[]{:S(2)}, u32[]{:S(2)}) %collective-permute-start.15) | collective-permute-done | bytes 524320 | tf_op jit(solution)/shard_map/ppermute | solution.py:167
  103.6 0.5 collective-permute-start.17
  104.1 0.7 collective-permute-start.21
  104.8 3.0 %fusion.14 = f32[64,1024]{1,0:T(8,128)S(1)} fusion(bf16[8192,1024]{1,0:T(8,128)(2,1)} %x_ref.1, s32[]{:T(128)S(6)} %select_n.60, bf16[128,2048]{1,0:T(8,128)(2,1)S(1)} %collective-permute-done.15.refs_7_), kind=kOutput, calls=%fused_computation.14 | convolution fusion | flops 268435456 | bytes 4718596 | tf_op jit(solution)/shard_map/dot_general | solution.py:14
  107.8 3.0 %fusion.12 = f32[64,1024]{1,0:T(8,128)S(1)} fusion(bf16[8192,1024]{1,0:T(8,128)(2,1)} %x_ref.1, s32[]{:T(128)S(6)} %select_n.60, bf16[128,2048]{1,0:T(8,128)(2,1)S(1)} %collective-permute-done.15.refs_7_), kind=kOutput, calls=%fused_computation.12 | convolution fusion | flops 268435456 | bytes 4718596 | tf_op jit(solution)/shard_map/dot_general | solution.py:14
  110.9 0.9 collective-permute-start.22
  111.8 2.4 %lend_near.1.rest_4_ = f32[512,1024]{1,0:T(8,128)S(1)} custom-call(s32[1]{0:T(128)} %bitcast.3.spot_ref, bf16[512,2048]{1,0:T(8,128)(2,1)S(1)} %copy-done.2, bf16[512,1024]{1,0:T(8,128)(2,1)S(1)} %pad_maximum_fusion.1.refs_1_, bf16[512,1024]{1,0:T(8,128)(2,1)S(1)} %collective-permute-done.11.refs_2_, bf16[512,1024]{1,0:T(8,128)(2,1)S(1)} %collective-permute-done.16.refs_3_, ...), custom_call_target="tpu_custom_call" | custom-call | flops 2147483648 | bytes 7340032 | tf_op jit(solution)/shard_map/lend_near/pallas_call | solution.py:118
  114.2 0.0 slice-start
  114.2 0.2 slice.86.refs_6_
  114.4 0.0 slice-start.1
  114.5 3.1 %lend_far.2 = bf16[384,1024]{1,0:T(8,128)(2,1)S(1)} custom-call(s32[1]{0:T(128)} %bitcast.3.spot_ref, bf16[192,2048]{1,0:T(8,128)(2,1)} %collective-permute-done.14.refs_0_, bf16[192,2048]{1,0:T(8,128)(2,1)S(1)} %collective-permute-done.19.refs_1_, bf16[512,1024]{1,0:T(8,128)(2,1)S(1)} %pad_maximum_fusion.refs_2_, ...), custom_call_target="tpu_custom_call" | custom-call | flops 1610612736 | bytes 6553600 | tf_op jit(solution)/shard_map/lend_far/pallas_call | solution.py:118
  117.6 0.0 slice-start.2
  117.6 1.6 %collective-permute-start.20 = (bf16[384,1024]{1,0:T(8,128)(2,1)S(1)}, bf16[384,1024]{1,0:T(8,128)(2,1)S(1)}, u32[]{:S(2)}, u32[]{:S(2)}) collective-permute-start(bf16[384,1024]{1,0:T(8,128)(2,1)S(1)} %lend_far.2), channel_id=1, source_target_pairs={{1,0},{2,3},{5,4},{6,7},{9,8},{10,11},{13,12},{14,15},{17,16},{18,... | collective-permute-start | bytes 2359304 | tf_op jit(solution)/shard_map/ppermute | solution.py:167
  119.2 4.0 %mix.1 = bf16[512,256]{1,0:T(8,128)(2,1)S(1)} custom-call(s32[512,1]{1,0:T(8,128)S(1)} %fusion.50.ids_ref, bf16[512,256]{1,0:T(8,128)(2,1)S(1)} %broadcast_select_fusion.coded_ref, bf16[8,256,256]{2,1,0:T(8,128)(2,1)S(1)} %copy-done.3, bf16[8,256,256]{2,1,0:T(8,128)(2,1)} %collective-permute-done.1.rest_1_, ...), custom_call_target="tpu_custom_call" | custom-call | flops 402653184 | bytes 4718592 | tf_op jit(solution)/shard_map/mix/pallas_call | solution.py:46
  123.2 0.5 add_add_fusion.refs_7_
  123.7 1.6 %lend_far.3 = bf16[128,1024]{1,0:T(8,128)(2,1)S(1)} custom-call(s32[1]{0:T(128)} %bitcast.3.spot_ref, bf16[64,2048]{1,0:T(8,128)(2,1)S(1)} %collective-permute-done.21.refs_0_.refs_8_, bf16[64,2048]{1,0:T(8,128)(2,1)S(1)} %collective-permute-done.22.refs_1_, bf16[512,1024]{1,0:T(8,128)(2,1)S(1)} %pad_maximum_fusion.refs_2_, ...), custom_call_target="tpu_custom_call" | custom-call | flops 536870912 | bytes 4980736 | tf_op jit(solution)/shard_map/lend_far/pallas_call | solution.py:118
  125.3 1.3 collective-permute-start.23
  126.6 2.2 %fusion.16 = f32[192,1024]{1,0:T(8,128)S(1)} fusion(bf16[192,2048]{1,0:T(8,128)(2,1)} %collective-permute-done.13, bf16[8192,1024]{1,0:T(8,128)(2,1)S(1)} %bitcast.18, s32[]{:T(128)S(6)} %select_n.60), kind=kOutput, calls=%fused_computation.16 | convolution fusion | flops 805306368 | bytes 5767172 | tf_op jit(solution)/shard_map/dot_general | solution.py:14
  128.8 19.8 %collective-permute-done.23 = bf16[128,1024]{1,0:T(8,128)(2,1)S(1)} collective-permute-done((bf16[128,1024]{1,0:T(8,128)(2,1)S(1)}, bf16[128,1024]{1,0:T(8,128)(2,1)S(1)}, u32[]{:S(2)}, u32[]{:S(2)}) %collective-permute-start.23) | collective-permute-done | bytes 262176 | tf_op jit(solution)/shard_map/ppermute | solution.py:167
  148.6 0.9 fusion.38
  149.5 0.9 fusion.35
  150.4 2.3 %fusion.46 = bf16[192,1024]{1,0:T(8,128)(2,1)S(1)} fusion(f32[192,1024]{1,0:T(8,128)S(1)} %fusion.18, f32[512,1024]{1,0:T(8,128)S(1)} %add_add_fusion.refs_7_, bf16[384,1024]{1,0:T(8,128)(2,1)S(1)} %collective-permute-done.20, bf16[192,2048]{1,0:T(8,128)(2,1)} %collective-permute-done.14.refs_0_, bf16[8192,1024]{1,0:T(8,128)(2,1)S(1)} %bitcast.18, ...), kind=kOutput, calls=%fused_computation.38 | convolution fusion | flops 806289408 | bytes 7340036 | tf_op jit(solution)/shard_map/dot_general | solution.py:14
  152.7 1.1 fusion.43
  153.8 1.0 pad_maximum_fusion.2
  (63 shorter events, 0.3 us)
Async XLA Ops:
  0.0 4.4 %copy-start = (bf16[2048,256]{1,0:T(8,128)(2,1)S(1)}, bf16[2048,256]{1,0:T(8,128)(2,1)}, u32[]{:S(2)}) copy-start(bf16[2048,256]{1,0:T(8,128)(2,1)} %param.9) | copy-start | bytes 3145732
  0.0 26.4 %collective-permute-start = (bf16[8,256,256]{2,1,0:T(8,128)(2,1)}, bf16[8,256,256]{2,1,0:T(8,128)(2,1)}, u32[]{:S(2)}, u32[]{:S(2)}) collective-permute-start(bf16[8,256,256]{2,1,0:T(8,128)(2,1)} %rest_0_.1), channel_id=1, source_target_pairs={{0,8},{4,12},{8,0},{12,4},{1,9},{5,13},{9,1},{13,5},{2,10},{6,14},... | collective-permute-start | bytes 3145736 | tf_op jit(solution)/shard_map/ppermute | solution.py:171
  2.9 23.5 %collective-permute-start.1 = (bf16[8,256,256]{2,1,0:T(8,128)(2,1)}, bf16[8,256,256]{2,1,0:T(8,128)(2,1)}, u32[]{:S(2)}, u32[]{:S(2)}) collective-permute-start(bf16[8,256,256]{2,1,0:T(8,128)(2,1)} %rest_0_.1), channel_id=1, source_target_pairs={{0,4},{4,0},{8,12},{12,8},{1,5},{5,1},{9,13},{13,9},{2,6},{6,2},{1... | collective-permute-start | bytes 3145736 | tf_op jit(solution)/shard_map/ppermute | solution.py:171
  2.9 59.2 %collective-permute-start.3 = (bf16[512,2048]{1,0:T(8,128)(2,1)}, bf16[512,2048]{1,0:T(8,128)(2,1)S(1)}, u32[]{:S(2)}, u32[]{:S(2)}) collective-permute-start(bf16[512,2048]{1,0:T(8,128)(2,1)} %param.6), channel_id=1, source_target_pairs={{1,2},{2,1},{5,6},{6,5},{9,10},{10,9},{13,14},{14,13},{17,18},{18,... | collective-permute-start | bytes 6291464 | tf_op jit(solution)/shard_map/ppermute | solution.py:167
  10.5 35.6 %collective-permute-start.4 = (bf16[512,1280]{1,0:T(8,128)(2,1)}, bf16[512,1280]{1,0:T(8,128)(2,1)}, u32[]{:S(2)}, u32[]{:S(2)}) collective-permute-start(bf16[512,1280]{1,0:T(8,128)(2,1)} %pick.1), channel_id=1, source_target_pairs={{0,1},{3,2},{4,5},{7,6},{8,9},{11,10},{12,13},{15,14},{16,17},{19,... | collective-permute-start | bytes 3932168 | tf_op jit(solution)/shard_map/ppermute | solution.py:167
  17.7 8.7 %copy-start.6 = (bf16[512,2048]{1,0:T(8,128)(2,1)S(1)}, bf16[512,2048]{1,0:T(8,128)(2,1)}, u32[]{:S(2)}) copy-start(bf16[512,2048]{1,0:T(8,128)(2,1)} %param.6) | copy-start | bytes 6291460
  24.3 25.1 %copy-start.7 = (f32[512,256]{1,0:T(8,128)S(1)}, f32[512,256]{1,0:T(8,128)}, u32[]{:S(2)}) copy-start(f32[512,256]{1,0:T(8,128)} %get-tuple-element.76) | copy-start | bytes 1572868
  26.4 20.9 %collective-permute-start.6 = (bf16[8,256,256]{2,1,0:T(8,128)(2,1)}, bf16[8,256,256]{2,1,0:T(8,128)(2,1)S(1)}, u32[]{:S(2)}, u32[]{:S(2)}) collective-permute-start(bf16[8,256,256]{2,1,0:T(8,128)(2,1)} %collective-permute-done.rest_2_), channel_id=1, source_target_pairs={{0,4},{4,0},{8,12},{12,8},{1,5},{5,1},{9,13},{13,9},{2,6},{6,2},{1... | collective-permute-start | bytes 3145736 | tf_op jit(solution)/shard_map/ppermute | solution.py:171
  27.5 34.6 %collective-permute-start.2 = (bf16[192,2048]{1,0:T(8,128)(2,1)S(1)}, bf16[192,2048]{1,0:T(8,128)(2,1)S(1)}, u32[]{:S(2)}, u32[]{:S(2)}) collective-permute-start(bf16[192,2048]{1,0:T(8,128)(2,1)S(1)} %get-tuple-element.69), channel_id=1, source_target_pairs={{0,1},{3,2},{1,0},{2,3},{4,5},{7,6},{5,4},{6,7},{8,9},{11,10},{9,8... | collective-permute-start | bytes 2359304 | tf_op jit(solution)/shard_map/ppermute | solution.py:167
  47.3 14.8 %copy-start.10 = (bf16[256,1024]{1,0:T(8,128)(2,1)}, bf16[256,1024]{1,0:T(8,128)(2,1)S(1)}, u32[]{:S(2)}) copy-start(bf16[256,1024]{1,0:T(8,128)(2,1)S(1)} %get-tuple-element.39) | copy-start | bytes 1572868
  47.3 17.3 %copy-start.4 = (bf16[8,256,256]{2,1,0:T(8,128)(2,1)}, bf16[8,256,256]{2,1,0:T(8,128)(2,1)S(1)}, u32[]{:S(2)}) copy-start(bf16[8,256,256]{2,1,0:T(8,128)(2,1)S(1)} %collective-permute-done.6.rest_3_) | copy-start | bytes 3145732
  47.4 14.8 %collective-permute-start.8 = (bf16[256,1024]{1,0:T(8,128)(2,1)S(1)}, bf16[256,1024]{1,0:T(8,128)(2,1)S(1)}, u32[]{:S(2)}, u32[]{:S(2)}) collective-permute-start(bf16[256,1024]{1,0:T(8,128)(2,1)S(1)} %get-tuple-element.41), channel_id=1, source_target_pairs={{0,8},{4,12},{8,0},{12,4},{1,9},{5,13},{9,1},{13,5},{2,10},{6,14},... | collective-permute-start | bytes 1572872 | tf_op jit(solution)/shard_map/ppermute | solution.py:171
  48.0 14.2 %collective-permute-start.7 = (bf16[256,1024]{1,0:T(8,128)(2,1)S(1)}, bf16[256,1024]{1,0:T(8,128)(2,1)S(1)}, u32[]{:S(2)}, u32[]{:S(2)}) collective-permute-start(bf16[256,1024]{1,0:T(8,128)(2,1)S(1)} %get-tuple-element.39), channel_id=1, source_target_pairs={{0,16},{16,0},{1,17},{17,1},{2,18},{18,2},{3,19},{19,3},{4,20},{20... | collective-permute-start | bytes 1572872 | tf_op jit(solution)/shard_map/ppermute | solution.py:175
  49.5 16.1 %copy-start.17 = (s32[512,1]{0,1:T(1,128)S(1)}, s32[512,1]{0,1:T(1,128)}, u32[]{:S(2)}) copy-start(s32[512,1]{0,1:T(1,128)} %param.7) | copy-start | bytes 6148
  50.5 11.6 %collective-permute-start.5 = (bf16[512,256]{1,0:T(8,128)(2,1)S(1)}, bf16[512,256]{1,0:T(8,128)(2,1)S(1)}, u32[]{:S(2)}, u32[]{:S(2)}) collective-permute-start(bf16[512,256]{1,0:T(8,128)(2,1)S(1)} %fusion.47), channel_id=1, source_target_pairs={{1,2},{2,1},{5,6},{6,5},{9,10},{10,9},{13,14},{14,13},{17,18},{18,... | collective-permute-start | bytes 786440 | tf_op jit(solution)/shard_map/ppermute | solution.py:167
  62.1 0.9 copy-start.11
  62.1 1.0 copy-start.16
  62.1 1.7 %copy-start.1 = (bf16[512,2048]{1,0:T(8,128)(2,1)}, bf16[512,2048]{1,0:T(8,128)(2,1)S(1)}, u32[]{:S(2)}) copy-start(bf16[512,2048]{1,0:T(8,128)(2,1)S(1)} %collective-permute-done.3.refs_0_) | copy-start | bytes 6291460
  63.8 0.8 copy-start.15
  64.7 7.1 %collective-permute-start.9 = (bf16[512,1024]{1,0:T(8,128)(2,1)S(1)}, bf16[512,1024]{1,0:T(8,128)(2,1)S(1)}, u32[]{:S(2)}, u32[]{:S(2)}) collective-permute-start(bf16[512,1024]{1,0:T(8,128)(2,1)S(1)} %pad_maximum_fusion.refs_2_), channel_id=1, source_target_pairs={{0,4},{4,0},{8,12},{12,8},{1,5},{5,1},{9,13},{13,9},{2,6},{6,2},{1... | collective-permute-start | bytes 3145736 | tf_op jit(solution)/shard_map/ppermute | solution.py:171
  65.7 21.3 %collective-permute-start.13 = (bf16[192,2048]{1,0:T(8,128)(2,1)}, bf16[192,2048]{1,0:T(8,128)(2,1)}, u32[]{:S(2)}, u32[]{:S(2)}) collective-permute-start(bf16[192,2048]{1,0:T(8,128)(2,1)} %get-tuple-element.50), channel_id=1, source_target_pairs={{0,1},{3,2},{1,0},{2,3},{4,5},{7,6},{5,4},{6,7},{8,9},{11,10},{9,8... | collective-permute-start | bytes 2359304 | tf_op jit(solution)/shard_map/ppermute | solution.py:167
  68.3 18.7 %collective-permute-start.14 = (bf16[192,2048]{1,0:T(8,128)(2,1)}, bf16[192,2048]{1,0:T(8,128)(2,1)}, u32[]{:S(2)}, u32[]{:S(2)}) collective-permute-start(bf16[192,2048]{1,0:T(8,128)(2,1)} %copy-done.11), channel_id=1, source_target_pairs={{1,2},{2,1},{5,6},{6,5},{9,10},{10,9},{13,14},{14,13},{17,18},{18,... | collective-permute-start | bytes 2359304 | tf_op jit(solution)/shard_map/ppermute | solution.py:167
  70.0 3.9 %copy-start.8 = (f32[512,256]{1,0:T(8,128)S(1)}, f32[512,256]{1,0:T(8,128)}, u32[]{:S(2)}) copy-start(f32[512,256]{1,0:T(8,128)} %get-tuple-element.76) | copy-start | bytes 1572868
  70.0 17.0 %copy-start.14 = (bf16[128,2048]{1,0:T(8,128)(2,1)S(1)}, bf16[128,2048]{1,0:T(8,128)(2,1)}, u32[]{:S(2)}) copy-start(bf16[128,2048]{1,0:T(8,128)(2,1)} %slice.67) | copy-start | bytes 1572868
  70.0 20.4 %copy-start.2 = (bf16[512,2048]{1,0:T(8,128)(2,1)S(1)}, bf16[512,2048]{1,0:T(8,128)(2,1)}, u32[]{:S(2)}) copy-start(bf16[512,2048]{1,0:T(8,128)(2,1)} %copy-done.1) | copy-start | bytes 6291460
  71.8 31.8 %collective-permute-start.11 = (bf16[512,1024]{1,0:T(8,128)(2,1)S(1)}, bf16[512,1024]{1,0:T(8,128)(2,1)S(1)}, u32[]{:S(2)}, u32[]{:S(2)}) collective-permute-start(bf16[512,1024]{1,0:T(8,128)(2,1)S(1)} %pad_maximum_fusion.1.refs_1_), channel_id=1, source_target_pairs={{0,8},{4,12},{8,0},{12,4},{1,9},{5,13},{9,1},{13,5},{2,10},{6,14},... | collective-permute-start | bytes 3145736 | tf_op jit(solution)/shard_map/ppermute | solution.py:171
  72.4 31.2 %collective-permute-start.10 = (bf16[512,1024]{1,0:T(8,128)(2,1)S(1)}, bf16[512,1024]{1,0:T(8,128)(2,1)S(1)}, u32[]{:S(2)}, u32[]{:S(2)}) collective-permute-start(bf16[512,1024]{1,0:T(8,128)(2,1)S(1)} %pad_maximum_fusion.refs_2_), channel_id=1, source_target_pairs={{0,16},{16,0},{1,17},{17,1},{2,18},{18,2},{3,19},{19,3},{4,20},{20... | collective-permute-start | bytes 3145736 | tf_op jit(solution)/shard_map/ppermute | solution.py:175
  75.0 20.0 %copy-start.12 = (bf16[192,2048]{1,0:T(8,128)(2,1)S(1)}, bf16[192,2048]{1,0:T(8,128)(2,1)}, u32[]{:S(2)}) copy-start(bf16[192,2048]{1,0:T(8,128)(2,1)} %copy-done.11) | copy-start | bytes 2359300
  75.0 23.2 %collective-permute-start.12 = (bf16[512,256]{1,0:T(8,128)(2,1)S(1)}, bf16[512,256]{1,0:T(8,128)(2,1)S(1)}, u32[]{:S(2)}, u32[]{:S(2)}) collective-permute-start(bf16[512,256]{1,0:T(8,128)(2,1)S(1)} %add_convert_fusion), channel_id=1, source_target_pairs={{1,0},{2,3},{5,4},{6,7},{9,8},{10,11},{13,12},{14,15},{17,16},{18,... | collective-permute-start | bytes 786440 | tf_op jit(solution)/shard_map/ppermute | solution.py:167
  87.0 16.5 %collective-permute-start.15 = (bf16[128,2048]{1,0:T(8,128)(2,1)S(1)}, bf16[128,2048]{1,0:T(8,128)(2,1)S(1)}, u32[]{:S(2)}, u32[]{:S(2)}) collective-permute-start(bf16[128,2048]{1,0:T(8,128)(2,1)S(1)} %copy-done.14), channel_id=1, source_target_pairs={{0,1},{3,2},{1,0},{2,3},{4,5},{7,6},{5,4},{6,7},{8,9},{11,10},{9,8... | collective-permute-start | bytes 1572872 | tf_op jit(solution)/shard_map/ppermute | solution.py:167
  98.2 12.7 %collective-permute-start.16 = (bf16[512,1024]{1,0:T(8,128)(2,1)S(1)}, bf16[512,1024]{1,0:T(8,128)(2,1)S(1)}, u32[]{:S(2)}, u32[]{:S(2)}) collective-permute-start(bf16[512,1024]{1,0:T(8,128)(2,1)S(1)} %pad_maximum_fusion.1.refs_1_), channel_id=1, source_target_pairs={{0,4},{4,0},{8,12},{12,8},{1,5},{5,1},{9,13},{13,9},{2,6},{6,2},{1... | collective-permute-start | bytes 3145736 | tf_op jit(solution)/shard_map/ppermute | solution.py:171
  98.3 16.1 %collective-permute-start.19 = (bf16[192,2048]{1,0:T(8,128)(2,1)}, bf16[192,2048]{1,0:T(8,128)(2,1)S(1)}, u32[]{:S(2)}, u32[]{:S(2)}) collective-permute-start(bf16[192,2048]{1,0:T(8,128)(2,1)} %collective-permute-done.13), channel_id=1, source_target_pairs={{1,2},{2,1},{5,6},{6,5},{9,10},{10,9},{13,14},{14,13},{17,18},{18,... | collective-permute-start | bytes 2359304 | tf_op jit(solution)/shard_map/ppermute | solution.py:167
  103.6 8.3 %collective-permute-start.18 = (bf16[512,1024]{1,0:T(8,128)(2,1)S(1)}, bf16[512,1024]{1,0:T(8,128)(2,1)S(1)}, u32[]{:S(2)}, u32[]{:S(2)}) collective-permute-start(bf16[512,1024]{1,0:T(8,128)(2,1)S(1)} %collective-permute-done.10.refs_3_), channel_id=1, source_target_pairs={{0,4},{4,0},{8,12},{12,8},{1,5},{5,1},{9,13},{13,9},{2,6},{6,2},{1... | collective-permute-start | bytes 3145736 | tf_op jit(solution)/shard_map/ppermute | solution.py:171
  103.6 8.3 %collective-permute-start.17 = (bf16[512,1024]{1,0:T(8,128)(2,1)S(1)}, bf16[512,1024]{1,0:T(8,128)(2,1)S(1)}, u32[]{:S(2)}, u32[]{:S(2)}) collective-permute-start(bf16[512,1024]{1,0:T(8,128)(2,1)S(1)} %collective-permute-done.11.refs_2_), channel_id=1, source_target_pairs={{0,4},{4,0},{8,12},{12,8},{1,5},{5,1},{9,13},{13,9},{2,6},{6,2},{1... | collective-permute-start | bytes 3145736 | tf_op jit(solution)/shard_map/ppermute | solution.py:171
  104.1 19.6 %collective-permute-start.21 = (bf16[64,2048]{1,0:T(8,128)(2,1)S(1)}, bf16[64,2048]{1,0:T(8,128)(2,1)S(1)}, u32[]{:S(2)}, u32[]{:S(2)}) collective-permute-start(bf16[64,2048]{1,0:T(8,128)(2,1)S(1)} %get-tuple-element.73), channel_id=1, source_target_pairs={{1,2},{2,1},{5,6},{6,5},{9,10},{10,9},{13,14},{14,13},{17,18},{18,... | collective-permute-start | bytes 786440 | tf_op jit(solution)/shard_map/ppermute | solution.py:167
  110.9 12.8 %collective-permute-start.22 = (bf16[64,2048]{1,0:T(8,128)(2,1)S(1)}, bf16[64,2048]{1,0:T(8,128)(2,1)S(1)}, u32[]{:S(2)}, u32[]{:S(2)}) collective-permute-start(bf16[64,2048]{1,0:T(8,128)(2,1)S(1)} %get-tuple-element.74), channel_id=1, source_target_pairs={{1,2},{2,1},{5,6},{6,5},{9,10},{10,9},{13,14},{14,13},{17,18},{18,... | collective-permute-start | bytes 786440 | tf_op jit(solution)/shard_map/ppermute | solution.py:167
  114.2 12.4 %slice-start = ((s8[16777216]{0:T(1024)(128)(4,1)}), s8[4194304]{0:T(1024)(128)(4,1)S(1)}, s32[]{:S(2)}) async-start(s8[16777216]{0:T(1024)(128)(4,1)} %bitcast.17), calls=%async_computation | async-start | bytes 8388608
  114.4 4.8 %copy-start.3 = (bf16[8,256,256]{2,1,0:T(8,128)(2,1)S(1)}, bf16[8,256,256]{2,1,0:T(8,128)(2,1)}, u32[]{:S(2)}) copy-start(bf16[8,256,256]{2,1,0:T(8,128)(2,1)} %rest_0_.1) | copy-start | bytes 3145732
  114.4 4.8 %copy-start.5 = (bf16[8,256,256]{2,1,0:T(8,128)(2,1)S(1)}, bf16[8,256,256]{2,1,0:T(8,128)(2,1)}, u32[]{:S(2)}) copy-start(bf16[8,256,256]{2,1,0:T(8,128)(2,1)} %copy-done.4) | copy-start | bytes 3145732
  114.4 12.2 %slice-start.1 = ((s8[16777216]{0:T(1024)(128)(4,1)}), s8[4194304]{0:T(1024)(128)(4,1)S(1)}, s32[]{:S(2)}) async-start(s8[16777216]{0:T(1024)(128)(4,1)} %bitcast.17), calls=%async_computation.1 | async-start | bytes 8388608
  117.6 5.6 %copy-start.9 = (f32[512,1024]{1,0:T(8,128)S(1)}, f32[512,1024]{1,0:T(8,128)}, u32[]{:S(2)}) copy-start(f32[512,1024]{1,0:T(8,128)} %fusion.20) | copy-start | bytes 6291460
  117.6 5.6 %copy-start.13 = (bf16[256,1024]{1,0:T(8,128)(2,1)S(1)}, bf16[256,1024]{1,0:T(8,128)(2,1)}, u32[]{:S(2)}) copy-start(bf16[256,1024]{1,0:T(8,128)(2,1)} %param.11) | copy-start | bytes 1572868
  117.6 9.0 %slice-start.2 = ((s8[16777216]{0:T(1024)(128)(4,1)}), s8[4194304]{0:T(1024)(128)(4,1)S(1)}, s32[]{:S(2)}) async-start(s8[16777216]{0:T(1024)(128)(4,1)} %bitcast.17), calls=%async_computation.2 | async-start | bytes 8388608
  117.6 32.8 %collective-permute-start.20 = (bf16[384,1024]{1,0:T(8,128)(2,1)S(1)}, bf16[384,1024]{1,0:T(8,128)(2,1)S(1)}, u32[]{:S(2)}, u32[]{:S(2)}) collective-permute-start(bf16[384,1024]{1,0:T(8,128)(2,1)S(1)} %lend_far.2), channel_id=1, source_target_pairs={{1,0},{2,3},{5,4},{6,7},{9,8},{10,11},{13,12},{14,15},{17,16},{18,... | collective-permute-start | bytes 2359304 | tf_op jit(solution)/shard_map/ppermute | solution.py:167
  123.2 3.4 %slice-start.3 = ((s8[16777216]{0:T(1024)(128)(4,1)}), s8[4194304]{0:T(1024)(128)(4,1)S(1)}, s32[]{:S(2)}) async-start(s8[16777216]{0:T(1024)(128)(4,1)} %bitcast.17), calls=%async_computation.3 | async-start | bytes 8388608
  125.3 23.3 %collective-permute-start.23 = (bf16[128,1024]{1,0:T(8,128)(2,1)S(1)}, bf16[128,1024]{1,0:T(8,128)(2,1)S(1)}, u32[]{:S(2)}, u32[]{:S(2)}) collective-permute-start(bf16[128,1024]{1,0:T(8,128)(2,1)S(1)} %lend_far.3), channel_id=1, source_target_pairs={{1,0},{2,3},{5,4},{6,7},{9,8},{10,11},{13,12},{14,15},{17,16},{18,... | collective-permute-start | bytes 786440 | tf_op jit(solution)/shard_map/ppermute | solution.py:167

commit v7 on v6

--- a/solution.py
+++ b/solution.py
@@ -59,31 +59,26 @@
     )(ids, coded, *cores, *waits)
 
 
-def pick_kernel(which_ref, x_ref, beside_ref, out_ref):
-    columns = x_ref.shape[1]
-    out_ref[:, :columns] = x_ref[...]
-    out_ref[:, columns:] = beside_ref[...]
-
-
-def pick(x, blocks, rows, beside):
-    columns, more = x.shape[1], beside.shape[1]
+def pick_kernel(which_ref, x_ref, out_ref):
+    out_ref[...] = x_ref[...]
+
+
+def pick(x, blocks, rows):
+    columns = x.shape[1]
     return pl.pallas_call(
         pick_kernel,
-        out_shape=jax.ShapeDtypeStruct((blocks.size * rows, columns + more), x.dtype),
+        out_shape=jax.ShapeDtypeStruct((blocks.size * rows, columns), x.dtype),
         grid_spec=pltpu.PrefetchScalarGridSpec(
             num_scalar_prefetch=1,
             grid=(blocks.size,),
-            in_specs=[
-                pl.BlockSpec((rows, columns), lambda i, which: (which[i], 0)),
-                pl.BlockSpec((rows, more), lambda i, which: (i, 0)),
-            ],
-            out_specs=pl.BlockSpec((rows, columns + more), lambda i, which: (i, 0)),
+            in_specs=[pl.BlockSpec((rows, columns), lambda i, which: (which[i], 0))],
+            out_specs=pl.BlockSpec((rows, columns), lambda i, which: (i, 0)),
         ),
         cost_estimate=pl.CostEstimate(
             flops=0, bytes_accessed=4 * blocks.size * rows * columns, transcendentals=0
         ),
         name="pick",
-    )(blocks, x, beside)
+    )(blocks, x)
 
 
 def lend_kernel(spot_ref, *refs, count, blocks, width, added):
@@ -142,24 +137,28 @@
 OUT = [(1, 0), (2, 3)]
 SWAP = [(1, 2), (2, 1)]
 
-TURNS = (3, 3, 2)
-CROSSINGS = (3, 3, 1, 1)
-LENDS = (2, 2)
+TURNS = (4, 2, 2)
+CROSSINGS = (4, 2, 2)
+LENDS = (1, 1, 1)
+RIDE = 1
 AFTER = {
     "corner": ("mate", "own"),
     "near1": ("corner",),
     "far1": ("corner",),
-    "near2": ("far3",),
-    "far2": ("far3",),
-    "turn1": ("turn0", "swap", "half", "near1", "far1"),
-    "turn2": ("turn1", "cross0", "far3"),
-    "near4": ("coded", "cross0", "turn1", "turn2"),
-    "far4": ("coded", "cross0", "turn2"),
-    "lend0": ("turn2",),
-    "lend1": ("base", "cross2"),
-    "mix": ("lent",),
+    "near2": ("near3", "far3"),
+    "far2": ("near3", "far3"),
+    "turn1": ("turn0", "near1", "far1"),
+    "turn2": ("turn1",),
+    "cross0": ("swap",),
+    "near4": ("cross0",),
+    "far4": ("cross0",),
+    "lend1": ("lend0",),
+    "lend2": ("lend1",),
+    "mix": ("lend1",),
     "lent": ("far4",),
-    "near3": ("coded",),
+    "half": ("swap dot",),
+    "turned": ("lend2",),
+    "cross2": ("lend0",),
 }
 
 
@@ -190,6 +189,7 @@
     near_out, far_out = jnp.where(left, 0, 3), jnp.where(left, 3, 0)
     spot = lax.axis_index("groups") * 4 + rep
     rows, depth = activations.shape
+    width = basis_up.shape[0]
     piece = depth // 8
     turns, crossings = row_cuts(rows, TURNS), row_cuts(rows, CROSSINGS)
     done = {}
@@ -214,10 +214,8 @@
 
     move("swap", activations, send, SWAP)
     eighths = jnp.stack([far_in * 8 + spot, far_out * 8 + spot]).astype(jnp.int32)
+    move("pieces", pick(base_weight, eighths, piece), send, IN)
     partial_value = dot(activations, basis_down)
-    pieces = pick(base_weight, eighths, piece, partial_value.astype(jnp.bfloat16))
-    move("pieces", pieces, send, IN)
-    columns = base_weight.shape[1]
 
     move("across", adapter_cores, swap_rep, 2)
     move("mate", adapter_cores, swap_rep, 1)
@@ -227,7 +225,15 @@
     ids = (row_adapter // each ^ rep) * each + row_adapter % each
 
     def turn(i):
-        move(f"turn{i}", activations[slice(*turns[i])], send, IN + OUT)
+        x = activations[slice(*turns[i])]
+        if i == RIDE:
+            blocks = partial_value.astype(jnp.bfloat16).reshape(-1, *x.shape[:1], width)
+            x = jnp.concatenate([x, *blocks], axis=1)
+        move(f"turn{i}", x, send, IN + OUT)
+        if i == RIDE:
+            x = done[f"turn{i}"]
+            blocks = jnp.split(x[:, depth:], (x.shape[1] - depth) // width, axis=1)
+            done[f"turn{i}"], done["part"] = x[:, :depth], jnp.concatenate(blocks, axis=0)
 
     def turned(a, b):
         j = [a >= start and b <= stop for start, stop in turns].index(True)
@@ -237,16 +243,12 @@
         move(f"cross{i}", turned(*crossings[i]), send, SWAP)
 
     turn(0)
-    side = done["pieces"][:, columns:].astype(jnp.float32) + partial_value
-    move("half", side.astype(jnp.bfloat16), send, SWAP)
-    move("near1", done["pieces"][:piece, :columns], swap_groups)
-    move("far1", done["pieces"][piece:, :columns], swap_rep, 2)
+    move("near1", done["pieces"][:piece], swap_groups)
+    move("far1", done["pieces"][piece:], swap_rep, 2)
     turn(1)
     done["swap dot"] = done["own"] + dot(after("swap dot", done["swap"]), weight_of(far_in))
-    coded = (side + done["half"].astype(jnp.float32)).astype(jnp.bfloat16)
-    move("coded", coded, send, OUT)
-    near = jnp.concatenate([done["pieces"][:piece, :columns], done["near1"]], axis=0)
-    far = jnp.concatenate([done["pieces"][piece:, :columns], done["far1"]], axis=0)
+    near = jnp.concatenate([done["pieces"][:piece], done["near1"]], axis=0)
+    far = jnp.concatenate([done["pieces"][piece:], done["far1"]], axis=0)
     move("near3", near, swap_rep, 1)
     move("far3", far, swap_rep, 1)
     move("near2", near, swap_rep, 2)
@@ -256,8 +258,11 @@
         turn(i)
     near_masks, far_masks = ((0, 4), (2, 6), (1, 5), (3, 7)), ((0, 2), (4, 6), (1, 3), (5, 7))
 
-    for i in range(1, len(crossings)):
-        cross(i)
+    cross(1)
+    side = done["part"].astype(jnp.float32) + partial_value
+    move("half", side.astype(jnp.bfloat16), send, SWAP)
+    coded = (side + done["half"].astype(jnp.float32)).astype(jnp.bfloat16)
+    move("coded", coded, send, OUT)
     move("near4", done["near2"], swap_rep, 1)
     move("far4", done["far2"], swap_rep, 1)
 
@@ -270,25 +275,29 @@
     for i, count in enumerate(LENDS):
         chunks = range(first, first + count)
         first += count
+        if i == len(LENDS) - 1:
+            cores = (adapter_cores, done["mate"], done["across"], done["corner"])
+            mixed = mix(ids, jnp.where(inner, coded, done["coded"]), cores, held("mix"))
+            done["base"] = done["swap dot"] + dot(mixed, basis_up)
         xs, add = [done[f"cross{j}"] for j in chunks], done["lent"]
         add = add[crossings[chunks[0]][0] : crossings[chunks[-1]][1]]
         done[f"lend{i}"] = lend(spot, xs, weights, far_masks, "lend_far", add, held(f"lend{i}"))
+        for j in range(2, len(crossings)) if i == 0 else ():
+            cross(j)
+        if i == len(LENDS) - 1:
+            x = jnp.concatenate([done[f"turn{j}"] for j in range(len(turns))], axis=0)
+            owner = jnp.where(inner, near_out, near_in)
+            last = done["base"] + dot(after("turned", x), weight_of(owner))
         move(f"back{i}", done[f"lend{i}"], send, OUT)
-        if i == 0:
-            cores = (adapter_cores, done["mate"], done["across"], done["corner"])
-            mixed = mix(ids, jnp.where(inner, coded, done["coded"]), cores, held("mix"))
-            done["base"] = done["swap dot"] + dot(mixed, basis_up)
 
     last_weight = weight_of(far_out)
-    turned_weight = weight_of(jnp.where(inner, near_out, near_in))
     back = [done[f"back{i}"] for i in range(len(LENDS))]
     out = []
     first = 0
     for i, count in enumerate(LENDS):
         start = crossings[first][0]
         for a, b in crossings[first : first + count]:
-            value = done["base"][a:b] + dot(turned(a, b), turned_weight)
-            value = value + dot(done[f"cross{len(out)}"], last_weight)
+            value = last[a:b] + dot(done[f"cross{len(out)}"], last_weight)
             value = value + back[i][a - start : b - start].astype(jnp.float32)
             out.append(value.astype(jnp.bfloat16))
         first += count

time: 156 us -> 141 us (0.904)
  waiting for transfers between devices: 64.6 us -> 51.8 us
  matrix products: 31.5 us -> 21.7 us
  local copies, waits for them, and re-layouts: 6.26 us -> 9.81 us
  other arithmetic: 5.66 us -> 8.41 us
  Pallas kernels: 13.9 us -> 16.4 us
    ppermute x13, waiting for transfers between devices: 62.5 us -> 45.9 us  [send(): return lax.ppermute(x, 'tp', pairs)]
    dot_general x12 -> x8, matrix products: 31.5 us -> 21.7 us  [dot(): return jnp.dot(a, b, preferred_element_type=jnp.float32)]
    pallas_call x3 -> x4, Pallas kernels: 7.06 us -> 11.6 us  [lend(): pl.pallas_call(functools.partial(lend_kernel, count=len(xs), blocks=tuple...]
    ppermute x9, waiting for transfers between devices: 2.09 us -> 5.64 us  [swap_rep(): return lax.ppermute(x, 'rep', [(i, i ^ bit) for i in range(4)])]
    pallas_call x1, Pallas kernels: 3.95 us -> 2.07 us  [mix(): pl.pallas_call(mix_kernel, out_shape=jax.ShapeDtypeStruct((rows, width),...]
    add x0 -> x1, other arithmetic: none -> 1.75 us  [on_line(): done['own'] + dot(after('swap dot', done['swap']), weight_of(far_in))]
    unnamed x45 -> x59, local copies, waits for them, and re-layouts: 2.68 us -> 4.29 us
    slice x4 -> x3, local copies, waits for them, and re-layouts: 3.17 us -> 4.51 us  [the longest x1 2.39 us: turn(): x = activations[slice(*turns[i])]]
  transfers between devices with their start and end apart: 24 -> 24, of which waited for: 6 -> 10; matrix products, arithmetic and copies ran while one was open for 23% -> 25% of each run, Pallas kernels for 9% -> 12%
where the time goes in v7:
time: 141 us; the launch traced here: 140 us
  waiting for transfers between devices  51.8 us (37%)
  starting transfers between devices  31.7 us (22%)
  matrix products  21.7 us (15%)
  Pallas kernels  16.4 us (12%)
  local copies, waits for them, and re-layouts  9.81 us (7%)
  other arithmetic  8.41 us (6%)
    ppermute x13, waiting for transfers between devices, send(): return lax.ppermute(x, 'tp', pairs)  45.9 us
    ppermute x13, starting transfers between devices, send(): return lax.ppermute(x, 'tp', pairs)  23.5 us
    dot_general x8, matrix products, dot(): return jnp.dot(a, b, preferred_element_type=jnp.float32)  21.7 us
    pallas_call x4, Pallas kernels, lend(): pl.pallas_call(functools.partial(lend_kernel, count=len(xs), blocks=tuple...  11.6 us
    ppermute x9, waiting for transfers between devices, swap_rep(): return lax.ppermute(x, 'rep', [(i, i ^ bit) for i in range(4)])  5.64 us
    ppermute x9, starting transfers between devices, swap_rep(): return lax.ppermute(x, 'rep', [(i, i ^ bit) for i in range(4)])  5.22 us
    unnamed x59, local copies, waits for them, and re-layouts  4.29 us
    ppermute x2, starting transfers between devices, swap_groups(): return lax.ppermute(x, 'groups', [(0, 1), (1, 0)])  3.04 us
  transfers between devices with their start and end apart: 24, of which 10 were waited for; matrix products, arithmetic and copies ran while one was open for 25% of the time, Pallas kernels for 12%

profile of v7, /device:TPU:0, one launch (start us, length us, event | category | flops | bytes accessed | tf_op | source)
XLA Modules:
  0.0 140.4 jit_solution(10752821729999080558)
XLA Ops:
  0.0 2.9 %collective-permute-start.2 = (bf16[8,256,256]{2,1,0:T(8,128)(2,1)}, bf16[8,256,256]{2,1,0:T(8,128)(2,1)S(1)}, u32[]{:S(2)}, u32[]{:S(2)}) collective-permute-start(bf16[8,256,256]{2,1,0:T(8,128)(2,1)} %rest_0_.1), channel_id=1, source_target_pairs={{0,8},{4,12},{8,0},{12,4},{1,9},{5,13},{9,1},{13,5},{2,10},{6,14},... | collective-permute-start | bytes 3145736 | tf_op jit(solution)/shard_map/ppermute | solution.py:170
  2.9 0.6 pad_add_fusion.which_ref
  3.6 2.7 %pick.1 = bf16[512,1024]{1,0:T(8,128)(2,1)} custom-call(s32[2]{0:T(128)} %pad_add_fusion.which_ref, bf16[8192,1024]{1,0:T(8,128)(2,1)} %x_ref.1), custom_call_target="tpu_custom_call" | custom-call | bytes 2097152 | tf_op jit(solution)/shard_map/pick/pallas_call | solution.py:68
  6.3 4.4 %collective-permute-start.1 = (bf16[512,1024]{1,0:T(8,128)(2,1)}, bf16[512,1024]{1,0:T(8,128)(2,1)}, u32[]{:S(2)}, u32[]{:S(2)}) collective-permute-start(bf16[512,1024]{1,0:T(8,128)(2,1)} %pick.1), channel_id=1, source_target_pairs={{0,1},{3,2},{4,5},{7,6},{8,9},{11,10},{12,13},{15,14},{16,17},{19,... | collective-permute-start | bytes 3145736 | tf_op jit(solution)/shard_map/ppermute | solution.py:166
  10.8 2.0 %collective-permute-start.8 = (bf16[512,2048]{1,0:T(8,128)(2,1)}, bf16[512,2048]{1,0:T(8,128)(2,1)}, u32[]{:S(2)}, u32[]{:S(2)}) collective-permute-start(bf16[512,2048]{1,0:T(8,128)(2,1)} %param.6), channel_id=1, source_target_pairs={{1,2},{2,1},{5,6},{6,5},{9,10},{10,9},{13,14},{14,13},{17,18},{18,... | collective-permute-start | bytes 6291464 | tf_op jit(solution)/shard_map/ppermute | solution.py:166
  12.8 2.4 %slice.48 = bf16[256,2048]{1,0:T(8,128)(2,1)} slice(bf16[512,2048]{1,0:T(8,128)(2,1)} %param.6), slice={[0:256], [0:2048]} | slice | bytes 2097152 | tf_op jit(solution)/shard_map/slice | solution.py:228
  15.2 6.7 %fusion.12 = f32[512,1024]{1,0:T(8,128)} fusion(bf16[512,2048]{1,0:T(8,128)(2,1)} %param.6, bf16[8192,1024]{1,0:T(8,128)(2,1)} %x_ref.1, s32[]{:T(128)S(6)} %select_n.51), kind=kOutput, calls=%fused_computation.15 | convolution fusion | flops 2147483648 | bytes 8388612 | tf_op jit(solution)/shard_map/dot_general | solution.py:14
  21.8 4.5 %collective-permute-done.2.rest_2_ = bf16[8,256,256]{2,1,0:T(8,128)(2,1)S(1)} collective-permute-done((bf16[8,256,256]{2,1,0:T(8,128)(2,1)}, bf16[8,256,256]{2,1,0:T(8,128)(2,1)S(1)}, u32[]{:S(2)}, u32[]{:S(2)}) %collective-permute-start.2) | collective-permute-done | bytes 1048608 | tf_op jit(solution)/shard_map/ppermute | solution.py:170
  26.4 1.5 %fusion.61 = (bf16[512,256]{1,0:T(8,128)(2,1)S(1)}, f32[512,256]{1,0:T(8,128)}) fusion(bf16[512,2048]{1,0:T(8,128)(2,1)S(1)} %copy-done.13, bf16[2048,256]{1,0:T(8,128)(2,1)S(1)} %copy-done), kind=kOutput, calls=%fused_computation.62 | convolution fusion | flops 537001984 | bytes 3932160 | tf_op jit(solution)/shard_map/dot_general | solution.py:14
  27.9 0.9 slice_dynamic-update-slice_fusion
  28.8 4.8 %collective-permute-done.1 = bf16[512,1024]{1,0:T(8,128)(2,1)} collective-permute-done((bf16[512,1024]{1,0:T(8,128)(2,1)}, bf16[512,1024]{1,0:T(8,128)(2,1)}, u32[]{:S(2)}, u32[]{:S(2)}) %collective-permute-start.1) | collective-permute-done | bytes 1048608 | tf_op jit(solution)/shard_map/ppermute | solution.py:166
  33.6 1.3 fusion.59
  34.9 1.0 copy-done.9
  35.9 0.5 collective-permute-start.6
  36.4 1.5 %collective-permute-start.5 = (bf16[256,1024]{1,0:T(8,128)(2,1)S(1)}, bf16[256,1024]{1,0:T(8,128)(2,1)S(1)}, u32[]{:S(2)}, u32[]{:S(2)}) collective-permute-start(bf16[256,1024]{1,0:T(8,128)(2,1)S(1)} %get-tuple-element.37), channel_id=1, source_target_pairs={{0,16},{16,0},{1,17},{17,1},{2,18},{18,2},{3,19},{19,3},{4,20},{20... | collective-permute-start | bytes 1572872 | tf_op jit(solution)/shard_map/ppermute | solution.py:174
  38.0 17.7 %collective-permute-done = bf16[256,2048]{1,0:T(8,128)(2,1)} collective-permute-done((bf16[256,2048]{1,0:T(8,128)(2,1)}, bf16[256,2048]{1,0:T(8,128)(2,1)}, u32[]{:S(2)}, u32[]{:S(2)}) %collective-permute-start) | collective-permute-done | bytes 1048608 | tf_op jit(solution)/shard_map/ppermute | solution.py:166
  55.7 0.1 pad_maximum_fusion.1.refs_1_
  55.8 0.1 collective-permute-start.13
  55.8 0.1 pad_maximum_fusion.2.refs_1_
  55.9 0.6 collective-permute-start.12
  56.5 0.8 collective-permute-start.16
  57.3 5.8 %collective-permute-start.7 = (bf16[128,3072]{1,0:T(8,128)(2,1)}, bf16[128,3072]{1,0:T(8,128)(2,1)S(1)}, u32[]{:S(2)}, u32[]{:S(2)}) collective-permute-start(bf16[128,3072]{1,0:T(8,128)(2,1)} %copy-done.21), channel_id=1, source_target_pairs={{0,1},{3,2},{1,0},{2,3},{4,5},{7,6},{5,4},{6,7},{8,9},{11,10},{9,8... | collective-permute-start | bytes 2359304 | tf_op jit(solution)/shard_map/ppermute | solution.py:166
  63.1 0.5 collective-permute-start.15
  63.7 1.5 %collective-permute-start.14 = (bf16[512,1024]{1,0:T(8,128)(2,1)S(1)}, bf16[512,1024]{1,0:T(8,128)(2,1)}, u32[]{:S(2)}, u32[]{:S(2)}) collective-permute-start(bf16[512,1024]{1,0:T(8,128)(2,1)S(1)} %pad_maximum_fusion.1.refs_1_), channel_id=1, source_target_pairs={{0,16},{16,0},{1,17},{17,1},{2,18},{18,2},{3,19},{19,3},{4,20},{20... | collective-permute-start | bytes 3145736 | tf_op jit(solution)/shard_map/ppermute | solution.py:174
  65.2 5.1 %fusion.2 = f32[1024,512]{0,1:T(8,128)S(1)} fusion(bf16[512,2048]{1,0:T(8,128)(2,1)} %collective-permute-done.8.refs_0_, bf16[8192,1024]{1,0:T(8,128)(2,1)} %x_ref.1, s32[]{:T(128)S(6)} %select_n.52), kind=kOutput, calls=%fused_computation.2 | convolution fusion | flops 2147483648 | bytes 8388612 | tf_op jit(solution)/shard_map/dot_general | solution.py:14
  70.4 1.8 %bitcast_add_fusion = f32[512,1024]{1,0:T(8,128)} fusion(f32[512,1024]{1,0:T(8,128)S(1)} %copy-done.16, f32[1024,512]{0,1:T(8,128)S(1)} %fusion.2), kind=kLoop, calls=%fused_computation.13 | loop fusion | flops 524288 | bytes 6291456 | tf_op jit(solution)/shard_map/add | solution.py:249
  72.1 8.4 %collective-permute-done.7 = bf16[128,3072]{1,0:T(8,128)(2,1)S(1)} collective-permute-done((bf16[128,3072]{1,0:T(8,128)(2,1)}, bf16[128,3072]{1,0:T(8,128)(2,1)S(1)}, u32[]{:S(2)}, u32[]{:S(2)}) %collective-permute-start.7) | collective-permute-done | bytes 786464 | tf_op jit(solution)/shard_map/ppermute | solution.py:166
  80.5 0.8 slice.61
  81.3 1.7 %collective-permute-start.19 = (bf16[128,2048]{1,0:T(8,128)(2,1)}, bf16[128,2048]{1,0:T(8,128)(2,1)}, u32[]{:S(2)}, u32[]{:S(2)}) collective-permute-start(bf16[128,2048]{1,0:T(8,128)(2,1)} %get-tuple-element.61), channel_id=1, source_target_pairs={{0,1},{3,2},{1,0},{2,3},{4,5},{7,6},{5,4},{6,7},{8,9},{11,10},{9,8... | collective-permute-start | bytes 1572872 | tf_op jit(solution)/shard_map/ppermute | solution.py:166
  83.1 0.8 fusion.42
  83.9 1.4 collective-permute-start.9
  85.3 1.0 copy-done.11
  86.3 1.2 collective-permute-done.15.refs_2_
  87.5 0.3 collective-permute-done.14.refs_2_
  87.7 0.5 collective-permute-start.18
  88.3 0.1 copy.11
  88.5 0.8 copy.16
  89.2 1.2 fusion.45.ids_ref
  90.4 0.7 collective-permute-start.11
  91.1 1.2 add_convert_fusion
  92.3 1.4 %collective-permute-start.10 = (bf16[512,256]{1,0:T(8,128)(2,1)S(1)}, bf16[512,256]{1,0:T(8,128)(2,1)S(1)}, u32[]{:S(2)}, u32[]{:S(2)}) collective-permute-start(bf16[512,256]{1,0:T(8,128)(2,1)S(1)} %add_convert_fusion), channel_id=1, source_target_pairs={{1,0},{2,3},{5,4},{6,7},{9,8},{10,11},{13,12},{14,15},{17,16},{18,... | collective-permute-start | bytes 786440 | tf_op jit(solution)/shard_map/ppermute | solution.py:166
  93.8 0.7 collective-permute-done.19
  94.4 1.6 %pad_maximum_fusion = bf16[512,2048]{1,0:T(8,128)(2,1)S(1)} fusion(bf16[128,2048]{1,0:T(8,128)(2,1)} %collective-permute-done.19, bf16[128,2048]{1,0:T(8,128)(2,1)S(1)} %copy-done.17, bf16[256,2048]{1,0:T(8,128)(2,1)} %collective-permute-done), kind=kLoop, calls=%fused_computation.12 | loop fusion | flops 6291456 | bytes 4194304 | tf_op jit(solution)/shard_map/concatenate | solution.py:288
  96.1 7.1 %collective-permute-done.10 = bf16[512,256]{1,0:T(8,128)(2,1)S(1)} collective-permute-done((bf16[512,256]{1,0:T(8,128)(2,1)S(1)}, bf16[512,256]{1,0:T(8,128)(2,1)S(1)}, u32[]{:S(2)}, u32[]{:S(2)}) %collective-permute-start.10) | collective-permute-done | bytes 262176 | tf_op jit(solution)/shard_map/ppermute | solution.py:166
  103.2 4.8 %lend_near.1 = f32[512,1024]{1,0:T(8,128)S(1)} custom-call(s32[1]{0:T(128)} %bitcast.4.spot_ref, bf16[512,2048]{1,0:T(8,128)(2,1)} %collective-permute-done.8.refs_0_, bf16[512,1024]{1,0:T(8,128)(2,1)S(1)} %copy-done.3, bf16[512,1024]{1,0:T(8,128)(2,1)} %collective-permute-done.15.refs_2_, bf16[512,1024]{1,0:T(8,128)(2,1)} %collective-permute-done.12.refs_3_, ...), custom_call_target="tpu_custom_call" | custom-call | flops 2147483648 | bytes 7340032 | tf_op jit(solution)/shard_map/lend_near/pallas_call | solution.py:113
  108.1 0.1 slice.63.refs_5_
  108.2 1.1 copy-done.12
  109.3 2.5 %lend_far.3.refs_6_ = bf16[256,1024]{1,0:T(8,128)(2,1)S(1)} custom-call(s32[1]{0:T(128)} %bitcast.4.spot_ref, bf16[256,2048]{1,0:T(8,128)(2,1)S(1)} %copy-done.12, bf16[512,1024]{1,0:T(8,128)(2,1)S(1)} %pad_maximum_fusion.1.refs_1_, bf16[512,1024]{1,0:T(8,128)(2,1)} %collective-permute-done.14.refs_2_, ...), custom_call_target="tpu_custom_call" | custom-call | flops 1073741824 | bytes 5767168 | tf_op jit(solution)/shard_map/lend_far/pallas_call | solution.py:113
  111.8 0.7 collective-permute-start.20
  112.5 1.3 collective-permute-start.21
  113.8 0.1 fusion.58
  113.9 2.1 %lend_far.4.rest_4_.refs_6_ = bf16[128,1024]{1,0:T(8,128)(2,1)S(1)} custom-call(s32[1]{0:T(128)} %bitcast.4.spot_ref, bf16[128,2048]{1,0:T(8,128)(2,1)S(1)} %collective-permute-done.11.refs_0_, bf16[512,1024]{1,0:T(8,128)(2,1)S(1)} %pad_maximum_fusion.1.refs_1_, bf16[512,1024]{1,0:T(8,128)(2,1)} %collective-permute-done.14.refs_2_, ...), custom_call_target="tpu_custom_call" | custom-call | flops 536870912 | bytes 4980736 | tf_op jit(solution)/shard_map/lend_far/pallas_call | solution.py:113
  116.1 1.6 %collective-permute-start.22 = (bf16[128,1024]{1,0:T(8,128)(2,1)S(1)}, bf16[128,1024]{1,0:T(8,128)(2,1)S(1)}, u32[]{:S(2)}, u32[]{:S(2)}) collective-permute-start(bf16[128,1024]{1,0:T(8,128)(2,1)S(1)} %lend_far.4.rest_4_.refs_6_), channel_id=1, source_target_pairs={{1,0},{2,3},{5,4},{6,7},{9,8},{10,11},{13,12},{14,15},{17,16},{18,... | collective-permute-start | bytes 786440 | tf_op jit(solution)/shard_map/ppermute | solution.py:166
  117.7 2.1 %mix.1 = bf16[512,256]{1,0:T(8,128)(2,1)S(1)} custom-call(s32[512,1]{1,0:T(8,128)S(1)} %fusion.45.ids_ref, bf16[512,256]{1,0:T(8,128)(2,1)S(1)} %broadcast_select_fusion.coded_ref, bf16[8,256,256]{2,1,0:T(8,128)(2,1)S(1)} %copy-done.4, bf16[8,256,256]{2,1,0:T(8,128)(2,1)S(1)} %copy-done.8, bf16[8,256,256]{2,1,0:T(8,128)(2,1)S(1)} %copy-done.6, ...), custom_call_target="tpu_custom_call" | custom-call | flops 402653184 | bytes 4718592 | tf_op jit(solution)/shard_map/mix/pallas_call | solution.py:46
  119.8 0.4 fusion.62
  120.3 2.1 %lend_far.5 = bf16[128,1024]{1,0:T(8,128)(2,1)S(1)} custom-call(s32[1]{0:T(128)} %bitcast.4.spot_ref, bf16[128,2048]{1,0:T(8,128)(2,1)S(1)} %collective-permute-done.20.refs_0_, bf16[512,1024]{1,0:T(8,128)(2,1)S(1)} %pad_maximum_fusion.1.refs_1_, bf16[512,1024]{1,0:T(8,128)(2,1)} %collective-permute-done.14.refs_2_, ...), custom_call_target="tpu_custom_call" | custom-call | flops 536870912 | bytes 4980736 | tf_op jit(solution)/shard_map/lend_far/pallas_call | solution.py:113
  122.5 1.6 %collective-permute-start.23 = (bf16[128,1024]{1,0:T(8,128)(2,1)S(1)}, bf16[128,1024]{1,0:T(8,128)(2,1)S(1)}, u32[]{:S(2)}, u32[]{:S(2)}) collective-permute-start(bf16[128,1024]{1,0:T(8,128)(2,1)S(1)} %lend_far.5), channel_id=1, source_target_pairs={{1,0},{2,3},{5,4},{6,7},{9,8},{10,11},{13,12},{14,15},{17,16},{18,... | collective-permute-start | bytes 786440 | tf_op jit(solution)/shard_map/ppermute | solution.py:166
  124.1 5.2 %add_add_fusion = f32[512,1024]{1,0:T(8,128)S(1)} fusion(f32[512,1024]{1,0:T(8,128)S(1)} %copy-done.15, f32[512,1024]{1,0:T(8,128)S(1)} %fusion.62, bf16[512,2048]{1,0:T(8,128)(2,1)S(1)} %pad_maximum_fusion, bf16[8192,1024]{1,0:T(8,128)(2,1)} %x_ref.1, s32[]{:T(128)S(6)} %select_n.60), kind=kOutput, calls=%fused_computation.14 | convolution fusion | flops 2148532224 | bytes 12582916 | tf_op jit(solution)/shard_map/dot_general | solution.py:14
  129.3 1.3 fusion.21
  130.6 4.3 %collective-permute-done.22 = bf16[128,1024]{1,0:T(8,128)(2,1)S(1)} collective-permute-done((bf16[128,1024]{1,0:T(8,128)(2,1)S(1)}, bf16[128,1024]{1,0:T(8,128)(2,1)S(1)}, u32[]{:S(2)}, u32[]{:S(2)}) %collective-permute-start.22) | collective-permute-done | bytes 262176 | tf_op jit(solution)/shard_map/ppermute | solution.py:166
  134.9 0.7 fusion.39
  135.6 3.0 %collective-permute-done.23 = bf16[128,1024]{1,0:T(8,128)(2,1)S(1)} collective-permute-done((bf16[128,1024]{1,0:T(8,128)(2,1)S(1)}, bf16[128,1024]{1,0:T(8,128)(2,1)S(1)}, u32[]{:S(2)}, u32[]{:S(2)}) %collective-permute-start.23) | collective-permute-done | bytes 262176 | tf_op jit(solution)/shard_map/ppermute | solution.py:166
  138.6 0.7 fusion.36
  139.3 1.0 pad_maximum_fusion.3
  (77 shorter events, 0.3 us)
Async XLA Ops:
  0.0 26.4 %copy-start = (bf16[2048,256]{1,0:T(8,128)(2,1)S(1)}, bf16[2048,256]{1,0:T(8,128)(2,1)}, u32[]{:S(2)}) copy-start(bf16[2048,256]{1,0:T(8,128)(2,1)} %param.9) | copy-start | bytes 3145732
  0.0 26.3 %collective-permute-start.2 = (bf16[8,256,256]{2,1,0:T(8,128)(2,1)}, bf16[8,256,256]{2,1,0:T(8,128)(2,1)S(1)}, u32[]{:S(2)}, u32[]{:S(2)}) collective-permute-start(bf16[8,256,256]{2,1,0:T(8,128)(2,1)} %rest_0_.1), channel_id=1, source_target_pairs={{0,8},{4,12},{8,0},{12,4},{1,9},{5,13},{9,1},{13,5},{2,10},{6,14},... | collective-permute-start | bytes 3145736 | tf_op jit(solution)/shard_map/ppermute | solution.py:170
  2.9 23.4 %collective-permute-start.3 = (bf16[8,256,256]{2,1,0:T(8,128)(2,1)}, bf16[8,256,256]{2,1,0:T(8,128)(2,1)S(1)}, u32[]{:S(2)}, u32[]{:S(2)}) collective-permute-start(bf16[8,256,256]{2,1,0:T(8,128)(2,1)} %rest_0_.1), channel_id=1, source_target_pairs={{0,4},{4,0},{8,12},{12,8},{1,5},{5,1},{9,13},{13,9},{2,6},{6,2},{1... | collective-permute-start | bytes 3145736 | tf_op jit(solution)/shard_map/ppermute | solution.py:170
  6.3 27.2 %collective-permute-start.1 = (bf16[512,1024]{1,0:T(8,128)(2,1)}, bf16[512,1024]{1,0:T(8,128)(2,1)}, u32[]{:S(2)}, u32[]{:S(2)}) collective-permute-start(bf16[512,1024]{1,0:T(8,128)(2,1)} %pick.1), channel_id=1, source_target_pairs={{0,1},{3,2},{4,5},{7,6},{8,9},{11,10},{12,13},{15,14},{16,17},{19,... | collective-permute-start | bytes 3145736 | tf_op jit(solution)/shard_map/ppermute | solution.py:166
  10.8 45.7 %collective-permute-start.8 = (bf16[512,2048]{1,0:T(8,128)(2,1)}, bf16[512,2048]{1,0:T(8,128)(2,1)}, u32[]{:S(2)}, u32[]{:S(2)}) collective-permute-start(bf16[512,2048]{1,0:T(8,128)(2,1)} %param.6), channel_id=1, source_target_pairs={{1,2},{2,1},{5,6},{6,5},{9,10},{10,9},{13,14},{14,13},{17,18},{18,... | collective-permute-start | bytes 6291464 | tf_op jit(solution)/shard_map/ppermute | solution.py:166
  15.2 40.5 %collective-permute-start = (bf16[256,2048]{1,0:T(8,128)(2,1)}, bf16[256,2048]{1,0:T(8,128)(2,1)}, u32[]{:S(2)}, u32[]{:S(2)}) collective-permute-start(bf16[256,2048]{1,0:T(8,128)(2,1)} %slice.48), channel_id=1, source_target_pairs={{0,1},{3,2},{1,0},{2,3},{4,5},{7,6},{5,4},{6,7},{8,9},{11,10},{9,8... | collective-permute-start | bytes 3145736 | tf_op jit(solution)/shard_map/ppermute | solution.py:166
  15.2 11.2 %copy-start.13 = (bf16[512,2048]{1,0:T(8,128)(2,1)S(1)}, bf16[512,2048]{1,0:T(8,128)(2,1)}, u32[]{:S(2)}) copy-start(bf16[512,2048]{1,0:T(8,128)(2,1)} %param.6) | copy-start | bytes 6291460
  26.3 2.5 %copy-start.5 = (bf16[8,256,256]{2,1,0:T(8,128)(2,1)}, bf16[8,256,256]{2,1,0:T(8,128)(2,1)S(1)}, u32[]{:S(2)}) copy-start(bf16[8,256,256]{2,1,0:T(8,128)(2,1)S(1)} %collective-permute-done.2.rest_2_) | copy-start | bytes 3145732
  26.3 2.5 %copy-start.7 = (bf16[8,256,256]{2,1,0:T(8,128)(2,1)}, bf16[8,256,256]{2,1,0:T(8,128)(2,1)S(1)}, u32[]{:S(2)}) copy-start(bf16[8,256,256]{2,1,0:T(8,128)(2,1)S(1)} %collective-permute-done.3.rest_1_) | copy-start | bytes 3145732
  26.3 8.5 %collective-permute-start.4 = (bf16[8,256,256]{2,1,0:T(8,128)(2,1)S(1)}, bf16[8,256,256]{2,1,0:T(8,128)(2,1)S(1)}, u32[]{:S(2)}, u32[]{:S(2)}) collective-permute-start(bf16[8,256,256]{2,1,0:T(8,128)(2,1)S(1)} %collective-permute-done.2.rest_2_), channel_id=1, source_target_pairs={{0,4},{4,0},{8,12},{12,8},{1,5},{5,1},{9,13},{13,9},{2,6},{6,2},{1... | collective-permute-start | bytes 3145736 | tf_op jit(solution)/shard_map/ppermute | solution.py:170
  34.9 1.0 copy-start.9
  35.9 19.8 %collective-permute-start.6 = (bf16[256,1024]{1,0:T(8,128)(2,1)S(1)}, bf16[256,1024]{1,0:T(8,128)(2,1)S(1)}, u32[]{:S(2)}, u32[]{:S(2)}) collective-permute-start(bf16[256,1024]{1,0:T(8,128)(2,1)S(1)} %get-tuple-element.39), channel_id=1, source_target_pairs={{0,8},{4,12},{8,0},{12,4},{1,9},{5,13},{9,1},{13,5},{2,10},{6,14},... | collective-permute-start | bytes 1572872 | tf_op jit(solution)/shard_map/ppermute | solution.py:170
  36.4 19.3 %collective-permute-start.5 = (bf16[256,1024]{1,0:T(8,128)(2,1)S(1)}, bf16[256,1024]{1,0:T(8,128)(2,1)S(1)}, u32[]{:S(2)}, u32[]{:S(2)}) collective-permute-start(bf16[256,1024]{1,0:T(8,128)(2,1)S(1)} %get-tuple-element.37), channel_id=1, source_target_pairs={{0,16},{16,0},{1,17},{17,1},{2,18},{18,2},{3,19},{19,3},{4,20},{20... | collective-permute-start | bytes 1572872 | tf_op jit(solution)/shard_map/ppermute | solution.py:174
  37.9 17.7 %copy-start.21 = (bf16[128,3072]{1,0:T(8,128)(2,1)}, bf16[128,3072]{1,0:T(8,128)(2,1)S(1)}, u32[]{:S(2)}) copy-start(bf16[128,3072]{1,0:T(8,128)(2,1)S(1)} %slice_dynamic-update-slice_fusion.1) | copy-start | bytes 2359300
  55.8 7.4 %collective-permute-start.13 = (bf16[512,1024]{1,0:T(8,128)(2,1)S(1)}, bf16[512,1024]{1,0:T(8,128)(2,1)S(1)}, u32[]{:S(2)}, u32[]{:S(2)}) collective-permute-start(bf16[512,1024]{1,0:T(8,128)(2,1)S(1)} %pad_maximum_fusion.1.refs_1_), channel_id=1, source_target_pairs={{0,4},{4,0},{8,12},{12,8},{1,5},{5,1},{9,13},{13,9},{2,6},{6,2},{1... | collective-permute-start | bytes 3145736 | tf_op jit(solution)/shard_map/ppermute | solution.py:170
  55.9 14.4 %copy-start.2 = (bf16[512,1024]{1,0:T(8,128)(2,1)}, bf16[512,1024]{1,0:T(8,128)(2,1)S(1)}, u32[]{:S(2)}) copy-start(bf16[512,1024]{1,0:T(8,128)(2,1)S(1)} %pad_maximum_fusion.2.refs_1_) | copy-start | bytes 3145732
  55.9 7.2 %collective-permute-start.12 = (bf16[512,1024]{1,0:T(8,128)(2,1)S(1)}, bf16[512,1024]{1,0:T(8,128)(2,1)}, u32[]{:S(2)}, u32[]{:S(2)}) collective-permute-start(bf16[512,1024]{1,0:T(8,128)(2,1)S(1)} %pad_maximum_fusion.2.refs_1_), channel_id=1, source_target_pairs={{0,4},{4,0},{8,12},{12,8},{1,5},{5,1},{9,13},{13,9},{2,6},{6,2},{1... | collective-permute-start | bytes 3145736 | tf_op jit(solution)/shard_map/ppermute | solution.py:170
  56.5 13.9 %copy-start.16 = (f32[512,1024]{1,0:T(8,128)S(1)}, f32[512,1024]{1,0:T(8,128)}, u32[]{:S(2)}) copy-start(f32[512,1024]{1,0:T(8,128)} %fusion.12) | copy-start | bytes 6291460
  56.5 28.8 %collective-permute-start.16 = (bf16[256,2048]{1,0:T(8,128)(2,1)}, bf16[256,2048]{1,0:T(8,128)(2,1)S(1)}, u32[]{:S(2)}, u32[]{:S(2)}) collective-permute-start(bf16[256,2048]{1,0:T(8,128)(2,1)} %collective-permute-done), channel_id=1, source_target_pairs={{1,2},{2,1},{5,6},{6,5},{9,10},{10,9},{13,14},{14,13},{17,18},{18,... | collective-permute-start | bytes 3145736 | tf_op jit(solution)/shard_map/ppermute | solution.py:166
  57.3 23.1 %collective-permute-start.7 = (bf16[128,3072]{1,0:T(8,128)(2,1)}, bf16[128,3072]{1,0:T(8,128)(2,1)S(1)}, u32[]{:S(2)}, u32[]{:S(2)}) collective-permute-start(bf16[128,3072]{1,0:T(8,128)(2,1)} %copy-done.21), channel_id=1, source_target_pairs={{0,1},{3,2},{1,0},{2,3},{4,5},{7,6},{5,4},{6,7},{8,9},{11,10},{9,8... | collective-permute-start | bytes 2359304 | tf_op jit(solution)/shard_map/ppermute | solution.py:166
  63.1 24.3 %collective-permute-start.15 = (bf16[512,1024]{1,0:T(8,128)(2,1)S(1)}, bf16[512,1024]{1,0:T(8,128)(2,1)}, u32[]{:S(2)}, u32[]{:S(2)}) collective-permute-start(bf16[512,1024]{1,0:T(8,128)(2,1)S(1)} %pad_maximum_fusion.2.refs_1_), channel_id=1, source_target_pairs={{0,8},{4,12},{8,0},{12,4},{1,9},{5,13},{9,1},{13,5},{2,10},{6,14},... | collective-permute-start | bytes 3145736 | tf_op jit(solution)/shard_map/ppermute | solution.py:170
  63.7 24.1 %collective-permute-start.14 = (bf16[512,1024]{1,0:T(8,128)(2,1)S(1)}, bf16[512,1024]{1,0:T(8,128)(2,1)}, u32[]{:S(2)}, u32[]{:S(2)}) collective-permute-start(bf16[512,1024]{1,0:T(8,128)(2,1)S(1)} %pad_maximum_fusion.1.refs_1_), channel_id=1, source_target_pairs={{0,16},{16,0},{1,17},{17,1},{2,18},{18,2},{3,19},{19,3},{4,20},{20... | collective-permute-start | bytes 3145736 | tf_op jit(solution)/shard_map/ppermute | solution.py:174
  70.4 12.8 %copy-start.14 = (f32[512,256]{1,0:T(8,128)S(1)}, f32[512,256]{1,0:T(8,128)}, u32[]{:S(2)}) copy-start(f32[512,256]{1,0:T(8,128)} %get-tuple-element.78) | copy-start | bytes 1572868
  72.1 16.1 %copy-start.22 = (s32[512,1]{0,1:T(1,128)S(1)}, s32[512,1]{0,1:T(1,128)}, u32[]{:S(2)}) copy-start(s32[512,1]{0,1:T(1,128)} %param.7) | copy-start | bytes 6148
  81.3 13.1 %collective-permute-start.19 = (bf16[128,2048]{1,0:T(8,128)(2,1)}, bf16[128,2048]{1,0:T(8,128)(2,1)}, u32[]{:S(2)}, u32[]{:S(2)}) collective-permute-start(bf16[128,2048]{1,0:T(8,128)(2,1)} %get-tuple-element.61), channel_id=1, source_target_pairs={{0,1},{3,2},{1,0},{2,3},{4,5},{7,6},{5,4},{6,7},{8,9},{11,10},{9,8... | collective-permute-start | bytes 1572872 | tf_op jit(solution)/shard_map/ppermute | solution.py:166
  83.1 5.2 %copy-start.18 = (bf16[128,256]{1,0:T(8,128)(2,1)}, bf16[128,256]{1,0:T(8,128)(2,1)S(1)}, u32[]{:S(2)}) copy-start(bf16[128,256]{1,0:T(8,128)(2,1)S(1)} %get-tuple-element.75) | copy-start | bytes 196612
  83.1 5.2 %copy-start.19 = (bf16[128,256]{1,0:T(8,128)(2,1)}, bf16[128,256]{1,0:T(8,128)(2,1)S(1)}, u32[]{:S(2)}) copy-start(bf16[128,256]{1,0:T(8,128)(2,1)S(1)} %get-tuple-element.76) | copy-start | bytes 196612
  83.9 7.2 %collective-permute-start.9 = (bf16[512,256]{1,0:T(8,128)(2,1)}, bf16[512,256]{1,0:T(8,128)(2,1)}, u32[]{:S(2)}, u32[]{:S(2)}) collective-permute-start(bf16[512,256]{1,0:T(8,128)(2,1)} %fusion.42), channel_id=1, source_target_pairs={{1,2},{2,1},{5,6},{6,5},{9,10},{10,9},{13,14},{14,13},{17,18},{18,... | collective-permute-start | bytes 786440 | tf_op jit(solution)/shard_map/ppermute | solution.py:166
  85.3 1.0 copy-start.11
  87.7 15.5 %collective-permute-start.17 = (bf16[512,1024]{1,0:T(8,128)(2,1)}, bf16[512,1024]{1,0:T(8,128)(2,1)S(1)}, u32[]{:S(2)}, u32[]{:S(2)}) collective-permute-start(bf16[512,1024]{1,0:T(8,128)(2,1)} %collective-permute-done.14.refs_2_), channel_id=1, source_target_pairs={{0,4},{4,0},{8,12},{12,8},{1,5},{5,1},{9,13},{13,9},{2,6},{6,2},{1... | collective-permute-start | bytes 3145736 | tf_op jit(solution)/shard_map/ppermute | solution.py:170
  87.7 15.5 %collective-permute-start.18 = (bf16[512,1024]{1,0:T(8,128)(2,1)}, bf16[512,1024]{1,0:T(8,128)(2,1)}, u32[]{:S(2)}, u32[]{:S(2)}) collective-permute-start(bf16[512,1024]{1,0:T(8,128)(2,1)} %collective-permute-done.15.refs_2_), channel_id=1, source_target_pairs={{0,4},{4,0},{8,12},{12,8},{1,5},{5,1},{9,13},{13,9},{2,6},{6,2},{1... | collective-permute-start | bytes 3145736 | tf_op jit(solution)/shard_map/ppermute | solution.py:170
  89.2 5.2 %copy-start.17 = (bf16[128,2048]{1,0:T(8,128)(2,1)S(1)}, bf16[128,2048]{1,0:T(8,128)(2,1)}, u32[]{:S(2)}) copy-start(bf16[128,2048]{1,0:T(8,128)(2,1)} %slice.61) | copy-start | bytes 1572868
  90.4 23.5 %collective-permute-start.11 = (bf16[128,2048]{1,0:T(8,128)(2,1)}, bf16[128,2048]{1,0:T(8,128)(2,1)S(1)}, u32[]{:S(2)}, u32[]{:S(2)}) collective-permute-start(bf16[128,2048]{1,0:T(8,128)(2,1)} %slice.61), channel_id=1, source_target_pairs={{1,2},{2,1},{5,6},{6,5},{9,10},{10,9},{13,14},{14,13},{17,18},{18,... | collective-permute-start | bytes 1572872 | tf_op jit(solution)/shard_map/ppermute | solution.py:166
  92.3 10.9 %copy-start.3 = (bf16[512,1024]{1,0:T(8,128)(2,1)S(1)}, bf16[512,1024]{1,0:T(8,128)(2,1)}, u32[]{:S(2)}) copy-start(bf16[512,1024]{1,0:T(8,128)(2,1)} %copy-done.2) | copy-start | bytes 3145732
  92.3 10.8 %collective-permute-start.10 = (bf16[512,256]{1,0:T(8,128)(2,1)S(1)}, bf16[512,256]{1,0:T(8,128)(2,1)S(1)}, u32[]{:S(2)}, u32[]{:S(2)}) collective-permute-start(bf16[512,256]{1,0:T(8,128)(2,1)S(1)} %add_convert_fusion), channel_id=1, source_target_pairs={{1,0},{2,3},{5,4},{6,7},{9,8},{10,11},{13,12},{14,15},{17,16},{18,... | collective-permute-start | bytes 786440 | tf_op jit(solution)/shard_map/ppermute | solution.py:166
  108.1 1.2 copy-start.12
  111.8 8.5 %collective-permute-start.20 = (bf16[128,2048]{1,0:T(8,128)(2,1)}, bf16[128,2048]{1,0:T(8,128)(2,1)S(1)}, u32[]{:S(2)}, u32[]{:S(2)}) collective-permute-start(bf16[128,2048]{1,0:T(8,128)(2,1)} %collective-permute-done.19), channel_id=1, source_target_pairs={{1,2},{2,1},{5,6},{6,5},{9,10},{10,9},{13,14},{14,13},{17,18},{18,... | collective-permute-start | bytes 1572872 | tf_op jit(solution)/shard_map/ppermute | solution.py:166
  112.5 16.8 %collective-permute-start.21 = (bf16[256,1024]{1,0:T(8,128)(2,1)S(1)}, bf16[256,1024]{1,0:T(8,128)(2,1)S(1)}, u32[]{:S(2)}, u32[]{:S(2)}) collective-permute-start(bf16[256,1024]{1,0:T(8,128)(2,1)S(1)} %lend_far.3.refs_6_), channel_id=1, source_target_pairs={{1,0},{2,3},{5,4},{6,7},{9,8},{10,11},{13,12},{14,15},{17,16},{18,... | collective-permute-start | bytes 1572872 | tf_op jit(solution)/shard_map/ppermute | solution.py:166
  113.9 3.8 %copy-start.4 = (bf16[8,256,256]{2,1,0:T(8,128)(2,1)S(1)}, bf16[8,256,256]{2,1,0:T(8,128)(2,1)}, u32[]{:S(2)}) copy-start(bf16[8,256,256]{2,1,0:T(8,128)(2,1)} %rest_0_.1) | copy-start | bytes 3145732
  113.9 3.8 %copy-start.6 = (bf16[8,256,256]{2,1,0:T(8,128)(2,1)S(1)}, bf16[8,256,256]{2,1,0:T(8,128)(2,1)}, u32[]{:S(2)}) copy-start(bf16[8,256,256]{2,1,0:T(8,128)(2,1)} %copy-done.5) | copy-start | bytes 3145732
  113.9 3.8 %copy-start.8 = (bf16[8,256,256]{2,1,0:T(8,128)(2,1)S(1)}, bf16[8,256,256]{2,1,0:T(8,128)(2,1)}, u32[]{:S(2)}) copy-start(bf16[8,256,256]{2,1,0:T(8,128)(2,1)} %copy-done.7) | copy-start | bytes 3145732
  113.9 3.8 %copy-start.10 = (bf16[8,256,256]{2,1,0:T(8,128)(2,1)S(1)}, bf16[8,256,256]{2,1,0:T(8,128)(2,1)}, u32[]{:S(2)}) copy-start(bf16[8,256,256]{2,1,0:T(8,128)(2,1)} %copy-done.9) | copy-start | bytes 3145732
  116.1 3.7 %copy-start.20 = (bf16[256,1024]{1,0:T(8,128)(2,1)S(1)}, bf16[256,1024]{1,0:T(8,128)(2,1)}, u32[]{:S(2)}) copy-start(bf16[256,1024]{1,0:T(8,128)(2,1)} %param.11) | copy-start | bytes 1572868
  116.1 18.8 %collective-permute-start.22 = (bf16[128,1024]{1,0:T(8,128)(2,1)S(1)}, bf16[128,1024]{1,0:T(8,128)(2,1)S(1)}, u32[]{:S(2)}, u32[]{:S(2)}) collective-permute-start(bf16[128,1024]{1,0:T(8,128)(2,1)S(1)} %lend_far.4.rest_4_.refs_6_), channel_id=1, source_target_pairs={{1,0},{2,3},{5,4},{6,7},{9,8},{10,11},{13,12},{14,15},{17,16},{18,... | collective-permute-start | bytes 786440 | tf_op jit(solution)/shard_map/ppermute | solution.py:166
  119.8 4.2 %copy-start.15 = (f32[512,1024]{1,0:T(8,128)S(1)}, f32[512,1024]{1,0:T(8,128)}, u32[]{:S(2)}) copy-start(f32[512,1024]{1,0:T(8,128)} %bitcast_add_fusion) | copy-start | bytes 6291460
  120.3 9.0 %slice-start = ((s8[16777216]{0:T(1024)(128)(4,1)}), s8[4194304]{0:T(1024)(128)(4,1)S(1)}, s32[]{:S(2)}) async-start(s8[16777216]{0:T(1024)(128)(4,1)} %bitcast.17), calls=%async_computation | async-start | bytes 8388608
  122.4 6.8 %slice-start.1 = ((s8[16777216]{0:T(1024)(128)(4,1)}), s8[4194304]{0:T(1024)(128)(4,1)S(1)}, s32[]{:S(2)}) async-start(s8[16777216]{0:T(1024)(128)(4,1)} %bitcast.17), calls=%async_computation.1 | async-start | bytes 8388608
  122.5 6.8 %slice-start.2 = ((s8[16777216]{0:T(1024)(128)(4,1)}), s8[4194304]{0:T(1024)(128)(4,1)S(1)}, s32[]{:S(2)}) async-start(s8[16777216]{0:T(1024)(128)(4,1)} %bitcast.17), calls=%async_computation.2 | async-start | bytes 8388608
  122.5 6.8 %slice-start.3 = ((s8[16777216]{0:T(1024)(128)(4,1)}), s8[4194304]{0:T(1024)(128)(4,1)S(1)}, s32[]{:S(2)}) async-start(s8[16777216]{0:T(1024)(128)(4,1)} %bitcast.17), calls=%async_computation.3 | async-start | bytes 8388608
  122.5 16.1 %collective-permute-start.23 = (bf16[128,1024]{1,0:T(8,128)(2,1)S(1)}, bf16[128,1024]{1,0:T(8,128)(2,1)S(1)}, u32[]{:S(2)}, u32[]{:S(2)}) collective-permute-start(bf16[128,1024]{1,0:T(8,128)(2,1)S(1)} %lend_far.5), channel_id=1, source_target_pairs={{1,0},{2,3},{5,4},{6,7},{9,8},{10,11},{13,12},{14,15},{17,16},{18,... | collective-permute-start | bytes 786440 | tf_op jit(solution)/shard_map/ppermute | solution.py:166
  138.6 1.8 %copy-start.1 = (bf16[2048,256]{1,0:T(8,128)(2,1)S(1)}, bf16[2048,256]{1,0:T(8,128)(2,1)}, u32[]{:S(2)}) copy-start(bf16[2048,256]{1,0:T(8,128)(2,1)} %param.9) | copy-start | bytes 3145732

commit v8 on v7

--- a/solution.py
+++ b/solution.py
@@ -14,12 +14,12 @@
     return jnp.dot(a, b, preferred_element_type=jnp.float32)
 
 
-def mix_kernel(ids_ref, coded_ref, *rest):
+def mix_kernel(rep_ref, ids_ref, coded_ref, *rest):
     cores, (mixed_ref, slots_ref) = rest[:4], rest[-2:]
     rows = coded_ref.shape[0]
     each = cores[0].shape[0]
     adapters = each * len(cores)
-    ids = ids_ref[...]
+    ids = ids_ref[...] ^ (rep_ref[0] * each)
     named = ids == lax.broadcasted_iota(jnp.int32, (rows, adapters), 1)
     below = lax.broadcasted_iota(jnp.int32, (rows, rows), 0) > lax.broadcasted_iota(
         jnp.int32, (rows, rows), 1
@@ -40,13 +40,14 @@
     mixed_ref[...] = dot(place, slots_ref[...]).astype(jnp.bfloat16)
 
 
-def mix(ids, coded, cores, waits):
+def mix(rep, ids, coded, cores, waits):
     rows, width = coded.shape
     adapters = sum(c.shape[0] for c in cores)
     return pl.pallas_call(
         mix_kernel,
         out_shape=jax.ShapeDtypeStruct((rows, width), jnp.bfloat16),
-        in_specs=[pl.BlockSpec(memory_space=pltpu.VMEM)] * (2 + len(cores))
+        in_specs=[pl.BlockSpec(memory_space=pltpu.SMEM)]
+        + [pl.BlockSpec(memory_space=pltpu.VMEM)] * (2 + len(cores))
         + [pl.BlockSpec(memory_space=pl.ANY)] * len(waits),
         scratch_shapes=[pltpu.VMEM((adapters * BLK, width), jnp.bfloat16)],
         compiler_params=pltpu.CompilerParams(vmem_limit_bytes=10 * 2**20),
@@ -56,7 +57,7 @@
             transcendentals=0,
         ),
         name="mix",
-    )(ids, coded, *cores, *waits)
+    )(rep.reshape(1), ids, coded, *cores, *waits)
 
 
 def pick_kernel(which_ref, x_ref, out_ref):
@@ -146,19 +147,21 @@
     "near1": ("corner",),
     "far1": ("corner",),
     "near2": ("near3", "far3"),
-    "far2": ("near3", "far3"),
-    "turn1": ("turn0", "near1", "far1"),
+    "far2": ("far3",),
+    "turn1": ("far1",),
     "turn2": ("turn1",),
-    "cross0": ("swap",),
-    "near4": ("cross0",),
-    "far4": ("cross0",),
-    "lend1": ("lend0",),
+    "cross0": ("far1", "near1"),
+    "near4": ("cross0", "turn1"),
+    "far4": ("cross0", "turn1"),
+    "lend1": ("lend0", "back0"),
     "lend2": ("lend1",),
-    "mix": ("lend1",),
+    "mix": ("lend0",),
     "lent": ("far4",),
-    "half": ("swap dot",),
+    "half": ("lent", "cross0"),
     "turned": ("lend2",),
     "cross2": ("lend0",),
+    "swap dot": ("turn0",),
+    "cross1": ("cross0",),
 }
 
 
@@ -221,8 +224,6 @@
     move("mate", adapter_cores, swap_rep, 1)
     done["own"] = dot(after("own", activations), weight_of(me))
     move("corner", done["across"], swap_rep, 1)
-    each = adapter_cores.shape[0]
-    ids = (row_adapter // each ^ rep) * each + row_adapter % each
 
     def turn(i):
         x = activations[slice(*turns[i])]
@@ -259,10 +260,6 @@
     near_masks, far_masks = ((0, 4), (2, 6), (1, 5), (3, 7)), ((0, 2), (4, 6), (1, 3), (5, 7))
 
     cross(1)
-    side = done["part"].astype(jnp.float32) + partial_value
-    move("half", side.astype(jnp.bfloat16), send, SWAP)
-    coded = (side + done["half"].astype(jnp.float32)).astype(jnp.bfloat16)
-    move("coded", coded, send, OUT)
     move("near4", done["near2"], swap_rep, 1)
     move("far4", done["far2"], swap_rep, 1)
 
@@ -277,17 +274,23 @@
         first += count
         if i == len(LENDS) - 1:
             cores = (adapter_cores, done["mate"], done["across"], done["corner"])
-            mixed = mix(ids, jnp.where(inner, coded, done["coded"]), cores, held("mix"))
+            mixed = mix(rep, row_adapter, jnp.where(inner, coded, done["coded"]), cores, held("mix"))
             done["base"] = done["swap dot"] + dot(mixed, basis_up)
         xs, add = [done[f"cross{j}"] for j in chunks], done["lent"]
         add = add[crossings[chunks[0]][0] : crossings[chunks[-1]][1]]
         done[f"lend{i}"] = lend(spot, xs, weights, far_masks, "lend_far", add, held(f"lend{i}"))
         for j in range(2, len(crossings)) if i == 0 else ():
             cross(j)
+        if i == 0:
+            side = done["part"].astype(jnp.float32) + partial_value
+            move("half", side.astype(jnp.bfloat16), send, SWAP)
+            coded = (side + done["half"].astype(jnp.float32)).astype(jnp.bfloat16)
+            move("coded", coded, send, OUT)
         if i == len(LENDS) - 1:
-            x = jnp.concatenate([done[f"turn{j}"] for j in range(len(turns))], axis=0)
+            x = after("turned", [done[f"turn{j}"] for j in range(len(turns))])
+            x = jnp.concatenate(x, axis=0)
             owner = jnp.where(inner, near_out, near_in)
-            last = done["base"] + dot(after("turned", x), weight_of(owner))
+            last = done["base"] + dot(x, weight_of(owner))
         move(f"back{i}", done[f"lend{i}"], send, OUT)
 
     last_weight = weight_of(far_out)

time: 141 us -> 141 us (level)
  other arithmetic: 8.41 us -> 3.06 us
  local copies, waits for them, and re-layouts: 9.81 us -> 12.8 us
  starting transfers between devices: 31.7 us -> 34 us
    ppermute x9, waiting for transfers between devices: 5.64 us -> 15.6 us  [swap_rep(): return lax.ppermute(x, 'rep', [(i, i ^ bit) for i in range(4)])]
    ppermute x13, waiting for transfers between devices: 45.9 us -> 36.7 us  [send(): return lax.ppermute(x, 'tp', pairs)]
    add x2 -> x0, other arithmetic: 2.92 us -> none  [the longest x1 1.75 us: on_line(): done['own'] + dot(after('swap dot', done['swap']), weight_of(far_in))]
    ppermute x13, starting transfers between devices: 23.5 us -> 25.7 us  [send(): return lax.ppermute(x, 'tp', pairs)]
    unnamed x59 -> x58, local copies, waits for them, and re-layouts: 4.29 us -> 6.24 us
    concatenate x1 -> x0, other arithmetic: 1.63 us -> none  [on_line(): x = jnp.concatenate([done[f'turn{j}'] for j in range(len(turns))], axis=0)]
    slice x1 -> x2, local copies, waits for them, and re-layouts: 2.39 us -> 3.26 us  [turn(): x = activations[slice(*turns[i])]]
  transfers between devices with their start and end apart: 24 -> 24, of which waited for: 10 -> 8; matrix products, arithmetic and copies ran while one was open for 25% -> 20% of each run, Pallas kernels for 12% -> 11%
where the time goes in v8:
time: 141 us; the launch traced here: 139 us
  waiting for transfers between devices  52.6 us (37%)
  starting transfers between devices  34 us (24%)
  matrix products  20.4 us (14%)
  Pallas kernels  16 us (11%)
  local copies, waits for them, and re-layouts  12.8 us (9%)
  other arithmetic  3.06 us (2%)
    ppermute x13, waiting for transfers between devices, send(): return lax.ppermute(x, 'tp', pairs)  36.7 us
    ppermute x13, starting transfers between devices, send(): return lax.ppermute(x, 'tp', pairs)  25.7 us
    dot_general x8, matrix products, dot(): return jnp.dot(a, b, preferred_element_type=jnp.float32)  20.4 us
    ppermute x9, waiting for transfers between devices, swap_rep(): return lax.ppermute(x, 'rep', [(i, i ^ bit) for i in range(4)])  15.6 us
    pallas_call x4, Pallas kernels, lend(): pl.pallas_call(functools.partial(lend_kernel, count=len(xs), blocks=tuple...  11.2 us
    unnamed x58, local copies, waits for them, and re-layouts  6.24 us
    ppermute x9, starting transfers between devices, swap_rep(): return lax.ppermute(x, 'rep', [(i, i ^ bit) for i in range(4)])  5.27 us
    slice x2, local copies, waits for them, and re-layouts, turn(): x = activations[slice(*turns[i])]  3.26 us
  transfers between devices with their start and end apart: 24, of which 8 were waited for; matrix products, arithmetic and copies ran while one was open for 20% of the time, Pallas kernels for 11%

profile of v8, /device:TPU:0, one launch (start us, length us, event | category | flops | bytes accessed | tf_op | source)
XLA Modules:
  0.0 139.4 jit_solution(4893662619092327549)
XLA Ops:
  0.0 2.9 %collective-permute-start = (bf16[8,256,256]{2,1,0:T(8,128)(2,1)}, bf16[8,256,256]{2,1,0:T(8,128)(2,1)S(1)}, u32[]{:S(2)}, u32[]{:S(2)}) collective-permute-start(bf16[8,256,256]{2,1,0:T(8,128)(2,1)} %rest_0_.1), channel_id=1, source_target_pairs={{0,8},{4,12},{8,0},{12,4},{1,9},{5,13},{9,1},{13,5},{2,10},{6,14},... | collective-permute-start | bytes 3145736 | tf_op jit(solution)/shard_map/ppermute | solution.py:173
  2.9 0.6 pad_add_fusion.which_ref
  3.6 2.7 %pick.1 = bf16[512,1024]{1,0:T(8,128)(2,1)} custom-call(s32[2]{0:T(128)} %pad_add_fusion.which_ref, bf16[8192,1024]{1,0:T(8,128)(2,1)} %x_ref.1), custom_call_target="tpu_custom_call" | custom-call | bytes 2097152 | tf_op jit(solution)/shard_map/pick/pallas_call | solution.py:69
  6.3 4.4 %collective-permute-start.4 = (bf16[512,1024]{1,0:T(8,128)(2,1)}, bf16[512,1024]{1,0:T(8,128)(2,1)}, u32[]{:S(2)}, u32[]{:S(2)}) collective-permute-start(bf16[512,1024]{1,0:T(8,128)(2,1)} %pick.1), channel_id=1, source_target_pairs={{0,1},{3,2},{4,5},{7,6},{8,9},{11,10},{12,13},{15,14},{16,17},{19,... | collective-permute-start | bytes 3145736 | tf_op jit(solution)/shard_map/ppermute | solution.py:169
  10.8 2.0 %collective-permute-start.2 = (bf16[512,2048]{1,0:T(8,128)(2,1)}, bf16[512,2048]{1,0:T(8,128)(2,1)}, u32[]{:S(2)}, u32[]{:S(2)}) collective-permute-start(bf16[512,2048]{1,0:T(8,128)(2,1)} %param.6), channel_id=1, source_target_pairs={{1,2},{2,1},{5,6},{6,5},{9,10},{10,9},{13,14},{14,13},{17,18},{18,... | collective-permute-start | bytes 6291464 | tf_op jit(solution)/shard_map/ppermute | solution.py:169
  12.8 2.4 %slice.47 = bf16[256,2048]{1,0:T(8,128)(2,1)} slice(bf16[512,2048]{1,0:T(8,128)(2,1)} %param.6), slice={[0:256], [0:2048]} | slice | bytes 2097152 | tf_op jit(solution)/shard_map/slice | solution.py:229
  15.2 6.7 %fusion.17 = f32[512,1024]{1,0:T(8,128)} fusion(bf16[512,2048]{1,0:T(8,128)(2,1)} %param.6, bf16[8192,1024]{1,0:T(8,128)(2,1)} %x_ref.1, s32[]{:T(128)S(6)} %select_n.37), kind=kOutput, calls=%fused_computation.18 | convolution fusion | flops 2147483648 | bytes 8388612 | tf_op jit(solution)/shard_map/dot_general | solution.py:14
  21.8 4.5 %collective-permute-done.rest_2_ = bf16[8,256,256]{2,1,0:T(8,128)(2,1)S(1)} collective-permute-done((bf16[8,256,256]{2,1,0:T(8,128)(2,1)}, bf16[8,256,256]{2,1,0:T(8,128)(2,1)S(1)}, u32[]{:S(2)}, u32[]{:S(2)}) %collective-permute-start) | collective-permute-done | bytes 1048608 | tf_op jit(solution)/shard_map/ppermute | solution.py:173
  26.4 1.5 %fusion.48 = (bf16[512,256]{1,0:T(8,128)(2,1)S(1)}, f32[512,256]{1,0:T(8,128)}) fusion(bf16[512,2048]{1,0:T(8,128)(2,1)S(1)} %copy-done.16, bf16[2048,256]{1,0:T(8,128)(2,1)S(1)} %copy-done), kind=kOutput, calls=%fused_computation.53 | convolution fusion | flops 537001984 | bytes 3932160 | tf_op jit(solution)/shard_map/dot_general | solution.py:14
  27.9 0.9 fusion.45
  28.8 4.8 %collective-permute-done.4 = bf16[512,1024]{1,0:T(8,128)(2,1)} collective-permute-done((bf16[512,1024]{1,0:T(8,128)(2,1)}, bf16[512,1024]{1,0:T(8,128)(2,1)}, u32[]{:S(2)}, u32[]{:S(2)}) %collective-permute-start.4) | collective-permute-done | bytes 1048608 | tf_op jit(solution)/shard_map/ppermute | solution.py:169
  33.6 1.3 fusion.46
  34.9 1.0 copy-done.12
  35.8 0.5 collective-permute-start.6
  36.4 1.5 %collective-permute-start.8 = (bf16[256,1024]{1,0:T(8,128)(2,1)S(1)}, bf16[256,1024]{1,0:T(8,128)(2,1)S(1)}, u32[]{:S(2)}, u32[]{:S(2)}) collective-permute-start(bf16[256,1024]{1,0:T(8,128)(2,1)S(1)} %get-tuple-element.47), channel_id=1, source_target_pairs={{0,16},{16,0},{1,17},{17,1},{2,18},{18,2},{3,19},{19,3},{4,20},{20... | collective-permute-start | bytes 1572872 | tf_op jit(solution)/shard_map/ppermute | solution.py:177
  37.9 11.1 %collective-permute-done.6 = bf16[256,1024]{1,0:T(8,128)(2,1)S(1)} collective-permute-done((bf16[256,1024]{1,0:T(8,128)(2,1)S(1)}, bf16[256,1024]{1,0:T(8,128)(2,1)S(1)}, u32[]{:S(2)}, u32[]{:S(2)}) %collective-permute-start.6) | collective-permute-done | bytes 524320 | tf_op jit(solution)/shard_map/ppermute | solution.py:173
  49.0 0.3 collective-permute-done.8
  49.2 0.1 pad_maximum_fusion.refs_1_
  49.3 0.1 collective-permute-start.9
  49.4 0.1 pad_maximum_fusion.1.refs_1_
  49.5 0.6 collective-permute-start.10
  50.1 5.6 %collective-permute-done.3 = bf16[256,2048]{1,0:T(8,128)(2,1)} collective-permute-done((bf16[256,2048]{1,0:T(8,128)(2,1)}, bf16[256,2048]{1,0:T(8,128)(2,1)}, u32[]{:S(2)}, u32[]{:S(2)}) %collective-permute-start.3) | collective-permute-done | bytes 1048608 | tf_op jit(solution)/shard_map/ppermute | solution.py:169
  55.7 0.7 collective-permute-start.12
  56.4 1.0 copy-done.5
  57.4 0.5 collective-permute-start.11
  57.9 1.5 %collective-permute-start.14 = (bf16[512,1024]{1,0:T(8,128)(2,1)S(1)}, bf16[512,1024]{1,0:T(8,128)(2,1)}, u32[]{:S(2)}, u32[]{:S(2)}) collective-permute-start(bf16[512,1024]{1,0:T(8,128)(2,1)S(1)} %pad_maximum_fusion.1.refs_1_), channel_id=1, source_target_pairs={{0,16},{16,0},{1,17},{17,1},{2,18},{18,2},{3,19},{19,3},{4,20},{20... | collective-permute-start | bytes 3145736 | tf_op jit(solution)/shard_map/ppermute | solution.py:177
  59.4 6.5 %collective-permute-start.7 = (bf16[128,3072]{1,0:T(8,128)(2,1)S(1)}, bf16[128,3072]{1,0:T(8,128)(2,1)S(1)}, u32[]{:S(2)}, u32[]{:S(2)}) collective-permute-start(bf16[128,3072]{1,0:T(8,128)(2,1)S(1)} %slice_dynamic-update-slice_fusion.1), channel_id=1, source_target_pairs={{0,1},{3,2},{1,0},{2,3},{4,5},{7,6},{5,4},{6,7},{8,9},{11,10},{9,8... | collective-permute-start | bytes 2359304 | tf_op jit(solution)/shard_map/ppermute | solution.py:169
  66.0 16.6 %collective-permute-done.7 = bf16[128,3072]{1,0:T(8,128)(2,1)S(1)} collective-permute-done((bf16[128,3072]{1,0:T(8,128)(2,1)S(1)}, bf16[128,3072]{1,0:T(8,128)(2,1)S(1)}, u32[]{:S(2)}, u32[]{:S(2)}) %collective-permute-start.7) | collective-permute-done | bytes 786464 | tf_op jit(solution)/shard_map/ppermute | solution.py:169
  82.6 0.9 slice.61
  83.4 1.0 copy-done.14
  84.4 0.6 collective-permute-start.15
  85.0 0.1 copy.10.ids_ref
  85.2 4.2 %collective-permute-start.18 = (bf16[128,2048]{1,0:T(8,128)(2,1)}, bf16[128,2048]{1,0:T(8,128)(2,1)S(1)}, u32[]{:S(2)}, u32[]{:S(2)}) collective-permute-start(bf16[128,2048]{1,0:T(8,128)(2,1)} %get-tuple-element.65), channel_id=1, source_target_pairs={{0,1},{3,2},{1,0},{2,3},{4,5},{7,6},{5,4},{6,7},{8,9},{11,10},{9,8... | collective-permute-start | bytes 1572872 | tf_op jit(solution)/shard_map/ppermute | solution.py:169
  89.3 1.0 fusion.47
  90.3 1.1 fusion.26
  91.4 0.7 collective-permute-start.20
  92.2 1.2 copy-done.6
  93.4 4.5 %lend_near.1 = f32[512,1024]{1,0:T(8,128)S(1)} custom-call(s32[1]{0:T(128)} %bitcast.4.spot_ref, bf16[512,2048]{1,0:T(8,128)(2,1)} %collective-permute-done.2.refs_0_, bf16[512,1024]{1,0:T(8,128)(2,1)S(1)} %copy-done.4, bf16[512,1024]{1,0:T(8,128)(2,1)} %collective-permute-done.11.refs_2_, bf16[512,1024]{1,0:T(8,128)(2,1)S(1)} %copy-done.6, ...), custom_call_target="tpu_custom_call" | custom-call | flops 2147483648 | bytes 7340032 | tf_op jit(solution)/shard_map/lend_near/pallas_call | solution.py:114
  97.9 0.1 slice.62.refs_5_
  98.0 0.8 collective-permute-start.16
  98.8 0.3 copy-done.2
  99.1 0.3 copy-done.15
  99.4 2.5 %lend_far.3.rest_4_.refs_6_ = bf16[256,1024]{1,0:T(8,128)(2,1)S(1)} custom-call(s32[1]{0:T(128)} %bitcast.4.spot_ref, bf16[256,2048]{1,0:T(8,128)(2,1)S(1)} %copy-done.15, bf16[512,1024]{1,0:T(8,128)(2,1)S(1)} %pad_maximum_fusion.1.refs_1_, bf16[512,1024]{1,0:T(8,128)(2,1)} %collective-permute-done.14.refs_2_, bf16[512,1024]{1,0:T(8,128)(2,1)S(1)} %copy-done.2, ...), custom_call_target="tpu_custom_call" | custom-call | flops 1073741824 | bytes 5767168 | tf_op jit(solution)/shard_map/lend_far/pallas_call | solution.py:114
  101.9 1.4 %collective-permute-start.21 = (bf16[256,1024]{1,0:T(8,128)(2,1)S(1)}, bf16[256,1024]{1,0:T(8,128)(2,1)S(1)}, u32[]{:S(2)}, u32[]{:S(2)}) collective-permute-start(bf16[256,1024]{1,0:T(8,128)(2,1)S(1)} %lend_far.3.rest_4_.refs_6_), channel_id=1, source_target_pairs={{1,0},{2,3},{5,4},{6,7},{9,8},{10,11},{13,12},{14,15},{17,16},{18,... | collective-permute-start | bytes 1572872 | tf_op jit(solution)/shard_map/ppermute | solution.py:169
  103.4 5.3 %fusion.2 = f32[512,1024]{1,0:T(8,128)S(1)} fusion(bf16[512,2048]{1,0:T(8,128)(2,1)} %collective-permute-done.2.refs_0_, bf16[8192,1024]{1,0:T(8,128)(2,1)} %x_ref.1, s32[]{:T(128)S(6)} %select_n.39), kind=kOutput, calls=%fused_computation.2 | convolution fusion | flops 2147483648 | bytes 8388612 | tf_op jit(solution)/shard_map/dot_general | solution.py:14
  108.7 0.7 collective-permute-start.19
  109.4 0.1 add_convert_fusion
  109.5 1.3 collective-permute-start.17
  110.8 0.1 fusion.44
  110.9 9.2 %collective-permute-done.21.refs_7_ = bf16[256,1024]{1,0:T(8,128)(2,1)S(1)} collective-permute-done((bf16[256,1024]{1,0:T(8,128)(2,1)S(1)}, bf16[256,1024]{1,0:T(8,128)(2,1)S(1)}, u32[]{:S(2)}, u32[]{:S(2)}) %collective-permute-start.21) | collective-permute-done | bytes 524320 | tf_op jit(solution)/shard_map/ppermute | solution.py:169
  120.1 2.1 %lend_far.4.refs_6_ = bf16[128,1024]{1,0:T(8,128)(2,1)S(1)} custom-call(s32[1]{0:T(128)} %bitcast.4.spot_ref, bf16[128,2048]{1,0:T(8,128)(2,1)S(1)} %collective-permute-done.20.refs_0_, bf16[512,1024]{1,0:T(8,128)(2,1)S(1)} %pad_maximum_fusion.1.refs_1_, bf16[512,1024]{1,0:T(8,128)(2,1)} %collective-permute-done.14.refs_2_, bf16[512,1024]{1,0:T(8,128)(2,1)S(1)} %copy-done.2, ...), custom_call_target="tpu_custom_call" | custom-call | flops 536870912 | bytes 4980736 | tf_op jit(solution)/shard_map/lend_far/pallas_call | solution.py:114
  122.2 1.3 collective-permute-start.22
  123.6 2.1 %lend_far.5 = bf16[128,1024]{1,0:T(8,128)(2,1)S(1)} custom-call(s32[1]{0:T(128)} %bitcast.4.spot_ref, bf16[128,2048]{1,0:T(8,128)(2,1)S(1)} %collective-permute-done.19.refs_0_, bf16[512,1024]{1,0:T(8,128)(2,1)S(1)} %pad_maximum_fusion.1.refs_1_, bf16[512,1024]{1,0:T(8,128)(2,1)} %collective-permute-done.14.refs_2_, bf16[512,1024]{1,0:T(8,128)(2,1)S(1)} %copy-done.2, ...), custom_call_target="tpu_custom_call" | custom-call | flops 536870912 | bytes 4980736 | tf_op jit(solution)/shard_map/lend_far/pallas_call | solution.py:114
  125.7 1.6 %collective-permute-start.23 = (bf16[128,1024]{1,0:T(8,128)(2,1)S(1)}, bf16[128,1024]{1,0:T(8,128)(2,1)S(1)}, u32[]{:S(2)}, u32[]{:S(2)}) collective-permute-start(bf16[128,1024]{1,0:T(8,128)(2,1)S(1)} %lend_far.5), channel_id=1, source_target_pairs={{1,0},{2,3},{5,4},{6,7},{9,8},{10,11},{13,12},{14,15},{17,16},{18,... | collective-permute-start | bytes 786440 | tf_op jit(solution)/shard_map/ppermute | solution.py:169
  127.5 2.1 %mix.1 = bf16[512,256]{1,0:T(8,128)(2,1)S(1)} custom-call(s32[1]{0:T(128)} %bitcast.1.rep_ref, s32[512,1]{1,0:T(8,128)S(1)} %copy.10.ids_ref, bf16[512,256]{1,0:T(8,128)(2,1)S(1)} %broadcast_select_fusion.coded_ref, bf16[8,256,256]{2,1,0:T(8,128)(2,1)S(1)} %copy-done.7, bf16[8,256,256]{2,1,0:T(8,128)(2,1)S(1)} %copy-done.11, ...), custom_call_target="tpu_custom_call" | custom-call | flops 402653184 | bytes 4718592 | tf_op jit(solution)/shard_map/mix/pallas_call | solution.py:46
  129.6 0.4 fusion.49
  130.1 0.5 copy-done.19
  130.6 0.7 copy-done.22
  131.3 3.6 %add_add_fusion = f32[512,1024]{1,0:T(8,128)S(1)} fusion(f32[512,1024]{1,0:T(8,128)S(1)} %fusion.49, f32[512,1024]{1,0:T(8,128)S(1)} %copy-done.22, f32[512,1024]{1,0:T(8,128)S(1)} %fusion.2, bf16[8192,1024]{1,0:T(8,128)(2,1)S(1)} %bitcast.16, s32[]{:T(128)S(6)} %select_n.46, bf16[128,2048]{1,0:T(8,128)(2,1)S(1)} %collective-permute-done.18, ...), kind=kOutput, calls=%fused_computation.17 | convolution fusion | flops 2155347968 | bytes 14680068 | tf_op jit(solution)/shard_map/dot_general | solution.py:14
  135.0 1.3 fusion.21
  136.3 0.6 collective-permute-done.23
  136.8 0.7 fusion.23
  137.6 0.8 fusion.25
  138.4 1.0 pad_maximum_fusion.2
  (72 shorter events, 0.3 us)
Async XLA Ops:
  0.0 26.4 %copy-start = (bf16[2048,256]{1,0:T(8,128)(2,1)S(1)}, bf16[2048,256]{1,0:T(8,128)(2,1)}, u32[]{:S(2)}) copy-start(bf16[2048,256]{1,0:T(8,128)(2,1)} %param.9) | copy-start | bytes 3145732
  0.0 26.3 %collective-permute-start = (bf16[8,256,256]{2,1,0:T(8,128)(2,1)}, bf16[8,256,256]{2,1,0:T(8,128)(2,1)S(1)}, u32[]{:S(2)}, u32[]{:S(2)}) collective-permute-start(bf16[8,256,256]{2,1,0:T(8,128)(2,1)} %rest_0_.1), channel_id=1, source_target_pairs={{0,8},{4,12},{8,0},{12,4},{1,9},{5,13},{9,1},{13,5},{2,10},{6,14},... | collective-permute-start | bytes 3145736 | tf_op jit(solution)/shard_map/ppermute | solution.py:173
  2.9 23.4 %collective-permute-start.1 = (bf16[8,256,256]{2,1,0:T(8,128)(2,1)}, bf16[8,256,256]{2,1,0:T(8,128)(2,1)S(1)}, u32[]{:S(2)}, u32[]{:S(2)}) collective-permute-start(bf16[8,256,256]{2,1,0:T(8,128)(2,1)} %rest_0_.1), channel_id=1, source_target_pairs={{0,4},{4,0},{8,12},{12,8},{1,5},{5,1},{9,13},{13,9},{2,6},{6,2},{1... | collective-permute-start | bytes 3145736 | tf_op jit(solution)/shard_map/ppermute | solution.py:173
  6.3 27.2 %collective-permute-start.4 = (bf16[512,1024]{1,0:T(8,128)(2,1)}, bf16[512,1024]{1,0:T(8,128)(2,1)}, u32[]{:S(2)}, u32[]{:S(2)}) collective-permute-start(bf16[512,1024]{1,0:T(8,128)(2,1)} %pick.1), channel_id=1, source_target_pairs={{0,1},{3,2},{4,5},{7,6},{8,9},{11,10},{12,13},{15,14},{16,17},{19,... | collective-permute-start | bytes 3145736 | tf_op jit(solution)/shard_map/ppermute | solution.py:169
  10.8 44.9 %collective-permute-start.2 = (bf16[512,2048]{1,0:T(8,128)(2,1)}, bf16[512,2048]{1,0:T(8,128)(2,1)}, u32[]{:S(2)}, u32[]{:S(2)}) collective-permute-start(bf16[512,2048]{1,0:T(8,128)(2,1)} %param.6), channel_id=1, source_target_pairs={{1,2},{2,1},{5,6},{6,5},{9,10},{10,9},{13,14},{14,13},{17,18},{18,... | collective-permute-start | bytes 6291464 | tf_op jit(solution)/shard_map/ppermute | solution.py:169
  15.2 40.5 %collective-permute-start.3 = (bf16[256,2048]{1,0:T(8,128)(2,1)}, bf16[256,2048]{1,0:T(8,128)(2,1)}, u32[]{:S(2)}, u32[]{:S(2)}) collective-permute-start(bf16[256,2048]{1,0:T(8,128)(2,1)} %slice.47), channel_id=1, source_target_pairs={{0,1},{3,2},{1,0},{2,3},{4,5},{7,6},{5,4},{6,7},{8,9},{11,10},{9,8... | collective-permute-start | bytes 3145736 | tf_op jit(solution)/shard_map/ppermute | solution.py:169
  15.2 11.2 %copy-start.16 = (bf16[512,2048]{1,0:T(8,128)(2,1)S(1)}, bf16[512,2048]{1,0:T(8,128)(2,1)}, u32[]{:S(2)}) copy-start(bf16[512,2048]{1,0:T(8,128)(2,1)} %param.6) | copy-start | bytes 6291460
  26.3 2.5 %copy-start.8 = (bf16[8,256,256]{2,1,0:T(8,128)(2,1)}, bf16[8,256,256]{2,1,0:T(8,128)(2,1)S(1)}, u32[]{:S(2)}) copy-start(bf16[8,256,256]{2,1,0:T(8,128)(2,1)S(1)} %collective-permute-done.rest_2_) | copy-start | bytes 3145732
  26.3 2.5 %copy-start.10 = (bf16[8,256,256]{2,1,0:T(8,128)(2,1)}, bf16[8,256,256]{2,1,0:T(8,128)(2,1)S(1)}, u32[]{:S(2)}) copy-start(bf16[8,256,256]{2,1,0:T(8,128)(2,1)S(1)} %collective-permute-done.1.rest_1_) | copy-start | bytes 3145732
  26.3 8.5 %collective-permute-start.5 = (bf16[8,256,256]{2,1,0:T(8,128)(2,1)S(1)}, bf16[8,256,256]{2,1,0:T(8,128)(2,1)S(1)}, u32[]{:S(2)}, u32[]{:S(2)}) collective-permute-start(bf16[8,256,256]{2,1,0:T(8,128)(2,1)S(1)} %collective-permute-done.rest_2_), channel_id=1, source_target_pairs={{0,4},{4,0},{8,12},{12,8},{1,5},{5,1},{9,13},{13,9},{2,6},{6,2},{1... | collective-permute-start | bytes 3145736 | tf_op jit(solution)/shard_map/ppermute | solution.py:173
  34.8 1.0 copy-start.12
  35.8 13.2 %collective-permute-start.6 = (bf16[256,1024]{1,0:T(8,128)(2,1)S(1)}, bf16[256,1024]{1,0:T(8,128)(2,1)S(1)}, u32[]{:S(2)}, u32[]{:S(2)}) collective-permute-start(bf16[256,1024]{1,0:T(8,128)(2,1)S(1)} %get-tuple-element.45), channel_id=1, source_target_pairs={{0,8},{4,12},{8,0},{12,4},{1,9},{5,13},{9,1},{13,5},{2,10},{6,14},... | collective-permute-start | bytes 1572872 | tf_op jit(solution)/shard_map/ppermute | solution.py:173
  36.4 12.9 %collective-permute-start.8 = (bf16[256,1024]{1,0:T(8,128)(2,1)S(1)}, bf16[256,1024]{1,0:T(8,128)(2,1)S(1)}, u32[]{:S(2)}, u32[]{:S(2)}) collective-permute-start(bf16[256,1024]{1,0:T(8,128)(2,1)S(1)} %get-tuple-element.47), channel_id=1, source_target_pairs={{0,16},{16,0},{1,17},{17,1},{2,18},{18,2},{3,19},{19,3},{4,20},{20... | collective-permute-start | bytes 1572872 | tf_op jit(solution)/shard_map/ppermute | solution.py:177
  49.3 35.1 %copy-start.3 = (bf16[512,1024]{1,0:T(8,128)(2,1)}, bf16[512,1024]{1,0:T(8,128)(2,1)S(1)}, u32[]{:S(2)}) copy-start(bf16[512,1024]{1,0:T(8,128)(2,1)S(1)} %pad_maximum_fusion.refs_1_) | copy-start | bytes 3145732
  49.3 35.7 %copy-start.21 = (s32[512,1]{0,1:T(1,128)S(1)}, s32[512,1]{0,1:T(1,128)}, u32[]{:S(2)}) copy-start(s32[512,1]{0,1:T(1,128)} %param.7) | copy-start | bytes 6148
  49.3 7.0 %collective-permute-start.9 = (bf16[512,1024]{1,0:T(8,128)(2,1)S(1)}, bf16[512,1024]{1,0:T(8,128)(2,1)S(1)}, u32[]{:S(2)}, u32[]{:S(2)}) collective-permute-start(bf16[512,1024]{1,0:T(8,128)(2,1)S(1)} %pad_maximum_fusion.refs_1_), channel_id=1, source_target_pairs={{0,4},{4,0},{8,12},{12,8},{1,5},{5,1},{9,13},{13,9},{2,6},{6,2},{1... | collective-permute-start | bytes 3145736 | tf_op jit(solution)/shard_map/ppermute | solution.py:173
  49.5 7.9 %collective-permute-start.10 = (bf16[512,1024]{1,0:T(8,128)(2,1)S(1)}, bf16[512,1024]{1,0:T(8,128)(2,1)S(1)}, u32[]{:S(2)}, u32[]{:S(2)}) collective-permute-start(bf16[512,1024]{1,0:T(8,128)(2,1)S(1)} %pad_maximum_fusion.1.refs_1_), channel_id=1, source_target_pairs={{0,4},{4,0},{8,12},{12,8},{1,5},{5,1},{9,13},{13,9},{2,6},{6,2},{1... | collective-permute-start | bytes 3145736 | tf_op jit(solution)/shard_map/ppermute | solution.py:173
  55.7 27.8 %collective-permute-start.12 = (bf16[256,2048]{1,0:T(8,128)(2,1)}, bf16[256,2048]{1,0:T(8,128)(2,1)S(1)}, u32[]{:S(2)}, u32[]{:S(2)}) collective-permute-start(bf16[256,2048]{1,0:T(8,128)(2,1)} %collective-permute-done.3), channel_id=1, source_target_pairs={{1,2},{2,1},{5,6},{6,5},{9,10},{10,9},{13,14},{14,13},{17,18},{18,... | collective-permute-start | bytes 3145736 | tf_op jit(solution)/shard_map/ppermute | solution.py:169
  56.4 1.0 copy-start.5
  57.4 27.0 %copy-start.1 = (bf16[512,1024]{1,0:T(8,128)(2,1)}, bf16[512,1024]{1,0:T(8,128)(2,1)S(1)}, u32[]{:S(2)}) copy-start(bf16[512,1024]{1,0:T(8,128)(2,1)S(1)} %collective-permute-done.10.refs_3_) | copy-start | bytes 3145732
  57.4 27.0 %collective-permute-start.11 = (bf16[512,1024]{1,0:T(8,128)(2,1)S(1)}, bf16[512,1024]{1,0:T(8,128)(2,1)}, u32[]{:S(2)}, u32[]{:S(2)}) collective-permute-start(bf16[512,1024]{1,0:T(8,128)(2,1)S(1)} %pad_maximum_fusion.refs_1_), channel_id=1, source_target_pairs={{0,8},{4,12},{8,0},{12,4},{1,9},{5,13},{9,1},{13,5},{2,10},{6,14},... | collective-permute-start | bytes 3145736 | tf_op jit(solution)/shard_map/ppermute | solution.py:173
  57.9 26.5 %collective-permute-start.14 = (bf16[512,1024]{1,0:T(8,128)(2,1)S(1)}, bf16[512,1024]{1,0:T(8,128)(2,1)}, u32[]{:S(2)}, u32[]{:S(2)}) collective-permute-start(bf16[512,1024]{1,0:T(8,128)(2,1)S(1)} %pad_maximum_fusion.1.refs_1_), channel_id=1, source_target_pairs={{0,16},{16,0},{1,17},{17,1},{2,18},{18,2},{3,19},{19,3},{4,20},{20... | collective-permute-start | bytes 3145736 | tf_op jit(solution)/shard_map/ppermute | solution.py:177
  59.4 23.1 %collective-permute-start.7 = (bf16[128,3072]{1,0:T(8,128)(2,1)S(1)}, bf16[128,3072]{1,0:T(8,128)(2,1)S(1)}, u32[]{:S(2)}, u32[]{:S(2)}) collective-permute-start(bf16[128,3072]{1,0:T(8,128)(2,1)S(1)} %slice_dynamic-update-slice_fusion.1), channel_id=1, source_target_pairs={{0,1},{3,2},{1,0},{2,3},{4,5},{7,6},{5,4},{6,7},{8,9},{11,10},{9,8... | collective-permute-start | bytes 2359304 | tf_op jit(solution)/shard_map/ppermute | solution.py:169
  82.6 1.9 %copy-start.18 = (bf16[128,3072]{1,0:T(8,128)(2,1)}, bf16[128,3072]{1,0:T(8,128)(2,1)S(1)}, u32[]{:S(2)}) copy-start(bf16[128,3072]{1,0:T(8,128)(2,1)S(1)} %collective-permute-done.7) | copy-start | bytes 2359300
  83.4 1.0 copy-start.14
  84.4 7.7 %collective-permute-start.13 = (bf16[512,1024]{1,0:T(8,128)(2,1)}, bf16[512,1024]{1,0:T(8,128)(2,1)}, u32[]{:S(2)}, u32[]{:S(2)}) collective-permute-start(bf16[512,1024]{1,0:T(8,128)(2,1)} %collective-permute-done.11.refs_2_), channel_id=1, source_target_pairs={{0,4},{4,0},{8,12},{12,8},{1,5},{5,1},{9,13},{13,9},{2,6},{6,2},{1... | collective-permute-start | bytes 3145736 | tf_op jit(solution)/shard_map/ppermute | solution.py:173
  84.4 7.7 %collective-permute-start.15 = (bf16[512,1024]{1,0:T(8,128)(2,1)}, bf16[512,1024]{1,0:T(8,128)(2,1)S(1)}, u32[]{:S(2)}, u32[]{:S(2)}) collective-permute-start(bf16[512,1024]{1,0:T(8,128)(2,1)} %collective-permute-done.14.refs_2_), channel_id=1, source_target_pairs={{0,4},{4,0},{8,12},{12,8},{1,5},{5,1},{9,13},{13,9},{2,6},{6,2},{1... | collective-permute-start | bytes 3145736 | tf_op jit(solution)/shard_map/ppermute | solution.py:173
  85.2 7.0 %copy-start.4 = (bf16[512,1024]{1,0:T(8,128)(2,1)S(1)}, bf16[512,1024]{1,0:T(8,128)(2,1)}, u32[]{:S(2)}) copy-start(bf16[512,1024]{1,0:T(8,128)(2,1)} %copy-done.3) | copy-start | bytes 3145732
  85.2 16.8 %collective-permute-start.18 = (bf16[128,2048]{1,0:T(8,128)(2,1)}, bf16[128,2048]{1,0:T(8,128)(2,1)S(1)}, u32[]{:S(2)}, u32[]{:S(2)}) collective-permute-start(bf16[128,2048]{1,0:T(8,128)(2,1)} %get-tuple-element.65), channel_id=1, source_target_pairs={{0,1},{3,2},{1,0},{2,3},{4,5},{7,6},{5,4},{6,7},{8,9},{11,10},{9,8... | collective-permute-start | bytes 1572872 | tf_op jit(solution)/shard_map/ppermute | solution.py:169
  91.4 19.5 %collective-permute-start.20 = (bf16[128,2048]{1,0:T(8,128)(2,1)}, bf16[128,2048]{1,0:T(8,128)(2,1)S(1)}, u32[]{:S(2)}, u32[]{:S(2)}) collective-permute-start(bf16[128,2048]{1,0:T(8,128)(2,1)} %slice.61), channel_id=1, source_target_pairs={{1,2},{2,1},{5,6},{6,5},{9,10},{10,9},{13,14},{14,13},{17,18},{18,... | collective-permute-start | bytes 1572872 | tf_op jit(solution)/shard_map/ppermute | solution.py:169
  92.2 1.2 copy-start.6
  97.9 1.2 copy-start.2
  97.9 1.5 %copy-start.15 = (bf16[256,2048]{1,0:T(8,128)(2,1)S(1)}, bf16[256,2048]{1,0:T(8,128)(2,1)}, u32[]{:S(2)}) copy-start(bf16[256,2048]{1,0:T(8,128)(2,1)} %copy-done.14) | copy-start | bytes 3145732
  98.0 11.4 %collective-permute-start.16 = (bf16[512,256]{1,0:T(8,128)(2,1)S(1)}, bf16[512,256]{1,0:T(8,128)(2,1)S(1)}, u32[]{:S(2)}, u32[]{:S(2)}) collective-permute-start(bf16[512,256]{1,0:T(8,128)(2,1)S(1)} %fusion.26), channel_id=1, source_target_pairs={{1,2},{2,1},{5,6},{6,5},{9,10},{10,9},{13,14},{14,13},{17,18},{18,... | collective-permute-start | bytes 786440 | tf_op jit(solution)/shard_map/ppermute | solution.py:169
  101.9 7.5 %copy-start.17 = (f32[512,256]{1,0:T(8,128)S(1)}, f32[512,256]{1,0:T(8,128)}, u32[]{:S(2)}) copy-start(f32[512,256]{1,0:T(8,128)} %get-tuple-element.88) | copy-start | bytes 1572868
  101.9 18.2 %collective-permute-start.21 = (bf16[256,1024]{1,0:T(8,128)(2,1)S(1)}, bf16[256,1024]{1,0:T(8,128)(2,1)S(1)}, u32[]{:S(2)}, u32[]{:S(2)}) collective-permute-start(bf16[256,1024]{1,0:T(8,128)(2,1)S(1)} %lend_far.3.rest_4_.refs_6_), channel_id=1, source_target_pairs={{1,0},{2,3},{5,4},{6,7},{9,8},{10,11},{13,12},{14,15},{17,16},{18,... | collective-permute-start | bytes 1572872 | tf_op jit(solution)/shard_map/ppermute | solution.py:169
  103.4 26.6 %slice-start = ((s8[16777216]{0:T(1024)(128)(4,1)}), s8[4194304]{0:T(1024)(128)(4,1)S(1)}, s32[]{:S(2)}) async-start(s8[16777216]{0:T(1024)(128)(4,1)} %bitcast.15), calls=%async_computation | async-start | bytes 8388608
  103.4 26.6 %slice-start.1 = ((s8[16777216]{0:T(1024)(128)(4,1)}), s8[4194304]{0:T(1024)(128)(4,1)S(1)}, s32[]{:S(2)}) async-start(s8[16777216]{0:T(1024)(128)(4,1)} %bitcast.15), calls=%async_computation.1 | async-start | bytes 8388608
  108.7 14.8 %collective-permute-start.19 = (bf16[128,2048]{1,0:T(8,128)(2,1)S(1)}, bf16[128,2048]{1,0:T(8,128)(2,1)S(1)}, u32[]{:S(2)}, u32[]{:S(2)}) collective-permute-start(bf16[128,2048]{1,0:T(8,128)(2,1)S(1)} %collective-permute-done.18), channel_id=1, source_target_pairs={{1,2},{2,1},{5,6},{6,5},{9,10},{10,9},{13,14},{14,13},{17,18},{18,... | collective-permute-start | bytes 1572872 | tf_op jit(solution)/shard_map/ppermute | solution.py:169
  109.5 17.8 %collective-permute-start.17 = (bf16[512,256]{1,0:T(8,128)(2,1)S(1)}, bf16[512,256]{1,0:T(8,128)(2,1)S(1)}, u32[]{:S(2)}, u32[]{:S(2)}) collective-permute-start(bf16[512,256]{1,0:T(8,128)(2,1)S(1)} %add_convert_fusion), channel_id=1, source_target_pairs={{1,0},{2,3},{5,4},{6,7},{9,8},{10,11},{13,12},{14,15},{17,16},{18,... | collective-permute-start | bytes 786440 | tf_op jit(solution)/shard_map/ppermute | solution.py:169
  120.1 9.9 %slice-start.2 = ((s8[16777216]{0:T(1024)(128)(4,1)}), s8[4194304]{0:T(1024)(128)(4,1)S(1)}, s32[]{:S(2)}) async-start(s8[16777216]{0:T(1024)(128)(4,1)} %bitcast.15), calls=%async_computation.2 | async-start | bytes 8388608
  122.2 15.3 %collective-permute-start.22 = (bf16[128,1024]{1,0:T(8,128)(2,1)S(1)}, bf16[128,1024]{1,0:T(8,128)(2,1)S(1)}, u32[]{:S(2)}, u32[]{:S(2)}) collective-permute-start(bf16[128,1024]{1,0:T(8,128)(2,1)S(1)} %lend_far.4.refs_6_), channel_id=1, source_target_pairs={{1,0},{2,3},{5,4},{6,7},{9,8},{10,11},{13,12},{14,15},{17,16},{18,... | collective-permute-start | bytes 786440 | tf_op jit(solution)/shard_map/ppermute | solution.py:169
  123.6 3.9 %copy-start.7 = (bf16[8,256,256]{2,1,0:T(8,128)(2,1)S(1)}, bf16[8,256,256]{2,1,0:T(8,128)(2,1)}, u32[]{:S(2)}) copy-start(bf16[8,256,256]{2,1,0:T(8,128)(2,1)} %rest_0_.1) | copy-start | bytes 3145732
  123.6 3.8 %copy-start.9 = (bf16[8,256,256]{2,1,0:T(8,128)(2,1)S(1)}, bf16[8,256,256]{2,1,0:T(8,128)(2,1)}, u32[]{:S(2)}) copy-start(bf16[8,256,256]{2,1,0:T(8,128)(2,1)} %copy-done.8) | copy-start | bytes 3145732
  123.6 3.8 %copy-start.11 = (bf16[8,256,256]{2,1,0:T(8,128)(2,1)S(1)}, bf16[8,256,256]{2,1,0:T(8,128)(2,1)}, u32[]{:S(2)}) copy-start(bf16[8,256,256]{2,1,0:T(8,128)(2,1)} %copy-done.10) | copy-start | bytes 3145732
  123.6 3.8 %copy-start.13 = (bf16[8,256,256]{2,1,0:T(8,128)(2,1)S(1)}, bf16[8,256,256]{2,1,0:T(8,128)(2,1)}, u32[]{:S(2)}) copy-start(bf16[8,256,256]{2,1,0:T(8,128)(2,1)} %copy-done.12) | copy-start | bytes 3145732
  123.6 6.5 %slice-start.3 = ((s8[16777216]{0:T(1024)(128)(4,1)}), s8[4194304]{0:T(1024)(128)(4,1)S(1)}, s32[]{:S(2)}) async-start(s8[16777216]{0:T(1024)(128)(4,1)} %bitcast.15), calls=%async_computation.3 | async-start | bytes 8388608
  125.7 11.1 %collective-permute-start.23 = (bf16[128,1024]{1,0:T(8,128)(2,1)S(1)}, bf16[128,1024]{1,0:T(8,128)(2,1)S(1)}, u32[]{:S(2)}, u32[]{:S(2)}) collective-permute-start(bf16[128,1024]{1,0:T(8,128)(2,1)S(1)} %lend_far.5), channel_id=1, source_target_pairs={{1,0},{2,3},{5,4},{6,7},{9,8},{10,11},{13,12},{14,15},{17,16},{18,... | collective-permute-start | bytes 786440 | tf_op jit(solution)/shard_map/ppermute | solution.py:169
  127.4 2.1 %copy-start.20 = (bf16[256,1024]{1,0:T(8,128)(2,1)S(1)}, bf16[256,1024]{1,0:T(8,128)(2,1)}, u32[]{:S(2)}) copy-start(bf16[256,1024]{1,0:T(8,128)(2,1)} %param.11) | copy-start | bytes 1572868
  129.5 1.0 copy-start.19
  129.6 1.8 %copy-start.22 = (f32[512,1024]{1,0:T(8,128)S(1)}, f32[512,1024]{1,0:T(8,128)}, u32[]{:S(2)}) copy-start(f32[512,1024]{1,0:T(8,128)} %fusion.17) | copy-start | bytes 6291460

commit v9 on v8

--- a/solution.py
+++ b/solution.py
@@ -64,16 +64,16 @@
     out_ref[...] = x_ref[...]
 
 
-def pick(x, blocks, rows):
-    columns = x.shape[1]
+def pick(x, blocks, rows, steps=4):
+    columns, part = x.shape[1], rows // steps
     return pl.pallas_call(
         pick_kernel,
         out_shape=jax.ShapeDtypeStruct((blocks.size * rows, columns), x.dtype),
         grid_spec=pltpu.PrefetchScalarGridSpec(
             num_scalar_prefetch=1,
-            grid=(blocks.size,),
-            in_specs=[pl.BlockSpec((rows, columns), lambda i, which: (which[i], 0))],
-            out_specs=pl.BlockSpec((rows, columns), lambda i, which: (i, 0)),
+            grid=(blocks.size, steps),
+            in_specs=[pl.BlockSpec((part, columns), lambda i, k, which: (which[i] * steps + k, 0))],
+            out_specs=pl.BlockSpec((part, columns), lambda i, k, which: (i * steps + k, 0)),
         ),
         cost_estimate=pl.CostEstimate(
             flops=0, bytes_accessed=4 * blocks.size * rows * columns, transcendentals=0

time: 141 us -> 144 us (1.021)
  Pallas kernels: 16 us -> 19.2 us
    ppermute x13, waiting for transfers between devices: 36.7 us -> 39.8 us  [send(): return lax.ppermute(x, 'tp', pairs)]
    ppermute x9, waiting for transfers between devices: 15.6 us -> 12.5 us  [swap_rep(): return lax.ppermute(x, 'rep', [(i, i ^ bit) for i in range(4)])]
    pallas_call x1, Pallas kernels: 2.72 us -> 5.85 us  [pick(): pl.pallas_call(pick_kernel, out_shape=jax.ShapeDtypeStruct((blocks.size *...]
  transfers between devices with their start and end apart: 24 -> 24, of which waited for: 8 -> 8; matrix products, arithmetic and copies ran while one was open for 20% -> 20% of each run, Pallas kernels for 11% -> 13%
where the time goes in v9:
time: 144 us; the launch traced here: 143 us
  waiting for transfers between devices  52.6 us (37%)
  starting transfers between devices  34 us (24%)
  matrix products  20.4 us (14%)
  Pallas kernels  19.2 us (13%)
  local copies, waits for them, and re-layouts  12.8 us (9%)
  other arithmetic  3.06 us (2%)
    ppermute x13, waiting for transfers between devices, send(): return lax.ppermute(x, 'tp', pairs)  39.8 us
    ppermute x13, starting transfers between devices, send(): return lax.ppermute(x, 'tp', pairs)  25.7 us
    dot_general x8, matrix products, dot(): return jnp.dot(a, b, preferred_element_type=jnp.float32)  20.4 us
    ppermute x9, waiting for transfers between devices, swap_rep(): return lax.ppermute(x, 'rep', [(i, i ^ bit) for i in range(4)])  12.5 us
    pallas_call x4, Pallas kernels, lend(): pl.pallas_call(functools.partial(lend_kernel, count=len(xs), blocks=tuple...  11.2 us
    unnamed x58, local copies, waits for them, and re-layouts  6.24 us
    pallas_call x1, Pallas kernels, pick(): pl.pallas_call(pick_kernel, out_shape=jax.ShapeDtypeStruct((blocks.size *...  5.85 us
    ppermute x9, starting transfers between devices, swap_rep(): return lax.ppermute(x, 'rep', [(i, i ^ bit) for i in range(4)])  5.27 us
  transfers between devices with their start and end apart: 24, of which 8 were waited for; matrix products, arithmetic and copies ran while one was open for 20% of the time, Pallas kernels for 13%

profile of v9, /device:TPU:0, one launch (start us, length us, event | category | flops | bytes accessed | tf_op | source)
XLA Modules:
  0.0 142.5 jit_solution(18236981348984249908)
XLA Ops:
  0.0 2.9 %collective-permute-start = (bf16[8,256,256]{2,1,0:T(8,128)(2,1)}, bf16[8,256,256]{2,1,0:T(8,128)(2,1)S(1)}, u32[]{:S(2)}, u32[]{:S(2)}) collective-permute-start(bf16[8,256,256]{2,1,0:T(8,128)(2,1)} %rest_0_.1), channel_id=1, source_target_pairs={{0,8},{4,12},{8,0},{12,4},{1,9},{5,13},{9,1},{13,5},{2,10},{6,14},... | collective-permute-start | bytes 3145736 | tf_op jit(solution)/shard_map/ppermute | solution.py:173
  2.9 0.6 pad_add_fusion.which_ref
  3.6 5.8 %pick.1 = bf16[512,1024]{1,0:T(8,128)(2,1)} custom-call(s32[2]{0:T(128)} %pad_add_fusion.which_ref, bf16[8192,1024]{1,0:T(8,128)(2,1)} %x_ref.1), custom_call_target="tpu_custom_call" | custom-call | bytes 2097152 | tf_op jit(solution)/shard_map/pick/pallas_call | solution.py:69
  9.4 4.4 %collective-permute-start.4 = (bf16[512,1024]{1,0:T(8,128)(2,1)}, bf16[512,1024]{1,0:T(8,128)(2,1)}, u32[]{:S(2)}, u32[]{:S(2)}) collective-permute-start(bf16[512,1024]{1,0:T(8,128)(2,1)} %pick.1), channel_id=1, source_target_pairs={{0,1},{3,2},{4,5},{7,6},{8,9},{11,10},{12,13},{15,14},{16,17},{19,... | collective-permute-start | bytes 3145736 | tf_op jit(solution)/shard_map/ppermute | solution.py:169
  13.9 2.0 %collective-permute-start.2 = (bf16[512,2048]{1,0:T(8,128)(2,1)}, bf16[512,2048]{1,0:T(8,128)(2,1)}, u32[]{:S(2)}, u32[]{:S(2)}) collective-permute-start(bf16[512,2048]{1,0:T(8,128)(2,1)} %param.6), channel_id=1, source_target_pairs={{1,2},{2,1},{5,6},{6,5},{9,10},{10,9},{13,14},{14,13},{17,18},{18,... | collective-permute-start | bytes 6291464 | tf_op jit(solution)/shard_map/ppermute | solution.py:169
  15.9 2.4 %slice.47 = bf16[256,2048]{1,0:T(8,128)(2,1)} slice(bf16[512,2048]{1,0:T(8,128)(2,1)} %param.6), slice={[0:256], [0:2048]} | slice | bytes 2097152 | tf_op jit(solution)/shard_map/slice | solution.py:229
  18.3 6.7 %fusion.17 = f32[512,1024]{1,0:T(8,128)} fusion(bf16[512,2048]{1,0:T(8,128)(2,1)} %param.6, bf16[8192,1024]{1,0:T(8,128)(2,1)} %x_ref.1, s32[]{:T(128)S(6)} %select_n.37), kind=kOutput, calls=%fused_computation.18 | convolution fusion | flops 2147483648 | bytes 8388612 | tf_op jit(solution)/shard_map/dot_general | solution.py:14
  25.0 1.4 collective-permute-done.rest_2_
  26.4 1.5 %fusion.48 = (bf16[512,256]{1,0:T(8,128)(2,1)S(1)}, f32[512,256]{1,0:T(8,128)}) fusion(bf16[512,2048]{1,0:T(8,128)(2,1)S(1)} %copy-done.16, bf16[2048,256]{1,0:T(8,128)(2,1)S(1)} %copy-done), kind=kOutput, calls=%fused_computation.53 | convolution fusion | flops 537001984 | bytes 3932160 | tf_op jit(solution)/shard_map/dot_general | solution.py:14
  27.9 0.9 fusion.45
  28.8 7.9 %collective-permute-done.4 = bf16[512,1024]{1,0:T(8,128)(2,1)} collective-permute-done((bf16[512,1024]{1,0:T(8,128)(2,1)}, bf16[512,1024]{1,0:T(8,128)(2,1)}, u32[]{:S(2)}, u32[]{:S(2)}) %collective-permute-start.4) | collective-permute-done | bytes 1048608 | tf_op jit(solution)/shard_map/ppermute | solution.py:169
  36.7 1.3 fusion.46
  38.0 1.0 copy-done.12
  38.9 0.5 collective-permute-start.6
  39.5 1.5 %collective-permute-start.8 = (bf16[256,1024]{1,0:T(8,128)(2,1)S(1)}, bf16[256,1024]{1,0:T(8,128)(2,1)S(1)}, u32[]{:S(2)}, u32[]{:S(2)}) collective-permute-start(bf16[256,1024]{1,0:T(8,128)(2,1)S(1)} %get-tuple-element.47), channel_id=1, source_target_pairs={{0,16},{16,0},{1,17},{17,1},{2,18},{18,2},{3,19},{19,3},{4,20},{20... | collective-permute-start | bytes 1572872 | tf_op jit(solution)/shard_map/ppermute | solution.py:177
  41.0 11.1 %collective-permute-done.6 = bf16[256,1024]{1,0:T(8,128)(2,1)S(1)} collective-permute-done((bf16[256,1024]{1,0:T(8,128)(2,1)S(1)}, bf16[256,1024]{1,0:T(8,128)(2,1)S(1)}, u32[]{:S(2)}, u32[]{:S(2)}) %collective-permute-start.6) | collective-permute-done | bytes 524320 | tf_op jit(solution)/shard_map/ppermute | solution.py:173
  52.1 0.3 collective-permute-done.8
  52.4 0.1 pad_maximum_fusion.refs_1_
  52.5 0.1 collective-permute-start.9
  52.5 0.1 pad_maximum_fusion.1.refs_1_
  52.6 0.6 collective-permute-start.10
  53.2 5.6 %collective-permute-done.3 = bf16[256,2048]{1,0:T(8,128)(2,1)} collective-permute-done((bf16[256,2048]{1,0:T(8,128)(2,1)}, bf16[256,2048]{1,0:T(8,128)(2,1)}, u32[]{:S(2)}, u32[]{:S(2)}) %collective-permute-start.3) | collective-permute-done | bytes 1048608 | tf_op jit(solution)/shard_map/ppermute | solution.py:169
  58.8 0.7 collective-permute-start.12
  59.5 1.0 copy-done.5
  60.5 0.5 collective-permute-start.11
  61.0 1.5 %collective-permute-start.14 = (bf16[512,1024]{1,0:T(8,128)(2,1)S(1)}, bf16[512,1024]{1,0:T(8,128)(2,1)}, u32[]{:S(2)}, u32[]{:S(2)}) collective-permute-start(bf16[512,1024]{1,0:T(8,128)(2,1)S(1)} %pad_maximum_fusion.1.refs_1_), channel_id=1, source_target_pairs={{0,16},{16,0},{1,17},{17,1},{2,18},{18,2},{3,19},{19,3},{4,20},{20... | collective-permute-start | bytes 3145736 | tf_op jit(solution)/shard_map/ppermute | solution.py:177
  62.6 6.5 %collective-permute-start.7 = (bf16[128,3072]{1,0:T(8,128)(2,1)S(1)}, bf16[128,3072]{1,0:T(8,128)(2,1)S(1)}, u32[]{:S(2)}, u32[]{:S(2)}) collective-permute-start(bf16[128,3072]{1,0:T(8,128)(2,1)S(1)} %slice_dynamic-update-slice_fusion.1), channel_id=1, source_target_pairs={{0,1},{3,2},{1,0},{2,3},{4,5},{7,6},{5,4},{6,7},{8,9},{11,10},{9,8... | collective-permute-start | bytes 2359304 | tf_op jit(solution)/shard_map/ppermute | solution.py:169
  69.1 16.6 %collective-permute-done.7 = bf16[128,3072]{1,0:T(8,128)(2,1)S(1)} collective-permute-done((bf16[128,3072]{1,0:T(8,128)(2,1)S(1)}, bf16[128,3072]{1,0:T(8,128)(2,1)S(1)}, u32[]{:S(2)}, u32[]{:S(2)}) %collective-permute-start.7) | collective-permute-done | bytes 786464 | tf_op jit(solution)/shard_map/ppermute | solution.py:169
  85.7 0.9 slice.61
  86.6 1.0 copy-done.14
  87.6 0.6 collective-permute-start.15
  88.1 0.1 copy.10.ids_ref
  88.3 4.2 %collective-permute-start.18 = (bf16[128,2048]{1,0:T(8,128)(2,1)}, bf16[128,2048]{1,0:T(8,128)(2,1)S(1)}, u32[]{:S(2)}, u32[]{:S(2)}) collective-permute-start(bf16[128,2048]{1,0:T(8,128)(2,1)} %get-tuple-element.65), channel_id=1, source_target_pairs={{0,1},{3,2},{1,0},{2,3},{4,5},{7,6},{5,4},{6,7},{8,9},{11,10},{9,8... | collective-permute-start | bytes 1572872 | tf_op jit(solution)/shard_map/ppermute | solution.py:169
  92.5 1.0 fusion.47
  93.4 1.1 fusion.26
  94.5 0.7 collective-permute-start.20
  95.3 1.2 copy-done.6
  96.5 4.5 %lend_near.1 = f32[512,1024]{1,0:T(8,128)S(1)} custom-call(s32[1]{0:T(128)} %bitcast.4.spot_ref, bf16[512,2048]{1,0:T(8,128)(2,1)} %collective-permute-done.2.refs_0_, bf16[512,1024]{1,0:T(8,128)(2,1)S(1)} %copy-done.4, bf16[512,1024]{1,0:T(8,128)(2,1)} %collective-permute-done.11.refs_2_, bf16[512,1024]{1,0:T(8,128)(2,1)S(1)} %copy-done.6, ...), custom_call_target="tpu_custom_call" | custom-call | flops 2147483648 | bytes 7340032 | tf_op jit(solution)/shard_map/lend_near/pallas_call | solution.py:114
  101.0 0.1 slice.62.refs_5_
  101.1 0.8 collective-permute-start.16
  102.0 0.3 copy-done.2
  102.2 0.3 copy-done.15
  102.6 2.5 %lend_far.3.rest_4_.refs_6_ = bf16[256,1024]{1,0:T(8,128)(2,1)S(1)} custom-call(s32[1]{0:T(128)} %bitcast.4.spot_ref, bf16[256,2048]{1,0:T(8,128)(2,1)S(1)} %copy-done.15, bf16[512,1024]{1,0:T(8,128)(2,1)S(1)} %pad_maximum_fusion.1.refs_1_, bf16[512,1024]{1,0:T(8,128)(2,1)} %collective-permute-done.14.refs_2_, bf16[512,1024]{1,0:T(8,128)(2,1)S(1)} %copy-done.2, ...), custom_call_target="tpu_custom_call" | custom-call | flops 1073741824 | bytes 5767168 | tf_op jit(solution)/shard_map/lend_far/pallas_call | solution.py:114
  105.1 1.4 collective-permute-start.21
  106.5 5.3 %fusion.2 = f32[512,1024]{1,0:T(8,128)S(1)} fusion(bf16[512,2048]{1,0:T(8,128)(2,1)} %collective-permute-done.2.refs_0_, bf16[8192,1024]{1,0:T(8,128)(2,1)} %x_ref.1, s32[]{:T(128)S(6)} %select_n.39), kind=kOutput, calls=%fused_computation.2 | convolution fusion | flops 2147483648 | bytes 8388612 | tf_op jit(solution)/shard_map/dot_general | solution.py:14
  111.8 0.7 collective-permute-start.19
  112.6 0.1 add_convert_fusion
  112.7 1.3 collective-permute-start.17
  114.0 0.1 fusion.44
  114.1 9.2 %collective-permute-done.21.refs_7_ = bf16[256,1024]{1,0:T(8,128)(2,1)S(1)} collective-permute-done((bf16[256,1024]{1,0:T(8,128)(2,1)S(1)}, bf16[256,1024]{1,0:T(8,128)(2,1)S(1)}, u32[]{:S(2)}, u32[]{:S(2)}) %collective-permute-start.21) | collective-permute-done | bytes 524320 | tf_op jit(solution)/shard_map/ppermute | solution.py:169
  123.2 2.1 %lend_far.4.refs_6_ = bf16[128,1024]{1,0:T(8,128)(2,1)S(1)} custom-call(s32[1]{0:T(128)} %bitcast.4.spot_ref, bf16[128,2048]{1,0:T(8,128)(2,1)S(1)} %collective-permute-done.20.refs_0_, bf16[512,1024]{1,0:T(8,128)(2,1)S(1)} %pad_maximum_fusion.1.refs_1_, bf16[512,1024]{1,0:T(8,128)(2,1)} %collective-permute-done.14.refs_2_, bf16[512,1024]{1,0:T(8,128)(2,1)S(1)} %copy-done.2, ...), custom_call_target="tpu_custom_call" | custom-call | flops 536870912 | bytes 4980736 | tf_op jit(solution)/shard_map/lend_far/pallas_call | solution.py:114
  125.4 1.3 collective-permute-start.22
  126.7 2.1 %lend_far.5 = bf16[128,1024]{1,0:T(8,128)(2,1)S(1)} custom-call(s32[1]{0:T(128)} %bitcast.4.spot_ref, bf16[128,2048]{1,0:T(8,128)(2,1)S(1)} %collective-permute-done.19.refs_0_, bf16[512,1024]{1,0:T(8,128)(2,1)S(1)} %pad_maximum_fusion.1.refs_1_, bf16[512,1024]{1,0:T(8,128)(2,1)} %collective-permute-done.14.refs_2_, bf16[512,1024]{1,0:T(8,128)(2,1)S(1)} %copy-done.2, ...), custom_call_target="tpu_custom_call" | custom-call | flops 536870912 | bytes 4980736 | tf_op jit(solution)/shard_map/lend_far/pallas_call | solution.py:114
  128.9 1.6 %collective-permute-start.23 = (bf16[128,1024]{1,0:T(8,128)(2,1)S(1)}, bf16[128,1024]{1,0:T(8,128)(2,1)S(1)}, u32[]{:S(2)}, u32[]{:S(2)}) collective-permute-start(bf16[128,1024]{1,0:T(8,128)(2,1)S(1)} %lend_far.5), channel_id=1, source_target_pairs={{1,0},{2,3},{5,4},{6,7},{9,8},{10,11},{13,12},{14,15},{17,16},{18,... | collective-permute-start | bytes 786440 | tf_op jit(solution)/shard_map/ppermute | solution.py:169
  130.6 2.1 %mix.1 = bf16[512,256]{1,0:T(8,128)(2,1)S(1)} custom-call(s32[1]{0:T(128)} %bitcast.1.rep_ref, s32[512,1]{1,0:T(8,128)S(1)} %copy.10.ids_ref, bf16[512,256]{1,0:T(8,128)(2,1)S(1)} %broadcast_select_fusion.coded_ref, bf16[8,256,256]{2,1,0:T(8,128)(2,1)S(1)} %copy-done.7, bf16[8,256,256]{2,1,0:T(8,128)(2,1)S(1)} %copy-done.11, ...), custom_call_target="tpu_custom_call" | custom-call | flops 402653184 | bytes 4718592 | tf_op jit(solution)/shard_map/mix/pallas_call | solution.py:46
  132.7 0.4 fusion.49
  133.2 0.5 copy-done.19
  133.7 0.7 copy-done.22
  134.4 3.6 %add_add_fusion = f32[512,1024]{1,0:T(8,128)S(1)} fusion(f32[512,1024]{1,0:T(8,128)S(1)} %fusion.49, f32[512,1024]{1,0:T(8,128)S(1)} %copy-done.22, f32[512,1024]{1,0:T(8,128)S(1)} %fusion.2, bf16[8192,1024]{1,0:T(8,128)(2,1)S(1)} %bitcast.16, s32[]{:T(128)S(6)} %select_n.46, bf16[128,2048]{1,0:T(8,128)(2,1)S(1)} %collective-permute-done.18, ...), kind=kOutput, calls=%fused_computation.17 | convolution fusion | flops 2155347968 | bytes 14680068 | tf_op jit(solution)/shard_map/dot_general | solution.py:14
  138.1 1.3 fusion.21
  139.4 0.6 collective-permute-done.23
  140.0 0.7 fusion.23
  140.7 0.8 fusion.25
  141.5 1.0 pad_maximum_fusion.2
  (72 shorter events, 0.3 us)
Async XLA Ops:
  0.0 26.4 %copy-start = (bf16[2048,256]{1,0:T(8,128)(2,1)S(1)}, bf16[2048,256]{1,0:T(8,128)(2,1)}, u32[]{:S(2)}) copy-start(bf16[2048,256]{1,0:T(8,128)(2,1)} %param.9) | copy-start | bytes 3145732
  0.0 26.3 %collective-permute-start = (bf16[8,256,256]{2,1,0:T(8,128)(2,1)}, bf16[8,256,256]{2,1,0:T(8,128)(2,1)S(1)}, u32[]{:S(2)}, u32[]{:S(2)}) collective-permute-start(bf16[8,256,256]{2,1,0:T(8,128)(2,1)} %rest_0_.1), channel_id=1, source_target_pairs={{0,8},{4,12},{8,0},{12,4},{1,9},{5,13},{9,1},{13,5},{2,10},{6,14},... | collective-permute-start | bytes 3145736 | tf_op jit(solution)/shard_map/ppermute | solution.py:173
  2.9 23.4 %collective-permute-start.1 = (bf16[8,256,256]{2,1,0:T(8,128)(2,1)}, bf16[8,256,256]{2,1,0:T(8,128)(2,1)S(1)}, u32[]{:S(2)}, u32[]{:S(2)}) collective-permute-start(bf16[8,256,256]{2,1,0:T(8,128)(2,1)} %rest_0_.1), channel_id=1, source_target_pairs={{0,4},{4,0},{8,12},{12,8},{1,5},{5,1},{9,13},{13,9},{2,6},{6,2},{1... | collective-permute-start | bytes 3145736 | tf_op jit(solution)/shard_map/ppermute | solution.py:173
  9.4 27.2 %collective-permute-start.4 = (bf16[512,1024]{1,0:T(8,128)(2,1)}, bf16[512,1024]{1,0:T(8,128)(2,1)}, u32[]{:S(2)}, u32[]{:S(2)}) collective-permute-start(bf16[512,1024]{1,0:T(8,128)(2,1)} %pick.1), channel_id=1, source_target_pairs={{0,1},{3,2},{4,5},{7,6},{8,9},{11,10},{12,13},{15,14},{16,17},{19,... | collective-permute-start | bytes 3145736 | tf_op jit(solution)/shard_map/ppermute | solution.py:169
  13.9 44.9 %collective-permute-start.2 = (bf16[512,2048]{1,0:T(8,128)(2,1)}, bf16[512,2048]{1,0:T(8,128)(2,1)}, u32[]{:S(2)}, u32[]{:S(2)}) collective-permute-start(bf16[512,2048]{1,0:T(8,128)(2,1)} %param.6), channel_id=1, source_target_pairs={{1,2},{2,1},{5,6},{6,5},{9,10},{10,9},{13,14},{14,13},{17,18},{18,... | collective-permute-start | bytes 6291464 | tf_op jit(solution)/shard_map/ppermute | solution.py:169
  18.3 40.5 %collective-permute-start.3 = (bf16[256,2048]{1,0:T(8,128)(2,1)}, bf16[256,2048]{1,0:T(8,128)(2,1)}, u32[]{:S(2)}, u32[]{:S(2)}) collective-permute-start(bf16[256,2048]{1,0:T(8,128)(2,1)} %slice.47), channel_id=1, source_target_pairs={{0,1},{3,2},{1,0},{2,3},{4,5},{7,6},{5,4},{6,7},{8,9},{11,10},{9,8... | collective-permute-start | bytes 3145736 | tf_op jit(solution)/shard_map/ppermute | solution.py:169
  18.3 8.1 %copy-start.16 = (bf16[512,2048]{1,0:T(8,128)(2,1)S(1)}, bf16[512,2048]{1,0:T(8,128)(2,1)}, u32[]{:S(2)}) copy-start(bf16[512,2048]{1,0:T(8,128)(2,1)} %param.6) | copy-start | bytes 6291460
  26.3 2.5 %copy-start.8 = (bf16[8,256,256]{2,1,0:T(8,128)(2,1)}, bf16[8,256,256]{2,1,0:T(8,128)(2,1)S(1)}, u32[]{:S(2)}) copy-start(bf16[8,256,256]{2,1,0:T(8,128)(2,1)S(1)} %collective-permute-done.rest_2_) | copy-start | bytes 3145732
  26.3 2.5 %copy-start.10 = (bf16[8,256,256]{2,1,0:T(8,128)(2,1)}, bf16[8,256,256]{2,1,0:T(8,128)(2,1)S(1)}, u32[]{:S(2)}) copy-start(bf16[8,256,256]{2,1,0:T(8,128)(2,1)S(1)} %collective-permute-done.1.rest_1_) | copy-start | bytes 3145732
  26.3 11.7 %collective-permute-start.5 = (bf16[8,256,256]{2,1,0:T(8,128)(2,1)S(1)}, bf16[8,256,256]{2,1,0:T(8,128)(2,1)S(1)}, u32[]{:S(2)}, u32[]{:S(2)}) collective-permute-start(bf16[8,256,256]{2,1,0:T(8,128)(2,1)S(1)} %collective-permute-done.rest_2_), channel_id=1, source_target_pairs={{0,4},{4,0},{8,12},{12,8},{1,5},{5,1},{9,13},{13,9},{2,6},{6,2},{1... | collective-permute-start | bytes 3145736 | tf_op jit(solution)/shard_map/ppermute | solution.py:173
  38.0 1.0 copy-start.12
  38.9 13.2 %collective-permute-start.6 = (bf16[256,1024]{1,0:T(8,128)(2,1)S(1)}, bf16[256,1024]{1,0:T(8,128)(2,1)S(1)}, u32[]{:S(2)}, u32[]{:S(2)}) collective-permute-start(bf16[256,1024]{1,0:T(8,128)(2,1)S(1)} %get-tuple-element.45), channel_id=1, source_target_pairs={{0,8},{4,12},{8,0},{12,4},{1,9},{5,13},{9,1},{13,5},{2,10},{6,14},... | collective-permute-start | bytes 1572872 | tf_op jit(solution)/shard_map/ppermute | solution.py:173
  39.5 12.9 %collective-permute-start.8 = (bf16[256,1024]{1,0:T(8,128)(2,1)S(1)}, bf16[256,1024]{1,0:T(8,128)(2,1)S(1)}, u32[]{:S(2)}, u32[]{:S(2)}) collective-permute-start(bf16[256,1024]{1,0:T(8,128)(2,1)S(1)} %get-tuple-element.47), channel_id=1, source_target_pairs={{0,16},{16,0},{1,17},{17,1},{2,18},{18,2},{3,19},{19,3},{4,20},{20... | collective-permute-start | bytes 1572872 | tf_op jit(solution)/shard_map/ppermute | solution.py:177
  52.4 35.1 %copy-start.3 = (bf16[512,1024]{1,0:T(8,128)(2,1)}, bf16[512,1024]{1,0:T(8,128)(2,1)S(1)}, u32[]{:S(2)}) copy-start(bf16[512,1024]{1,0:T(8,128)(2,1)S(1)} %pad_maximum_fusion.refs_1_) | copy-start | bytes 3145732
  52.5 35.7 %copy-start.21 = (s32[512,1]{0,1:T(1,128)S(1)}, s32[512,1]{0,1:T(1,128)}, u32[]{:S(2)}) copy-start(s32[512,1]{0,1:T(1,128)} %param.7) | copy-start | bytes 6148
  52.5 7.0 %collective-permute-start.9 = (bf16[512,1024]{1,0:T(8,128)(2,1)S(1)}, bf16[512,1024]{1,0:T(8,128)(2,1)S(1)}, u32[]{:S(2)}, u32[]{:S(2)}) collective-permute-start(bf16[512,1024]{1,0:T(8,128)(2,1)S(1)} %pad_maximum_fusion.refs_1_), channel_id=1, source_target_pairs={{0,4},{4,0},{8,12},{12,8},{1,5},{5,1},{9,13},{13,9},{2,6},{6,2},{1... | collective-permute-start | bytes 3145736 | tf_op jit(solution)/shard_map/ppermute | solution.py:173
  52.6 7.9 %collective-permute-start.10 = (bf16[512,1024]{1,0:T(8,128)(2,1)S(1)}, bf16[512,1024]{1,0:T(8,128)(2,1)S(1)}, u32[]{:S(2)}, u32[]{:S(2)}) collective-permute-start(bf16[512,1024]{1,0:T(8,128)(2,1)S(1)} %pad_maximum_fusion.1.refs_1_), channel_id=1, source_target_pairs={{0,4},{4,0},{8,12},{12,8},{1,5},{5,1},{9,13},{13,9},{2,6},{6,2},{1... | collective-permute-start | bytes 3145736 | tf_op jit(solution)/shard_map/ppermute | solution.py:173
  58.8 27.8 %collective-permute-start.12 = (bf16[256,2048]{1,0:T(8,128)(2,1)}, bf16[256,2048]{1,0:T(8,128)(2,1)S(1)}, u32[]{:S(2)}, u32[]{:S(2)}) collective-permute-start(bf16[256,2048]{1,0:T(8,128)(2,1)} %collective-permute-done.3), channel_id=1, source_target_pairs={{1,2},{2,1},{5,6},{6,5},{9,10},{10,9},{13,14},{14,13},{17,18},{18,... | collective-permute-start | bytes 3145736 | tf_op jit(solution)/shard_map/ppermute | solution.py:169
  59.5 1.0 copy-start.5
  60.5 27.0 %copy-start.1 = (bf16[512,1024]{1,0:T(8,128)(2,1)}, bf16[512,1024]{1,0:T(8,128)(2,1)S(1)}, u32[]{:S(2)}) copy-start(bf16[512,1024]{1,0:T(8,128)(2,1)S(1)} %collective-permute-done.10.refs_3_) | copy-start | bytes 3145732
  60.5 27.0 %collective-permute-start.11 = (bf16[512,1024]{1,0:T(8,128)(2,1)S(1)}, bf16[512,1024]{1,0:T(8,128)(2,1)}, u32[]{:S(2)}, u32[]{:S(2)}) collective-permute-start(bf16[512,1024]{1,0:T(8,128)(2,1)S(1)} %pad_maximum_fusion.refs_1_), channel_id=1, source_target_pairs={{0,8},{4,12},{8,0},{12,4},{1,9},{5,13},{9,1},{13,5},{2,10},{6,14},... | collective-permute-start | bytes 3145736 | tf_op jit(solution)/shard_map/ppermute | solution.py:173
  61.0 26.5 %collective-permute-start.14 = (bf16[512,1024]{1,0:T(8,128)(2,1)S(1)}, bf16[512,1024]{1,0:T(8,128)(2,1)}, u32[]{:S(2)}, u32[]{:S(2)}) collective-permute-start(bf16[512,1024]{1,0:T(8,128)(2,1)S(1)} %pad_maximum_fusion.1.refs_1_), channel_id=1, source_target_pairs={{0,16},{16,0},{1,17},{17,1},{2,18},{18,2},{3,19},{19,3},{4,20},{20... | collective-permute-start | bytes 3145736 | tf_op jit(solution)/shard_map/ppermute | solution.py:177
  62.6 23.1 %collective-permute-start.7 = (bf16[128,3072]{1,0:T(8,128)(2,1)S(1)}, bf16[128,3072]{1,0:T(8,128)(2,1)S(1)}, u32[]{:S(2)}, u32[]{:S(2)}) collective-permute-start(bf16[128,3072]{1,0:T(8,128)(2,1)S(1)} %slice_dynamic-update-slice_fusion.1), channel_id=1, source_target_pairs={{0,1},{3,2},{1,0},{2,3},{4,5},{7,6},{5,4},{6,7},{8,9},{11,10},{9,8... | collective-permute-start | bytes 2359304 | tf_op jit(solution)/shard_map/ppermute | solution.py:169
  85.7 1.9 %copy-start.18 = (bf16[128,3072]{1,0:T(8,128)(2,1)}, bf16[128,3072]{1,0:T(8,128)(2,1)S(1)}, u32[]{:S(2)}) copy-start(bf16[128,3072]{1,0:T(8,128)(2,1)S(1)} %collective-permute-done.7) | copy-start | bytes 2359300
  86.6 1.0 copy-start.14
  87.5 7.7 %collective-permute-start.13 = (bf16[512,1024]{1,0:T(8,128)(2,1)}, bf16[512,1024]{1,0:T(8,128)(2,1)}, u32[]{:S(2)}, u32[]{:S(2)}) collective-permute-start(bf16[512,1024]{1,0:T(8,128)(2,1)} %collective-permute-done.11.refs_2_), channel_id=1, source_target_pairs={{0,4},{4,0},{8,12},{12,8},{1,5},{5,1},{9,13},{13,9},{2,6},{6,2},{1... | collective-permute-start | bytes 3145736 | tf_op jit(solution)/shard_map/ppermute | solution.py:173
  87.6 7.7 %collective-permute-start.15 = (bf16[512,1024]{1,0:T(8,128)(2,1)}, bf16[512,1024]{1,0:T(8,128)(2,1)S(1)}, u32[]{:S(2)}, u32[]{:S(2)}) collective-permute-start(bf16[512,1024]{1,0:T(8,128)(2,1)} %collective-permute-done.14.refs_2_), channel_id=1, source_target_pairs={{0,4},{4,0},{8,12},{12,8},{1,5},{5,1},{9,13},{13,9},{2,6},{6,2},{1... | collective-permute-start | bytes 3145736 | tf_op jit(solution)/shard_map/ppermute | solution.py:173
  88.3 7.0 %copy-start.4 = (bf16[512,1024]{1,0:T(8,128)(2,1)S(1)}, bf16[512,1024]{1,0:T(8,128)(2,1)}, u32[]{:S(2)}) copy-start(bf16[512,1024]{1,0:T(8,128)(2,1)} %copy-done.3) | copy-start | bytes 3145732
  88.3 16.8 %collective-permute-start.18 = (bf16[128,2048]{1,0:T(8,128)(2,1)}, bf16[128,2048]{1,0:T(8,128)(2,1)S(1)}, u32[]{:S(2)}, u32[]{:S(2)}) collective-permute-start(bf16[128,2048]{1,0:T(8,128)(2,1)} %get-tuple-element.65), channel_id=1, source_target_pairs={{0,1},{3,2},{1,0},{2,3},{4,5},{7,6},{5,4},{6,7},{8,9},{11,10},{9,8... | collective-permute-start | bytes 1572872 | tf_op jit(solution)/shard_map/ppermute | solution.py:169
  94.5 19.5 %collective-permute-start.20 = (bf16[128,2048]{1,0:T(8,128)(2,1)}, bf16[128,2048]{1,0:T(8,128)(2,1)S(1)}, u32[]{:S(2)}, u32[]{:S(2)}) collective-permute-start(bf16[128,2048]{1,0:T(8,128)(2,1)} %slice.61), channel_id=1, source_target_pairs={{1,2},{2,1},{5,6},{6,5},{9,10},{10,9},{13,14},{14,13},{17,18},{18,... | collective-permute-start | bytes 1572872 | tf_op jit(solution)/shard_map/ppermute | solution.py:169
  95.3 1.2 copy-start.6
  101.0 1.2 copy-start.2
  101.0 1.5 %copy-start.15 = (bf16[256,2048]{1,0:T(8,128)(2,1)S(1)}, bf16[256,2048]{1,0:T(8,128)(2,1)}, u32[]{:S(2)}) copy-start(bf16[256,2048]{1,0:T(8,128)(2,1)} %copy-done.14) | copy-start | bytes 3145732
  101.1 11.4 %collective-permute-start.16 = (bf16[512,256]{1,0:T(8,128)(2,1)S(1)}, bf16[512,256]{1,0:T(8,128)(2,1)S(1)}, u32[]{:S(2)}, u32[]{:S(2)}) collective-permute-start(bf16[512,256]{1,0:T(8,128)(2,1)S(1)} %fusion.26), channel_id=1, source_target_pairs={{1,2},{2,1},{5,6},{6,5},{9,10},{10,9},{13,14},{14,13},{17,18},{18,... | collective-permute-start | bytes 786440 | tf_op jit(solution)/shard_map/ppermute | solution.py:169
  105.1 7.5 %copy-start.17 = (f32[512,256]{1,0:T(8,128)S(1)}, f32[512,256]{1,0:T(8,128)}, u32[]{:S(2)}) copy-start(f32[512,256]{1,0:T(8,128)} %get-tuple-element.88) | copy-start | bytes 1572868
  105.1 18.2 %collective-permute-start.21 = (bf16[256,1024]{1,0:T(8,128)(2,1)S(1)}, bf16[256,1024]{1,0:T(8,128)(2,1)S(1)}, u32[]{:S(2)}, u32[]{:S(2)}) collective-permute-start(bf16[256,1024]{1,0:T(8,128)(2,1)S(1)} %lend_far.3.rest_4_.refs_6_), channel_id=1, source_target_pairs={{1,0},{2,3},{5,4},{6,7},{9,8},{10,11},{13,12},{14,15},{17,16},{18,... | collective-permute-start | bytes 1572872 | tf_op jit(solution)/shard_map/ppermute | solution.py:169
  106.5 26.6 %slice-start = ((s8[16777216]{0:T(1024)(128)(4,1)}), s8[4194304]{0:T(1024)(128)(4,1)S(1)}, s32[]{:S(2)}) async-start(s8[16777216]{0:T(1024)(128)(4,1)} %bitcast.15), calls=%async_computation | async-start | bytes 8388608
  106.5 26.6 %slice-start.1 = ((s8[16777216]{0:T(1024)(128)(4,1)}), s8[4194304]{0:T(1024)(128)(4,1)S(1)}, s32[]{:S(2)}) async-start(s8[16777216]{0:T(1024)(128)(4,1)} %bitcast.15), calls=%async_computation.1 | async-start | bytes 8388608
  111.8 14.8 %collective-permute-start.19 = (bf16[128,2048]{1,0:T(8,128)(2,1)S(1)}, bf16[128,2048]{1,0:T(8,128)(2,1)S(1)}, u32[]{:S(2)}, u32[]{:S(2)}) collective-permute-start(bf16[128,2048]{1,0:T(8,128)(2,1)S(1)} %collective-permute-done.18), channel_id=1, source_target_pairs={{1,2},{2,1},{5,6},{6,5},{9,10},{10,9},{13,14},{14,13},{17,18},{18,... | collective-permute-start | bytes 1572872 | tf_op jit(solution)/shard_map/ppermute | solution.py:169
  112.7 17.8 %collective-permute-start.17 = (bf16[512,256]{1,0:T(8,128)(2,1)S(1)}, bf16[512,256]{1,0:T(8,128)(2,1)S(1)}, u32[]{:S(2)}, u32[]{:S(2)}) collective-permute-start(bf16[512,256]{1,0:T(8,128)(2,1)S(1)} %add_convert_fusion), channel_id=1, source_target_pairs={{1,0},{2,3},{5,4},{6,7},{9,8},{10,11},{13,12},{14,15},{17,16},{18,... | collective-permute-start | bytes 786440 | tf_op jit(solution)/shard_map/ppermute | solution.py:169
  123.2 9.9 %slice-start.2 = ((s8[16777216]{0:T(1024)(128)(4,1)}), s8[4194304]{0:T(1024)(128)(4,1)S(1)}, s32[]{:S(2)}) async-start(s8[16777216]{0:T(1024)(128)(4,1)} %bitcast.15), calls=%async_computation.2 | async-start | bytes 8388608
  125.4 15.3 %collective-permute-start.22 = (bf16[128,1024]{1,0:T(8,128)(2,1)S(1)}, bf16[128,1024]{1,0:T(8,128)(2,1)S(1)}, u32[]{:S(2)}, u32[]{:S(2)}) collective-permute-start(bf16[128,1024]{1,0:T(8,128)(2,1)S(1)} %lend_far.4.refs_6_), channel_id=1, source_target_pairs={{1,0},{2,3},{5,4},{6,7},{9,8},{10,11},{13,12},{14,15},{17,16},{18,... | collective-permute-start | bytes 786440 | tf_op jit(solution)/shard_map/ppermute | solution.py:169
  126.7 3.8 %copy-start.7 = (bf16[8,256,256]{2,1,0:T(8,128)(2,1)S(1)}, bf16[8,256,256]{2,1,0:T(8,128)(2,1)}, u32[]{:S(2)}) copy-start(bf16[8,256,256]{2,1,0:T(8,128)(2,1)} %rest_0_.1) | copy-start | bytes 3145732
  126.7 3.8 %copy-start.9 = (bf16[8,256,256]{2,1,0:T(8,128)(2,1)S(1)}, bf16[8,256,256]{2,1,0:T(8,128)(2,1)}, u32[]{:S(2)}) copy-start(bf16[8,256,256]{2,1,0:T(8,128)(2,1)} %copy-done.8) | copy-start | bytes 3145732
  126.7 3.8 %copy-start.11 = (bf16[8,256,256]{2,1,0:T(8,128)(2,1)S(1)}, bf16[8,256,256]{2,1,0:T(8,128)(2,1)}, u32[]{:S(2)}) copy-start(bf16[8,256,256]{2,1,0:T(8,128)(2,1)} %copy-done.10) | copy-start | bytes 3145732
  126.7 3.8 %copy-start.13 = (bf16[8,256,256]{2,1,0:T(8,128)(2,1)S(1)}, bf16[8,256,256]{2,1,0:T(8,128)(2,1)}, u32[]{:S(2)}) copy-start(bf16[8,256,256]{2,1,0:T(8,128)(2,1)} %copy-done.12) | copy-start | bytes 3145732
  126.7 6.4 %slice-start.3 = ((s8[16777216]{0:T(1024)(128)(4,1)}), s8[4194304]{0:T(1024)(128)(4,1)S(1)}, s32[]{:S(2)}) async-start(s8[16777216]{0:T(1024)(128)(4,1)} %bitcast.15), calls=%async_computation.3 | async-start | bytes 8388608
  128.9 11.1 %collective-permute-start.23 = (bf16[128,1024]{1,0:T(8,128)(2,1)S(1)}, bf16[128,1024]{1,0:T(8,128)(2,1)S(1)}, u32[]{:S(2)}, u32[]{:S(2)}) collective-permute-start(bf16[128,1024]{1,0:T(8,128)(2,1)S(1)} %lend_far.5), channel_id=1, source_target_pairs={{1,0},{2,3},{5,4},{6,7},{9,8},{10,11},{13,12},{14,15},{17,16},{18,... | collective-permute-start | bytes 786440 | tf_op jit(solution)/shard_map/ppermute | solution.py:169
  130.6 2.1 %copy-start.20 = (bf16[256,1024]{1,0:T(8,128)(2,1)S(1)}, bf16[256,1024]{1,0:T(8,128)(2,1)}, u32[]{:S(2)}) copy-start(bf16[256,1024]{1,0:T(8,128)(2,1)} %param.11) | copy-start | bytes 1572868
  132.7 1.0 copy-start.19
  132.7 1.8 %copy-start.22 = (f32[512,1024]{1,0:T(8,128)S(1)}, f32[512,1024]{1,0:T(8,128)}, u32[]{:S(2)}) copy-start(f32[512,1024]{1,0:T(8,128)} %fusion.17) | copy-start | bytes 6291460
